TPU v7x, 768 devices: a whole 4x8x12 slice. The times are simulated.
768 devices in a mesh: grp: 96 (over x, z, core), feat: 8 (over y).
Axes of the slice: x: 4, y: 8, z: 12, core: 2. Of those that a mesh axis runs over, the one named last changes fastest.
Arguments:
- feature_table: bfloat16 [196608, 4096], P(('grp', 'feat')), may hold values from -6 to 6
- sample_ids: int32 [98304], P(('grp', 'feat')), may hold values from 0 to 255
- block_ids: int32 [768, 4], P('grp'), may hold values from 0 to 7, as said below
- block_counts: int32 [768], P('grp'), may hold values from 1 to 4, as said below
- block_tiles: bfloat16 [768, 4, 128, 128], P('grp'), may hold values from 0.049804688 to 1
- weight: bfloat16 [4096, 1024], P('feat'), may hold values from -0.09375 to 0.09375
- target: bfloat16 [98304, 1024], P(('grp', 'feat')), may hold values from -6 to 6
Outputs:
- embedding: bfloat16 [98304, 1024], P(('grp', 'feat'))
- weight_grad: float32 [4096, 1024], P('feat')
Inputs may be any that keep to these rules, and one draw needn't show every extreme that they name: `block_ids`: each row's 4 entries are distinct block numbers within the row block's group. `block_counts`: in every group some row block has all 4 slots live.
All inputs are finite; a program needn't handle non-finite values.
Results may differ from a plain program's by a relative error of at most 0.019.
Values may be sent and summed in bfloat16 or wider, within the bound.
No kernel may reach another device: no remote copies, remote signals or barrier semaphores. Data moves between devices by JAX's collectives and lax.ppermute only.
A program may use at most 32 MiB of HBM per device.

v0:
```python
import jax
import jax.numpy as jnp
from jax import lax
from jax.sharding import PartitionSpec as P


def shards(feature_table, sample_ids, block_ids, block_counts, block_tiles, weight, target):
    picked = jnp.take(feature_table, sample_ids, axis=0)
    slices = lax.all_to_all(picked, "feat", split_axis=1, concat_axis=0, tiled=True)
    node_total, slice_width = slices.shape
    block_total, slot_total, block_rows, block_width = block_tiles.shape
    blocked = slices.reshape(block_total, block_rows, slice_width)
    live_mask = jnp.arange(slot_total, dtype=jnp.int32)[None, :] < block_counts[:, None]
    masked = jnp.where(live_mask[:, :, None, None], block_tiles, jnp.zeros((), jnp.bfloat16))
    neighbor_rows = blocked[block_ids]
    summed = jnp.einsum("rsij,rsjf->rif", masked, neighbor_rows, preferred_element_type=jnp.float32)
    degree = jnp.sum(masked.astype(jnp.float32), axis=(1, 3))
    aggregate = (summed / degree[:, :, None]).reshape(node_total, slice_width).astype(jnp.bfloat16)
    selected = aggregate
    preact = lax.psum_scatter(
        jnp.dot(selected, weight, preferred_element_type=jnp.float32).astype(jnp.bfloat16),
        "feat",
        scatter_dimension=0,
        tiled=True,
    ).astype(jnp.float32)
    sigmoid_part = jax.nn.sigmoid(preact)
    hidden = preact * sigmoid_part
    hidden_width = hidden.shape[1]
    scales = lax.rsqrt(jnp.mean(hidden * hidden, axis=1, keepdims=True) + 1e-05)
    embedding = (hidden * scales).astype(jnp.bfloat16)
    cotangent = (embedding.astype(jnp.float32) - target.astype(jnp.float32)) / node_total
    projected = jnp.sum(cotangent * hidden, axis=1, keepdims=True)
    grad_hidden = scales * cotangent - scales**3 / hidden_width * hidden * projected
    slope = sigmoid_part * (1.0 + preact * (1.0 - sigmoid_part))
    grad_pre = (grad_hidden * slope).astype(jnp.bfloat16)
    selected = aggregate
    folded = lax.dot_general(
        selected,
        lax.all_gather(grad_pre, "feat", axis=0, tiled=True),
        (((0,), (0,)), ((), ())),
        preferred_element_type=jnp.float32,
    )
    weight_grad = lax.psum(folded, "grp")
    return (embedding, weight_grad)


def solution(mesh):
    return jax.shard_map(
        shards,
        mesh=mesh,
        in_specs=(
            P(("grp", "feat"), None),
            P(("grp", "feat")),
            P("grp", None),
            P("grp"),
            P("grp", None, None, None),
            P("feat", None),
            P(("grp", "feat"), None),
        ),
        out_specs=(P(("grp", "feat"), None), P("feat", None)),
        check_vma=False,
    )
```

profile of v0, /device:TPU:1, one launch (start us, length us, event | category | flops | bytes accessed | tf_op | source)
XLA Modules:
  0.0 453.0 jit_solution(18422345387873470613)
XLA Ops:
  7.2 0.0 copy-start
  7.2 0.8 compare_and_fusion
  8.0 0.7 compare_select_fusion.1
  8.7 0.1 copy-done
  8.8 1.2 gather_fusion
  10.0 0.0 copy-start.3
  10.0 0.0 copy-start.5
  10.0 1.1 bitcast_select_fusion
  11.1 7.7 %all-to-all-start = ((bf16[128,8,512]{2,0,1:T(8,128)(2,1)}), bf16[128,8,512]{2,0,1:T(8,128)(2,1)S(1)}, u32[]{:S(2)}, u32[]{:S(2)}) async-start(bf16[128,8,512]{2,0,1:T(8,128)(2,1)} %bitcast_select_fusion), calls=%async_computation | async-start | bytes 2097152 | tf_op jit(solution)/shard_map/all_to_all | solution.py:9
  18.8 0.0 reduce-scatter.2.cloned.1.call-start
  18.8 0.1 copy.12
  18.9 0.1 reshape.71
  19.0 0.1 iota_compare_fusion
  19.1 1.6 convert_reduce_fusion
  20.7 23.0 %all-to-all-done = bf16[128,8,512]{2,0,1:T(8,128)(2,1)S(1)} async-done(((bf16[128,8,512]{2,0,1:T(8,128)(2,1)}), bf16[128,8,512]{2,0,1:T(8,128)(2,1)S(1)}, u32[]{:S(2)}, u32[]{:S(2)}) %all-to-all-start) | async-done | bytes 1048608 | tf_op jit(solution)/shard_map/all_to_all | solution.py:9
  43.7 2.8 gather_fusion.1
  46.4 3.4 fusion
  49.8 2.6 convolution_convert_fusion
  52.4 0.0 reduce-scatter.2.cloned.1.call-update
  52.4 0.0 all-gather.2.cloned.1.call-start
  52.4 48.6 %reduce-scatter.2.cloned.1.call-done = bf16[128,1024]{1,0:T(8,128)(2,1)} async-done(((bf16[1024,1024]{1,0:T(8,128)(2,1)}), bf16[128,1024]{1,0:T(8,128)(2,1)}) %reduce-scatter.2.cloned.1.call-update) | async-done | bytes 262160 | tf_op jit(solution)/shard_map/reduce_scatter | solution.py:20
  101.1 1.2 multiply_reduce_fusion.1
  102.3 1.3 multiply_reduce_fusion
  103.6 0.7 copy-done.2
  104.3 2.0 fusion.7
  106.3 0.0 all-gather.2.cloned.1.call-update
  106.3 0.0 all-reduce.2.cloned.1.call-start
  106.4 46.3 %all-gather.2.cloned.1.call-done = bf16[1024,1024]{1,0:T(8,128)(2,1)} async-done(((bf16[128,1024]{1,0:T(8,128)(2,1)}), bf16[1024,1024]{1,0:T(8,128)(2,1)}) %all-gather.2.cloned.1.call-update) | async-done | bytes 2097168 | tf_op jit(solution)/shard_map/all_gather | solution.py:39
  152.6 4.2 fusion.11
  156.8 0.0 all-reduce.2.cloned.1.call-update
  156.8 286.5 %all-reduce.2.cloned.1.call-done = f32[512,1024]{1,0:T(8,128)} async-done(((f32[512,1024]{1,0:T(8,128)}), f32[512,1024]{1,0:T(8,128)}) %all-reduce.2.cloned.1.call-update) | async-done | bytes 2097168 | tf_op jit(solution)/shard_map/psum | solution.py:43
  443.3 3.2 copy.17
  (12 shorter events, 0.1 us)
Async XLA Ops:
  7.2 1.6 copy-start
  10.0 8.9 %copy-start.3 = (s32[8,4]{0,1:T(4,128)S(1)}, s32[8,4]{0,1:T(4,128)}, u32[]{:S(2)}) copy-start(s32[8,4]{0,1:T(4,128)} %param.9) | copy-start | bytes 388
  10.0 9.0 %copy-start.5 = (s32[8]{0:T(128)S(1)}, s32[8]{0:T(128)}, u32[]{:S(2)}) copy-start(s32[8]{0:T(128)} %param.10) | copy-start | bytes 100
  11.1 32.5 %all-to-all-start = ((bf16[128,8,512]{2,0,1:T(8,128)(2,1)}), bf16[128,8,512]{2,0,1:T(8,128)(2,1)S(1)}, u32[]{:S(2)}, u32[]{:S(2)}) async-start(bf16[128,8,512]{2,0,1:T(8,128)(2,1)} %bitcast_select_fusion), calls=%async_computation | async-start | bytes 2097152 | tf_op jit(solution)/shard_map/all_to_all | solution.py:9
  18.8 82.3 %reduce-scatter.2.cloned.1.call-start = ((), (), s32[]{:S(2)}) async-start(), calls=%async_computation.2 | async-start | bytes 2359296 | tf_op jit(solution)/shard_map/reduce_scatter | solution.py:20
  46.4 3.4 copy-start.4
  52.4 49.9 %copy-start.1 = (bf16[128,1024]{1,0:T(8,128)(2,1)S(1)}, bf16[128,1024]{1,0:T(8,128)(2,1)}, u32[]{:S(2)}) copy-start(bf16[128,1024]{1,0:T(8,128)(2,1)} %param.13) | copy-start | bytes 786436
  52.4 100.3 %all-gather.2.cloned.1.call-start = ((), (), s32[]{:S(2)}) async-start(), calls=%async_computation.3 | async-start | bytes 2359296 | tf_op jit(solution)/shard_map/all_gather | solution.py:39
  103.6 0.7 copy-start.2
  106.3 337.0 %all-reduce.2.cloned.1.call-start = ((), (), s32[]{:S(2)}) async-start(), calls=%async_computation.4 | async-start | bytes 4194304 | tf_op jit(solution)/shard_map/psum | solution.py:43
Sparse Core Ops, SparseCore 0:
  52.5 48.5 reduce-scatter.1
  106.4 46.1 all-gather.1
  157.0 286.3 all-reduce.1
where the time goes:
time: 453 us
  waiting for transfers between devices  404 us (89%)
  between operations  13.8 us (3%)
  matrix products  10.1 us (2%)
  other arithmetic  8.77 us (2%)
  local copies, waits for them, and re-layouts  8.11 us (2%)
  starting transfers between devices  7.77 us (2%)
    psum x1, waiting for transfers between devices, shards(): weight_grad = lax.psum(folded, 'grp')  287 us
    reduce_scatter x1, waiting for transfers between devices, shards(): lax.psum_scatter(jnp.dot(selected, weight, preferred_element_type=jnp.flo...  48.6 us
    all_gather x1, waiting for transfers between devices, shards(): lax.all_gather(grad_pre, 'feat', axis=0, tiled=True)  46.3 us
    all_to_all x1, waiting for transfers between devices, shards(): lax.all_to_all(picked, 'feat', split_axis=1, concat_axis=0, tiled=True)  23 us
  transfers between devices with their start and end apart: 4, of which 4 were waited for; matrix products, arithmetic and copies ran while one was open for 0% of the time, Pallas kernels for 0%

commit v1 on v0

v1 whole, which is shorter than its diff:
```python
import jax
import jax.numpy as jnp
from jax import lax
from jax.sharding import Mesh, PartitionSpec as P

GRP = ("x", "zo", "zi", "core")
ALL = GRP + ("feat",)


def exchange_sum(parts, axis):
    got = lax.all_to_all(parts, axis, 0, 0)
    return jnp.sum(got.astype(jnp.float32), axis=0)


def group_sum(term):
    rows, cols = term.shape
    with jax.named_scope("sum_core"):
        part = exchange_sum(term.astype(jnp.bfloat16).reshape(2, rows // 2, cols), "core")
    with jax.named_scope("sum_x"):
        part = exchange_sum(part.astype(jnp.bfloat16).reshape(4, rows // 8, cols), "x")
    with jax.named_scope("sum_zi"):
        part = exchange_sum(part.astype(jnp.bfloat16).reshape(4, rows // 32, cols), "zi")
    with jax.named_scope("sum_zo"):
        part = jnp.sum(lax.all_gather(part, "zo"), axis=0).astype(jnp.bfloat16)
    with jax.named_scope("gather_zi"):
        part = lax.all_gather(part, "zi", axis=0, tiled=True)
    with jax.named_scope("gather_x"):
        part = lax.all_gather(part, "x", axis=0, tiled=True)
    with jax.named_scope("gather_core"):
        other = lax.ppermute(part, "core", [(0, 1), (1, 0)])
        mine = lax.axis_index("core")
        both = jnp.stack([jnp.where(mine == 0, part, other), jnp.where(mine == 0, other, part)])
    return both.reshape(rows, cols).astype(jnp.float32)


def ring_gather(block):
    n = 8
    to_right = [(i, (i + 1) % n) for i in range(n)]
    to_left = [(i, (i - 1) % n) for i in range(n)]
    held = {0: block}
    for k in range(1, 5):
        held[k] = lax.ppermute(held[k - 1], "feat", to_right)
        if k < 4:
            held[n - k] = lax.ppermute(held[(n - k + 1) % n], "feat", to_left)
    return [held[k] for k in range(n)]


def shards(feature_table, sample_ids, block_ids, block_counts, block_tiles, weight, target):
    with jax.named_scope("pick"):
        picked = feature_table.at[sample_ids].get(mode="promise_in_bounds")
        slices = lax.all_to_all(picked, "feat", split_axis=1, concat_axis=0, tiled=True)
    node_total, slice_width = slices.shape
    block_total, slot_total, block_rows, block_width = block_tiles.shape
    with jax.named_scope("aggregate"):
        blocked = slices.reshape(block_total, block_rows, slice_width)
        live_mask = jnp.arange(slot_total, dtype=jnp.int32)[None, :] < block_counts[:, None]
        masked = jnp.where(live_mask[:, :, None, None], block_tiles, jnp.zeros((), jnp.bfloat16))
        neighbor_rows = blocked.at[block_ids].get(mode="promise_in_bounds")
        summed = jnp.einsum("rsij,rsjf->rif", masked, neighbor_rows, preferred_element_type=jnp.float32)
        degree = jnp.sum(masked.astype(jnp.float32), axis=(1, 3))
        aggregate = (summed / degree[:, :, None]).reshape(node_total, slice_width).astype(jnp.bfloat16)
    with jax.named_scope("preact"):
        partial = jnp.dot(aggregate, weight, preferred_element_type=jnp.float32).astype(jnp.bfloat16)
        preact = exchange_sum(partial.reshape(block_total, block_rows, -1), "feat")
    with jax.named_scope("grad"):
        sigmoid_part = jax.nn.sigmoid(preact)
        hidden = preact * sigmoid_part
        hidden_width = hidden.shape[1]
        scales = lax.rsqrt(jnp.mean(hidden * hidden, axis=1, keepdims=True) + 1e-05)
        embedding = (hidden * scales).astype(jnp.bfloat16)
        cotangent = (embedding.astype(jnp.float32) - target.astype(jnp.float32)) / node_total
        projected = jnp.sum(cotangent * hidden, axis=1, keepdims=True)
        grad_hidden = scales * cotangent - scales**3 / hidden_width * hidden * projected
        slope = sigmoid_part * (1.0 + preact * (1.0 - sigmoid_part))
        grad_pre = (grad_hidden * slope).astype(jnp.bfloat16)
    with jax.named_scope("fold"):
        order = (lax.axis_index("feat") - jnp.arange(block_total)) % block_total
        turned = aggregate.reshape(block_total, block_rows, slice_width).at[order].get(mode="promise_in_bounds")
        folded = lax.dot_general(
            turned.reshape(node_total, slice_width),
            jnp.concatenate(ring_gather(grad_pre), axis=0),
            (((0,), (0,)), ((), ())),
            preferred_element_type=jnp.float32,
        )
    weight_grad = group_sum(folded)
    return (embedding, weight_grad)


def solution(mesh):
    fine = Mesh(mesh.devices.reshape(4, 3, 4, 2, 8), ALL)
    return jax.shard_map(
        shards,
        mesh=fine,
        in_specs=(
            P(ALL, None),
            P(ALL),
            P(GRP, None),
            P(GRP),
            P(GRP, None, None, None),
            P("feat", None),
            P(ALL, None),
        ),
        out_specs=(P(ALL, None), P("feat", None)),
        check_vma=False,
    )
```

time: 453 us -> 244 us (0.54)
  waiting for transfers between devices: 404 us -> 39 us
  blocking collectives: 0 us -> 128 us
  starting transfers between devices: 7.77 us -> 42.4 us
  between operations: 13.8 us -> 0.88 us
  local copies, waits for them, and re-layouts: 8.11 us -> 17.9 us
    psum x1 -> x0, waiting for transfers between devices: 287 us -> none  [shards(): weight_grad = lax.psum(folded, 'grp')]
    all_to_all x0 -> x4, blocking collectives: none -> 87.5 us  [exchange_sum(): got = lax.all_to_all(parts, axis, 0, 0)]
    reduce_scatter x1 -> x0, waiting for transfers between devices: 48.6 us -> none  [shards(): lax.psum_scatter(jnp.dot(selected, weight, preferred_element_type=jnp.flo...]
    all_gather x1 -> x0, waiting for transfers between devices: 46.3 us -> none  [shards(): lax.all_gather(grad_pre, 'feat', axis=0, tiled=True)]
    all_gather x0 -> x3, blocking collectives: none -> 40.6 us  [the longest x1 19.5 us: group_sum(): part = jnp.sum(lax.all_gather(part, 'zo'), axis=0).astype(jnp.bfloat16)]
    ppermute x0 -> x8, starting transfers between devices: none -> 34.7 us  [the longest x3 13.7 us: ring_gather(): held[n - k] = lax.ppermute(held[(n - k + 1) % n], 'feat', to_left)]
    ppermute x0 -> x8, waiting for transfers between devices: none -> 16 us  [the longest x4 12.4 us: ring_gather(): held[k] = lax.ppermute(held[k - 1], 'feat', to_right)]
    unnamed x13 -> x22, local copies, waits for them, and re-layouts: 4 us -> 9.26 us
  transfers between devices with their start and end apart: 4 -> 9, of which waited for: 4 -> 6; matrix products, arithmetic and copies ran while one was open for 0% -> 4% of each run, Pallas kernels for 0% -> 0%
where the time goes in v1:
time: 244 us; the launch traced here: 243 us
  blocking collectives  128 us (52%)
  starting transfers between devices  42.4 us (17%)
  waiting for transfers between devices  39 us (16%)
  local copies, waits for them, and re-layouts  17.9 us (7%)
  other arithmetic  7.54 us (3%)
  matrix products  7.46 us (3%)
    all_to_all x4, blocking collectives, exchange_sum(): got = lax.all_to_all(parts, axis, 0, 0)  87.5 us
    all_to_all x1, waiting for transfers between devices, shards(): lax.all_to_all(picked, 'feat', split_axis=1, concat_axis=0, tiled=True)  23 us
    all_gather x1, blocking collectives, group_sum(): part = jnp.sum(lax.all_gather(part, 'zo'), axis=0).astype(jnp.bfloat16)  19.5 us
    ppermute x3, starting transfers between devices, ring_gather(): held[n - k] = lax.ppermute(held[(n - k + 1) % n], 'feat', to_left)  13.7 us
    ppermute x1, starting transfers between devices, group_sum(): other = lax.ppermute(part, 'core', [(0, 1), (1, 0)])  13 us
    ppermute x4, waiting for transfers between devices, ring_gather(): held[k] = lax.ppermute(held[k - 1], 'feat', to_right)  12.4 us
    all_gather x1, blocking collectives, group_sum(): part = lax.all_gather(part, 'zi', axis=0, tiled=True)  10.9 us
    all_gather x1, blocking collectives, group_sum(): part = lax.all_gather(part, 'x', axis=0, tiled=True)  10.2 us
  transfers between devices with their start and end apart: 9, of which 6 were waited for; matrix products, arithmetic and copies ran while one was open for 4% of the time, Pallas kernels for 0%

profile of v1, /device:TPU:1, one launch (start us, length us, event | category | flops | bytes accessed | tf_op | source)
XLA Modules:
  0.0 243.3 jit_solution(3345116665639596898)
XLA Ops:
  4.5 7.7 %all-to-all-start = ((bf16[128,8,512]{2,0,1:T(8,128)(2,1)}), bf16[128,8,512]{2,0,1:T(8,128)(2,1)S(1)}, u32[]{:S(2)}, u32[]{:S(2)}) async-start(bf16[128,8,512]{2,0,1:T(8,128)(2,1)} %bitcast.34), calls=%async_computation | async-start | bytes 2097152 | tf_op jit(solution)/shard_map/pick/all_to_all | solution.py:51
  12.5 1.6 convert_reduce_fusion.1
  14.0 23.0 %all-to-all-done = bf16[128,8,512]{2,0,1:T(8,128)(2,1)S(1)} async-done(((bf16[128,8,512]{2,0,1:T(8,128)(2,1)}), bf16[128,8,512]{2,0,1:T(8,128)(2,1)S(1)}, u32[]{:S(2)}, u32[]{:S(2)}) %all-to-all-start) | async-done | bytes 1048608 | tf_op jit(solution)/shard_map/pick/all_to_all | solution.py:51
  37.1 2.7 %gather_fusion.1 = bf16[32,128,512]{2,1,0:T(8,128)(2,1)} fusion(bf16[8,128,512]{2,1,0:T(8,128)(2,1)S(1)} %bitcast.32, s32[1024]{0:T(1024)S(1)} %pad_clamp_fusion.1), kind=kCustom, calls=%fused_computation.1 | custom fusion | bytes 8388736 | tf_op jit(solution)/shard_map/aggregate/gather | solution.py:58
  39.8 3.4 %fusion = bf16[8,128,512]{2,1,0:T(8,128)(2,1)S(1)} fusion(bf16[8,4,128,512]{3,2,1,0:T(8,128)(2,1)} %bitcast.36, f32[8,128]{1,0:T(8,128)S(1)} %convert_reduce_fusion.1, bf16[8,4,128,128]{3,2,1,0:T(8,128)(2,1)} %param.11, pred[8,4]{1,0:T(8,128)(4,1)S(1)} %iota_compare_fusion), kind=kOutput, calls=%fused_computation.5 | convolution fusion | flops 538443776 | bytes 6295584 | tf_op jit(solution)/shard_map/aggregate/rsij,rsjf->rif/dot_general | solution.py:59
  44.5 47.8 %all_to_all.36 = bf16[8,128,1024]{2,1,0:T(8,128)(2,1)S(1)} all-to-all(bf16[8,128,1024]{2,1,0:T(8,128)(2,1)S(1)} %bitcast.38), channel_id=1, replica_groups=mesh['x'=4,'zo'=3,'zi'=4,'core'=2,'feat'=8] {'feat'}, dimensions={0} | all-to-all | bytes 4194304 | tf_op jit(solution)/shard_map/preact/all_to_all | solution.py:11
  94.7 2.3 collective-permute-start
  97.0 6.0 %collective-permute-done = bf16[128,1024]{1,0:T(8,128)(2,1)S(1)} collective-permute-done((bf16[128,1024]{1,0:T(8,128)(2,1)S(1)}, bf16[128,1024]{1,0:T(8,128)(2,1)S(1)}, u32[]{:S(2)}, u32[]{:S(2)}) %collective-permute-start) | collective-permute-done | bytes 262176 | tf_op jit(solution)/shard_map/fold/ppermute | solution.py:42
  103.0 1.9 collective-permute-start.1
  104.9 4.6 %collective-permute-start.4 = (bf16[128,1024]{1,0:T(8,128)(2,1)S(1)}, bf16[128,1024]{1,0:T(8,128)(2,1)}, u32[]{:S(2)}, u32[]{:S(2)}) collective-permute-start(bf16[128,1024]{1,0:T(8,128)(2,1)S(1)} %get-tuple-element.3), channel_id=1, source_target_pairs={{0,7},{1,0},{2,1},{3,2},{4,3},{5,4},{6,5},{7,6},{8,15},{9,8},{10,9... | collective-permute-start | bytes 786440 | tf_op jit(solution)/shard_map/fold/ppermute | solution.py:44
  109.5 3.6 %collective-permute-done.1 = bf16[128,1024]{1,0:T(8,128)(2,1)} collective-permute-done((bf16[128,1024]{1,0:T(8,128)(2,1)S(1)}, bf16[128,1024]{1,0:T(8,128)(2,1)}, u32[]{:S(2)}, u32[]{:S(2)}) %collective-permute-start.1) | collective-permute-done | bytes 262176 | tf_op jit(solution)/shard_map/fold/ppermute | solution.py:42
  113.1 1.9 collective-permute-start.2
  115.0 4.6 %collective-permute-start.5 = (bf16[128,1024]{1,0:T(8,128)(2,1)}, bf16[128,1024]{1,0:T(8,128)(2,1)}, u32[]{:S(2)}, u32[]{:S(2)}) collective-permute-start(bf16[128,1024]{1,0:T(8,128)(2,1)} %collective-permute-done.4), channel_id=1, source_target_pairs={{0,7},{1,0},{2,1},{3,2},{4,3},{5,4},{6,5},{7,6},{8,15},{9,8},{10,9... | collective-permute-start | bytes 786440 | tf_op jit(solution)/shard_map/fold/ppermute | solution.py:44
  119.6 1.8 gather_fusion.2
  121.4 2.8 %collective-permute-done.2 = bf16[128,1024]{1,0:T(8,128)(2,1)} collective-permute-done((bf16[128,1024]{1,0:T(8,128)(2,1)}, bf16[128,1024]{1,0:T(8,128)(2,1)}, u32[]{:S(2)}, u32[]{:S(2)}) %collective-permute-start.2) | collective-permute-done | bytes 262176 | tf_op jit(solution)/shard_map/fold/ppermute | solution.py:42
  124.2 1.9 collective-permute-start.3
  126.1 1.7 constant_dynamic-update-slice_fusion.6
  127.8 4.6 %collective-permute-start.6 = (bf16[128,1024]{1,0:T(8,128)(2,1)}, bf16[128,1024]{1,0:T(8,128)(2,1)S(1)}, u32[]{:S(2)}, u32[]{:S(2)}) collective-permute-start(bf16[128,1024]{1,0:T(8,128)(2,1)} %collective-permute-done.5), channel_id=1, source_target_pairs={{0,7},{1,0},{2,1},{3,2},{4,3},{5,4},{6,5},{7,6},{8,15},{9,8},{10,9... | collective-permute-start | bytes 786440 | tf_op jit(solution)/shard_map/fold/ppermute | solution.py:44
  132.4 1.7 constant_dynamic-update-slice_fusion.5
  134.1 1.7 constant_dynamic-update-slice_fusion.4
  136.5 2.1 collective-permute-done.6
  139.3 1.7 constant_dynamic-update-slice_fusion.1
  140.9 1.7 constant_dynamic-update-slice_fusion
  142.6 2.9 %convolution_convert_fusion.1 = bf16[512,1024]{1,0:T(8,128)(2,1)S(1)} fusion(bf16[1024,512]{1,0:T(8,128)(2,1)S(1)} %bitcast.35, bf16[1024,1024]{1,0:T(8,128)(2,1)} %constant_dynamic-update-slice_fusion), kind=kOutput, calls=%fused_computation.8 | convolution fusion | flops 1074266112 | bytes 4194304 | tf_op jit(solution)/shard_map/fold/dot_general | solution.py:79
  145.5 14.9 %all_to_all.37 = bf16[2,256,1024]{2,1,0:T(8,128)(2,1)S(1)} all-to-all(bf16[2,256,1024]{2,1,0:T(8,128)(2,1)S(1)} %bitcast.37), channel_id=1, replica_groups=mesh['x'=4,'zo'=3,'zi'=4,'core'=2,'feat'=8] {'core'}, dimensions={0} | all-to-all | bytes 2097152 | tf_op jit(solution)/shard_map/sum_core/all_to_all | solution.py:11
  161.5 13.2 %all_to_all.38 = bf16[4,64,1024]{2,1,0:T(8,128)(2,1)S(1)} all-to-all(bf16[4,64,1024]{2,1,0:T(8,128)(2,1)} %bitcast.39), channel_id=1, replica_groups=mesh['x'=4,'zo'=3,'zi'=4,'core'=2,'feat'=8] {'x'}, dimensions={0} | all-to-all | bytes 1048576 | tf_op jit(solution)/shard_map/sum_x/all_to_all | solution.py:11
  174.8 11.5 %all_to_all.39 = bf16[4,16,1024]{2,1,0:T(8,128)(2,1)S(1)} all-to-all(bf16[4,16,1024]{2,1,0:T(8,128)(2,1)S(1)} %bitcast.42), channel_id=1, replica_groups=mesh['x'=4,'zo'=3,'zi'=4,'core'=2,'feat'=8] {'zi'}, dimensions={0} | all-to-all | bytes 262144 | tf_op jit(solution)/shard_map/sum_zi/all_to_all | solution.py:11
  186.3 19.5 %all-gather = f32[48,1024]{1,0:T(8,128)S(1)} all-gather(f32[16,1024]{1,0:T(8,128)S(1)} %convert_reduce_fusion.2), channel_id=2, replica_groups=mesh['x'=4,'zo'=3,'zi'=4,'core'=2,'feat'=8] {'zo'}, dimensions={0}, use_global_device_ids=true | all-gather | bytes 262144 | tf_op jit(solution)/shard_map/sum_zo/all_gather | solution.py:24
  205.9 10.9 %all_gather.14 = bf16[64,1024]{1,0:T(8,128)(2,1)S(1)} all-gather(bf16[16,1024]{1,0:T(8,128)(2,1)S(1)} %reduce_sum.85), channel_id=1, replica_groups=mesh['x'=4,'zo'=3,'zi'=4,'core'=2,'feat'=8] {'zi'}, dimensions={0}, use_global_device_ids=true | all-gather | bytes 163840 | tf_op jit(solution)/shard_map/gather_zi/all_gather | solution.py:26
  216.8 10.2 %all_gather.15 = bf16[256,1024]{1,0:T(8,128)(2,1)S(1)} all-gather(bf16[64,1024]{1,0:T(8,128)(2,1)S(1)} %all_gather.14), channel_id=1, replica_groups=mesh['x'=4,'zo'=3,'zi'=4,'core'=2,'feat'=8] {'x'}, dimensions={0}, use_global_device_ids=true | all-gather | bytes 655360 | tf_op jit(solution)/shard_map/gather_x/all_gather | solution.py:28
  227.0 13.0 %collective-permute-start.7 = (bf16[256,1024]{1,0:T(8,128)(2,1)S(1)}, bf16[256,1024]{1,0:T(8,128)(2,1)S(1)}, u32[]{:S(2)}, u32[]{:S(2)}) collective-permute-start(bf16[256,1024]{1,0:T(8,128)(2,1)S(1)} %all_gather.15), channel_id=1, source_target_pairs={{0,8},{8,0},{1,9},{9,1},{2,10},{10,2},{3,11},{11,3},{4,12},{12,4},... | collective-permute-start | bytes 1572872 | tf_op jit(solution)/shard_map/gather_core/ppermute | solution.py:30
  241.7 1.6 bitcast_convert_fusion
  (45 shorter events, 12.1 us)
Async XLA Ops:
  0.6 1.6 copy-start
  3.4 8.7 %copy-start.5 = (s32[8,4]{0,1:T(4,128)S(1)}, s32[8,4]{0,1:T(4,128)}, u32[]{:S(2)}) copy-start(s32[8,4]{0,1:T(4,128)} %param.9) | copy-start | bytes 388
  3.4 8.9 %copy-start.7 = (s32[8]{0:T(128)S(1)}, s32[8]{0:T(128)}, u32[]{:S(2)}) copy-start(s32[8]{0:T(128)} %param.10) | copy-start | bytes 100
  4.5 32.5 %all-to-all-start = ((bf16[128,8,512]{2,0,1:T(8,128)(2,1)}), bf16[128,8,512]{2,0,1:T(8,128)(2,1)S(1)}, u32[]{:S(2)}, u32[]{:S(2)}) async-start(bf16[128,8,512]{2,0,1:T(8,128)(2,1)} %bitcast.34), calls=%async_computation | async-start | bytes 2097152 | tf_op jit(solution)/shard_map/pick/all_to_all | solution.py:51
  39.8 3.4 %copy-start.6 = (bf16[512,1024]{1,0:T(8,128)(2,1)S(1)}, bf16[512,1024]{1,0:T(8,128)(2,1)}, u32[]{:S(2)}) copy-start(bf16[512,1024]{1,0:T(8,128)(2,1)} %param.12) | copy-start | bytes 3145732
  43.2 1.3 copy-start.3
  92.3 1.0 copy-start.1
  93.6 34.2 %copy-start.2 = (bf16[128,1024]{1,0:T(8,128)(2,1)}, bf16[128,1024]{1,0:T(8,128)(2,1)S(1)}, u32[]{:S(2)}) copy-start(bf16[128,1024]{1,0:T(8,128)(2,1)S(1)} %get-tuple-element.7) | copy-start | bytes 786436
  94.7 8.3 %collective-permute-start = (bf16[128,1024]{1,0:T(8,128)(2,1)S(1)}, bf16[128,1024]{1,0:T(8,128)(2,1)S(1)}, u32[]{:S(2)}, u32[]{:S(2)}) collective-permute-start(bf16[128,1024]{1,0:T(8,128)(2,1)S(1)} %get-tuple-element.3), channel_id=1, source_target_pairs={{0,1},{1,2},{2,3},{3,4},{4,5},{5,6},{6,7},{7,0},{8,9},{9,10},{10,1... | collective-permute-start | bytes 786440 | tf_op jit(solution)/shard_map/fold/ppermute | solution.py:42
  103.0 16.6 %copy-start.4 = (bf16[128,1024]{1,0:T(8,128)(2,1)}, bf16[128,1024]{1,0:T(8,128)(2,1)S(1)}, u32[]{:S(2)}) copy-start(bf16[128,1024]{1,0:T(8,128)(2,1)S(1)} %collective-permute-done) | copy-start | bytes 786436
  103.0 10.1 %collective-permute-start.1 = (bf16[128,1024]{1,0:T(8,128)(2,1)S(1)}, bf16[128,1024]{1,0:T(8,128)(2,1)}, u32[]{:S(2)}, u32[]{:S(2)}) collective-permute-start(bf16[128,1024]{1,0:T(8,128)(2,1)S(1)} %collective-permute-done), channel_id=1, source_target_pairs={{0,1},{1,2},{2,3},{3,4},{4,5},{5,6},{6,7},{7,0},{8,9},{9,10},{10,1... | collective-permute-start | bytes 786440 | tf_op jit(solution)/shard_map/fold/ppermute | solution.py:42
  104.9 10.1 %collective-permute-start.4 = (bf16[128,1024]{1,0:T(8,128)(2,1)S(1)}, bf16[128,1024]{1,0:T(8,128)(2,1)}, u32[]{:S(2)}, u32[]{:S(2)}) collective-permute-start(bf16[128,1024]{1,0:T(8,128)(2,1)S(1)} %get-tuple-element.3), channel_id=1, source_target_pairs={{0,7},{1,0},{2,1},{3,2},{4,3},{5,4},{6,5},{7,6},{8,15},{9,8},{10,9... | collective-permute-start | bytes 786440 | tf_op jit(solution)/shard_map/fold/ppermute | solution.py:44
  113.1 11.1 %collective-permute-start.2 = (bf16[128,1024]{1,0:T(8,128)(2,1)}, bf16[128,1024]{1,0:T(8,128)(2,1)}, u32[]{:S(2)}, u32[]{:S(2)}) collective-permute-start(bf16[128,1024]{1,0:T(8,128)(2,1)} %collective-permute-done.1), channel_id=1, source_target_pairs={{0,1},{1,2},{2,3},{3,4},{4,5},{5,6},{6,7},{7,0},{8,9},{9,10},{10,1... | collective-permute-start | bytes 786440 | tf_op jit(solution)/shard_map/fold/ppermute | solution.py:42
  115.0 12.8 %collective-permute-start.5 = (bf16[128,1024]{1,0:T(8,128)(2,1)}, bf16[128,1024]{1,0:T(8,128)(2,1)}, u32[]{:S(2)}, u32[]{:S(2)}) collective-permute-start(bf16[128,1024]{1,0:T(8,128)(2,1)} %collective-permute-done.4), channel_id=1, source_target_pairs={{0,7},{1,0},{2,1},{3,2},{4,3},{5,4},{6,5},{7,6},{8,15},{9,8},{10,9... | collective-permute-start | bytes 786440 | tf_op jit(solution)/shard_map/fold/ppermute | solution.py:44
  124.2 11.5 %collective-permute-start.3 = (bf16[128,1024]{1,0:T(8,128)(2,1)}, bf16[128,1024]{1,0:T(8,128)(2,1)S(1)}, u32[]{:S(2)}, u32[]{:S(2)}) collective-permute-start(bf16[128,1024]{1,0:T(8,128)(2,1)} %collective-permute-done.2), channel_id=1, source_target_pairs={{0,1},{1,2},{2,3},{3,4},{4,5},{5,6},{6,7},{7,0},{8,9},{9,10},{10,1... | collective-permute-start | bytes 786440 | tf_op jit(solution)/shard_map/fold/ppermute | solution.py:42
  127.8 10.7 %collective-permute-start.6 = (bf16[128,1024]{1,0:T(8,128)(2,1)}, bf16[128,1024]{1,0:T(8,128)(2,1)S(1)}, u32[]{:S(2)}, u32[]{:S(2)}) collective-permute-start(bf16[128,1024]{1,0:T(8,128)(2,1)} %collective-permute-done.5), channel_id=1, source_target_pairs={{0,7},{1,0},{2,1},{3,2},{4,3},{5,4},{6,5},{7,6},{8,15},{9,8},{10,9... | collective-permute-start | bytes 786440 | tf_op jit(solution)/shard_map/fold/ppermute | solution.py:44
  227.0 14.5 %collective-permute-start.7 = (bf16[256,1024]{1,0:T(8,128)(2,1)S(1)}, bf16[256,1024]{1,0:T(8,128)(2,1)S(1)}, u32[]{:S(2)}, u32[]{:S(2)}) collective-permute-start(bf16[256,1024]{1,0:T(8,128)(2,1)S(1)} %all_gather.15), channel_id=1, source_target_pairs={{0,8},{8,0},{1,9},{9,1},{2,10},{10,2},{3,11},{11,3},{4,12},{12,4},... | collective-permute-start | bytes 1572872 | tf_op jit(solution)/shard_map/gather_core/ppermute | solution.py:30

commit v2 on v1

v2 whole, which is shorter than its diff:
```python
import jax
import jax.numpy as jnp
from jax import lax
from jax.experimental import pallas as pl
from jax.experimental.pallas import tpu as pltpu
from jax.sharding import Mesh, PartitionSpec as P

GRP = ("x", "zo", "zi", "core")
ALL = GRP + ("feat",)
SWAP = [(0, 1), (1, 0)]


def exchange_sum(parts, axis):
    got = lax.all_to_all(parts, axis, 0, 0)
    return jnp.sum(got.astype(jnp.float32), axis=0)


def group_sum(term):
    rows, cols = term.shape
    with jax.named_scope("sum_x_zi"):
        part = exchange_sum(term.reshape(16, rows // 16, cols), ("x", "zi"))
    with jax.named_scope("sum_zo"):
        part = jnp.sum(lax.all_gather(part, "zo"), axis=0).astype(jnp.bfloat16)
    with jax.named_scope("gather_zi"):
        part = lax.all_gather(part, "zi", axis=0, tiled=True)
    with jax.named_scope("gather_x"):
        part = lax.all_gather(part, "x", axis=0, tiled=True)
    with jax.named_scope("gather_core"):
        other = lax.ppermute(part, "core", SWAP)
        first = lax.axis_index("core") == 0
        return jnp.concatenate([jnp.where(first, part, other), jnp.where(first, other, part)], axis=1).astype(jnp.float32)


def fold_kernel(me_ref, rows_ref, *refs):
    *grad_refs, out_ref = refs
    me = me_ref[0]
    total = None
    for k, grad_ref in enumerate(grad_refs):
        rows = rows_ref[lax.rem(me - k + len(grad_refs), len(grad_refs))]
        term = lax.dot_general(rows, grad_ref[...], (((0,), (0,)), ((), ())), preferred_element_type=jnp.float32)
        total = term if total is None else total + term
    out_ref[...] = total.astype(out_ref.dtype)


def fold(me, rows, grads):
    width, cols = rows.shape[2], grads[0].shape[1]
    vmem = pl.BlockSpec(memory_space=pltpu.VMEM)
    return pl.pallas_call(
        fold_kernel,
        out_shape=jax.ShapeDtypeStruct((width, cols), jnp.bfloat16),
        in_specs=[pl.BlockSpec(memory_space=pltpu.SMEM), vmem] + [vmem] * len(grads),
        out_specs=vmem,
        compiler_params=pltpu.CompilerParams(vmem_limit_bytes=32 * 2**20),
    )(me.reshape(1), rows, *grads)


def ring_gather(block):
    n = 8
    to_right = [(i, (i + 1) % n) for i in range(n)]
    to_left = [(i, (i - 1) % n) for i in range(n)]
    held = {0: block}
    for k in range(1, 5):
        held[k] = lax.ppermute(held[k - 1], "feat", to_right)
        if k < 4:
            held[n - k] = lax.ppermute(held[(n - k + 1) % n], "feat", to_left)
    return [held[k] for k in range(n)]


def shards(feature_table, sample_ids, block_ids, block_counts, block_tiles, weight, target):
    with jax.named_scope("pick"):
        picked = feature_table.at[sample_ids].get(mode="promise_in_bounds", wrap_negative_indices=False)
        slices = lax.all_to_all(picked, "feat", split_axis=1, concat_axis=0, tiled=True)
    node_total, slice_width = slices.shape
    block_total, slot_total, block_rows, block_width = block_tiles.shape
    with jax.named_scope("aggregate"):
        blocked = slices.reshape(block_total, block_rows, slice_width)
        live_mask = jnp.arange(slot_total, dtype=jnp.int32)[None, :] < block_counts[:, None]
        masked = jnp.where(live_mask[:, :, None, None], block_tiles, jnp.zeros((), jnp.bfloat16))
        neighbor_rows = blocked.at[block_ids].get(mode="promise_in_bounds", wrap_negative_indices=False)
        summed = jnp.einsum("rsij,rsjf->rif", masked, neighbor_rows, preferred_element_type=jnp.float32)
        degree = jnp.sum(masked.astype(jnp.float32), axis=(1, 3))
        aggregate = (summed / degree[:, :, None]).reshape(node_total, slice_width).astype(jnp.bfloat16)
        blocked_agg = aggregate.reshape(block_total, block_rows, slice_width)
        other_agg = lax.ppermute(blocked_agg, "core", SWAP)
    with jax.named_scope("preact"):
        partial = jnp.dot(aggregate, weight, preferred_element_type=jnp.float32).astype(jnp.bfloat16)
        preact = exchange_sum(partial.reshape(block_total, block_rows, -1), "feat")
    with jax.named_scope("grad"):
        sigmoid_part = jax.nn.sigmoid(preact)
        hidden = preact * sigmoid_part
        hidden_width = hidden.shape[1]
        scales = lax.rsqrt(jnp.mean(hidden * hidden, axis=1, keepdims=True) + 1e-05)
        embedding = (hidden * scales).astype(jnp.bfloat16)
        cotangent = (embedding.astype(jnp.float32) - target.astype(jnp.float32)) / node_total
        projected = jnp.sum(cotangent * hidden, axis=1, keepdims=True)
        grad_hidden = scales * cotangent - scales**3 / hidden_width * hidden * projected
        slope = sigmoid_part * (1.0 + preact * (1.0 - sigmoid_part))
        grad_pre = (grad_hidden * slope).astype(jnp.bfloat16)
    with jax.named_scope("swap"):
        half = hidden_width // 2
        paired = lax.all_to_all(grad_pre.reshape(block_rows, 2, half).swapaxes(0, 1), "core", 0, 0)
    with jax.named_scope("fold"):
        first = lax.axis_index("core") == 0
        rows = jnp.concatenate([jnp.where(first, blocked_agg, other_agg), jnp.where(first, other_agg, blocked_agg)], axis=1)
        folded = fold(lax.axis_index("feat"), rows, ring_gather(paired.reshape(2 * block_rows, half)))
    weight_grad = group_sum(folded)
    return (embedding, weight_grad)


def solution(mesh):
    fine = Mesh(mesh.devices.reshape(4, 3, 4, 2, 8), ALL)
    return jax.shard_map(
        shards,
        mesh=fine,
        in_specs=(
            P(ALL, None),
            P(ALL),
            P(GRP, None),
            P(GRP),
            P(GRP, None, None, None),
            P("feat", None),
            P(ALL, None),
        ),
        out_specs=(P(ALL, None), P("feat", None)),
        check_vma=False,
    )
```

time: 244 us -> 232 us (0.951)
  blocking collectives: 128 us -> 72.4 us
  waiting for transfers between devices: 39 us -> 79.8 us
  local copies, waits for them, and re-layouts: 17.9 us -> 6.01 us
  starting transfers between devices: 42.4 us -> 53.2 us
    all_to_all x4 -> x1, blocking collectives: 87.5 us -> 23.8 us  [exchange_sum(): got = lax.all_to_all(parts, axis, 0, 0)]
    all_to_all x0 -> x1, waiting for transfers between devices: none -> 40.8 us  [exchange_sum(): got = lax.all_to_all(parts, axis, 0, 0)]
    unnamed x22 -> x13, local copies, waits for them, and re-layouts: 9.26 us -> 0.9 us
    all_to_all x0 -> x1, blocking collectives: none -> 8 us  [shards(): lax.all_to_all(grad_pre.reshape(block_rows, 2, half).swapaxes(0, 1), 'cor...]
    ppermute x1 -> x2, starting transfers between devices: 13 us -> 19.9 us  [the longest x1 13 us: group_sum(): other = lax.ppermute(part, 'core', SWAP)]
    all_to_all x0 -> x1, starting transfers between devices: none -> 4.35 us  [exchange_sum(): got = lax.all_to_all(parts, axis, 0, 0)]
    dot_general x1 -> x0, matrix products: 2.85 us -> none  [shards(): lax.dot_general(turned.reshape(node_total, slice_width), jnp.concatenate(...]
    dot_general x1, matrix products: 1.25 us -> 3.8 us  [shards(): jnp.dot(aggregate, weight, preferred_element_type=jnp.float32)]
  transfers between devices with their start and end apart: 9 -> 11, of which waited for: 6 -> 7; matrix products, arithmetic and copies ran while one was open for 4% -> 3% of each run, Pallas kernels for 0% -> 0%
where the time goes in v2:
time: 232 us
  waiting for transfers between devices  79.8 us (34%)
  blocking collectives  72.4 us (31%)
  starting transfers between devices  53.2 us (23%)
  other arithmetic  9.01 us (4%)
  matrix products  8.13 us (4%)
  local copies, waits for them, and re-layouts  6.01 us (3%)
    all_to_all x1, waiting for transfers between devices, exchange_sum(): got = lax.all_to_all(parts, axis, 0, 0)  40.8 us
    all_to_all x1, blocking collectives, exchange_sum(): got = lax.all_to_all(parts, axis, 0, 0)  23.8 us
    all_to_all x1, waiting for transfers between devices, shards(): lax.all_to_all(picked, 'feat', split_axis=1, concat_axis=0, tiled=True)  23 us
    all_gather x1, blocking collectives, group_sum(): part = jnp.sum(lax.all_gather(part, 'zo'), axis=0).astype(jnp.bfloat16)  19.7 us
    ppermute x4, waiting for transfers between devices, ring_gather(): held[k] = lax.ppermute(held[k - 1], 'feat', to_right)  14.4 us
    ppermute x3, starting transfers between devices, ring_gather(): held[n - k] = lax.ppermute(held[(n - k + 1) % n], 'feat', to_left)  13.4 us
    ppermute x1, starting transfers between devices, group_sum(): other = lax.ppermute(part, 'core', SWAP)  13 us
    all_gather x1, blocking collectives, group_sum(): part = lax.all_gather(part, 'zi', axis=0, tiled=True)  10.8 us
  transfers between devices with their start and end apart: 11, of which 7 were waited for; matrix products, arithmetic and copies ran while one was open for 3% of the time, Pallas kernels for 0%

profile of v2, /device:TPU:1, one launch (start us, length us, event | category | flops | bytes accessed | tf_op | source)
XLA Modules:
  0.0 231.7 jit_solution(13842336672845912965)
XLA Ops:
  2.2 1.2 gather_fusion
  4.5 7.7 %all-to-all-start = ((bf16[128,8,512]{2,0,1:T(8,128)(2,1)}), bf16[128,8,512]{2,0,1:T(8,128)(2,1)S(1)}, u32[]{:S(2)}, u32[]{:S(2)}) async-start(bf16[128,8,512]{2,0,1:T(8,128)(2,1)} %bitcast.33), calls=%async_computation | async-start | bytes 2097152 | tf_op jit(solution)/shard_map/pick/all_to_all | solution.py:72
  12.4 1.6 convert_reduce_fusion.1
  14.0 23.0 %all-to-all-done = bf16[128,8,512]{2,0,1:T(8,128)(2,1)S(1)} async-done(((bf16[128,8,512]{2,0,1:T(8,128)(2,1)}), bf16[128,8,512]{2,0,1:T(8,128)(2,1)S(1)}, u32[]{:S(2)}, u32[]{:S(2)}) %all-to-all-start) | async-done | bytes 1048608 | tf_op jit(solution)/shard_map/pick/all_to_all | solution.py:72
  37.1 2.7 %gather_fusion.1 = bf16[32,128,512]{2,1,0:T(8,128)(2,1)} fusion(bf16[8,128,512]{2,1,0:T(8,128)(2,1)S(1)} %bitcast.31, s32[1024]{0:T(1024)S(1)} %pad_clamp_fusion), kind=kCustom, calls=%fused_computation.1 | custom fusion | bytes 8388736 | tf_op jit(solution)/shard_map/aggregate/gather | solution.py:79
  39.8 4.3 %fusion = bf16[8,128,512]{2,1,0:T(8,128)(2,1)} fusion(bf16[8,4,128,512]{3,2,1,0:T(8,128)(2,1)} %bitcast.34, f32[8,128]{1,0:T(8,128)S(1)} %convert_reduce_fusion.1, bf16[8,4,128,128]{3,2,1,0:T(8,128)(2,1)} %param.11, pred[8,4]{1,0:T(8,128)(4,1)S(1)} %iota_compare_fusion), kind=kOutput, calls=%fused_computation.5 | convolution fusion | flops 538443776 | bytes 6295584 | tf_op jit(solution)/shard_map/aggregate/rsij,rsjf->rif/dot_general | solution.py:80
  44.2 3.8 %convolution_convert_fusion = bf16[1024,1024]{1,0:T(8,128)(2,1)} fusion(bf16[1024,512]{1,0:T(8,128)(2,1)} %bitcast.4, bf16[512,1024]{1,0:T(8,128)(2,1)S(1)} %copy-done.4), kind=kOutput, calls=%fused_computation.7 | convolution fusion | flops 1074790400 | bytes 4194304 | tf_op jit(solution)/shard_map/preact/dot_general | solution.py:86
  48.0 4.3 %all-to-all-start.1 = ((bf16[8,128,1024]{2,1,0:T(8,128)(2,1)}), bf16[8,128,1024]{2,1,0:T(8,128)(2,1)}, u32[]{:S(2)}, u32[]{:S(2)}) async-start(bf16[8,128,1024]{2,1,0:T(8,128)(2,1)} %bitcast.35), calls=%async_computation.1 | async-start | bytes 4194304 | tf_op jit(solution)/shard_map/preact/all_to_all | solution.py:14
  52.3 6.9 %collective-permute-start = (bf16[8,128,512]{2,1,0:T(8,128)(2,1)}, bf16[8,128,512]{2,1,0:T(8,128)(2,1)}, u32[]{:S(2)}, u32[]{:S(2)}) collective-permute-start(bf16[8,128,512]{2,1,0:T(8,128)(2,1)} %fusion), channel_id=1, source_target_pairs={{0,8},{8,0},{1,9},{9,1},{2,10},{10,2},{3,11},{11,3},{4,12},{12,4},... | collective-permute-start | bytes 3145736 | tf_op jit(solution)/shard_map/aggregate/ppermute | solution.py:84
  59.2 40.8 %all-to-all-done.1 = bf16[8,128,1024]{2,1,0:T(8,128)(2,1)} async-done(((bf16[8,128,1024]{2,1,0:T(8,128)(2,1)}), bf16[8,128,1024]{2,1,0:T(8,128)(2,1)}, u32[]{:S(2)}, u32[]{:S(2)}) %all-to-all-start.1) | async-done | bytes 2097184 | tf_op jit(solution)/shard_map/preact/all_to_all | solution.py:14
  100.0 2.0 convert_reduce_fusion
  103.1 8.0 %all_to_all.31 = bf16[2,128,512]{2,1,0:T(8,128)(2,1)S(1)} all-to-all(bf16[2,128,512]{2,1,0:T(8,128)(2,1)S(1)} %bitcast.36), channel_id=1, replica_groups=mesh['x'=4,'zo'=3,'zi'=4,'core'=2,'feat'=8] {'core'}, dimensions={0} | all-to-all | bytes 524288 | tf_op jit(solution)/shard_map/swap/all_to_all | solution.py:101
  111.1 2.2 collective-permute-start.1
  113.3 4.3 %collective-permute-start.5 = (bf16[256,512]{1,0:T(8,128)(2,1)S(1)}, bf16[256,512]{1,0:T(8,128)(2,1)S(1)}, u32[]{:S(2)}, u32[]{:S(2)}) collective-permute-start(bf16[256,512]{1,0:T(8,128)(2,1)S(1)} %bitcast.29), channel_id=1, source_target_pairs={{0,7},{1,0},{2,1},{3,2},{4,3},{5,4},{6,5},{7,6},{8,15},{9,8},{10,9... | collective-permute-start | bytes 786440 | tf_op jit(solution)/shard_map/fold/ppermute | solution.py:65
  117.6 4.1 %collective-permute-done.1.refs_1_ = bf16[256,512]{1,0:T(8,128)(2,1)S(1)} collective-permute-done((bf16[256,512]{1,0:T(8,128)(2,1)S(1)}, bf16[256,512]{1,0:T(8,128)(2,1)S(1)}, u32[]{:S(2)}, u32[]{:S(2)}) %collective-permute-start.1) | collective-permute-done | bytes 262176 | tf_op jit(solution)/shard_map/fold/ppermute | solution.py:63
  121.7 1.9 collective-permute-start.2
  123.6 4.6 %collective-permute-start.6 = (bf16[256,512]{1,0:T(8,128)(2,1)S(1)}, bf16[256,512]{1,0:T(8,128)(2,1)S(1)}, u32[]{:S(2)}, u32[]{:S(2)}) collective-permute-start(bf16[256,512]{1,0:T(8,128)(2,1)S(1)} %collective-permute-done.5.refs_7_), channel_id=1, source_target_pairs={{0,7},{1,0},{2,1},{3,2},{4,3},{5,4},{6,5},{7,6},{8,15},{9,8},{10,9... | collective-permute-start | bytes 786440 | tf_op jit(solution)/shard_map/fold/ppermute | solution.py:65
  128.2 3.2 %collective-permute-done.2.refs_2_ = bf16[256,512]{1,0:T(8,128)(2,1)S(1)} collective-permute-done((bf16[256,512]{1,0:T(8,128)(2,1)S(1)}, bf16[256,512]{1,0:T(8,128)(2,1)S(1)}, u32[]{:S(2)}, u32[]{:S(2)}) %collective-permute-start.2) | collective-permute-done | bytes 262176 | tf_op jit(solution)/shard_map/fold/ppermute | solution.py:63
  131.4 1.9 collective-permute-start.3
  133.3 4.6 %collective-permute-start.7 = (bf16[256,512]{1,0:T(8,128)(2,1)S(1)}, bf16[256,512]{1,0:T(8,128)(2,1)S(1)}, u32[]{:S(2)}, u32[]{:S(2)}) collective-permute-start(bf16[256,512]{1,0:T(8,128)(2,1)S(1)} %collective-permute-done.6.refs_6_), channel_id=1, source_target_pairs={{0,7},{1,0},{2,1},{3,2},{4,3},{5,4},{6,5},{7,6},{8,15},{9,8},{10,9... | collective-permute-start | bytes 786440 | tf_op jit(solution)/shard_map/fold/ppermute | solution.py:65
  137.9 2.4 %collective-permute-done.3.refs_3_ = bf16[256,512]{1,0:T(8,128)(2,1)} collective-permute-done((bf16[256,512]{1,0:T(8,128)(2,1)S(1)}, bf16[256,512]{1,0:T(8,128)(2,1)}, u32[]{:S(2)}, u32[]{:S(2)}) %collective-permute-start.3) | collective-permute-done | bytes 262176 | tf_op jit(solution)/shard_map/fold/ppermute | solution.py:63
  140.3 1.9 collective-permute-start.4
  142.2 1.7 broadcast_select_fusion.1
  144.0 4.8 %collective-permute-done.4.refs_4_ = bf16[256,512]{1,0:T(8,128)(2,1)S(1)} collective-permute-done((bf16[256,512]{1,0:T(8,128)(2,1)}, bf16[256,512]{1,0:T(8,128)(2,1)S(1)}, u32[]{:S(2)}, u32[]{:S(2)}) %collective-permute-start.4) | collective-permute-done | bytes 262176 | tf_op jit(solution)/shard_map/fold/ppermute | solution.py:63
  148.8 2.2 fold.1
  151.0 23.8 %all_to_all.32 = bf16[16,32,512]{2,1,0:T(8,128)(2,1)S(1)} all-to-all(bf16[16,32,512]{2,1,0:T(8,128)(2,1)S(1)} %bitcast.27), channel_id=1, replica_groups=mesh['x'=4,'zo'=3,'zi'=4,'core'=2,'feat'=8] {'x','zi'}, dimensions={0} | all-to-all | bytes 1048576 | tf_op jit(solution)/shard_map/sum_x_zi/all_to_all | solution.py:14
  174.9 19.7 %all-gather = f32[96,512]{1,0:T(8,128)S(1)} all-gather(f32[32,512]{1,0:T(8,128)S(1)} %convert_reduce_fusion.2), channel_id=2, replica_groups=mesh['x'=4,'zo'=3,'zi'=4,'core'=2,'feat'=8] {'zo'}, dimensions={0}, use_global_device_ids=true | all-gather | bytes 262144 | tf_op jit(solution)/shard_map/sum_zo/all_gather | solution.py:23
  194.6 10.8 %all_gather.14 = bf16[128,512]{1,0:T(8,128)(2,1)S(1)} all-gather(bf16[32,512]{1,0:T(8,128)(2,1)S(1)} %reduce_sum.59), channel_id=1, replica_groups=mesh['x'=4,'zo'=3,'zi'=4,'core'=2,'feat'=8] {'zi'}, dimensions={0}, use_global_device_ids=true | all-gather | bytes 163840 | tf_op jit(solution)/shard_map/gather_zi/all_gather | solution.py:25
  205.3 10.2 %all_gather.15 = bf16[512,512]{1,0:T(8,128)(2,1)S(1)} all-gather(bf16[128,512]{1,0:T(8,128)(2,1)S(1)} %all_gather.14), channel_id=1, replica_groups=mesh['x'=4,'zo'=3,'zi'=4,'core'=2,'feat'=8] {'x'}, dimensions={0}, use_global_device_ids=true | all-gather | bytes 655360 | tf_op jit(solution)/shard_map/gather_x/all_gather | solution.py:27
  215.5 13.0 %collective-permute-start.8 = (bf16[512,512]{1,0:T(8,128)(2,1)S(1)}, bf16[512,512]{1,0:T(8,128)(2,1)S(1)}, u32[]{:S(2)}, u32[]{:S(2)}) collective-permute-start(bf16[512,512]{1,0:T(8,128)(2,1)S(1)} %all_gather.15), channel_id=1, source_target_pairs={{0,8},{8,0},{1,9},{9,1},{2,10},{10,2},{3,11},{11,3},{4,12},{12,4},... | collective-permute-start | bytes 1572872 | tf_op jit(solution)/shard_map/gather_core/ppermute | solution.py:29
  228.5 1.5 collective-permute-done.8
  230.1 1.6 maximum_convert_fusion
  (32 shorter events, 4.2 us)
Async XLA Ops:
  0.6 1.6 copy-start
  3.4 8.7 %copy-start.3 = (s32[8,4]{0,1:T(4,128)S(1)}, s32[8,4]{0,1:T(4,128)}, u32[]{:S(2)}) copy-start(s32[8,4]{0,1:T(4,128)} %param.9) | copy-start | bytes 388
  3.5 8.9 %copy-start.5 = (s32[8]{0:T(128)S(1)}, s32[8]{0:T(128)}, u32[]{:S(2)}) copy-start(s32[8]{0:T(128)} %param.10) | copy-start | bytes 100
  4.5 32.5 %all-to-all-start = ((bf16[128,8,512]{2,0,1:T(8,128)(2,1)}), bf16[128,8,512]{2,0,1:T(8,128)(2,1)S(1)}, u32[]{:S(2)}, u32[]{:S(2)}) async-start(bf16[128,8,512]{2,0,1:T(8,128)(2,1)} %bitcast.33), calls=%async_computation | async-start | bytes 2097152 | tf_op jit(solution)/shard_map/pick/all_to_all | solution.py:72
  39.8 4.3 %copy-start.4 = (bf16[512,1024]{1,0:T(8,128)(2,1)S(1)}, bf16[512,1024]{1,0:T(8,128)(2,1)}, u32[]{:S(2)}) copy-start(bf16[512,1024]{1,0:T(8,128)(2,1)} %param.12) | copy-start | bytes 3145732
  48.0 52.1 %all-to-all-start.1 = ((bf16[8,128,1024]{2,1,0:T(8,128)(2,1)}), bf16[8,128,1024]{2,1,0:T(8,128)(2,1)}, u32[]{:S(2)}, u32[]{:S(2)}) async-start(bf16[8,128,1024]{2,1,0:T(8,128)(2,1)} %bitcast.35), calls=%async_computation.1 | async-start | bytes 4194304 | tf_op jit(solution)/shard_map/preact/all_to_all | solution.py:14
  52.3 50.0 %copy-start.1 = (bf16[128,1024]{1,0:T(8,128)(2,1)S(1)}, bf16[128,1024]{1,0:T(8,128)(2,1)}, u32[]{:S(2)}) copy-start(bf16[128,1024]{1,0:T(8,128)(2,1)} %param.13) | copy-start | bytes 786436
  52.3 89.9 %collective-permute-start = (bf16[8,128,512]{2,1,0:T(8,128)(2,1)}, bf16[8,128,512]{2,1,0:T(8,128)(2,1)}, u32[]{:S(2)}, u32[]{:S(2)}) collective-permute-start(bf16[8,128,512]{2,1,0:T(8,128)(2,1)} %fusion), channel_id=1, source_target_pairs={{0,8},{8,0},{1,9},{9,1},{2,10},{10,2},{3,11},{11,3},{4,12},{12,4},... | collective-permute-start | bytes 3145736 | tf_op jit(solution)/shard_map/aggregate/ppermute | solution.py:84
  102.6 28.7 %copy-start.2 = (bf16[128,1024]{1,0:T(8,128)(2,1)}, bf16[128,1024]{1,0:T(8,128)(2,1)S(1)}, u32[]{:S(2)}) copy-start(bf16[128,1024]{1,0:T(8,128)(2,1)S(1)} %get-tuple-element.5) | copy-start | bytes 786436
  111.1 10.6 %collective-permute-start.1 = (bf16[256,512]{1,0:T(8,128)(2,1)S(1)}, bf16[256,512]{1,0:T(8,128)(2,1)S(1)}, u32[]{:S(2)}, u32[]{:S(2)}) collective-permute-start(bf16[256,512]{1,0:T(8,128)(2,1)S(1)} %bitcast.28), channel_id=1, source_target_pairs={{0,1},{1,2},{2,3},{3,4},{4,5},{5,6},{6,7},{7,0},{8,9},{9,10},{10,1... | collective-permute-start | bytes 786440 | tf_op jit(solution)/shard_map/fold/ppermute | solution.py:63
  113.3 10.3 %collective-permute-start.5 = (bf16[256,512]{1,0:T(8,128)(2,1)S(1)}, bf16[256,512]{1,0:T(8,128)(2,1)S(1)}, u32[]{:S(2)}, u32[]{:S(2)}) collective-permute-start(bf16[256,512]{1,0:T(8,128)(2,1)S(1)} %bitcast.29), channel_id=1, source_target_pairs={{0,7},{1,0},{2,1},{3,2},{4,3},{5,4},{6,5},{7,6},{8,15},{9,8},{10,9... | collective-permute-start | bytes 786440 | tf_op jit(solution)/shard_map/fold/ppermute | solution.py:65
  121.7 9.7 %collective-permute-start.2 = (bf16[256,512]{1,0:T(8,128)(2,1)S(1)}, bf16[256,512]{1,0:T(8,128)(2,1)S(1)}, u32[]{:S(2)}, u32[]{:S(2)}) collective-permute-start(bf16[256,512]{1,0:T(8,128)(2,1)S(1)} %collective-permute-done.1.refs_1_), channel_id=1, source_target_pairs={{0,1},{1,2},{2,3},{3,4},{4,5},{5,6},{6,7},{7,0},{8,9},{9,10},{10,1... | collective-permute-start | bytes 786440 | tf_op jit(solution)/shard_map/fold/ppermute | solution.py:63
  123.6 9.7 %collective-permute-start.6 = (bf16[256,512]{1,0:T(8,128)(2,1)S(1)}, bf16[256,512]{1,0:T(8,128)(2,1)S(1)}, u32[]{:S(2)}, u32[]{:S(2)}) collective-permute-start(bf16[256,512]{1,0:T(8,128)(2,1)S(1)} %collective-permute-done.5.refs_7_), channel_id=1, source_target_pairs={{0,7},{1,0},{2,1},{3,2},{4,3},{5,4},{6,5},{7,6},{8,15},{9,8},{10,9... | collective-permute-start | bytes 786440 | tf_op jit(solution)/shard_map/fold/ppermute | solution.py:65
  131.4 8.9 %collective-permute-start.3 = (bf16[256,512]{1,0:T(8,128)(2,1)S(1)}, bf16[256,512]{1,0:T(8,128)(2,1)}, u32[]{:S(2)}, u32[]{:S(2)}) collective-permute-start(bf16[256,512]{1,0:T(8,128)(2,1)S(1)} %collective-permute-done.2.refs_2_), channel_id=1, source_target_pairs={{0,1},{1,2},{2,3},{3,4},{4,5},{5,6},{6,7},{7,0},{8,9},{9,10},{10,1... | collective-permute-start | bytes 786440 | tf_op jit(solution)/shard_map/fold/ppermute | solution.py:63
  133.3 10.7 %collective-permute-start.7 = (bf16[256,512]{1,0:T(8,128)(2,1)S(1)}, bf16[256,512]{1,0:T(8,128)(2,1)S(1)}, u32[]{:S(2)}, u32[]{:S(2)}) collective-permute-start(bf16[256,512]{1,0:T(8,128)(2,1)S(1)} %collective-permute-done.6.refs_6_), channel_id=1, source_target_pairs={{0,7},{1,0},{2,1},{3,2},{4,3},{5,4},{6,5},{7,6},{8,15},{9,8},{10,9... | collective-permute-start | bytes 786440 | tf_op jit(solution)/shard_map/fold/ppermute | solution.py:65
  140.3 8.5 %collective-permute-start.4 = (bf16[256,512]{1,0:T(8,128)(2,1)}, bf16[256,512]{1,0:T(8,128)(2,1)S(1)}, u32[]{:S(2)}, u32[]{:S(2)}) collective-permute-start(bf16[256,512]{1,0:T(8,128)(2,1)} %collective-permute-done.3.refs_3_), channel_id=1, source_target_pairs={{0,1},{1,2},{2,3},{3,4},{4,5},{5,6},{6,7},{7,0},{8,9},{9,10},{10,1... | collective-permute-start | bytes 786440 | tf_op jit(solution)/shard_map/fold/ppermute | solution.py:63
  215.5 14.5 %collective-permute-start.8 = (bf16[512,512]{1,0:T(8,128)(2,1)S(1)}, bf16[512,512]{1,0:T(8,128)(2,1)S(1)}, u32[]{:S(2)}, u32[]{:S(2)}) collective-permute-start(bf16[512,512]{1,0:T(8,128)(2,1)S(1)} %all_gather.15), channel_id=1, source_target_pairs={{0,8},{8,0},{1,9},{9,1},{2,10},{10,2},{3,11},{11,3},{4,12},{12,4},... | collective-permute-start | bytes 1572872 | tf_op jit(solution)/shard_map/gather_core/ppermute | solution.py:29

commit v3 on v2

--- a/solution.py
+++ b/solution.py
@@ -8,6 +8,8 @@
 GRP = ("x", "zo", "zi", "core")
 ALL = GRP + ("feat",)
 SWAP = [(0, 1), (1, 0)]
+TO_RIGHT = [(i, (i + 1) % 8) for i in range(8)]
+TO_LEFT = [(i, (i - 1) % 8) for i in range(8)]
 
 
 def exchange_sum(parts, axis):
@@ -19,16 +21,90 @@
     rows, cols = term.shape
     with jax.named_scope("sum_x_zi"):
         part = exchange_sum(term.reshape(16, rows // 16, cols), ("x", "zi"))
-    with jax.named_scope("sum_zo"):
-        part = jnp.sum(lax.all_gather(part, "zo"), axis=0).astype(jnp.bfloat16)
-    with jax.named_scope("gather_zi"):
-        part = lax.all_gather(part, "zi", axis=0, tiled=True)
+    with jax.named_scope("sum_z"):
+        parts = lax.all_gather(part.astype(jnp.bfloat16), ("zo", "zi"), axis=0, tiled=True)
+        parts = parts.reshape(3, rows // 4, cols).astype(jnp.float32)
+        part = jnp.sum(parts, axis=0).astype(jnp.bfloat16)
     with jax.named_scope("gather_x"):
         part = lax.all_gather(part, "x", axis=0, tiled=True)
     with jax.named_scope("gather_core"):
         other = lax.ppermute(part, "core", SWAP)
         first = lax.axis_index("core") == 0
         return jnp.concatenate([jnp.where(first, part, other), jnp.where(first, other, part)], axis=1).astype(jnp.float32)
+
+
+def pick_kernel(ids_ref, table_ref, out_ref):
+    wanted = lax.broadcasted_iota(jnp.int32, (table_ref.shape[0], ids_ref.shape[1]), 0) == ids_ref[...]
+    rows = lax.dot_general(
+        wanted.astype(table_ref.dtype), table_ref[...], (((0,), (0,)), ((), ())), preferred_element_type=jnp.float32
+    )
+    out_ref[0] = rows.astype(out_ref.dtype)
+
+
+def pick(table, ids, slices):
+    rows, width = table.shape[0], table.shape[1] // slices
+    return pl.pallas_call(
+        pick_kernel,
+        grid=(slices,),
+        out_shape=jax.ShapeDtypeStruct((slices, ids.shape[0], width), table.dtype),
+        in_specs=[
+            pl.BlockSpec((1, ids.shape[0]), lambda j: (0, 0)),
+            pl.BlockSpec((rows, width), lambda j: (0, j)),
+        ],
+        out_specs=pl.BlockSpec((1, ids.shape[0], width), lambda j: (j, 0, 0)),
+    )(ids.reshape(1, -1), table)
+
+
+def aggregate_kernel(me_ref, ids_ref, counts_ref, slices_ref, tiles_ref, weight_ref, agg_ref, *refs):
+    *part_refs, turned = refs
+    blocks, block_rows, width = slices_ref.shape
+    slots = tiles_ref.shape[1]
+    ones = jnp.ones((slots * tiles_ref.shape[3], 128), jnp.bfloat16)
+    for k in range(blocks):
+        own = lax.rem(me_ref[0] + blocks // 2 - k + blocks, blocks)
+        lhs = [
+            jnp.where(s < counts_ref[own], tiles_ref[own, s], jnp.zeros((), jnp.bfloat16)) for s in range(slots)
+        ]
+        rhs = [slices_ref[ids_ref[own, s]] for s in range(slots)]
+        lhs, rhs = jnp.concatenate(lhs, axis=1), jnp.concatenate(rhs, axis=0)
+        summed = jnp.dot(lhs, rhs, preferred_element_type=jnp.float32)
+        degree = jnp.dot(lhs, ones, preferred_element_type=jnp.float32)
+        agg = (summed / jnp.concatenate([degree] * (width // 128), axis=1)).astype(jnp.bfloat16)
+        agg_ref[own] = agg
+        turned[pl.ds(k * block_rows, block_rows)] = agg
+    step = 4
+    for k in range(0, blocks, step):
+        lhs = turned[pl.ds(k * block_rows, step * block_rows)]
+        parts = jnp.dot(lhs, weight_ref[...], preferred_element_type=jnp.float32).astype(jnp.bfloat16)
+        for i in range(step):
+            part_refs[k + i][...] = parts[i * block_rows:(i + 1) * block_rows]
+
+
+def aggregate_and_project(me, ids, counts, slices, tiles, weight):
+    blocks, block_rows, width = slices.shape
+    vmem, smem = pl.BlockSpec(memory_space=pltpu.VMEM), pl.BlockSpec(memory_space=pltpu.SMEM)
+    part = jax.ShapeDtypeStruct((block_rows, weight.shape[1]), jnp.bfloat16)
+    agg, *parts = pl.pallas_call(
+        aggregate_kernel,
+        out_shape=[jax.ShapeDtypeStruct(slices.shape, jnp.bfloat16)] + [part] * blocks,
+        in_specs=[smem] * 3 + [vmem] * 3,
+        out_specs=[vmem] * (1 + blocks),
+        scratch_shapes=[pltpu.VMEM((blocks * block_rows, width), jnp.bfloat16)],
+        compiler_params=pltpu.CompilerParams(vmem_limit_bytes=32 * 2**20),
+    )(me.reshape(1), ids, counts, slices, tiles, weight)
+    return agg, parts
+
+
+def ring_sum(parts):
+    right, left = parts[0], parts[7]
+    for k in range(1, 5):
+        right = lax.ppermute(right, "feat", TO_RIGHT).astype(jnp.float32) + parts[k].astype(jnp.float32)
+        right = right.astype(jnp.bfloat16) if k < 4 else right
+        if k < 4:
+            left = lax.ppermute(left, "feat", TO_LEFT)
+            if k < 3:
+                left = (left.astype(jnp.float32) + parts[7 - k].astype(jnp.float32)).astype(jnp.bfloat16)
+    return right + left.astype(jnp.float32)
 
 
 def fold_kernel(me_ref, rows_ref, *refs):
@@ -56,35 +132,25 @@
 
 def ring_gather(block):
     n = 8
-    to_right = [(i, (i + 1) % n) for i in range(n)]
-    to_left = [(i, (i - 1) % n) for i in range(n)]
     held = {0: block}
     for k in range(1, 5):
-        held[k] = lax.ppermute(held[k - 1], "feat", to_right)
+        held[k] = lax.ppermute(held[k - 1], "feat", TO_RIGHT)
         if k < 4:
-            held[n - k] = lax.ppermute(held[(n - k + 1) % n], "feat", to_left)
+            held[n - k] = lax.ppermute(held[(n - k + 1) % n], "feat", TO_LEFT)
     return [held[k] for k in range(n)]
 
 
 def shards(feature_table, sample_ids, block_ids, block_counts, block_tiles, weight, target):
+    block_total, slot_total, block_rows, block_width = block_tiles.shape
+    node_total = block_total * block_rows
+    me = lax.axis_index("feat")
     with jax.named_scope("pick"):
-        picked = feature_table.at[sample_ids].get(mode="promise_in_bounds", wrap_negative_indices=False)
-        slices = lax.all_to_all(picked, "feat", split_axis=1, concat_axis=0, tiled=True)
-    node_total, slice_width = slices.shape
-    block_total, slot_total, block_rows, block_width = block_tiles.shape
+        slices = lax.all_to_all(pick(feature_table, sample_ids, block_total), "feat", 0, 0)
     with jax.named_scope("aggregate"):
-        blocked = slices.reshape(block_total, block_rows, slice_width)
-        live_mask = jnp.arange(slot_total, dtype=jnp.int32)[None, :] < block_counts[:, None]
-        masked = jnp.where(live_mask[:, :, None, None], block_tiles, jnp.zeros((), jnp.bfloat16))
-        neighbor_rows = blocked.at[block_ids].get(mode="promise_in_bounds", wrap_negative_indices=False)
-        summed = jnp.einsum("rsij,rsjf->rif", masked, neighbor_rows, preferred_element_type=jnp.float32)
-        degree = jnp.sum(masked.astype(jnp.float32), axis=(1, 3))
-        aggregate = (summed / degree[:, :, None]).reshape(node_total, slice_width).astype(jnp.bfloat16)
-        blocked_agg = aggregate.reshape(block_total, block_rows, slice_width)
-        other_agg = lax.ppermute(blocked_agg, "core", SWAP)
+        agg, parts = aggregate_and_project(me, block_ids, block_counts, slices, block_tiles, weight)
+        other_agg = lax.ppermute(agg, "core", SWAP)
     with jax.named_scope("preact"):
-        partial = jnp.dot(aggregate, weight, preferred_element_type=jnp.float32).astype(jnp.bfloat16)
-        preact = exchange_sum(partial.reshape(block_total, block_rows, -1), "feat")
+        preact = ring_sum(parts)
     with jax.named_scope("grad"):
         sigmoid_part = jax.nn.sigmoid(preact)
         hidden = preact * sigmoid_part
@@ -101,8 +167,8 @@
         paired = lax.all_to_all(grad_pre.reshape(block_rows, 2, half).swapaxes(0, 1), "core", 0, 0)
     with jax.named_scope("fold"):
         first = lax.axis_index("core") == 0
-        rows = jnp.concatenate([jnp.where(first, blocked_agg, other_agg), jnp.where(first, other_agg, blocked_agg)], axis=1)
-        folded = fold(lax.axis_index("feat"), rows, ring_gather(paired.reshape(2 * block_rows, half)))
+        rows = jnp.concatenate([jnp.where(first, agg, other_agg), jnp.where(first, other_agg, agg)], axis=1)
+        folded = fold(me, rows, ring_gather(paired.reshape(2 * block_rows, half)))
     weight_grad = group_sum(folded)
     return (embedding, weight_grad)
 

time: 232 us -> 206 us (0.89)
  waiting for transfers between devices: 79.8 us -> 46.9 us
  starting transfers between devices: 53.2 us -> 75.4 us
  Pallas kernels: 2.22 us -> 10.4 us
  matrix products: 8.13 us -> 0 us
  blocking collectives: 72.4 us -> 66.3 us
  local copies, waits for them, and re-layouts: 6.01 us -> 0.13 us
  other arithmetic: 9.01 us -> 4.76 us
    all_to_all x2 -> x1, waiting for transfers between devices: 63.9 us -> 24.8 us  [shards(): lax.all_to_all(pick(feature_table, sample_ids, block_total), 'feat', 0, 0)]
    ppermute x8 -> x15, starting transfers between devices: 28.2 us -> 55 us  [the longest x3 13.7 us: ring_gather(): held[n - k] = lax.ppermute(held[(n - k + 1) % n], 'feat', TO_LEFT)]
    pallas_call x0 -> x2, Pallas kernels: none -> 9.09 us  [the longest x1 6.32 us: pick(): pl.pallas_call(pick_kernel, grid=(slices,), out_shape=jax.ShapeDtypeStruc...]
    dot_general x2 -> x0, matrix products: 8.13 us -> none  [the longest x1 4.34 us: shards(): jnp.einsum('rsij,rsjf->rif', masked, neighbor_rows, preferred_element_typ...]
    all_gather x2 -> x1, blocking collectives: 30.4 us -> 24 us  [group_sum(): lax.all_gather(part.astype(jnp.bfloat16), ('zo', 'zi'), axis=0, tiled=True)]
    ppermute x8 -> x15, waiting for transfers between devices: 14.5 us -> 20.6 us  [the longest x4 14.4 us: ring_gather(): held[k] = lax.ppermute(held[k - 1], 'feat', TO_RIGHT)]
    all_to_all x2 -> x1, starting transfers between devices: 12 us -> 7.65 us  [shards(): lax.all_to_all(pick(feature_table, sample_ids, block_total), 'feat', 0, 0)]
    gather x2 -> x0, local copies, waits for them, and re-layouts: 3.93 us -> none  [the longest x1 2.75 us: shards(): blocked.at[block_ids]]
  transfers between devices with their start and end apart: 11 -> 17, of which waited for: 7 -> 9; matrix products, arithmetic and copies ran while one was open for 3% -> 1% of each run, Pallas kernels for 0% -> 0%
where the time goes in v3:
time: 206 us; the launch traced here: 205 us
  starting transfers between devices  75.4 us (37%)
  blocking collectives  66.3 us (32%)
  waiting for transfers between devices  46.9 us (23%)
  Pallas kernels  10.4 us (5%)
  other arithmetic  4.76 us (2%)
    all_to_all x1, waiting for transfers between devices, shards(): lax.all_to_all(pick(feature_table, sample_ids, block_total), 'feat', 0, 0)  24.8 us
    all_gather x1, blocking collectives, group_sum(): lax.all_gather(part.astype(jnp.bfloat16), ('zo', 'zi'), axis=0, tiled=True)  24 us
    all_to_all x1, blocking collectives, exchange_sum(): got = lax.all_to_all(parts, axis, 0, 0)  22.7 us
    ppermute x4, waiting for transfers between devices, ring_gather(): held[k] = lax.ppermute(held[k - 1], 'feat', TO_RIGHT)  14.4 us
    ppermute x3, starting transfers between devices, ring_gather(): held[n - k] = lax.ppermute(held[(n - k + 1) % n], 'feat', TO_LEFT)  13.7 us
    ppermute x3, starting transfers between devices, ring_sum(): left = lax.ppermute(left, 'feat', TO_LEFT)  13.7 us
    ppermute x1, starting transfers between devices, group_sum(): other = lax.ppermute(part, 'core', SWAP)  12.8 us
    ppermute x1, starting transfers between devices, shards(): other_agg = lax.ppermute(agg, 'core', SWAP)  12.1 us
  transfers between devices with their start and end apart: 17, of which 9 were waited for; matrix products, arithmetic and copies ran while one was open for 1% of the time, Pallas kernels for 0%

profile of v3, /device:TPU:1, one launch (start us, length us, event | category | flops | bytes accessed | tf_op | source)
XLA Modules:
  0.0 204.8 jit_solution(13133313560668835534)
XLA Ops:
  0.7 6.3 %pick.1 = bf16[8,128,512]{2,1,0:T(8,128)(2,1)} custom-call(s32[1,128]{1,0:T(1,128)} %bitcast.19, bf16[256,4096]{1,0:T(8,128)(2,1)} %table_ref.1), custom_call_target="tpu_custom_call" | custom-call | tf_op jit(solution)/shard_map/pick/pallas_call | solution.py:46
  7.0 7.7 %all-to-all-start = ((bf16[8,128,512]{2,1,0:T(8,128)(2,1)}), bf16[8,128,512]{2,1,0:T(8,128)(2,1)S(1)}, u32[]{:S(2)}, u32[]{:S(2)}) async-start(bf16[8,128,512]{2,1,0:T(8,128)(2,1)} %pick.1), calls=%async_computation | async-start | bytes 2097152 | tf_op jit(solution)/shard_map/pick/all_to_all | solution.py:148
  14.7 24.8 %all-to-all-done.slices_ref = bf16[8,128,512]{2,1,0:T(8,128)(2,1)S(1)} async-done(((bf16[8,128,512]{2,1,0:T(8,128)(2,1)}), bf16[8,128,512]{2,1,0:T(8,128)(2,1)S(1)}, u32[]{:S(2)}, u32[]{:S(2)}) %all-to-all-start) | async-done | bytes 1048608 | tf_op jit(solution)/shard_map/pick/all_to_all | solution.py:148
  39.5 2.8 %aggregate.1 = (bf16[8,128,512]{2,1,0:T(8,128)(2,1)}, bf16[128,1024]{1,0:T(8,128)(2,1)S(1)}, bf16[128,1024]{1,0:T(8,128)(2,1)S(1)}, bf16[128,1024]{1,0:T(8,128)(...) custom-call(s32[1]{0:T(128)} %bitcast.me_ref, ...), custom_call_target="tpu_custom_call" | custom-call | tf_op jit(solution)/shard_map/aggregate/pallas_call | solution.py:87
  42.3 1.9 collective-permute-start
  44.2 4.6 %collective-permute-start.4 = (bf16[128,1024]{1,0:T(8,128)(2,1)S(1)}, bf16[128,1024]{1,0:T(8,128)(2,1)S(1)}, u32[]{:S(2)}, u32[]{:S(2)}) collective-permute-start(bf16[128,1024]{1,0:T(8,128)(2,1)S(1)} %get-tuple-element.16), channel_id=1, source_target_pairs={{0,7},{1,0},{2,1},{3,2},{4,3},{5,4},{6,5},{7,6},{8,15},{9,8},{10,9... | collective-permute-start | bytes 786440 | tf_op jit(solution)/shard_map/preact/ppermute | solution.py:104
  48.8 1.8 collective-permute-done
  50.7 2.1 %collective-permute-start.1 = (bf16[128,1024]{1,0:T(8,128)(2,1)S(1)}, bf16[128,1024]{1,0:T(8,128)(2,1)S(1)}, u32[]{:S(2)}, u32[]{:S(2)}) collective-permute-start(bf16[128,1024]{1,0:T(8,128)(2,1)S(1)} %add_convert_fusion.4), channel_id=1, source_target_pairs={{0,1},{1,2},{2,3},{3,4},{4,5},{5,6},{6,7},{7,0},{8,9},{9,10},{10,1... | collective-permute-start | bytes 786440 | tf_op jit(solution)/shard_map/preact/ppermute | solution.py:101
  52.9 4.6 %collective-permute-start.5 = (bf16[128,1024]{1,0:T(8,128)(2,1)S(1)}, bf16[128,1024]{1,0:T(8,128)(2,1)S(1)}, u32[]{:S(2)}, u32[]{:S(2)}) collective-permute-start(bf16[128,1024]{1,0:T(8,128)(2,1)S(1)} %add_convert_fusion.1), channel_id=1, source_target_pairs={{0,7},{1,0},{2,1},{3,2},{4,3},{5,4},{6,5},{7,6},{8,15},{9,8},{10,9... | collective-permute-start | bytes 786440 | tf_op jit(solution)/shard_map/preact/ppermute | solution.py:104
  57.5 1.7 collective-permute-done.1
  59.3 1.9 collective-permute-start.2
  61.3 4.6 %collective-permute-start.6 = (bf16[128,1024]{1,0:T(8,128)(2,1)S(1)}, bf16[128,1024]{1,0:T(8,128)(2,1)S(1)}, u32[]{:S(2)}, u32[]{:S(2)}) collective-permute-start(bf16[128,1024]{1,0:T(8,128)(2,1)S(1)} %add_convert_fusion), channel_id=1, source_target_pairs={{0,7},{1,0},{2,1},{3,2},{4,3},{5,4},{6,5},{7,6},{8,15},{9,8},{10,9... | collective-permute-start | bytes 786440 | tf_op jit(solution)/shard_map/preact/ppermute | solution.py:104
  65.9 2.6 %collective-permute-done.2 = bf16[128,1024]{1,0:T(8,128)(2,1)S(1)} collective-permute-done((bf16[128,1024]{1,0:T(8,128)(2,1)S(1)}, bf16[128,1024]{1,0:T(8,128)(2,1)S(1)}, u32[]{:S(2)}, u32[]{:S(2)}) %collective-permute-start.2) | collective-permute-done | bytes 262176 | tf_op jit(solution)/shard_map/preact/ppermute | solution.py:101
  68.5 1.9 collective-permute-start.3
  70.5 12.1 %collective-permute-start.7 = (bf16[8,128,512]{2,1,0:T(8,128)(2,1)}, bf16[8,128,512]{2,1,0:T(8,128)(2,1)S(1)}, u32[]{:S(2)}, u32[]{:S(2)}) collective-permute-start(bf16[8,128,512]{2,1,0:T(8,128)(2,1)} %get-tuple-element.19), channel_id=1, source_target_pairs={{0,8},{8,0},{1,9},{9,1},{2,10},{10,2},{3,11},{11,3},{4,12},{12,4},... | collective-permute-start | bytes 3145736 | tf_op jit(solution)/shard_map/aggregate/ppermute | solution.py:151
  83.7 9.2 %all_to_all.15 = bf16[2,128,512]{2,1,0:T(8,128)(2,1)S(1)} all-to-all(bf16[2,128,512]{2,1,0:T(8,128)(2,1)S(1)} %bitcast.18), channel_id=1, replica_groups=mesh['x'=4,'zo'=3,'zi'=4,'core'=2,'feat'=8] {'core'}, dimensions={0} | all-to-all | bytes 524288 | tf_op jit(solution)/shard_map/swap/all_to_all | solution.py:167
  92.9 1.9 collective-permute-start.8
  94.8 4.6 %collective-permute-start.12 = (bf16[256,512]{1,0:T(8,128)(2,1)S(1)}, bf16[256,512]{1,0:T(8,128)(2,1)S(1)}, u32[]{:S(2)}, u32[]{:S(2)}) collective-permute-start(bf16[256,512]{1,0:T(8,128)(2,1)S(1)} %bitcast.14), channel_id=1, source_target_pairs={{0,7},{1,0},{2,1},{3,2},{4,3},{5,4},{6,5},{7,6},{8,15},{9,8},{10,9... | collective-permute-start | bytes 786440 | tf_op jit(solution)/shard_map/fold/ppermute | solution.py:139
  99.4 4.1 %collective-permute-done.8.refs_1_ = bf16[256,512]{1,0:T(8,128)(2,1)S(1)} collective-permute-done((bf16[256,512]{1,0:T(8,128)(2,1)S(1)}, bf16[256,512]{1,0:T(8,128)(2,1)S(1)}, u32[]{:S(2)}, u32[]{:S(2)}) %collective-permute-start.8) | collective-permute-done | bytes 262176 | tf_op jit(solution)/shard_map/fold/ppermute | solution.py:137
  103.6 1.9 collective-permute-start.9
  105.5 4.6 %collective-permute-start.13 = (bf16[256,512]{1,0:T(8,128)(2,1)S(1)}, bf16[256,512]{1,0:T(8,128)(2,1)S(1)}, u32[]{:S(2)}, u32[]{:S(2)}) collective-permute-start(bf16[256,512]{1,0:T(8,128)(2,1)S(1)} %collective-permute-done.12.refs_7_), channel_id=1, source_target_pairs={{0,7},{1,0},{2,1},{3,2},{4,3},{5,4},{6,5},{7,6},{8,15},{9,8},{10,9... | collective-permute-start | bytes 786440 | tf_op jit(solution)/shard_map/fold/ppermute | solution.py:139
  110.1 3.2 %collective-permute-done.9.refs_2_ = bf16[256,512]{1,0:T(8,128)(2,1)S(1)} collective-permute-done((bf16[256,512]{1,0:T(8,128)(2,1)S(1)}, bf16[256,512]{1,0:T(8,128)(2,1)S(1)}, u32[]{:S(2)}, u32[]{:S(2)}) %collective-permute-start.9) | collective-permute-done | bytes 262176 | tf_op jit(solution)/shard_map/fold/ppermute | solution.py:137
  113.3 1.9 collective-permute-start.10
  115.2 4.6 %collective-permute-start.14 = (bf16[256,512]{1,0:T(8,128)(2,1)S(1)}, bf16[256,512]{1,0:T(8,128)(2,1)S(1)}, u32[]{:S(2)}, u32[]{:S(2)}) collective-permute-start(bf16[256,512]{1,0:T(8,128)(2,1)S(1)} %collective-permute-done.13.refs_6_), channel_id=1, source_target_pairs={{0,7},{1,0},{2,1},{3,2},{4,3},{5,4},{6,5},{7,6},{8,15},{9,8},{10,9... | collective-permute-start | bytes 786440 | tf_op jit(solution)/shard_map/fold/ppermute | solution.py:139
  119.8 2.3 %collective-permute-done.10.refs_3_ = bf16[256,512]{1,0:T(8,128)(2,1)S(1)} collective-permute-done((bf16[256,512]{1,0:T(8,128)(2,1)S(1)}, bf16[256,512]{1,0:T(8,128)(2,1)S(1)}, u32[]{:S(2)}, u32[]{:S(2)}) %collective-permute-start.10) | collective-permute-done | bytes 262176 | tf_op jit(solution)/shard_map/fold/ppermute | solution.py:137
  122.0 1.9 collective-permute-start.11
  125.5 4.9 %collective-permute-done.11.refs_4_ = bf16[256,512]{1,0:T(8,128)(2,1)S(1)} collective-permute-done((bf16[256,512]{1,0:T(8,128)(2,1)S(1)}, bf16[256,512]{1,0:T(8,128)(2,1)S(1)}, u32[]{:S(2)}, u32[]{:S(2)}) %collective-permute-start.11) | collective-permute-done | bytes 262176 | tf_op jit(solution)/shard_map/fold/ppermute | solution.py:137
  131.6 22.7 %all_to_all.16 = bf16[16,32,512]{2,1,0:T(8,128)(2,1)S(1)} all-to-all(bf16[16,32,512]{2,1,0:T(8,128)(2,1)S(1)} %bitcast.12), channel_id=1, replica_groups=mesh['x'=4,'zo'=3,'zi'=4,'core'=2,'feat'=8] {'x','zi'}, dimensions={0} | all-to-all | bytes 1048576 | tf_op jit(solution)/shard_map/sum_x_zi/all_to_all | solution.py:16
  154.4 24.0 %all_gather.6 = bf16[384,512]{1,0:T(8,128)(2,1)S(1)} all-gather(bf16[32,512]{1,0:T(8,128)(2,1)S(1)} %reduce_sum.44), channel_id=1, replica_groups=mesh['x'=4,'zo'=3,'zi'=4,'core'=2,'feat'=8] {'zo','zi'}, dimensions={0}, use_global_device_ids=true | all-gather | bytes 425984 | tf_op jit(solution)/shard_map/sum_z/all_gather | solution.py:25
  178.5 10.3 %all_gather.7 = bf16[512,512]{1,0:T(8,128)(2,1)S(1)} all-gather(bf16[128,512]{1,0:T(8,128)(2,1)S(1)} %reduce_sum.45), channel_id=1, replica_groups=mesh['x'=4,'zo'=3,'zi'=4,'core'=2,'feat'=8] {'x'}, dimensions={0}, use_global_device_ids=true | all-gather | bytes 655360 | tf_op jit(solution)/shard_map/gather_x/all_gather | solution.py:29
  188.9 12.8 %collective-permute-start.15 = (bf16[512,512]{1,0:T(8,128)(2,1)S(1)}, bf16[512,512]{1,0:T(8,128)(2,1)S(1)}, u32[]{:S(2)}, u32[]{:S(2)}) collective-permute-start(bf16[512,512]{1,0:T(8,128)(2,1)S(1)} %all_gather.7), channel_id=1, source_target_pairs={{0,8},{8,0},{1,9},{9,1},{2,10},{10,2},{3,11},{11,3},{4,12},{12,4},... | collective-permute-start | bytes 1572872 | tf_op jit(solution)/shard_map/gather_core/ppermute | solution.py:31
  203.2 1.6 maximum_convert_fusion
  (39 shorter events, 6.1 us)
Async XLA Ops:
  0.6 14.0 %copy-start.5 = (s32[8,4]{0,1:T(4,128)S(1)}, s32[8,4]{0,1:T(4,128)}, u32[]{:S(2)}) copy-start(s32[8,4]{0,1:T(4,128)} %param.9) | copy-start | bytes 388
  0.6 38.9 %copy-start = (bf16[8,4,128,128]{3,2,1,0:T(8,128)(2,1)S(1)}, bf16[8,4,128,128]{3,2,1,0:T(8,128)(2,1)}, u32[]{:S(2)}) copy-start(bf16[8,4,128,128]{3,2,1,0:T(8,128)(2,1)} %tiles_ref.1) | copy-start | bytes 3145732
  0.7 38.9 %copy-start.1 = (bf16[512,1024]{1,0:T(8,128)(2,1)S(1)}, bf16[512,1024]{1,0:T(8,128)(2,1)}, u32[]{:S(2)}) copy-start(bf16[512,1024]{1,0:T(8,128)(2,1)} %weight_ref.1) | copy-start | bytes 3145732
  0.7 38.9 %copy-start.2 = (s32[8]{0:T(128)S(1)}, s32[8]{0:T(128)}, u32[]{:S(2)}) copy-start(s32[8]{0:T(128)} %counts_ref.1) | copy-start | bytes 100
  7.0 32.5 %all-to-all-start = ((bf16[8,128,512]{2,1,0:T(8,128)(2,1)}), bf16[8,128,512]{2,1,0:T(8,128)(2,1)S(1)}, u32[]{:S(2)}, u32[]{:S(2)}) async-start(bf16[8,128,512]{2,1,0:T(8,128)(2,1)} %pick.1), calls=%async_computation | async-start | bytes 2097152 | tf_op jit(solution)/shard_map/pick/all_to_all | solution.py:148
  42.3 8.3 %collective-permute-start = (bf16[128,1024]{1,0:T(8,128)(2,1)S(1)}, bf16[128,1024]{1,0:T(8,128)(2,1)S(1)}, u32[]{:S(2)}, u32[]{:S(2)}) collective-permute-start(bf16[128,1024]{1,0:T(8,128)(2,1)S(1)} %get-tuple-element.11), channel_id=1, source_target_pairs={{0,1},{1,2},{2,3},{3,4},{4,5},{5,6},{6,7},{7,0},{8,9},{9,10},{10,1... | collective-permute-start | bytes 786440 | tf_op jit(solution)/shard_map/preact/ppermute | solution.py:101
  44.2 8.5 %collective-permute-start.4 = (bf16[128,1024]{1,0:T(8,128)(2,1)S(1)}, bf16[128,1024]{1,0:T(8,128)(2,1)S(1)}, u32[]{:S(2)}, u32[]{:S(2)}) collective-permute-start(bf16[128,1024]{1,0:T(8,128)(2,1)S(1)} %get-tuple-element.16), channel_id=1, source_target_pairs={{0,7},{1,0},{2,1},{3,2},{4,3},{5,4},{6,5},{7,6},{8,15},{9,8},{10,9... | collective-permute-start | bytes 786440 | tf_op jit(solution)/shard_map/preact/ppermute | solution.py:104
  50.7 32.2 %copy-start.3 = (bf16[128,1024]{1,0:T(8,128)(2,1)S(1)}, bf16[128,1024]{1,0:T(8,128)(2,1)}, u32[]{:S(2)}) copy-start(bf16[128,1024]{1,0:T(8,128)(2,1)} %param.13) | copy-start | bytes 786436
  50.7 8.5 %collective-permute-start.1 = (bf16[128,1024]{1,0:T(8,128)(2,1)S(1)}, bf16[128,1024]{1,0:T(8,128)(2,1)S(1)}, u32[]{:S(2)}, u32[]{:S(2)}) collective-permute-start(bf16[128,1024]{1,0:T(8,128)(2,1)S(1)} %add_convert_fusion.4), channel_id=1, source_target_pairs={{0,1},{1,2},{2,3},{3,4},{4,5},{5,6},{6,7},{7,0},{8,9},{9,10},{10,1... | collective-permute-start | bytes 786440 | tf_op jit(solution)/shard_map/preact/ppermute | solution.py:101
  52.9 8.3 %collective-permute-start.5 = (bf16[128,1024]{1,0:T(8,128)(2,1)S(1)}, bf16[128,1024]{1,0:T(8,128)(2,1)S(1)}, u32[]{:S(2)}, u32[]{:S(2)}) collective-permute-start(bf16[128,1024]{1,0:T(8,128)(2,1)S(1)} %add_convert_fusion.1), channel_id=1, source_target_pairs={{0,7},{1,0},{2,1},{3,2},{4,3},{5,4},{6,5},{7,6},{8,15},{9,8},{10,9... | collective-permute-start | bytes 786440 | tf_op jit(solution)/shard_map/preact/ppermute | solution.py:104
  59.3 9.2 %collective-permute-start.2 = (bf16[128,1024]{1,0:T(8,128)(2,1)S(1)}, bf16[128,1024]{1,0:T(8,128)(2,1)S(1)}, u32[]{:S(2)}, u32[]{:S(2)}) collective-permute-start(bf16[128,1024]{1,0:T(8,128)(2,1)S(1)} %add_convert_fusion.3), channel_id=1, source_target_pairs={{0,1},{1,2},{2,3},{3,4},{4,5},{5,6},{6,7},{7,0},{8,9},{9,10},{10,1... | collective-permute-start | bytes 786440 | tf_op jit(solution)/shard_map/preact/ppermute | solution.py:101
  61.3 21.3 %collective-permute-start.6 = (bf16[128,1024]{1,0:T(8,128)(2,1)S(1)}, bf16[128,1024]{1,0:T(8,128)(2,1)S(1)}, u32[]{:S(2)}, u32[]{:S(2)}) collective-permute-start(bf16[128,1024]{1,0:T(8,128)(2,1)S(1)} %add_convert_fusion), channel_id=1, source_target_pairs={{0,7},{1,0},{2,1},{3,2},{4,3},{5,4},{6,5},{7,6},{8,15},{9,8},{10,9... | collective-permute-start | bytes 786440 | tf_op jit(solution)/shard_map/preact/ppermute | solution.py:104
  68.5 14.0 %collective-permute-start.3 = (bf16[128,1024]{1,0:T(8,128)(2,1)S(1)}, bf16[128,1024]{1,0:T(8,128)(2,1)S(1)}, u32[]{:S(2)}, u32[]{:S(2)}) collective-permute-start(bf16[128,1024]{1,0:T(8,128)(2,1)S(1)} %add_convert_fusion.2), channel_id=1, source_target_pairs={{0,1},{1,2},{2,3},{3,4},{4,5},{5,6},{6,7},{7,0},{8,9},{9,10},{10,1... | collective-permute-start | bytes 786440 | tf_op jit(solution)/shard_map/preact/ppermute | solution.py:101
  70.5 53.5 %collective-permute-start.7 = (bf16[8,128,512]{2,1,0:T(8,128)(2,1)}, bf16[8,128,512]{2,1,0:T(8,128)(2,1)S(1)}, u32[]{:S(2)}, u32[]{:S(2)}) collective-permute-start(bf16[8,128,512]{2,1,0:T(8,128)(2,1)} %get-tuple-element.19), channel_id=1, source_target_pairs={{0,8},{8,0},{1,9},{9,1},{2,10},{10,2},{3,11},{11,3},{4,12},{12,4},... | collective-permute-start | bytes 3145736 | tf_op jit(solution)/shard_map/aggregate/ppermute | solution.py:151
  83.3 42.1 %copy-start.4 = (bf16[128,1024]{1,0:T(8,128)(2,1)}, bf16[128,1024]{1,0:T(8,128)(2,1)S(1)}, u32[]{:S(2)}) copy-start(bf16[128,1024]{1,0:T(8,128)(2,1)S(1)} %get-tuple-element.23) | copy-start | bytes 786436
  92.9 10.6 %collective-permute-start.8 = (bf16[256,512]{1,0:T(8,128)(2,1)S(1)}, bf16[256,512]{1,0:T(8,128)(2,1)S(1)}, u32[]{:S(2)}, u32[]{:S(2)}) collective-permute-start(bf16[256,512]{1,0:T(8,128)(2,1)S(1)} %bitcast.13), channel_id=1, source_target_pairs={{0,1},{1,2},{2,3},{3,4},{4,5},{5,6},{6,7},{7,0},{8,9},{9,10},{10,1... | collective-permute-start | bytes 786440 | tf_op jit(solution)/shard_map/fold/ppermute | solution.py:137
  94.8 10.6 %collective-permute-start.12 = (bf16[256,512]{1,0:T(8,128)(2,1)S(1)}, bf16[256,512]{1,0:T(8,128)(2,1)S(1)}, u32[]{:S(2)}, u32[]{:S(2)}) collective-permute-start(bf16[256,512]{1,0:T(8,128)(2,1)S(1)} %bitcast.14), channel_id=1, source_target_pairs={{0,7},{1,0},{2,1},{3,2},{4,3},{5,4},{6,5},{7,6},{8,15},{9,8},{10,9... | collective-permute-start | bytes 786440 | tf_op jit(solution)/shard_map/fold/ppermute | solution.py:139
  103.6 9.7 %collective-permute-start.9 = (bf16[256,512]{1,0:T(8,128)(2,1)S(1)}, bf16[256,512]{1,0:T(8,128)(2,1)S(1)}, u32[]{:S(2)}, u32[]{:S(2)}) collective-permute-start(bf16[256,512]{1,0:T(8,128)(2,1)S(1)} %collective-permute-done.8.refs_1_), channel_id=1, source_target_pairs={{0,1},{1,2},{2,3},{3,4},{4,5},{5,6},{6,7},{7,0},{8,9},{9,10},{10,1... | collective-permute-start | bytes 786440 | tf_op jit(solution)/shard_map/fold/ppermute | solution.py:137
  105.5 9.7 %collective-permute-start.13 = (bf16[256,512]{1,0:T(8,128)(2,1)S(1)}, bf16[256,512]{1,0:T(8,128)(2,1)S(1)}, u32[]{:S(2)}, u32[]{:S(2)}) collective-permute-start(bf16[256,512]{1,0:T(8,128)(2,1)S(1)} %collective-permute-done.12.refs_7_), channel_id=1, source_target_pairs={{0,7},{1,0},{2,1},{3,2},{4,3},{5,4},{6,5},{7,6},{8,15},{9,8},{10,9... | collective-permute-start | bytes 786440 | tf_op jit(solution)/shard_map/fold/ppermute | solution.py:139
  113.3 8.8 %collective-permute-start.10 = (bf16[256,512]{1,0:T(8,128)(2,1)S(1)}, bf16[256,512]{1,0:T(8,128)(2,1)S(1)}, u32[]{:S(2)}, u32[]{:S(2)}) collective-permute-start(bf16[256,512]{1,0:T(8,128)(2,1)S(1)} %collective-permute-done.9.refs_2_), channel_id=1, source_target_pairs={{0,1},{1,2},{2,3},{3,4},{4,5},{5,6},{6,7},{7,0},{8,9},{9,10},{10,1... | collective-permute-start | bytes 786440 | tf_op jit(solution)/shard_map/fold/ppermute | solution.py:137
  115.2 10.3 %collective-permute-start.14 = (bf16[256,512]{1,0:T(8,128)(2,1)S(1)}, bf16[256,512]{1,0:T(8,128)(2,1)S(1)}, u32[]{:S(2)}, u32[]{:S(2)}) collective-permute-start(bf16[256,512]{1,0:T(8,128)(2,1)S(1)} %collective-permute-done.13.refs_6_), channel_id=1, source_target_pairs={{0,7},{1,0},{2,1},{3,2},{4,3},{5,4},{6,5},{7,6},{8,15},{9,8},{10,9... | collective-permute-start | bytes 786440 | tf_op jit(solution)/shard_map/fold/ppermute | solution.py:139
  122.0 8.3 %collective-permute-start.11 = (bf16[256,512]{1,0:T(8,128)(2,1)S(1)}, bf16[256,512]{1,0:T(8,128)(2,1)S(1)}, u32[]{:S(2)}, u32[]{:S(2)}) collective-permute-start(bf16[256,512]{1,0:T(8,128)(2,1)S(1)} %collective-permute-done.10.refs_3_), channel_id=1, source_target_pairs={{0,1},{1,2},{2,3},{3,4},{4,5},{5,6},{6,7},{7,0},{8,9},{9,10},{10,1... | collective-permute-start | bytes 786440 | tf_op jit(solution)/shard_map/fold/ppermute | solution.py:137
  188.9 14.3 %collective-permute-start.15 = (bf16[512,512]{1,0:T(8,128)(2,1)S(1)}, bf16[512,512]{1,0:T(8,128)(2,1)S(1)}, u32[]{:S(2)}, u32[]{:S(2)}) collective-permute-start(bf16[512,512]{1,0:T(8,128)(2,1)S(1)} %all_gather.7), channel_id=1, source_target_pairs={{0,8},{8,0},{1,9},{9,1},{2,10},{10,2},{3,11},{11,3},{4,12},{12,4},... | collective-permute-start | bytes 1572872 | tf_op jit(solution)/shard_map/gather_core/ppermute | solution.py:31

commit v4 on v3

--- a/solution.py
+++ b/solution.py
@@ -8,8 +8,23 @@
 GRP = ("x", "zo", "zi", "core")
 ALL = GRP + ("feat",)
 SWAP = [(0, 1), (1, 0)]
-TO_RIGHT = [(i, (i + 1) % 8) for i in range(8)]
-TO_LEFT = [(i, (i - 1) % 8) for i in range(8)]
+FEAT = 8
+CORE_FEAT = ("core", "feat")
+
+
+def ring_step(ahead):
+    pairs = []
+    for i in range(FEAT):
+        pairs.append((i, (i + ahead) % FEAT))
+        pairs.append((FEAT + i, FEAT + (i - ahead) % FEAT))
+    return pairs
+
+
+FORTH, BACK = ring_step(1), ring_step(-1)
+
+
+def turn():
+    return 1 - 2 * lax.axis_index("core")
 
 
 def exchange_sum(parts, axis):
@@ -34,34 +49,32 @@
 
 
 def pick_kernel(ids_ref, table_ref, out_ref):
+    slices, _, width = out_ref.shape
     wanted = lax.broadcasted_iota(jnp.int32, (table_ref.shape[0], ids_ref.shape[1]), 0) == ids_ref[...]
-    rows = lax.dot_general(
-        wanted.astype(table_ref.dtype), table_ref[...], (((0,), (0,)), ((), ())), preferred_element_type=jnp.float32
-    )
-    out_ref[0] = rows.astype(out_ref.dtype)
+    wanted = wanted.astype(jnp.float32).T.astype(table_ref.dtype)
+    for j in range(slices):
+        rows = jnp.dot(wanted, table_ref[:, j * width:(j + 1) * width], preferred_element_type=jnp.float32)
+        out_ref[j] = rows.astype(out_ref.dtype)
 
 
 def pick(table, ids, slices):
-    rows, width = table.shape[0], table.shape[1] // slices
+    vmem = pl.BlockSpec(memory_space=pltpu.VMEM)
     return pl.pallas_call(
         pick_kernel,
-        grid=(slices,),
-        out_shape=jax.ShapeDtypeStruct((slices, ids.shape[0], width), table.dtype),
-        in_specs=[
-            pl.BlockSpec((1, ids.shape[0]), lambda j: (0, 0)),
-            pl.BlockSpec((rows, width), lambda j: (0, j)),
-        ],
-        out_specs=pl.BlockSpec((1, ids.shape[0], width), lambda j: (j, 0, 0)),
+        out_shape=jax.ShapeDtypeStruct((slices, ids.shape[0], table.shape[1] // slices), table.dtype),
+        in_specs=[vmem, vmem],
+        out_specs=vmem,
+        compiler_params=pltpu.CompilerParams(vmem_limit_bytes=32 * 2**20),
     )(ids.reshape(1, -1), table)
 
 
-def aggregate_kernel(me_ref, ids_ref, counts_ref, slices_ref, tiles_ref, weight_ref, agg_ref, *refs):
+def aggregate_kernel(place_ref, ids_ref, counts_ref, slices_ref, tiles_ref, weight_ref, agg_ref, *refs):
     *part_refs, turned = refs
     blocks, block_rows, width = slices_ref.shape
     slots = tiles_ref.shape[1]
     ones = jnp.ones((slots * tiles_ref.shape[3], 128), jnp.bfloat16)
     for k in range(blocks):
-        own = lax.rem(me_ref[0] + blocks // 2 - k + blocks, blocks)
+        own = lax.rem(place_ref[0] + place_ref[1] * (blocks // 2 - k) + blocks, blocks)
         lhs = [
             jnp.where(s < counts_ref[own], tiles_ref[own, s], jnp.zeros((), jnp.bfloat16)) for s in range(slots)
         ]
@@ -80,7 +93,7 @@
             part_refs[k + i][...] = parts[i * block_rows:(i + 1) * block_rows]
 
 
-def aggregate_and_project(me, ids, counts, slices, tiles, weight):
+def aggregate_and_project(place, ids, counts, slices, tiles, weight):
     blocks, block_rows, width = slices.shape
     vmem, smem = pl.BlockSpec(memory_space=pltpu.VMEM), pl.BlockSpec(memory_space=pltpu.SMEM)
     part = jax.ShapeDtypeStruct((block_rows, weight.shape[1]), jnp.bfloat16)
@@ -91,34 +104,43 @@
         out_specs=[vmem] * (1 + blocks),
         scratch_shapes=[pltpu.VMEM((blocks * block_rows, width), jnp.bfloat16)],
         compiler_params=pltpu.CompilerParams(vmem_limit_bytes=32 * 2**20),
-    )(me.reshape(1), ids, counts, slices, tiles, weight)
+    )(place, ids, counts, slices, tiles, weight)
     return agg, parts
 
 
 def ring_sum(parts):
-    right, left = parts[0], parts[7]
+    forth, back = parts[0], parts[7]
     for k in range(1, 5):
-        right = lax.ppermute(right, "feat", TO_RIGHT).astype(jnp.float32) + parts[k].astype(jnp.float32)
-        right = right.astype(jnp.bfloat16) if k < 4 else right
+        forth = lax.ppermute(forth, CORE_FEAT, FORTH).astype(jnp.float32) + parts[k].astype(jnp.float32)
+        forth = forth.astype(jnp.bfloat16) if k < 4 else forth
         if k < 4:
-            left = lax.ppermute(left, "feat", TO_LEFT)
+            back = lax.ppermute(back, CORE_FEAT, BACK)
             if k < 3:
-                left = (left.astype(jnp.float32) + parts[7 - k].astype(jnp.float32)).astype(jnp.bfloat16)
-    return right + left.astype(jnp.float32)
-
-
-def fold_kernel(me_ref, rows_ref, *refs):
+                back = (back.astype(jnp.float32) + parts[7 - k].astype(jnp.float32)).astype(jnp.bfloat16)
+    return forth + back.astype(jnp.float32)
+
+
+def ring_gather(block):
+    held = {0: block}
+    for k in range(1, 5):
+        held[k] = lax.ppermute(held[k - 1], CORE_FEAT, FORTH)
+        if k < 4:
+            held[FEAT - k] = lax.ppermute(held[(FEAT - k + 1) % FEAT], CORE_FEAT, BACK)
+    return [held[k] for k in range(FEAT)]
+
+
+def fold_kernel(place_ref, rows_ref, *refs):
     *grad_refs, out_ref = refs
-    me = me_ref[0]
+    me, turned = place_ref[0], place_ref[1]
     total = None
     for k, grad_ref in enumerate(grad_refs):
-        rows = rows_ref[lax.rem(me - k + len(grad_refs), len(grad_refs))]
+        rows = rows_ref[lax.rem(me - turned * k + len(grad_refs), len(grad_refs))]
         term = lax.dot_general(rows, grad_ref[...], (((0,), (0,)), ((), ())), preferred_element_type=jnp.float32)
         total = term if total is None else total + term
     out_ref[...] = total.astype(out_ref.dtype)
 
 
-def fold(me, rows, grads):
+def fold(place, rows, grads):
     width, cols = rows.shape[2], grads[0].shape[1]
     vmem = pl.BlockSpec(memory_space=pltpu.VMEM)
     return pl.pallas_call(
@@ -127,27 +149,17 @@
         in_specs=[pl.BlockSpec(memory_space=pltpu.SMEM), vmem] + [vmem] * len(grads),
         out_specs=vmem,
         compiler_params=pltpu.CompilerParams(vmem_limit_bytes=32 * 2**20),
-    )(me.reshape(1), rows, *grads)
-
-
-def ring_gather(block):
-    n = 8
-    held = {0: block}
-    for k in range(1, 5):
-        held[k] = lax.ppermute(held[k - 1], "feat", TO_RIGHT)
-        if k < 4:
-            held[n - k] = lax.ppermute(held[(n - k + 1) % n], "feat", TO_LEFT)
-    return [held[k] for k in range(n)]
+    )(place, rows, *grads)
 
 
 def shards(feature_table, sample_ids, block_ids, block_counts, block_tiles, weight, target):
     block_total, slot_total, block_rows, block_width = block_tiles.shape
     node_total = block_total * block_rows
-    me = lax.axis_index("feat")
+    place = jnp.stack([lax.axis_index("feat"), turn()])
     with jax.named_scope("pick"):
         slices = lax.all_to_all(pick(feature_table, sample_ids, block_total), "feat", 0, 0)
     with jax.named_scope("aggregate"):
-        agg, parts = aggregate_and_project(me, block_ids, block_counts, slices, block_tiles, weight)
+        agg, parts = aggregate_and_project(place, block_ids, block_counts, slices, block_tiles, weight)
         other_agg = lax.ppermute(agg, "core", SWAP)
     with jax.named_scope("preact"):
         preact = ring_sum(parts)
@@ -168,7 +180,7 @@
     with jax.named_scope("fold"):
         first = lax.axis_index("core") == 0
         rows = jnp.concatenate([jnp.where(first, agg, other_agg), jnp.where(first, other_agg, agg)], axis=1)
-        folded = fold(me, rows, ring_gather(paired.reshape(2 * block_rows, half)))
+        folded = fold(place, rows, ring_gather(paired.reshape(2 * block_rows, half)))
     weight_grad = group_sum(folded)
     return (embedding, weight_grad)
 

time: 206 us -> 209 us (1.015)
  blocking collectives: 66.3 us -> 71.4 us
  Pallas kernels: 10.4 us -> 6 us
  local copies, waits for them, and re-layouts: 0.13 us -> 2.36 us
    ppermute x1, starting transfers between devices: 12.8 us -> 18.2 us  [group_sum(): other = lax.ppermute(part, 'core', SWAP)]
    pallas_call x1, Pallas kernels: 6.32 us -> 1.46 us  [pick(): pl.pallas_call(pick_kernel, out_shape=jax.ShapeDtypeStruct((slices, ids.s...]
    ppermute x1, starting transfers between devices: 12.1 us -> 8.31 us  [shards(): other_agg = lax.ppermute(agg, 'core', SWAP)]
    all_to_all x1, blocking collectives: 22.7 us -> 26.4 us  [exchange_sum(): got = lax.all_to_all(parts, axis, 0, 0)]
    ppermute x14, starting transfers between devices: 42.9 us -> 40.4 us  [the longest x4 13.8 us: ring_gather(): held[k] = lax.ppermute(held[k - 1], CORE_FEAT, FORTH)]
    unnamed x13 -> x17, local copies, waits for them, and re-layouts: 0.11 us -> 2.35 us
  transfers between devices with their start and end apart: 17 -> 17, of which waited for: 9 -> 11; matrix products, arithmetic and copies ran while one was open for 1% -> 2% of each run, Pallas kernels for 0% -> 0%
where the time goes in v4:
time: 209 us; the launch traced here: 208 us
  starting transfers between devices  74.5 us (36%)
  blocking collectives  71.4 us (34%)
  waiting for transfers between devices  47.9 us (23%)
  Pallas kernels  6 us (3%)
  other arithmetic  5.15 us (2%)
  local copies, waits for them, and re-layouts  2.36 us (1%)
    all_to_all x1, blocking collectives, exchange_sum(): got = lax.all_to_all(parts, axis, 0, 0)  26.4 us
    all_gather x1, blocking collectives, group_sum(): lax.all_gather(part.astype(jnp.bfloat16), ('zo', 'zi'), axis=0, tiled=True)  25.3 us
    all_to_all x1, waiting for transfers between devices, shards(): lax.all_to_all(pick(feature_table, sample_ids, block_total), 'feat', 0, 0)  24.7 us
    ppermute x1, starting transfers between devices, group_sum(): other = lax.ppermute(part, 'core', SWAP)  18.2 us
    ppermute x4, starting transfers between devices, ring_gather(): held[k] = lax.ppermute(held[k - 1], CORE_FEAT, FORTH)  13.8 us
    ppermute x4, starting transfers between devices, ring_sum(): lax.ppermute(forth, CORE_FEAT, FORTH).astype(jnp.float32)  11 us
    all_gather x1, blocking collectives, group_sum(): part = lax.all_gather(part, 'x', axis=0, tiled=True)  10.5 us
    ppermute x4, waiting for transfers between devices, ring_sum(): lax.ppermute(forth, CORE_FEAT, FORTH).astype(jnp.float32)  9.28 us
  transfers between devices with their start and end apart: 17, of which 11 were waited for; matrix products, arithmetic and copies ran while one was open for 2% of the time, Pallas kernels for 0%

profile of v4, /device:TPU:1, one launch (start us, length us, event | category | flops | bytes accessed | tf_op | source)
XLA Modules:
  0.0 208.3 jit_solution(11468161777298972304)
XLA Ops:
  4.4 7.7 %all-to-all-start = ((bf16[8,128,512]{2,1,0:T(8,128)(2,1)}), bf16[8,128,512]{2,1,0:T(8,128)(2,1)S(1)}, u32[]{:S(2)}, u32[]{:S(2)}) async-start(bf16[8,128,512]{2,1,0:T(8,128)(2,1)} %pick.1), calls=%async_computation | async-start | bytes 2097152 | tf_op jit(solution)/shard_map/pick/all_to_all | solution.py:160
  12.2 24.7 %all-to-all-done.slices_ref = bf16[8,128,512]{2,1,0:T(8,128)(2,1)S(1)} async-done(((bf16[8,128,512]{2,1,0:T(8,128)(2,1)}), bf16[8,128,512]{2,1,0:T(8,128)(2,1)S(1)}, u32[]{:S(2)}, u32[]{:S(2)}) %all-to-all-start) | async-done | bytes 1048608 | tf_op jit(solution)/shard_map/pick/all_to_all | solution.py:160
  36.9 2.7 %aggregate.1 = (bf16[8,128,512]{2,1,0:T(8,128)(2,1)}, bf16[128,1024]{1,0:T(8,128)(2,1)S(1)}, bf16[128,1024]{1,0:T(8,128)(2,1)S(1)}, bf16[128,1024]{1,0:T(8,128)(...) custom-call(s32[2]{0:T(128)S(1)} %pad_add_fusion.place_ref, ...), custom_call_target="tpu_custom_call" | custom-call | tf_op jit(solution)/shard_map/aggregate/pallas_call | solution.py:100
  39.6 1.9 collective-permute-start
  41.5 3.4 %collective-permute-start.4 = (bf16[128,1024]{1,0:T(8,128)(2,1)S(1)}, bf16[128,1024]{1,0:T(8,128)(2,1)S(1)}, u32[]{:S(2)}, u32[]{:S(2)}) collective-permute-start(bf16[128,1024]{1,0:T(8,128)(2,1)S(1)} %get-tuple-element.16), channel_id=1, source_target_pairs={{0,7},{8,9},{1,0},{9,10},{2,1},{10,11},{3,2},{11,12},{4,3},{12,13}... | collective-permute-start | bytes 786440 | tf_op jit(solution)/shard_map/preact/ppermute | solution.py:117
  44.9 1.8 collective-permute-done
  46.8 3.3 %collective-permute-start.1 = (bf16[128,1024]{1,0:T(8,128)(2,1)S(1)}, bf16[128,1024]{1,0:T(8,128)(2,1)S(1)}, u32[]{:S(2)}, u32[]{:S(2)}) collective-permute-start(bf16[128,1024]{1,0:T(8,128)(2,1)S(1)} %add_convert_fusion.4), channel_id=1, source_target_pairs={{0,1},{8,15},{1,2},{9,8},{2,3},{10,9},{3,4},{11,10},{4,5},{12,11},... | collective-permute-start | bytes 786440 | tf_op jit(solution)/shard_map/preact/ppermute | solution.py:114
  50.2 2.8 %collective-permute-start.5 = (bf16[128,1024]{1,0:T(8,128)(2,1)S(1)}, bf16[128,1024]{1,0:T(8,128)(2,1)S(1)}, u32[]{:S(2)}, u32[]{:S(2)}) collective-permute-start(bf16[128,1024]{1,0:T(8,128)(2,1)S(1)} %add_convert_fusion.1), channel_id=1, source_target_pairs={{0,7},{8,9},{1,0},{9,10},{2,1},{10,11},{3,2},{11,12},{4,3},{12,13}... | collective-permute-start | bytes 786440 | tf_op jit(solution)/shard_map/preact/ppermute | solution.py:117
  52.9 3.9 %collective-permute-done.1 = bf16[128,1024]{1,0:T(8,128)(2,1)S(1)} collective-permute-done((bf16[128,1024]{1,0:T(8,128)(2,1)S(1)}, bf16[128,1024]{1,0:T(8,128)(2,1)S(1)}, u32[]{:S(2)}, u32[]{:S(2)}) %collective-permute-start.1) | collective-permute-done | bytes 262176 | tf_op jit(solution)/shard_map/preact/ppermute | solution.py:114
  56.9 3.0 %collective-permute-start.2 = (bf16[128,1024]{1,0:T(8,128)(2,1)S(1)}, bf16[128,1024]{1,0:T(8,128)(2,1)S(1)}, u32[]{:S(2)}, u32[]{:S(2)}) collective-permute-start(bf16[128,1024]{1,0:T(8,128)(2,1)S(1)} %add_convert_fusion.3), channel_id=1, source_target_pairs={{0,1},{8,15},{1,2},{9,8},{2,3},{10,9},{3,4},{11,10},{4,5},{12,11},... | collective-permute-start | bytes 786440 | tf_op jit(solution)/shard_map/preact/ppermute | solution.py:114
  60.0 2.3 %collective-permute-start.6 = (bf16[128,1024]{1,0:T(8,128)(2,1)S(1)}, bf16[128,1024]{1,0:T(8,128)(2,1)S(1)}, u32[]{:S(2)}, u32[]{:S(2)}) collective-permute-start(bf16[128,1024]{1,0:T(8,128)(2,1)S(1)} %add_convert_fusion), channel_id=1, source_target_pairs={{0,7},{8,9},{1,0},{9,10},{2,1},{10,11},{3,2},{11,12},{4,3},{12,13}... | collective-permute-start | bytes 786440 | tf_op jit(solution)/shard_map/preact/ppermute | solution.py:117
  62.3 3.6 %collective-permute-done.2 = bf16[128,1024]{1,0:T(8,128)(2,1)S(1)} collective-permute-done((bf16[128,1024]{1,0:T(8,128)(2,1)S(1)}, bf16[128,1024]{1,0:T(8,128)(2,1)S(1)}, u32[]{:S(2)}, u32[]{:S(2)}) %collective-permute-start.2) | collective-permute-done | bytes 262176 | tf_op jit(solution)/shard_map/preact/ppermute | solution.py:114
  65.9 2.8 %collective-permute-start.3 = (bf16[128,1024]{1,0:T(8,128)(2,1)S(1)}, bf16[128,1024]{1,0:T(8,128)(2,1)S(1)}, u32[]{:S(2)}, u32[]{:S(2)}) collective-permute-start(bf16[128,1024]{1,0:T(8,128)(2,1)S(1)} %add_convert_fusion.2), channel_id=1, source_target_pairs={{0,1},{8,15},{1,2},{9,8},{2,3},{10,9},{3,4},{11,10},{4,5},{12,11},... | collective-permute-start | bytes 786440 | tf_op jit(solution)/shard_map/preact/ppermute | solution.py:114
  68.8 8.3 %collective-permute-start.7 = (bf16[8,128,512]{2,1,0:T(8,128)(2,1)}, bf16[8,128,512]{2,1,0:T(8,128)(2,1)}, u32[]{:S(2)}, u32[]{:S(2)}) collective-permute-start(bf16[8,128,512]{2,1,0:T(8,128)(2,1)} %get-tuple-element.19), channel_id=1, source_target_pairs={{0,8},{8,0},{1,9},{9,1},{2,10},{10,2},{3,11},{11,3},{4,12},{12,4},... | collective-permute-start | bytes 3145736 | tf_op jit(solution)/shard_map/aggregate/ppermute | solution.py:163
  78.3 9.2 %all_to_all.15 = bf16[2,128,512]{2,1,0:T(8,128)(2,1)S(1)} all-to-all(bf16[2,128,512]{2,1,0:T(8,128)(2,1)S(1)} %bitcast.20), channel_id=1, replica_groups=mesh['x'=4,'zo'=3,'zi'=4,'core'=2,'feat'=8] {'core'}, dimensions={0} | all-to-all | bytes 524288 | tf_op jit(solution)/shard_map/swap/all_to_all | solution.py:179
  87.5 1.9 collective-permute-start.8
  89.4 3.4 %collective-permute-start.12 = (bf16[256,512]{1,0:T(8,128)(2,1)S(1)}, bf16[256,512]{1,0:T(8,128)(2,1)S(1)}, u32[]{:S(2)}, u32[]{:S(2)}) collective-permute-start(bf16[256,512]{1,0:T(8,128)(2,1)S(1)} %bitcast.15), channel_id=1, source_target_pairs={{0,7},{8,9},{1,0},{9,10},{2,1},{10,11},{3,2},{11,12},{4,3},{12,13}... | collective-permute-start | bytes 786440 | tf_op jit(solution)/shard_map/fold/ppermute | solution.py:128
  92.8 2.1 %collective-permute-done.8.refs_1_ = bf16[256,512]{1,0:T(8,128)(2,1)S(1)} collective-permute-done((bf16[256,512]{1,0:T(8,128)(2,1)S(1)}, bf16[256,512]{1,0:T(8,128)(2,1)S(1)}, u32[]{:S(2)}, u32[]{:S(2)}) %collective-permute-start.8) | collective-permute-done | bytes 262176 | tf_op jit(solution)/shard_map/fold/ppermute | solution.py:126
  94.9 2.8 %collective-permute-start.9 = (bf16[256,512]{1,0:T(8,128)(2,1)S(1)}, bf16[256,512]{1,0:T(8,128)(2,1)S(1)}, u32[]{:S(2)}, u32[]{:S(2)}) collective-permute-start(bf16[256,512]{1,0:T(8,128)(2,1)S(1)} %collective-permute-done.8.refs_1_), channel_id=1, source_target_pairs={{0,1},{8,15},{1,2},{9,8},{2,3},{10,9},{3,4},{11,10},{4,5},{12,11},... | collective-permute-start | bytes 786440 | tf_op jit(solution)/shard_map/fold/ppermute | solution.py:126
  97.7 1.7 collective-permute-done.12.refs_7_
  99.4 1.9 collective-permute-start.13
  102.0 4.2 %collective-permute-start.10 = (bf16[256,512]{1,0:T(8,128)(2,1)S(1)}, bf16[256,512]{1,0:T(8,128)(2,1)S(1)}, u32[]{:S(2)}, u32[]{:S(2)}) collective-permute-start(bf16[256,512]{1,0:T(8,128)(2,1)S(1)} %collective-permute-done.9.refs_2_), channel_id=1, source_target_pairs={{0,1},{8,15},{1,2},{9,8},{2,3},{10,9},{3,4},{11,10},{4,5},{12,11},... | collective-permute-start | bytes 786440 | tf_op jit(solution)/shard_map/fold/ppermute | solution.py:126
  106.2 4.6 %collective-permute-done.13.refs_6_ = bf16[256,512]{1,0:T(8,128)(2,1)S(1)} collective-permute-done((bf16[256,512]{1,0:T(8,128)(2,1)S(1)}, bf16[256,512]{1,0:T(8,128)(2,1)S(1)}, u32[]{:S(2)}, u32[]{:S(2)}) %collective-permute-start.13) | collective-permute-done | bytes 262176 | tf_op jit(solution)/shard_map/fold/ppermute | solution.py:128
  110.8 1.9 collective-permute-start.14
  112.7 4.8 %collective-permute-start.11 = (bf16[256,512]{1,0:T(8,128)(2,1)S(1)}, bf16[256,512]{1,0:T(8,128)(2,1)S(1)}, u32[]{:S(2)}, u32[]{:S(2)}) collective-permute-start(bf16[256,512]{1,0:T(8,128)(2,1)S(1)} %collective-permute-done.10.refs_3_), channel_id=1, source_target_pairs={{0,1},{8,15},{1,2},{9,8},{2,3},{10,9},{3,4},{11,10},{4,5},{12,11},... | collective-permute-start | bytes 786440 | tf_op jit(solution)/shard_map/fold/ppermute | solution.py:126
  117.6 1.7 broadcast_select_fusion.1
  119.4 1.9 collective-permute-done.14.refs_5_
  122.8 1.8 fold.1
  124.6 26.4 %all_to_all.16 = bf16[16,32,512]{2,1,0:T(8,128)(2,1)S(1)} all-to-all(bf16[16,32,512]{2,1,0:T(8,128)(2,1)S(1)} %bitcast.13), channel_id=1, replica_groups=mesh['x'=4,'zo'=3,'zi'=4,'core'=2,'feat'=8] {'x','zi'}, dimensions={0} | all-to-all | bytes 1048576 | tf_op jit(solution)/shard_map/sum_x_zi/all_to_all | solution.py:31
  151.1 25.3 %all_gather.6 = bf16[384,512]{1,0:T(8,128)(2,1)S(1)} all-gather(bf16[32,512]{1,0:T(8,128)(2,1)S(1)} %reduce_sum.44), channel_id=1, replica_groups=mesh['x'=4,'zo'=3,'zi'=4,'core'=2,'feat'=8] {'zo','zi'}, dimensions={0}, use_global_device_ids=true | all-gather | bytes 425984 | tf_op jit(solution)/shard_map/sum_z/all_gather | solution.py:40
  176.5 10.5 %all_gather.7 = bf16[512,512]{1,0:T(8,128)(2,1)S(1)} all-gather(bf16[128,512]{1,0:T(8,128)(2,1)S(1)} %reduce_sum.45), channel_id=1, replica_groups=mesh['x'=4,'zo'=3,'zi'=4,'core'=2,'feat'=8] {'x'}, dimensions={0}, use_global_device_ids=true | all-gather | bytes 655360 | tf_op jit(solution)/shard_map/gather_x/all_gather | solution.py:44
  187.0 18.2 %collective-permute-start.15 = (bf16[512,512]{1,0:T(8,128)(2,1)S(1)}, bf16[512,512]{1,0:T(8,128)(2,1)S(1)}, u32[]{:S(2)}, u32[]{:S(2)}) collective-permute-start(bf16[512,512]{1,0:T(8,128)(2,1)S(1)} %all_gather.7), channel_id=1, source_target_pairs={{0,8},{8,0},{1,9},{9,1},{2,10},{10,2},{3,11},{11,3},{4,12},{12,4},... | collective-permute-start | bytes 1572872 | tf_op jit(solution)/shard_map/gather_core/ppermute | solution.py:46
  (44 shorter events, 10.9 us)
Async XLA Ops:
  0.6 1.6 copy-start
  2.2 0.7 copy-start.4
  2.9 9.1 %copy-start.7 = (s32[8,4]{0,1:T(4,128)S(1)}, s32[8,4]{0,1:T(4,128)}, u32[]{:S(2)}) copy-start(s32[8,4]{0,1:T(4,128)} %param.9) | copy-start | bytes 388
  2.9 34.0 %copy-start.1 = (bf16[8,4,128,128]{3,2,1,0:T(8,128)(2,1)S(1)}, bf16[8,4,128,128]{3,2,1,0:T(8,128)(2,1)}, u32[]{:S(2)}) copy-start(bf16[8,4,128,128]{3,2,1,0:T(8,128)(2,1)} %tiles_ref.1) | copy-start | bytes 3145732
  2.9 34.0 %copy-start.2 = (bf16[512,1024]{1,0:T(8,128)(2,1)S(1)}, bf16[512,1024]{1,0:T(8,128)(2,1)}, u32[]{:S(2)}) copy-start(bf16[512,1024]{1,0:T(8,128)(2,1)} %weight_ref.1) | copy-start | bytes 3145732
  2.9 34.0 %copy-start.3 = (s32[8]{0:T(128)S(1)}, s32[8]{0:T(128)}, u32[]{:S(2)}) copy-start(s32[8]{0:T(128)} %counts_ref.1) | copy-start | bytes 100
  4.4 32.5 %all-to-all-start = ((bf16[8,128,512]{2,1,0:T(8,128)(2,1)}), bf16[8,128,512]{2,1,0:T(8,128)(2,1)S(1)}, u32[]{:S(2)}, u32[]{:S(2)}) async-start(bf16[8,128,512]{2,1,0:T(8,128)(2,1)} %pick.1), calls=%async_computation | async-start | bytes 2097152 | tf_op jit(solution)/shard_map/pick/all_to_all | solution.py:160
  39.6 7.1 %collective-permute-start = (bf16[128,1024]{1,0:T(8,128)(2,1)S(1)}, bf16[128,1024]{1,0:T(8,128)(2,1)S(1)}, u32[]{:S(2)}, u32[]{:S(2)}) collective-permute-start(bf16[128,1024]{1,0:T(8,128)(2,1)S(1)} %get-tuple-element.11), channel_id=1, source_target_pairs={{0,1},{8,15},{1,2},{9,8},{2,3},{10,9},{3,4},{11,10},{4,5},{12,11},... | collective-permute-start | bytes 786440 | tf_op jit(solution)/shard_map/preact/ppermute | solution.py:114
  41.5 8.5 %collective-permute-start.4 = (bf16[128,1024]{1,0:T(8,128)(2,1)S(1)}, bf16[128,1024]{1,0:T(8,128)(2,1)S(1)}, u32[]{:S(2)}, u32[]{:S(2)}) collective-permute-start(bf16[128,1024]{1,0:T(8,128)(2,1)S(1)} %get-tuple-element.16), channel_id=1, source_target_pairs={{0,7},{8,9},{1,0},{9,10},{2,1},{10,11},{3,2},{11,12},{4,3},{12,13}... | collective-permute-start | bytes 786440 | tf_op jit(solution)/shard_map/preact/ppermute | solution.py:117
  46.8 30.6 %copy-start.5 = (bf16[128,1024]{1,0:T(8,128)(2,1)S(1)}, bf16[128,1024]{1,0:T(8,128)(2,1)}, u32[]{:S(2)}) copy-start(bf16[128,1024]{1,0:T(8,128)(2,1)} %param.13) | copy-start | bytes 786436
  46.8 10.0 %collective-permute-start.1 = (bf16[128,1024]{1,0:T(8,128)(2,1)S(1)}, bf16[128,1024]{1,0:T(8,128)(2,1)S(1)}, u32[]{:S(2)}, u32[]{:S(2)}) collective-permute-start(bf16[128,1024]{1,0:T(8,128)(2,1)S(1)} %add_convert_fusion.4), channel_id=1, source_target_pairs={{0,1},{8,15},{1,2},{9,8},{2,3},{10,9},{3,4},{11,10},{4,5},{12,11},... | collective-permute-start | bytes 786440 | tf_op jit(solution)/shard_map/preact/ppermute | solution.py:114
  50.2 9.7 %collective-permute-start.5 = (bf16[128,1024]{1,0:T(8,128)(2,1)S(1)}, bf16[128,1024]{1,0:T(8,128)(2,1)S(1)}, u32[]{:S(2)}, u32[]{:S(2)}) collective-permute-start(bf16[128,1024]{1,0:T(8,128)(2,1)S(1)} %add_convert_fusion.1), channel_id=1, source_target_pairs={{0,7},{8,9},{1,0},{9,10},{2,1},{10,11},{3,2},{11,12},{4,3},{12,13}... | collective-permute-start | bytes 786440 | tf_op jit(solution)/shard_map/preact/ppermute | solution.py:117
  56.9 9.0 %collective-permute-start.2 = (bf16[128,1024]{1,0:T(8,128)(2,1)S(1)}, bf16[128,1024]{1,0:T(8,128)(2,1)S(1)}, u32[]{:S(2)}, u32[]{:S(2)}) collective-permute-start(bf16[128,1024]{1,0:T(8,128)(2,1)S(1)} %add_convert_fusion.3), channel_id=1, source_target_pairs={{0,1},{8,15},{1,2},{9,8},{2,3},{10,9},{3,4},{11,10},{4,5},{12,11},... | collective-permute-start | bytes 786440 | tf_op jit(solution)/shard_map/preact/ppermute | solution.py:114
  60.0 17.1 %collective-permute-start.6 = (bf16[128,1024]{1,0:T(8,128)(2,1)S(1)}, bf16[128,1024]{1,0:T(8,128)(2,1)S(1)}, u32[]{:S(2)}, u32[]{:S(2)}) collective-permute-start(bf16[128,1024]{1,0:T(8,128)(2,1)S(1)} %add_convert_fusion), channel_id=1, source_target_pairs={{0,7},{8,9},{1,0},{9,10},{2,1},{10,11},{3,2},{11,12},{4,3},{12,13}... | collective-permute-start | bytes 786440 | tf_op jit(solution)/shard_map/preact/ppermute | solution.py:117
  65.9 11.2 %collective-permute-start.3 = (bf16[128,1024]{1,0:T(8,128)(2,1)S(1)}, bf16[128,1024]{1,0:T(8,128)(2,1)S(1)}, u32[]{:S(2)}, u32[]{:S(2)}) collective-permute-start(bf16[128,1024]{1,0:T(8,128)(2,1)S(1)} %add_convert_fusion.2), channel_id=1, source_target_pairs={{0,1},{8,15},{1,2},{9,8},{2,3},{10,9},{3,4},{11,10},{4,5},{12,11},... | collective-permute-start | bytes 786440 | tf_op jit(solution)/shard_map/preact/ppermute | solution.py:114
  68.8 48.8 %collective-permute-start.7 = (bf16[8,128,512]{2,1,0:T(8,128)(2,1)}, bf16[8,128,512]{2,1,0:T(8,128)(2,1)}, u32[]{:S(2)}, u32[]{:S(2)}) collective-permute-start(bf16[8,128,512]{2,1,0:T(8,128)(2,1)} %get-tuple-element.19), channel_id=1, source_target_pairs={{0,8},{8,0},{1,9},{9,1},{2,10},{10,2},{3,11},{11,3},{4,12},{12,4},... | collective-permute-start | bytes 3145736 | tf_op jit(solution)/shard_map/aggregate/ppermute | solution.py:163
  77.8 41.5 %copy-start.6 = (bf16[128,1024]{1,0:T(8,128)(2,1)}, bf16[128,1024]{1,0:T(8,128)(2,1)S(1)}, u32[]{:S(2)}) copy-start(bf16[128,1024]{1,0:T(8,128)(2,1)S(1)} %get-tuple-element.23) | copy-start | bytes 786436
  87.5 7.4 %collective-permute-start.8 = (bf16[256,512]{1,0:T(8,128)(2,1)S(1)}, bf16[256,512]{1,0:T(8,128)(2,1)S(1)}, u32[]{:S(2)}, u32[]{:S(2)}) collective-permute-start(bf16[256,512]{1,0:T(8,128)(2,1)S(1)} %bitcast.14), channel_id=1, source_target_pairs={{0,1},{8,15},{1,2},{9,8},{2,3},{10,9},{3,4},{11,10},{4,5},{12,11},... | collective-permute-start | bytes 786440 | tf_op jit(solution)/shard_map/fold/ppermute | solution.py:126
  89.4 10.0 %collective-permute-start.12 = (bf16[256,512]{1,0:T(8,128)(2,1)S(1)}, bf16[256,512]{1,0:T(8,128)(2,1)S(1)}, u32[]{:S(2)}, u32[]{:S(2)}) collective-permute-start(bf16[256,512]{1,0:T(8,128)(2,1)S(1)} %bitcast.15), channel_id=1, source_target_pairs={{0,7},{8,9},{1,0},{9,10},{2,1},{10,11},{3,2},{11,12},{4,3},{12,13}... | collective-permute-start | bytes 786440 | tf_op jit(solution)/shard_map/fold/ppermute | solution.py:128
  94.9 7.1 %collective-permute-start.9 = (bf16[256,512]{1,0:T(8,128)(2,1)S(1)}, bf16[256,512]{1,0:T(8,128)(2,1)S(1)}, u32[]{:S(2)}, u32[]{:S(2)}) collective-permute-start(bf16[256,512]{1,0:T(8,128)(2,1)S(1)} %collective-permute-done.8.refs_1_), channel_id=1, source_target_pairs={{0,1},{8,15},{1,2},{9,8},{2,3},{10,9},{3,4},{11,10},{4,5},{12,11},... | collective-permute-start | bytes 786440 | tf_op jit(solution)/shard_map/fold/ppermute | solution.py:126
  99.4 11.4 %collective-permute-start.13 = (bf16[256,512]{1,0:T(8,128)(2,1)S(1)}, bf16[256,512]{1,0:T(8,128)(2,1)S(1)}, u32[]{:S(2)}, u32[]{:S(2)}) collective-permute-start(bf16[256,512]{1,0:T(8,128)(2,1)S(1)} %collective-permute-done.12.refs_7_), channel_id=1, source_target_pairs={{0,7},{8,9},{1,0},{9,10},{2,1},{10,11},{3,2},{11,12},{4,3},{12,13}... | collective-permute-start | bytes 786440 | tf_op jit(solution)/shard_map/fold/ppermute | solution.py:128
  102.0 10.7 %collective-permute-start.10 = (bf16[256,512]{1,0:T(8,128)(2,1)S(1)}, bf16[256,512]{1,0:T(8,128)(2,1)S(1)}, u32[]{:S(2)}, u32[]{:S(2)}) collective-permute-start(bf16[256,512]{1,0:T(8,128)(2,1)S(1)} %collective-permute-done.9.refs_2_), channel_id=1, source_target_pairs={{0,1},{8,15},{1,2},{9,8},{2,3},{10,9},{3,4},{11,10},{4,5},{12,11},... | collective-permute-start | bytes 786440 | tf_op jit(solution)/shard_map/fold/ppermute | solution.py:126
  110.8 10.5 %collective-permute-start.14 = (bf16[256,512]{1,0:T(8,128)(2,1)S(1)}, bf16[256,512]{1,0:T(8,128)(2,1)S(1)}, u32[]{:S(2)}, u32[]{:S(2)}) collective-permute-start(bf16[256,512]{1,0:T(8,128)(2,1)S(1)} %collective-permute-done.13.refs_6_), channel_id=1, source_target_pairs={{0,7},{8,9},{1,0},{9,10},{2,1},{10,11},{3,2},{11,12},{4,3},{12,13}... | collective-permute-start | bytes 786440 | tf_op jit(solution)/shard_map/fold/ppermute | solution.py:128
  112.7 10.0 %collective-permute-start.11 = (bf16[256,512]{1,0:T(8,128)(2,1)S(1)}, bf16[256,512]{1,0:T(8,128)(2,1)S(1)}, u32[]{:S(2)}, u32[]{:S(2)}) collective-permute-start(bf16[256,512]{1,0:T(8,128)(2,1)S(1)} %collective-permute-done.10.refs_3_), channel_id=1, source_target_pairs={{0,1},{8,15},{1,2},{9,8},{2,3},{10,9},{3,4},{11,10},{4,5},{12,11},... | collective-permute-start | bytes 786440 | tf_op jit(solution)/shard_map/fold/ppermute | solution.py:126
  187.0 19.7 %collective-permute-start.15 = (bf16[512,512]{1,0:T(8,128)(2,1)S(1)}, bf16[512,512]{1,0:T(8,128)(2,1)S(1)}, u32[]{:S(2)}, u32[]{:S(2)}) collective-permute-start(bf16[512,512]{1,0:T(8,128)(2,1)S(1)} %all_gather.7), channel_id=1, source_target_pairs={{0,8},{8,0},{1,9},{9,1},{2,10},{10,2},{3,11},{11,3},{4,12},{12,4},... | collective-permute-start | bytes 1572872 | tf_op jit(solution)/shard_map/gather_core/ppermute | solution.py:46

commit v5 on v4

v5 whole, which is shorter than its diff:
```python
import jax
import jax.numpy as jnp
from jax import lax
from jax.experimental import pallas as pl
from jax.experimental.pallas import tpu as pltpu
from jax.sharding import Mesh, PartitionSpec as P

GRP = ("x", "zo", "zi", "core")
ALL = GRP + ("feat",)
SWAP = [(0, 1), (1, 0)]
FEAT = 8


def neighbours(chain, odd_step):
    first = (chain + odd_step) % 2
    pairs = [((i + first) % FEAT, (i + 1 + first) % FEAT) for i in range(0, FEAT, 2)]
    return pairs + [(j, i) for i, j in pairs]


def with_neighbour(block, chain, odd_step):
    return lax.ppermute(block, "feat", neighbours(chain, odd_step))


def is_second(chain):
    return (lax.axis_index("feat") + chain) % 2 == 1


def exchange_sum(parts, axis):
    got = lax.all_to_all(parts, axis, 0, 0)
    return jnp.sum(got.astype(jnp.float32), axis=0)


def group_sum(term):
    rows, cols = term.shape
    with jax.named_scope("sum_x_zi"):
        part = exchange_sum(term.reshape(16, rows // 16, cols), ("x", "zi"))
    with jax.named_scope("sum_z"):
        parts = lax.all_gather(part.astype(jnp.bfloat16), ("zo", "zi"), axis=0, tiled=True)
        parts = parts.reshape(3, rows // 4, cols).astype(jnp.float32)
        part = jnp.sum(parts, axis=0).astype(jnp.bfloat16)
    with jax.named_scope("gather_x"):
        part = lax.all_gather(part, "x", axis=0, tiled=True)
    with jax.named_scope("gather_core"):
        other = lax.ppermute(part, "core", SWAP)
        first = lax.axis_index("core") == 0
        return jnp.concatenate([jnp.where(first, part, other), jnp.where(first, other, part)], axis=1).astype(jnp.float32)


def pick_kernel(ids_ref, table_ref, out_ref):
    slices, _, width = out_ref.shape
    wanted = lax.broadcasted_iota(jnp.int32, (table_ref.shape[0], ids_ref.shape[1]), 0) == ids_ref[...]
    wanted = wanted.astype(jnp.float32).T.astype(table_ref.dtype)
    for j in range(slices):
        rows = jnp.dot(wanted, table_ref[:, j * width:(j + 1) * width], preferred_element_type=jnp.float32)
        out_ref[j] = rows.astype(out_ref.dtype)


def pick(table, ids, slices):
    vmem = pl.BlockSpec(memory_space=pltpu.VMEM)
    return pl.pallas_call(
        pick_kernel,
        out_shape=jax.ShapeDtypeStruct((slices, ids.shape[0], table.shape[1] // slices), table.dtype),
        in_specs=[vmem, vmem],
        out_specs=vmem,
        compiler_params=pltpu.CompilerParams(vmem_limit_bytes=32 * 2**20),
    )(ids.reshape(1, -1), table)


def pair_block(me, chain, k, member):
    rank = lax.rem(me + chain, FEAT)
    side = 2 * lax.rem(rank, 2) - 1
    pair = lax.div(rank, 2) + (0, side, -side, 2)[k] + FEAT // 2
    return lax.rem(2 * lax.rem(pair, FEAT // 2) + member + FEAT - chain, FEAT)


def aggregate_kernel(me_ref, ids_ref, counts_ref, slices_ref, tiles_ref, weight_ref, agg_ref, *part_refs):
    blocks, _, width = slices_ref.shape
    slots = tiles_ref.shape[1]
    ones = jnp.ones((slots * tiles_ref.shape[3], 128), jnp.bfloat16)
    for own in range(blocks):
        lhs = [
            jnp.where(s < counts_ref[own], tiles_ref[own, s], jnp.zeros((), jnp.bfloat16)) for s in range(slots)
        ]
        rhs = [slices_ref[ids_ref[own, s]] for s in range(slots)]
        lhs, rhs = jnp.concatenate(lhs, axis=1), jnp.concatenate(rhs, axis=0)
        summed = jnp.dot(lhs, rhs, preferred_element_type=jnp.float32)
        degree = jnp.dot(lhs, ones, preferred_element_type=jnp.float32)
        agg_ref[own] = (summed / jnp.concatenate([degree] * (width // 128), axis=1)).astype(jnp.bfloat16)
    for chain in range(2):
        refs = part_refs[4 * chain:4 * chain + 4]
        cols = refs[0].shape[2]
        order = [(k, member) for k in (3, 2, 1, 0) for member in range(2)]
        lhs = jnp.concatenate([agg_ref[pair_block(me_ref[0], chain, k, member)] for k, member in order], axis=0)
        parts = jnp.dot(lhs, weight_ref[:, chain * cols:(chain + 1) * cols], preferred_element_type=jnp.float32)
        parts = parts.astype(jnp.bfloat16)
        rows = parts.shape[0] // blocks
        for i, (k, member) in enumerate(order):
            refs[k][member] = parts[i * rows:(i + 1) * rows]


def aggregate_and_project(me, ids, counts, slices, tiles, weight):
    block_rows = slices.shape[1]
    vmem, smem = pl.BlockSpec(memory_space=pltpu.VMEM), pl.BlockSpec(memory_space=pltpu.SMEM)
    pair = jax.ShapeDtypeStruct((2, block_rows, weight.shape[1] // 2), jnp.bfloat16)
    agg, *parts = pl.pallas_call(
        aggregate_kernel,
        out_shape=[jax.ShapeDtypeStruct(slices.shape, jnp.bfloat16)] + [pair] * 8,
        in_specs=[smem] * 3 + [vmem] * 3,
        out_specs=[vmem] * 9,
        compiler_params=pltpu.CompilerParams(vmem_limit_bytes=32 * 2**20),
    )(me.reshape(1), ids, counts, slices, tiles, weight)
    return agg, (parts[:4], parts[4:])


def add(a, b):
    return a.astype(jnp.float32) + b.astype(jnp.float32)


def chain_sum(pairs):
    held = [pairs[chain][3] for chain in range(2)]
    for k in (2, 1):
        got = [with_neighbour(held[chain], chain, (k + 1) % 2) for chain in range(2)]
        held = [add(got[chain], pairs[chain][k]).astype(jnp.bfloat16) for chain in range(2)]
    sums = []
    got = [with_neighbour(held[chain], chain, 1) for chain in range(2)]
    both = [add(got[chain], pairs[chain][0]) for chain in range(2)]
    for chain in range(2):
        second = is_second(chain)
        give = jnp.where(second, both[chain][0], both[chain][1]).astype(jnp.bfloat16)
        keep = jnp.where(second, both[chain][1], both[chain][0])
        sums.append(keep + with_neighbour(give, chain, 0).astype(jnp.float32))
    return jnp.concatenate(sums, axis=1)


def chain_gather(blocks):
    got = [with_neighbour(blocks[chain], chain, 0) for chain in range(2)]
    held = []
    for chain in range(2):
        second = is_second(chain)
        mine, other = blocks[chain], got[chain]
        held.append([jnp.stack([jnp.where(second, other, mine), jnp.where(second, mine, other)])])
    for k in range(1, 4):
        for chain in range(2):
            held[chain].append(with_neighbour(held[chain][-1], chain, k % 2))
    return held[0] + held[1]


def fold_kernel(me_ref, rows_ref, *refs):
    *grad_refs, out_ref = refs
    for chain in range(2):
        cols = grad_refs[0].shape[2]
        total = None
        for k in range(4):
            for member in range(2):
                rows = rows_ref[pair_block(me_ref[0], chain, k, member)]
                term = lax.dot_general(
                    rows, grad_refs[4 * chain + k][member], (((0,), (0,)), ((), ())), preferred_element_type=jnp.float32
                )
                total = term if total is None else total + term
        out_ref[:, chain * cols:(chain + 1) * cols] = total.astype(out_ref.dtype)


def fold(me, rows, grads):
    vmem = pl.BlockSpec(memory_space=pltpu.VMEM)
    return pl.pallas_call(
        fold_kernel,
        out_shape=jax.ShapeDtypeStruct((rows.shape[2], 2 * grads[0].shape[2]), jnp.bfloat16),
        in_specs=[pl.BlockSpec(memory_space=pltpu.SMEM), vmem] + [vmem] * len(grads),
        out_specs=vmem,
        compiler_params=pltpu.CompilerParams(vmem_limit_bytes=32 * 2**20),
    )(me.reshape(1), rows, *grads)


def shards(feature_table, sample_ids, block_ids, block_counts, block_tiles, weight, target):
    block_total, slot_total, block_rows, block_width = block_tiles.shape
    node_total = block_total * block_rows
    me = lax.axis_index("feat")
    with jax.named_scope("pick"):
        slices = lax.all_to_all(pick(feature_table, sample_ids, block_total), "feat", 0, 0)
    with jax.named_scope("aggregate"):
        agg, parts = aggregate_and_project(me, block_ids, block_counts, slices, block_tiles, weight)
        other_agg = lax.ppermute(agg, "core", SWAP)
    with jax.named_scope("preact"):
        preact = chain_sum(parts)
    with jax.named_scope("grad"):
        sigmoid_part = jax.nn.sigmoid(preact)
        hidden = preact * sigmoid_part
        hidden_width = hidden.shape[1]
        scales = lax.rsqrt(jnp.mean(hidden * hidden, axis=1, keepdims=True) + 1e-05)
        embedding = (hidden * scales).astype(jnp.bfloat16)
        cotangent = (embedding.astype(jnp.float32) - target.astype(jnp.float32)) / node_total
        projected = jnp.sum(cotangent * hidden, axis=1, keepdims=True)
        grad_hidden = scales * cotangent - scales**3 / hidden_width * hidden * projected
        slope = sigmoid_part * (1.0 + preact * (1.0 - sigmoid_part))
        grad_pre = (grad_hidden * slope).astype(jnp.bfloat16)
    with jax.named_scope("swap"):
        half = hidden_width // 2
        paired = lax.all_to_all(grad_pre.reshape(block_rows, 2, half).swapaxes(0, 1), "core", 0, 0)
    with jax.named_scope("fold"):
        first = lax.axis_index("core") == 0
        rows = jnp.concatenate([jnp.where(first, agg, other_agg), jnp.where(first, other_agg, agg)], axis=1)
        paired = paired.reshape(2 * block_rows, half)
        folded = fold(me, rows, chain_gather([paired[:, :half // 2], paired[:, half // 2:]]))
    weight_grad = group_sum(folded)
    return (embedding, weight_grad)


def solution(mesh):
    fine = Mesh(mesh.devices.reshape(4, 3, 4, 2, 8), ALL)
    return jax.shard_map(
        shards,
        mesh=fine,
        in_specs=(
            P(ALL, None),
            P(ALL),
            P(GRP, None),
            P(GRP),
            P(GRP, None, None, None),
            P("feat", None),
            P(ALL, None),
        ),
        out_specs=(P(ALL, None), P("feat", None)),
        check_vma=False,
    )
```

time: 209 us -> 204 us (0.976)
  starting transfers between devices: 74.5 us -> 63.1 us
  waiting for transfers between devices: 47.9 us -> 56.6 us
  blocking collectives: 71.4 us -> 67 us
    ppermute x14 -> x16, waiting for transfers between devices: 21.7 us -> 30.3 us  [with_neighbour(): return lax.ppermute(block, 'feat', neighbours(chain, odd_step))]
    ppermute x1, starting transfers between devices: 8.31 us -> 2.55 us  [shards(): other_agg = lax.ppermute(agg, 'core', SWAP)]
    all_to_all x1, blocking collectives: 26.4 us -> 20.8 us  [exchange_sum(): got = lax.all_to_all(parts, axis, 0, 0)]
    all_to_all x1, blocking collectives: 9.19 us -> 12.9 us  [shards(): lax.all_to_all(grad_pre.reshape(block_rows, 2, half).swapaxes(0, 1), 'cor...]
    ppermute x14 -> x16, starting transfers between devices: 40.4 us -> 36.9 us  [with_neighbour(): return lax.ppermute(block, 'feat', neighbours(chain, odd_step))]
    all_gather x1, blocking collectives: 25.3 us -> 23.1 us  [group_sum(): lax.all_gather(part.astype(jnp.bfloat16), ('zo', 'zi'), axis=0, tiled=True)]
    ppermute x1, starting transfers between devices: 18.2 us -> 16 us  [group_sum(): other = lax.ppermute(part, 'core', SWAP)]
  transfers between devices with their start and end apart: 17 -> 19, of which waited for: 11 -> 14; matrix products, arithmetic and copies ran while one was open for 2% -> 2% of each run, Pallas kernels for 0% -> 0%
where the time goes in v5:
time: 204 us; the launch traced here: 203 us
  blocking collectives  67 us (33%)
  starting transfers between devices  63.1 us (31%)
  waiting for transfers between devices  56.6 us (28%)
  other arithmetic  5.84 us (3%)
  Pallas kernels  5.6 us (3%)
  local copies, waits for them, and re-layouts  3.36 us (2%)
    ppermute x16, starting transfers between devices, with_neighbour(): return lax.ppermute(block, 'feat', neighbours(chain, odd_step))  36.9 us
    ppermute x16, waiting for transfers between devices, with_neighbour(): return lax.ppermute(block, 'feat', neighbours(chain, odd_step))  30.3 us
    all_to_all x1, waiting for transfers between devices, shards(): lax.all_to_all(pick(feature_table, sample_ids, block_total), 'feat', 0, 0)  24.8 us
    all_gather x1, blocking collectives, group_sum(): lax.all_gather(part.astype(jnp.bfloat16), ('zo', 'zi'), axis=0, tiled=True)  23.1 us
    all_to_all x1, blocking collectives, exchange_sum(): got = lax.all_to_all(parts, axis, 0, 0)  20.8 us
    ppermute x1, starting transfers between devices, group_sum(): other = lax.ppermute(part, 'core', SWAP)  16 us
    all_to_all x1, blocking collectives, shards(): lax.all_to_all(grad_pre.reshape(block_rows, 2, half).swapaxes(0, 1), 'cor...  12.9 us
    all_gather x1, blocking collectives, group_sum(): part = lax.all_gather(part, 'x', axis=0, tiled=True)  10.2 us
  transfers between devices with their start and end apart: 19, of which 14 were waited for; matrix products, arithmetic and copies ran while one was open for 2% of the time, Pallas kernels for 0%

profile of v5, /device:TPU:1, one launch (start us, length us, event | category | flops | bytes accessed | tf_op | source)
XLA Modules:
  0.0 202.5 jit_solution(15114994416461934566)
XLA Ops:
  4.4 7.7 %all-to-all-start = ((bf16[8,128,512]{2,1,0:T(8,128)(2,1)}), bf16[8,128,512]{2,1,0:T(8,128)(2,1)S(1)}, u32[]{:S(2)}, u32[]{:S(2)}) async-start(bf16[8,128,512]{2,1,0:T(8,128)(2,1)} %pick.1), calls=%async_computation | async-start | bytes 2097152 | tf_op jit(solution)/shard_map/pick/all_to_all | solution.py:179
  12.1 24.8 %all-to-all-done.slices_ref = bf16[8,128,512]{2,1,0:T(8,128)(2,1)S(1)} async-done(((bf16[8,128,512]{2,1,0:T(8,128)(2,1)}), bf16[8,128,512]{2,1,0:T(8,128)(2,1)S(1)}, u32[]{:S(2)}, u32[]{:S(2)}) %all-to-all-start) | async-done | bytes 1048608 | tf_op jit(solution)/shard_map/pick/all_to_all | solution.py:179
  36.9 2.8 %aggregate.1 = (bf16[8,128,512]{2,1,0:T(8,128)(2,1)S(1)}, bf16[2,128,512]{2,1,0:T(8,128)(2,1)S(1)}, bf16[2,128,512]{2,1,0:T(8,128)(2,1)S(1)}, bf16[2,128,512]{2,...) custom-call(s32[1]{0:T(128)} %bitcast.me_ref, ...), custom_call_target="tpu_custom_call" | custom-call | tf_op jit(solution)/shard_map/aggregate/pallas_call | solution.py:105
  40.7 1.9 collective-permute-start.4
  42.6 2.2 %collective-permute-start = (bf16[2,128,512]{2,1,0:T(8,128)(2,1)S(1)}, bf16[2,128,512]{2,1,0:T(8,128)(2,1)S(1)}, u32[]{:S(2)}, u32[]{:S(2)}) collective-permute-start(bf16[2,128,512]{2,1,0:T(8,128)(2,1)S(1)} %get-tuple-element.11), channel_id=1, source_target_pairs={{1,2},{3,4},{5,6},{7,0},{2,1},{4,3},{6,5},{0,7},{9,10},{11,12},{13... | collective-permute-start | bytes 786440 | tf_op jit(solution)/shard_map/preact/ppermute | solution.py:21
  44.8 3.0 %collective-permute-done.4 = bf16[2,128,512]{2,1,0:T(8,128)(2,1)S(1)} collective-permute-done((bf16[2,128,512]{2,1,0:T(8,128)(2,1)S(1)}, bf16[2,128,512]{2,1,0:T(8,128)(2,1)S(1)}, u32[]{:S(2)}, u32[]{:S(2)}) %collective-permute-start.4) | collective-permute-done | bytes 262176 | tf_op jit(solution)/shard_map/preact/ppermute | solution.py:21
  47.9 1.9 collective-permute-start.5
  51.0 2.4 %collective-permute-start.1 = (bf16[2,128,512]{2,1,0:T(8,128)(2,1)S(1)}, bf16[2,128,512]{2,1,0:T(8,128)(2,1)S(1)}, u32[]{:S(2)}, u32[]{:S(2)}) collective-permute-start(bf16[2,128,512]{2,1,0:T(8,128)(2,1)S(1)} %add_convert_fusion.3), channel_id=1, source_target_pairs={{0,1},{2,3},{4,5},{6,7},{1,0},{3,2},{5,4},{7,6},{8,9},{10,11},{12,... | collective-permute-start | bytes 786440 | tf_op jit(solution)/shard_map/preact/ppermute | solution.py:21
  53.5 5.3 %collective-permute-done.5 = bf16[2,128,512]{2,1,0:T(8,128)(2,1)S(1)} collective-permute-done((bf16[2,128,512]{2,1,0:T(8,128)(2,1)S(1)}, bf16[2,128,512]{2,1,0:T(8,128)(2,1)S(1)}, u32[]{:S(2)}, u32[]{:S(2)}) %collective-permute-start.5) | collective-permute-done | bytes 262176 | tf_op jit(solution)/shard_map/preact/ppermute | solution.py:21
  58.8 1.9 collective-permute-start.6
  60.9 1.9 collective-permute-start.2
  62.8 4.8 %collective-permute-done.6 = bf16[2,128,512]{2,1,0:T(8,128)(2,1)S(1)} collective-permute-done((bf16[2,128,512]{2,1,0:T(8,128)(2,1)S(1)}, bf16[2,128,512]{2,1,0:T(8,128)(2,1)S(1)}, u32[]{:S(2)}, u32[]{:S(2)}) %collective-permute-start.6) | collective-permute-done | bytes 262176 | tf_op jit(solution)/shard_map/preact/ppermute | solution.py:21
  68.7 2.1 %collective-permute-start.7 = (bf16[128,512]{1,0:T(8,128)(2,1)S(1)}, bf16[128,512]{1,0:T(8,128)(2,1)S(1)}, u32[]{:S(2)}, u32[]{:S(2)}) collective-permute-start(bf16[128,512]{1,0:T(8,128)(2,1)S(1)} %fusion.2), channel_id=1, source_target_pairs={{1,2},{3,4},{5,6},{7,0},{2,1},{4,3},{6,5},{0,7},{9,10},{11,12},{13... | collective-permute-start | bytes 393224 | tf_op jit(solution)/shard_map/preact/ppermute | solution.py:21
  70.9 2.2 %collective-permute-start.3 = (bf16[128,512]{1,0:T(8,128)(2,1)S(1)}, bf16[128,512]{1,0:T(8,128)(2,1)S(1)}, u32[]{:S(2)}, u32[]{:S(2)}) collective-permute-start(bf16[128,512]{1,0:T(8,128)(2,1)S(1)} %fusion.1), channel_id=1, source_target_pairs={{0,1},{2,3},{4,5},{6,7},{1,0},{3,2},{5,4},{7,6},{8,9},{10,11},{12,... | collective-permute-start | bytes 393224 | tf_op jit(solution)/shard_map/preact/ppermute | solution.py:21
  73.1 3.1 %collective-permute-done.7 = bf16[128,512]{1,0:T(8,128)(2,1)S(1)} collective-permute-done((bf16[128,512]{1,0:T(8,128)(2,1)S(1)}, bf16[128,512]{1,0:T(8,128)(2,1)S(1)}, u32[]{:S(2)}, u32[]{:S(2)}) %collective-permute-start.7) | collective-permute-done | bytes 131104 | tf_op jit(solution)/shard_map/preact/ppermute | solution.py:21
  77.9 12.9 %all_to_all.15 = bf16[2,128,512]{2,1,0:T(8,128)(2,1)S(1)} all-to-all(bf16[2,128,512]{2,1,0:T(8,128)(2,1)S(1)} %bitcast.33), channel_id=1, replica_groups=mesh['x'=4,'zo'=3,'zi'=4,'core'=2,'feat'=8] {'core'}, dimensions={0} | all-to-all | bytes 524288 | tf_op jit(solution)/shard_map/swap/all_to_all | solution.py:198
  90.9 1.9 collective-permute-start.13
  92.8 1.9 collective-permute-start.9
  94.7 2.6 %collective-permute-start.8 = (bf16[8,128,512]{2,1,0:T(8,128)(2,1)S(1)}, bf16[8,128,512]{2,1,0:T(8,128)(2,1)}, u32[]{:S(2)}, u32[]{:S(2)}) collective-permute-start(bf16[8,128,512]{2,1,0:T(8,128)(2,1)S(1)} %copy-done.4), channel_id=1, source_target_pairs={{0,8},{8,0},{1,9},{9,1},{2,10},{10,2},{3,11},{11,3},{4,12},{12,4},... | collective-permute-start | bytes 3145736 | tf_op jit(solution)/shard_map/aggregate/ppermute | solution.py:182
  99.2 4.6 %collective-permute-start.10 = (bf16[2,256,256]{2,1,0:T(8,128)(2,1)S(1)}, bf16[2,256,256]{2,1,0:T(8,128)(2,1)S(1)}, u32[]{:S(2)}, u32[]{:S(2)}) collective-permute-start(bf16[2,256,256]{2,1,0:T(8,128)(2,1)S(1)} %pad_maximum_fusion.2.refs_0_), channel_id=1, source_target_pairs={{1,2},{3,4},{5,6},{7,0},{2,1},{4,3},{6,5},{0,7},{9,10},{11,12},{13... | collective-permute-start | bytes 786440 | tf_op jit(solution)/shard_map/fold/ppermute | solution.py:21
  103.8 1.9 collective-permute-start.14
  105.7 2.9 %collective-permute-done.10.refs_1_ = bf16[2,256,256]{2,1,0:T(8,128)(2,1)S(1)} collective-permute-done((bf16[2,256,256]{2,1,0:T(8,128)(2,1)S(1)}, bf16[2,256,256]{2,1,0:T(8,128)(2,1)S(1)}, u32[]{:S(2)}, u32[]{:S(2)}) %collective-permute-start.10) | collective-permute-done | bytes 262176 | tf_op jit(solution)/shard_map/fold/ppermute | solution.py:21
  108.6 1.9 collective-permute-start.11
  111.7 3.4 %collective-permute-start.15 = (bf16[2,256,256]{2,1,0:T(8,128)(2,1)S(1)}, bf16[2,256,256]{2,1,0:T(8,128)(2,1)S(1)}, u32[]{:S(2)}, u32[]{:S(2)}) collective-permute-start(bf16[2,256,256]{2,1,0:T(8,128)(2,1)S(1)} %collective-permute-done.14.refs_5_), channel_id=1, source_target_pairs={{1,2},{3,4},{5,6},{7,0},{2,1},{4,3},{6,5},{0,7},{9,10},{11,12},{13... | collective-permute-start | bytes 786440 | tf_op jit(solution)/shard_map/fold/ppermute | solution.py:21
  115.1 2.4 %collective-permute-done.11.refs_2_ = bf16[2,256,256]{2,1,0:T(8,128)(2,1)S(1)} collective-permute-done((bf16[2,256,256]{2,1,0:T(8,128)(2,1)S(1)}, bf16[2,256,256]{2,1,0:T(8,128)(2,1)S(1)}, u32[]{:S(2)}, u32[]{:S(2)}) %collective-permute-start.11) | collective-permute-done | bytes 262176 | tf_op jit(solution)/shard_map/fold/ppermute | solution.py:21
  117.5 2.7 %collective-permute-start.12 = (bf16[2,256,256]{2,1,0:T(8,128)(2,1)S(1)}, bf16[2,256,256]{2,1,0:T(8,128)(2,1)S(1)}, u32[]{:S(2)}, u32[]{:S(2)}) collective-permute-start(bf16[2,256,256]{2,1,0:T(8,128)(2,1)S(1)} %collective-permute-done.11.refs_2_), channel_id=1, source_target_pairs={{1,2},{3,4},{5,6},{7,0},{2,1},{4,3},{6,5},{0,7},{9,10},{11,12},{13... | collective-permute-start | bytes 786440 | tf_op jit(solution)/shard_map/fold/ppermute | solution.py:21
  120.3 1.9 collective-permute-start.16
  123.7 4.1 %collective-permute-done.12.refs_3_ = bf16[2,256,256]{2,1,0:T(8,128)(2,1)S(1)} collective-permute-done((bf16[2,256,256]{2,1,0:T(8,128)(2,1)S(1)}, bf16[2,256,256]{2,1,0:T(8,128)(2,1)S(1)}, u32[]{:S(2)}, u32[]{:S(2)}) %collective-permute-start.12) | collective-permute-done | bytes 262176 | tf_op jit(solution)/shard_map/fold/ppermute | solution.py:21
  129.1 20.8 %all_to_all.16 = bf16[16,32,512]{2,1,0:T(8,128)(2,1)S(1)} all-to-all(bf16[16,32,512]{2,1,0:T(8,128)(2,1)S(1)} %bitcast.28), channel_id=1, replica_groups=mesh['x'=4,'zo'=3,'zi'=4,'core'=2,'feat'=8] {'x','zi'}, dimensions={0} | all-to-all | bytes 1048576 | tf_op jit(solution)/shard_map/sum_x_zi/all_to_all | solution.py:29
  150.0 23.1 %all_gather.6 = bf16[384,512]{1,0:T(8,128)(2,1)S(1)} all-gather(bf16[32,512]{1,0:T(8,128)(2,1)S(1)} %reduce_sum.44), channel_id=1, replica_groups=mesh['x'=4,'zo'=3,'zi'=4,'core'=2,'feat'=8] {'zo','zi'}, dimensions={0}, use_global_device_ids=true | all-gather | bytes 425984 | tf_op jit(solution)/shard_map/sum_z/all_gather | solution.py:38
  173.2 10.2 %all_gather.7 = bf16[512,512]{1,0:T(8,128)(2,1)S(1)} all-gather(bf16[128,512]{1,0:T(8,128)(2,1)S(1)} %reduce_sum.45), channel_id=1, replica_groups=mesh['x'=4,'zo'=3,'zi'=4,'core'=2,'feat'=8] {'x'}, dimensions={0}, use_global_device_ids=true | all-gather | bytes 655360 | tf_op jit(solution)/shard_map/gather_x/all_gather | solution.py:42
  183.3 16.0 %collective-permute-start.17 = (bf16[512,512]{1,0:T(8,128)(2,1)S(1)}, bf16[512,512]{1,0:T(8,128)(2,1)S(1)}, u32[]{:S(2)}, u32[]{:S(2)}) collective-permute-start(bf16[512,512]{1,0:T(8,128)(2,1)S(1)} %all_gather.7), channel_id=1, source_target_pairs={{0,8},{8,0},{1,9},{9,1},{2,10},{10,2},{3,11},{11,3},{4,12},{12,4},... | collective-permute-start | bytes 1572872 | tf_op jit(solution)/shard_map/gather_core/ppermute | solution.py:44
  (66 shorter events, 18.2 us)
Async XLA Ops:
  0.6 1.6 copy-start
  2.2 0.7 copy-start.9
  2.9 9.1 %copy-start.12 = (s32[8,4]{0,1:T(4,128)S(1)}, s32[8,4]{0,1:T(4,128)}, u32[]{:S(2)}) copy-start(s32[8,4]{0,1:T(4,128)} %param.9) | copy-start | bytes 388
  2.9 34.0 %copy-start.1 = (bf16[8,4,128,128]{3,2,1,0:T(8,128)(2,1)S(1)}, bf16[8,4,128,128]{3,2,1,0:T(8,128)(2,1)}, u32[]{:S(2)}) copy-start(bf16[8,4,128,128]{3,2,1,0:T(8,128)(2,1)} %tiles_ref.1) | copy-start | bytes 3145732
  2.9 34.0 %copy-start.2 = (bf16[512,1024]{1,0:T(8,128)(2,1)S(1)}, bf16[512,1024]{1,0:T(8,128)(2,1)}, u32[]{:S(2)}) copy-start(bf16[512,1024]{1,0:T(8,128)(2,1)} %weight_ref.1) | copy-start | bytes 3145732
  2.9 34.0 %copy-start.8 = (s32[8]{0:T(128)S(1)}, s32[8]{0:T(128)}, u32[]{:S(2)}) copy-start(s32[8]{0:T(128)} %counts_ref.1) | copy-start | bytes 100
  4.4 32.5 %all-to-all-start = ((bf16[8,128,512]{2,1,0:T(8,128)(2,1)}), bf16[8,128,512]{2,1,0:T(8,128)(2,1)S(1)}, u32[]{:S(2)}, u32[]{:S(2)}) async-start(bf16[8,128,512]{2,1,0:T(8,128)(2,1)} %pick.1), calls=%async_computation | async-start | bytes 2097152 | tf_op jit(solution)/shard_map/pick/all_to_all | solution.py:179
  39.7 1.0 copy-start.3
  40.7 18.1 %copy-start.5 = (bf16[2,128,512]{2,1,0:T(8,128)(2,1)}, bf16[2,128,512]{2,1,0:T(8,128)(2,1)S(1)}, u32[]{:S(2)}) copy-start(bf16[2,128,512]{2,1,0:T(8,128)(2,1)S(1)} %get-tuple-element.14) | copy-start | bytes 786436
  40.7 18.1 %copy-start.7 = (bf16[2,128,512]{2,1,0:T(8,128)(2,1)}, bf16[2,128,512]{2,1,0:T(8,128)(2,1)S(1)}, u32[]{:S(2)}) copy-start(bf16[2,128,512]{2,1,0:T(8,128)(2,1)S(1)} %get-tuple-element.18) | copy-start | bytes 786436
  40.7 7.1 %collective-permute-start.4 = (bf16[2,128,512]{2,1,0:T(8,128)(2,1)S(1)}, bf16[2,128,512]{2,1,0:T(8,128)(2,1)S(1)}, u32[]{:S(2)}, u32[]{:S(2)}) collective-permute-start(bf16[2,128,512]{2,1,0:T(8,128)(2,1)S(1)} %get-tuple-element.15), channel_id=1, source_target_pairs={{0,1},{2,3},{4,5},{6,7},{1,0},{3,2},{5,4},{7,6},{8,9},{10,11},{12,... | collective-permute-start | bytes 786440 | tf_op jit(solution)/shard_map/preact/ppermute | solution.py:21
  42.6 8.3 %collective-permute-start = (bf16[2,128,512]{2,1,0:T(8,128)(2,1)S(1)}, bf16[2,128,512]{2,1,0:T(8,128)(2,1)S(1)}, u32[]{:S(2)}, u32[]{:S(2)}) collective-permute-start(bf16[2,128,512]{2,1,0:T(8,128)(2,1)S(1)} %get-tuple-element.11), channel_id=1, source_target_pairs={{1,2},{3,4},{5,6},{7,0},{2,1},{4,3},{6,5},{0,7},{9,10},{11,12},{13... | collective-permute-start | bytes 786440 | tf_op jit(solution)/shard_map/preact/ppermute | solution.py:21
  47.9 10.9 %collective-permute-start.5 = (bf16[2,128,512]{2,1,0:T(8,128)(2,1)S(1)}, bf16[2,128,512]{2,1,0:T(8,128)(2,1)S(1)}, u32[]{:S(2)}, u32[]{:S(2)}) collective-permute-start(bf16[2,128,512]{2,1,0:T(8,128)(2,1)S(1)} %add_convert_fusion.1), channel_id=1, source_target_pairs={{1,2},{3,4},{5,6},{7,0},{2,1},{4,3},{6,5},{0,7},{9,10},{11,12},{13... | collective-permute-start | bytes 786440 | tf_op jit(solution)/shard_map/preact/ppermute | solution.py:21
  51.0 9.8 %collective-permute-start.1 = (bf16[2,128,512]{2,1,0:T(8,128)(2,1)S(1)}, bf16[2,128,512]{2,1,0:T(8,128)(2,1)S(1)}, u32[]{:S(2)}, u32[]{:S(2)}) collective-permute-start(bf16[2,128,512]{2,1,0:T(8,128)(2,1)S(1)} %add_convert_fusion.3), channel_id=1, source_target_pairs={{0,1},{2,3},{4,5},{6,7},{1,0},{3,2},{5,4},{7,6},{8,9},{10,11},{12,... | collective-permute-start | bytes 786440 | tf_op jit(solution)/shard_map/preact/ppermute | solution.py:21
  58.8 8.8 %collective-permute-start.6 = (bf16[2,128,512]{2,1,0:T(8,128)(2,1)S(1)}, bf16[2,128,512]{2,1,0:T(8,128)(2,1)S(1)}, u32[]{:S(2)}, u32[]{:S(2)}) collective-permute-start(bf16[2,128,512]{2,1,0:T(8,128)(2,1)S(1)} %add_convert_fusion), channel_id=1, source_target_pairs={{0,1},{2,3},{4,5},{6,7},{1,0},{3,2},{5,4},{7,6},{8,9},{10,11},{12,... | collective-permute-start | bytes 786440 | tf_op jit(solution)/shard_map/preact/ppermute | solution.py:21
  60.8 10.0 %copy-start.6 = (bf16[2,128,512]{2,1,0:T(8,128)(2,1)S(1)}, bf16[2,128,512]{2,1,0:T(8,128)(2,1)}, u32[]{:S(2)}) copy-start(bf16[2,128,512]{2,1,0:T(8,128)(2,1)} %copy-done.5) | copy-start | bytes 786436
  60.9 9.9 %collective-permute-start.2 = (bf16[2,128,512]{2,1,0:T(8,128)(2,1)S(1)}, bf16[2,128,512]{2,1,0:T(8,128)(2,1)S(1)}, u32[]{:S(2)}, u32[]{:S(2)}) collective-permute-start(bf16[2,128,512]{2,1,0:T(8,128)(2,1)S(1)} %add_convert_fusion.2), channel_id=1, source_target_pairs={{1,2},{3,4},{5,6},{7,0},{2,1},{4,3},{6,5},{0,7},{9,10},{11,12},{13... | collective-permute-start | bytes 786440 | tf_op jit(solution)/shard_map/preact/ppermute | solution.py:21
  68.6 8.6 %copy-start.10 = (bf16[128,1024]{1,0:T(8,128)(2,1)S(1)}, bf16[128,1024]{1,0:T(8,128)(2,1)}, u32[]{:S(2)}) copy-start(bf16[128,1024]{1,0:T(8,128)(2,1)} %param.13) | copy-start | bytes 786436
  68.7 7.6 %collective-permute-start.7 = (bf16[128,512]{1,0:T(8,128)(2,1)S(1)}, bf16[128,512]{1,0:T(8,128)(2,1)S(1)}, u32[]{:S(2)}, u32[]{:S(2)}) collective-permute-start(bf16[128,512]{1,0:T(8,128)(2,1)S(1)} %fusion.2), channel_id=1, source_target_pairs={{1,2},{3,4},{5,6},{7,0},{2,1},{4,3},{6,5},{0,7},{9,10},{11,12},{13... | collective-permute-start | bytes 393224 | tf_op jit(solution)/shard_map/preact/ppermute | solution.py:21
  70.9 6.0 %collective-permute-start.3 = (bf16[128,512]{1,0:T(8,128)(2,1)S(1)}, bf16[128,512]{1,0:T(8,128)(2,1)S(1)}, u32[]{:S(2)}, u32[]{:S(2)}) collective-permute-start(bf16[128,512]{1,0:T(8,128)(2,1)S(1)} %fusion.1), channel_id=1, source_target_pairs={{0,1},{2,3},{4,5},{6,7},{1,0},{3,2},{5,4},{7,6},{8,9},{10,11},{12,... | collective-permute-start | bytes 393224 | tf_op jit(solution)/shard_map/preact/ppermute | solution.py:21
  77.2 17.6 %copy-start.4 = (bf16[8,128,512]{2,1,0:T(8,128)(2,1)S(1)}, bf16[8,128,512]{2,1,0:T(8,128)(2,1)}, u32[]{:S(2)}) copy-start(bf16[8,128,512]{2,1,0:T(8,128)(2,1)} %copy-done.3) | copy-start | bytes 3145732
  77.5 21.6 %copy-start.11 = (bf16[128,1024]{1,0:T(8,128)(2,1)}, bf16[128,1024]{1,0:T(8,128)(2,1)S(1)}, u32[]{:S(2)}) copy-start(bf16[128,1024]{1,0:T(8,128)(2,1)S(1)} %get-tuple-element.23) | copy-start | bytes 786436
  90.9 7.8 %collective-permute-start.13 = (bf16[256,256]{1,0:T(8,128)(2,1)S(1)}, bf16[256,256]{1,0:T(8,128)(2,1)S(1)}, u32[]{:S(2)}, u32[]{:S(2)}) collective-permute-start(bf16[256,256]{1,0:T(8,128)(2,1)S(1)} %get-tuple-element.34), channel_id=1, source_target_pairs={{1,2},{3,4},{5,6},{7,0},{2,1},{4,3},{6,5},{0,7},{9,10},{11,12},{13... | collective-permute-start | bytes 393224 | tf_op jit(solution)/shard_map/fold/ppermute | solution.py:21
  92.8 6.3 %collective-permute-start.9 = (bf16[256,256]{1,0:T(8,128)(2,1)S(1)}, bf16[256,256]{1,0:T(8,128)(2,1)S(1)}, u32[]{:S(2)}, u32[]{:S(2)}) collective-permute-start(bf16[256,256]{1,0:T(8,128)(2,1)S(1)} %get-tuple-element.35), channel_id=1, source_target_pairs={{0,1},{2,3},{4,5},{6,7},{1,0},{3,2},{5,4},{7,6},{8,9},{10,11},{12,... | collective-permute-start | bytes 393224 | tf_op jit(solution)/shard_map/fold/ppermute | solution.py:21
  94.7 27.5 %collective-permute-start.8 = (bf16[8,128,512]{2,1,0:T(8,128)(2,1)S(1)}, bf16[8,128,512]{2,1,0:T(8,128)(2,1)}, u32[]{:S(2)}, u32[]{:S(2)}) collective-permute-start(bf16[8,128,512]{2,1,0:T(8,128)(2,1)S(1)} %copy-done.4), channel_id=1, source_target_pairs={{0,8},{8,0},{1,9},{9,1},{2,10},{10,2},{3,11},{11,3},{4,12},{12,4},... | collective-permute-start | bytes 3145736 | tf_op jit(solution)/shard_map/aggregate/ppermute | solution.py:182
  99.2 9.4 %collective-permute-start.10 = (bf16[2,256,256]{2,1,0:T(8,128)(2,1)S(1)}, bf16[2,256,256]{2,1,0:T(8,128)(2,1)S(1)}, u32[]{:S(2)}, u32[]{:S(2)}) collective-permute-start(bf16[2,256,256]{2,1,0:T(8,128)(2,1)S(1)} %pad_maximum_fusion.2.refs_0_), channel_id=1, source_target_pairs={{1,2},{3,4},{5,6},{7,0},{2,1},{4,3},{6,5},{0,7},{9,10},{11,12},{13... | collective-permute-start | bytes 786440 | tf_op jit(solution)/shard_map/fold/ppermute | solution.py:21
  103.8 7.9 %collective-permute-start.14 = (bf16[2,256,256]{2,1,0:T(8,128)(2,1)S(1)}, bf16[2,256,256]{2,1,0:T(8,128)(2,1)S(1)}, u32[]{:S(2)}, u32[]{:S(2)}) collective-permute-start(bf16[2,256,256]{2,1,0:T(8,128)(2,1)S(1)} %pad_maximum_fusion.3.refs_4_), channel_id=1, source_target_pairs={{0,1},{2,3},{4,5},{6,7},{1,0},{3,2},{5,4},{7,6},{8,9},{10,11},{12,... | collective-permute-start | bytes 786440 | tf_op jit(solution)/shard_map/fold/ppermute | solution.py:21
  108.6 9.0 %collective-permute-start.11 = (bf16[2,256,256]{2,1,0:T(8,128)(2,1)S(1)}, bf16[2,256,256]{2,1,0:T(8,128)(2,1)S(1)}, u32[]{:S(2)}, u32[]{:S(2)}) collective-permute-start(bf16[2,256,256]{2,1,0:T(8,128)(2,1)S(1)} %collective-permute-done.10.refs_1_), channel_id=1, source_target_pairs={{0,1},{2,3},{4,5},{6,7},{1,0},{3,2},{5,4},{7,6},{8,9},{10,11},{12,... | collective-permute-start | bytes 786440 | tf_op jit(solution)/shard_map/fold/ppermute | solution.py:21
  111.7 8.6 %collective-permute-start.15 = (bf16[2,256,256]{2,1,0:T(8,128)(2,1)S(1)}, bf16[2,256,256]{2,1,0:T(8,128)(2,1)S(1)}, u32[]{:S(2)}, u32[]{:S(2)}) collective-permute-start(bf16[2,256,256]{2,1,0:T(8,128)(2,1)S(1)} %collective-permute-done.14.refs_5_), channel_id=1, source_target_pairs={{1,2},{3,4},{5,6},{7,0},{2,1},{4,3},{6,5},{0,7},{9,10},{11,12},{13... | collective-permute-start | bytes 786440 | tf_op jit(solution)/shard_map/fold/ppermute | solution.py:21
  117.5 10.2 %collective-permute-start.12 = (bf16[2,256,256]{2,1,0:T(8,128)(2,1)S(1)}, bf16[2,256,256]{2,1,0:T(8,128)(2,1)S(1)}, u32[]{:S(2)}, u32[]{:S(2)}) collective-permute-start(bf16[2,256,256]{2,1,0:T(8,128)(2,1)S(1)} %collective-permute-done.11.refs_2_), channel_id=1, source_target_pairs={{1,2},{3,4},{5,6},{7,0},{2,1},{4,3},{6,5},{0,7},{9,10},{11,12},{13... | collective-permute-start | bytes 786440 | tf_op jit(solution)/shard_map/fold/ppermute | solution.py:21
  120.3 7.5 %collective-permute-start.16 = (bf16[2,256,256]{2,1,0:T(8,128)(2,1)S(1)}, bf16[2,256,256]{2,1,0:T(8,128)(2,1)S(1)}, u32[]{:S(2)}, u32[]{:S(2)}) collective-permute-start(bf16[2,256,256]{2,1,0:T(8,128)(2,1)S(1)} %collective-permute-done.15.refs_6_), channel_id=1, source_target_pairs={{0,1},{2,3},{4,5},{6,7},{1,0},{3,2},{5,4},{7,6},{8,9},{10,11},{12,... | collective-permute-start | bytes 786440 | tf_op jit(solution)/shard_map/fold/ppermute | solution.py:21
  183.3 17.5 %collective-permute-start.17 = (bf16[512,512]{1,0:T(8,128)(2,1)S(1)}, bf16[512,512]{1,0:T(8,128)(2,1)S(1)}, u32[]{:S(2)}, u32[]{:S(2)}) collective-permute-start(bf16[512,512]{1,0:T(8,128)(2,1)S(1)} %all_gather.7), channel_id=1, source_target_pairs={{0,8},{8,0},{1,9},{9,1},{2,10},{10,2},{3,11},{11,3},{4,12},{12,4},... | collective-permute-start | bytes 1572872 | tf_op jit(solution)/shard_map/gather_core/ppermute | solution.py:44

commit v6 on v5

--- a/solution.py
+++ b/solution.py
@@ -46,24 +46,39 @@
         return jnp.concatenate([jnp.where(first, part, other), jnp.where(first, other, part)], axis=1).astype(jnp.float32)
 
 
-def pick_kernel(ids_ref, table_ref, out_ref):
+def pick_kernel(ids_ref, table_ref, out_ref, ids, table, ids_sem, sems):
     slices, _, width = out_ref.shape
-    wanted = lax.broadcasted_iota(jnp.int32, (table_ref.shape[0], ids_ref.shape[1]), 0) == ids_ref[...]
-    wanted = wanted.astype(jnp.float32).T.astype(table_ref.dtype)
+    copies = [pltpu.make_async_copy(ids_ref, ids, ids_sem)]
     for j in range(slices):
-        rows = jnp.dot(wanted, table_ref[:, j * width:(j + 1) * width], preferred_element_type=jnp.float32)
+        cols = pl.ds(j * width, width)
+        copies.append(pltpu.make_async_copy(table_ref.at[:, cols], table.at[:, cols], sems.at[j]))
+    for copy in copies:
+        copy.start()
+    copies[0].wait()
+    wanted = lax.broadcasted_iota(jnp.int32, (table.shape[0], ids.shape[1]), 0) == ids[...]
+    wanted = wanted.astype(jnp.float32).T.astype(table.dtype)
+    for j in range(slices):
+        copies[j + 1].wait()
+        rows = jnp.dot(wanted, table[:, j * width:(j + 1) * width], preferred_element_type=jnp.float32)
         out_ref[j] = rows.astype(out_ref.dtype)
 
 
 def pick(table, ids, slices):
-    vmem = pl.BlockSpec(memory_space=pltpu.VMEM)
+    hbm = pl.BlockSpec(memory_space=pltpu.HBM)
+    ids = ids.reshape(1, -1)
     return pl.pallas_call(
         pick_kernel,
-        out_shape=jax.ShapeDtypeStruct((slices, ids.shape[0], table.shape[1] // slices), table.dtype),
-        in_specs=[vmem, vmem],
-        out_specs=vmem,
-        compiler_params=pltpu.CompilerParams(vmem_limit_bytes=32 * 2**20),
-    )(ids.reshape(1, -1), table)
+        out_shape=jax.ShapeDtypeStruct((slices, ids.shape[1], table.shape[1] // slices), table.dtype),
+        in_specs=[hbm, hbm],
+        out_specs=pl.BlockSpec(memory_space=pltpu.VMEM),
+        scratch_shapes=[
+            pltpu.VMEM(ids.shape, ids.dtype),
+            pltpu.VMEM(table.shape, table.dtype),
+            pltpu.SemaphoreType.DMA,
+            pltpu.SemaphoreType.DMA((slices,)),
+        ],
+        compiler_params=pltpu.CompilerParams(vmem_limit_bytes=60 * 2**20),
+    )(ids, table)
 
 
 def pair_block(me, chain, k, member):
@@ -107,7 +122,7 @@
         out_shape=[jax.ShapeDtypeStruct(slices.shape, jnp.bfloat16)] + [pair] * 8,
         in_specs=[smem] * 3 + [vmem] * 3,
         out_specs=[vmem] * 9,
-        compiler_params=pltpu.CompilerParams(vmem_limit_bytes=32 * 2**20),
+        compiler_params=pltpu.CompilerParams(vmem_limit_bytes=16 * 2**20),
     )(me.reshape(1), ids, counts, slices, tiles, weight)
     return agg, (parts[:4], parts[4:])
 
@@ -123,12 +138,13 @@
         held = [add(got[chain], pairs[chain][k]).astype(jnp.bfloat16) for chain in range(2)]
     sums = []
     got = [with_neighbour(held[chain], chain, 1) for chain in range(2)]
-    both = [add(got[chain], pairs[chain][0]) for chain in range(2)]
     for chain in range(2):
         second = is_second(chain)
-        give = jnp.where(second, both[chain][0], both[chain][1]).astype(jnp.bfloat16)
-        keep = jnp.where(second, both[chain][1], both[chain][0])
-        sums.append(keep + with_neighbour(give, chain, 0).astype(jnp.float32))
+        give, keep = (
+            add(jnp.where(second, x[0], x[1]), jnp.where(second, y[0], y[1]))
+            for x, y in ((got[chain], pairs[chain][0]), (got[chain][::-1], pairs[chain][0][::-1]))
+        )
+        sums.append(keep + with_neighbour(give.astype(jnp.bfloat16), chain, 0).astype(jnp.float32))
     return jnp.concatenate(sums, axis=1)
 
 
@@ -145,14 +161,15 @@
     return held[0] + held[1]
 
 
-def fold_kernel(me_ref, rows_ref, *refs):
+def fold_kernel(me_ref, agg_ref, other_ref, *refs):
     *grad_refs, out_ref = refs
     for chain in range(2):
         cols = grad_refs[0].shape[2]
         total = None
         for k in range(4):
             for member in range(2):
-                rows = rows_ref[pair_block(me_ref[0], chain, k, member)]
+                block = pair_block(me_ref[0], chain, k, member)
+                rows = jnp.concatenate([agg_ref[block], other_ref[block]], axis=0)
                 term = lax.dot_general(
                     rows, grad_refs[4 * chain + k][member], (((0,), (0,)), ((), ())), preferred_element_type=jnp.float32
                 )
@@ -160,15 +177,15 @@
         out_ref[:, chain * cols:(chain + 1) * cols] = total.astype(out_ref.dtype)
 
 
-def fold(me, rows, grads):
+def fold(me, agg, other_agg, grads):
     vmem = pl.BlockSpec(memory_space=pltpu.VMEM)
     return pl.pallas_call(
         fold_kernel,
-        out_shape=jax.ShapeDtypeStruct((rows.shape[2], 2 * grads[0].shape[2]), jnp.bfloat16),
-        in_specs=[pl.BlockSpec(memory_space=pltpu.SMEM), vmem] + [vmem] * len(grads),
+        out_shape=jax.ShapeDtypeStruct((agg.shape[2], 2 * grads[0].shape[2]), jnp.bfloat16),
+        in_specs=[pl.BlockSpec(memory_space=pltpu.SMEM)] + [vmem] * (2 + len(grads)),
         out_specs=vmem,
-        compiler_params=pltpu.CompilerParams(vmem_limit_bytes=32 * 2**20),
-    )(me.reshape(1), rows, *grads)
+        compiler_params=pltpu.CompilerParams(vmem_limit_bytes=12 * 2**20),
+    )(me.reshape(1), agg, other_agg, *grads)
 
 
 def shards(feature_table, sample_ids, block_ids, block_counts, block_tiles, weight, target):
@@ -195,12 +212,12 @@
         grad_pre = (grad_hidden * slope).astype(jnp.bfloat16)
     with jax.named_scope("swap"):
         half = hidden_width // 2
-        paired = lax.all_to_all(grad_pre.reshape(block_rows, 2, half).swapaxes(0, 1), "core", 0, 0)
+        first = lax.axis_index("core") == 0
+        left, right = grad_pre[:, :half], grad_pre[:, half:]
+        mine, other = jnp.where(first, left, right), lax.ppermute(jnp.where(first, right, left), "core", SWAP)
+        paired = jnp.concatenate([mine, other], axis=0)
     with jax.named_scope("fold"):
-        first = lax.axis_index("core") == 0
-        rows = jnp.concatenate([jnp.where(first, agg, other_agg), jnp.where(first, other_agg, agg)], axis=1)
-        paired = paired.reshape(2 * block_rows, half)
-        folded = fold(me, rows, chain_gather([paired[:, :half // 2], paired[:, half // 2:]]))
+        folded = fold(me, agg, other_agg, chain_gather([paired[:, :half // 2], paired[:, half // 2:]]))
     weight_grad = group_sum(folded)
     return (embedding, weight_grad)
 

time: 204 us -> 205 us (level)
  blocking collectives: 67 us -> 58.9 us
  starting transfers between devices: 63.1 us -> 70.8 us
  waiting for transfers between devices: 56.6 us -> 60.1 us
  Pallas kernels: 5.6 us -> 8.28 us
  other arithmetic: 5.84 us -> 3.44 us
    all_to_all x1 -> x0, blocking collectives: 12.9 us -> none  [shards(): lax.all_to_all(grad_pre.reshape(block_rows, 2, half).swapaxes(0, 1), 'cor...]
    ppermute x0 -> x1, starting transfers between devices: none -> 10.3 us  [shards(): lax.ppermute(jnp.where(first, right, left), 'core', SWAP)]
    ppermute x1, starting transfers between devices: 16 us -> 11.7 us  [group_sum(): other = lax.ppermute(part, 'core', SWAP)]
    all_to_all x1, blocking collectives: 20.8 us -> 24.3 us  [exchange_sum(): got = lax.all_to_all(parts, axis, 0, 0)]
    pallas_call x1, Pallas kernels: 1.46 us -> 4.07 us  [pick(): pl.pallas_call(pick_kernel, out_shape=jax.ShapeDtypeStruct((slices, ids.s...]
    ppermute x16, waiting for transfers between devices: 30.3 us -> 32.8 us  [with_neighbour(): return lax.ppermute(block, 'feat', neighbours(chain, odd_step))]
  transfers between devices with their start and end apart: 19 -> 20, of which waited for: 14 -> 15; matrix products, arithmetic and copies ran while one was open for 2% -> 0% of each run, Pallas kernels for 0% -> 0%
where the time goes in v6:
time: 205 us; the launch traced here: 204 us
  starting transfers between devices  70.8 us (35%)
  waiting for transfers between devices  60.1 us (29%)
  blocking collectives  58.9 us (29%)
  Pallas kernels  8.28 us (4%)
  other arithmetic  3.44 us (2%)
    ppermute x16, starting transfers between devices, with_neighbour(): return lax.ppermute(block, 'feat', neighbours(chain, odd_step))  38.9 us
    ppermute x16, waiting for transfers between devices, with_neighbour(): return lax.ppermute(block, 'feat', neighbours(chain, odd_step))  32.8 us
    all_to_all x1, waiting for transfers between devices, shards(): lax.all_to_all(pick(feature_table, sample_ids, block_total), 'feat', 0, 0)  24.8 us
    all_to_all x1, blocking collectives, exchange_sum(): got = lax.all_to_all(parts, axis, 0, 0)  24.3 us
    all_gather x1, blocking collectives, group_sum(): lax.all_gather(part.astype(jnp.bfloat16), ('zo', 'zi'), axis=0, tiled=True)  24.1 us
    ppermute x1, starting transfers between devices, group_sum(): other = lax.ppermute(part, 'core', SWAP)  11.7 us
    all_gather x1, blocking collectives, group_sum(): part = lax.all_gather(part, 'x', axis=0, tiled=True)  10.5 us
    ppermute x1, starting transfers between devices, shards(): lax.ppermute(jnp.where(first, right, left), 'core', SWAP)  10.3 us
  transfers between devices with their start and end apart: 20, of which 15 were waited for; matrix products, arithmetic and copies ran while one was open for 0% of the time, Pallas kernels for 0%

profile of v6, /device:TPU:1, one launch (start us, length us, event | category | flops | bytes accessed | tf_op | source)
XLA Modules:
  0.0 204.4 jit_solution(16649073226818082502)
XLA Ops:
  0.7 4.1 %pick.1 = bf16[8,128,512]{2,1,0:T(8,128)(2,1)} custom-call(s32[1,128]{1,0:T(1,128)} %bitcast.22, bf16[256,4096]{1,0:T(8,128)(2,1)} %table_ref.1), custom_call_target="tpu_custom_call" | custom-call | tf_op jit(solution)/shard_map/pick/pallas_call | solution.py:69
  4.7 7.7 %all-to-all-start = ((bf16[8,128,512]{2,1,0:T(8,128)(2,1)}), bf16[8,128,512]{2,1,0:T(8,128)(2,1)S(1)}, u32[]{:S(2)}, u32[]{:S(2)}) async-start(bf16[8,128,512]{2,1,0:T(8,128)(2,1)} %pick.1), calls=%async_computation | async-start | bytes 2097152 | tf_op jit(solution)/shard_map/pick/all_to_all | solution.py:196
  12.5 24.8 %all-to-all-done.slices_ref = bf16[8,128,512]{2,1,0:T(8,128)(2,1)S(1)} async-done(((bf16[8,128,512]{2,1,0:T(8,128)(2,1)}), bf16[8,128,512]{2,1,0:T(8,128)(2,1)S(1)}, u32[]{:S(2)}, u32[]{:S(2)}) %all-to-all-start) | async-done | bytes 1048608 | tf_op jit(solution)/shard_map/pick/all_to_all | solution.py:196
  37.3 2.9 %aggregate.1 = (bf16[8,128,512]{2,1,0:T(8,128)(2,1)S(1)}, bf16[2,128,512]{2,1,0:T(8,128)(2,1)S(1)}, bf16[2,128,512]{2,1,0:T(8,128)(2,1)S(1)}, bf16[2,128,512]{2,...) custom-call(s32[1]{0:T(128)} %bitcast.me_ref, ...), custom_call_target="tpu_custom_call" | custom-call | tf_op jit(solution)/shard_map/aggregate/pallas_call | solution.py:120
  41.9 2.0 collective-permute-start
  43.9 1.9 collective-permute-start.4
  45.9 4.5 %collective-permute-done = bf16[2,128,512]{2,1,0:T(8,128)(2,1)S(1)} collective-permute-done((bf16[2,128,512]{2,1,0:T(8,128)(2,1)S(1)}, bf16[2,128,512]{2,1,0:T(8,128)(2,1)S(1)}, u32[]{:S(2)}, u32[]{:S(2)}) %collective-permute-start) | collective-permute-done | bytes 262176 | tf_op jit(solution)/shard_map/preact/ppermute | solution.py:21
  50.4 1.9 collective-permute-start.1
  52.4 3.6 %collective-permute-start.5 = (bf16[2,128,512]{2,1,0:T(8,128)(2,1)S(1)}, bf16[2,128,512]{2,1,0:T(8,128)(2,1)S(1)}, u32[]{:S(2)}, u32[]{:S(2)}) collective-permute-start(bf16[2,128,512]{2,1,0:T(8,128)(2,1)S(1)} %add_convert_fusion.1), channel_id=1, source_target_pairs={{1,2},{3,4},{5,6},{7,0},{2,1},{4,3},{6,5},{0,7},{9,10},{11,12},{13... | collective-permute-start | bytes 786440 | tf_op jit(solution)/shard_map/preact/ppermute | solution.py:21
  56.0 3.2 %collective-permute-done.1 = bf16[2,128,512]{2,1,0:T(8,128)(2,1)S(1)} collective-permute-done((bf16[2,128,512]{2,1,0:T(8,128)(2,1)S(1)}, bf16[2,128,512]{2,1,0:T(8,128)(2,1)S(1)}, u32[]{:S(2)}, u32[]{:S(2)}) %collective-permute-start.1) | collective-permute-done | bytes 262176 | tf_op jit(solution)/shard_map/preact/ppermute | solution.py:21
  59.2 1.9 collective-permute-start.2
  61.3 2.2 %collective-permute-start.6 = (bf16[2,128,512]{2,1,0:T(8,128)(2,1)S(1)}, bf16[2,128,512]{2,1,0:T(8,128)(2,1)S(1)}, u32[]{:S(2)}, u32[]{:S(2)}) collective-permute-start(bf16[2,128,512]{2,1,0:T(8,128)(2,1)S(1)} %add_convert_fusion), channel_id=1, source_target_pairs={{0,1},{2,3},{4,5},{6,7},{1,0},{3,2},{5,4},{7,6},{8,9},{10,11},{12,... | collective-permute-start | bytes 786440 | tf_op jit(solution)/shard_map/preact/ppermute | solution.py:21
  63.5 7.1 %collective-permute-done.2 = bf16[2,128,512]{2,1,0:T(8,128)(2,1)S(1)} collective-permute-done((bf16[2,128,512]{2,1,0:T(8,128)(2,1)S(1)}, bf16[2,128,512]{2,1,0:T(8,128)(2,1)S(1)}, u32[]{:S(2)}, u32[]{:S(2)}) %collective-permute-start.2) | collective-permute-done | bytes 262176 | tf_op jit(solution)/shard_map/preact/ppermute | solution.py:21
  70.7 1.9 collective-permute-start.3
  72.7 1.9 collective-permute-start.7
  74.6 2.6 %collective-permute-done.3 = bf16[128,512]{1,0:T(8,128)(2,1)S(1)} collective-permute-done((bf16[128,512]{1,0:T(8,128)(2,1)S(1)}, bf16[128,512]{1,0:T(8,128)(2,1)S(1)}, u32[]{:S(2)}, u32[]{:S(2)}) %collective-permute-start.3) | collective-permute-done | bytes 131104 | tf_op jit(solution)/shard_map/preact/ppermute | solution.py:21
  77.3 2.3 %collective-permute-done.7 = bf16[128,512]{1,0:T(8,128)(2,1)S(1)} collective-permute-done((bf16[128,512]{1,0:T(8,128)(2,1)S(1)}, bf16[128,512]{1,0:T(8,128)(2,1)S(1)}, u32[]{:S(2)}, u32[]{:S(2)}) %collective-permute-start.7) | collective-permute-done | bytes 131104 | tf_op jit(solution)/shard_map/preact/ppermute | solution.py:21
  80.7 10.3 %collective-permute-start.9 = (bf16[128,512]{1,0:T(8,128)(2,1)S(1)}, bf16[128,512]{1,0:T(8,128)(2,1)S(1)}, u32[]{:S(2)}, u32[]{:S(2)}) collective-permute-start(bf16[128,512]{1,0:T(8,128)(2,1)S(1)} %get-tuple-element.32), channel_id=1, source_target_pairs={{0,8},{8,0},{1,9},{9,1},{2,10},{10,2},{3,11},{11,3},{4,12},{12,4},... | collective-permute-start | bytes 393224 | tf_op jit(solution)/shard_map/swap/ppermute | solution.py:217
  92.0 1.9 collective-permute-start.10
  93.9 2.3 %collective-permute-start.8 = (bf16[8,128,512]{2,1,0:T(8,128)(2,1)S(1)}, bf16[8,128,512]{2,1,0:T(8,128)(2,1)S(1)}, u32[]{:S(2)}, u32[]{:S(2)}) collective-permute-start(bf16[8,128,512]{2,1,0:T(8,128)(2,1)S(1)} %copy-done.3), channel_id=1, source_target_pairs={{0,8},{8,0},{1,9},{9,1},{2,10},{10,2},{3,11},{11,3},{4,12},{12,4},... | collective-permute-start | bytes 3145736 | tf_op jit(solution)/shard_map/aggregate/ppermute | solution.py:199
  98.7 4.1 %collective-permute-start.11 = (bf16[2,256,256]{2,1,0:T(8,128)(2,1)S(1)}, bf16[2,256,256]{2,1,0:T(8,128)(2,1)S(1)}, u32[]{:S(2)}, u32[]{:S(2)}) collective-permute-start(bf16[2,256,256]{2,1,0:T(8,128)(2,1)S(1)} %pad_maximum_fusion.1.refs_0_), channel_id=1, source_target_pairs={{1,2},{3,4},{5,6},{7,0},{2,1},{4,3},{6,5},{0,7},{9,10},{11,12},{13... | collective-permute-start | bytes 786440 | tf_op jit(solution)/shard_map/fold/ppermute | solution.py:21
  104.3 2.6 %collective-permute-start.15 = (bf16[2,256,256]{2,1,0:T(8,128)(2,1)S(1)}, bf16[2,256,256]{2,1,0:T(8,128)(2,1)S(1)}, u32[]{:S(2)}, u32[]{:S(2)}) collective-permute-start(bf16[2,256,256]{2,1,0:T(8,128)(2,1)S(1)} %pad_maximum_fusion.2.refs_4_), channel_id=1, source_target_pairs={{0,1},{2,3},{4,5},{6,7},{1,0},{3,2},{5,4},{7,6},{8,9},{10,11},{12,... | collective-permute-start | bytes 786440 | tf_op jit(solution)/shard_map/fold/ppermute | solution.py:21
  106.9 2.1 %collective-permute-done.11.refs_1_ = bf16[2,256,256]{2,1,0:T(8,128)(2,1)S(1)} collective-permute-done((bf16[2,256,256]{2,1,0:T(8,128)(2,1)S(1)}, bf16[2,256,256]{2,1,0:T(8,128)(2,1)S(1)}, u32[]{:S(2)}, u32[]{:S(2)}) %collective-permute-start.11) | collective-permute-done | bytes 262176 | tf_op jit(solution)/shard_map/fold/ppermute | solution.py:21
  109.1 3.4 %collective-permute-start.12 = (bf16[2,256,256]{2,1,0:T(8,128)(2,1)S(1)}, bf16[2,256,256]{2,1,0:T(8,128)(2,1)S(1)}, u32[]{:S(2)}, u32[]{:S(2)}) collective-permute-start(bf16[2,256,256]{2,1,0:T(8,128)(2,1)S(1)} %collective-permute-done.11.refs_1_), channel_id=1, source_target_pairs={{0,1},{2,3},{4,5},{6,7},{1,0},{3,2},{5,4},{7,6},{8,9},{10,11},{12,... | collective-permute-start | bytes 786440 | tf_op jit(solution)/shard_map/fold/ppermute | solution.py:21
  112.8 2.7 %collective-permute-start.16 = (bf16[2,256,256]{2,1,0:T(8,128)(2,1)S(1)}, bf16[2,256,256]{2,1,0:T(8,128)(2,1)S(1)}, u32[]{:S(2)}, u32[]{:S(2)}) collective-permute-start(bf16[2,256,256]{2,1,0:T(8,128)(2,1)S(1)} %collective-permute-done.15.refs_5_), channel_id=1, source_target_pairs={{1,2},{3,4},{5,6},{7,0},{2,1},{4,3},{6,5},{0,7},{9,10},{11,12},{13... | collective-permute-start | bytes 786440 | tf_op jit(solution)/shard_map/fold/ppermute | solution.py:21
  115.5 3.3 %collective-permute-done.12.refs_2_ = bf16[2,256,256]{2,1,0:T(8,128)(2,1)S(1)} collective-permute-done((bf16[2,256,256]{2,1,0:T(8,128)(2,1)S(1)}, bf16[2,256,256]{2,1,0:T(8,128)(2,1)S(1)}, u32[]{:S(2)}, u32[]{:S(2)}) %collective-permute-start.12) | collective-permute-done | bytes 262176 | tf_op jit(solution)/shard_map/fold/ppermute | solution.py:21
  118.8 3.0 %collective-permute-start.13 = (bf16[2,256,256]{2,1,0:T(8,128)(2,1)S(1)}, bf16[2,256,256]{2,1,0:T(8,128)(2,1)S(1)}, u32[]{:S(2)}, u32[]{:S(2)}) collective-permute-start(bf16[2,256,256]{2,1,0:T(8,128)(2,1)S(1)} %collective-permute-done.12.refs_2_), channel_id=1, source_target_pairs={{1,2},{3,4},{5,6},{7,0},{2,1},{4,3},{6,5},{0,7},{9,10},{11,12},{13... | collective-permute-start | bytes 786440 | tf_op jit(solution)/shard_map/fold/ppermute | solution.py:21
  123.7 4.6 %collective-permute-done.13.refs_3_ = bf16[2,256,256]{2,1,0:T(8,128)(2,1)S(1)} collective-permute-done((bf16[2,256,256]{2,1,0:T(8,128)(2,1)S(1)}, bf16[2,256,256]{2,1,0:T(8,128)(2,1)S(1)}, u32[]{:S(2)}, u32[]{:S(2)}) %collective-permute-start.13) | collective-permute-done | bytes 262176 | tf_op jit(solution)/shard_map/fold/ppermute | solution.py:21
  130.5 24.3 %all_to_all.10 = bf16[16,32,512]{2,1,0:T(8,128)(2,1)S(1)} all-to-all(bf16[16,32,512]{2,1,0:T(8,128)(2,1)S(1)} %bitcast.20), channel_id=1, replica_groups=mesh['x'=4,'zo'=3,'zi'=4,'core'=2,'feat'=8] {'x','zi'}, dimensions={0} | all-to-all | bytes 1048576 | tf_op jit(solution)/shard_map/sum_x_zi/all_to_all | solution.py:29
  154.8 24.1 %all_gather.6 = bf16[384,512]{1,0:T(8,128)(2,1)S(1)} all-gather(bf16[32,512]{1,0:T(8,128)(2,1)S(1)} %reduce_sum.44), channel_id=1, replica_groups=mesh['x'=4,'zo'=3,'zi'=4,'core'=2,'feat'=8] {'zo','zi'}, dimensions={0}, use_global_device_ids=true | all-gather | bytes 425984 | tf_op jit(solution)/shard_map/sum_z/all_gather | solution.py:38
  179.1 10.5 %all_gather.7 = bf16[512,512]{1,0:T(8,128)(2,1)S(1)} all-gather(bf16[128,512]{1,0:T(8,128)(2,1)S(1)} %reduce_sum.45), channel_id=1, replica_groups=mesh['x'=4,'zo'=3,'zi'=4,'core'=2,'feat'=8] {'x'}, dimensions={0}, use_global_device_ids=true | all-gather | bytes 655360 | tf_op jit(solution)/shard_map/gather_x/all_gather | solution.py:42
  189.5 11.7 %collective-permute-start.18 = (bf16[512,512]{1,0:T(8,128)(2,1)S(1)}, bf16[512,512]{1,0:T(8,128)(2,1)S(1)}, u32[]{:S(2)}, u32[]{:S(2)}) collective-permute-start(bf16[512,512]{1,0:T(8,128)(2,1)S(1)} %all_gather.7), channel_id=1, source_target_pairs={{0,8},{8,0},{1,9},{9,1},{2,10},{10,2},{3,11},{11,3},{4,12},{12,4},... | collective-permute-start | bytes 1572872 | tf_op jit(solution)/shard_map/gather_core/ppermute | solution.py:44
  (58 shorter events, 15.9 us)
Async XLA Ops:
  0.6 11.8 %copy-start.9 = (s32[8,4]{0,1:T(4,128)S(1)}, s32[8,4]{0,1:T(4,128)}, u32[]{:S(2)}) copy-start(s32[8,4]{0,1:T(4,128)} %param.9) | copy-start | bytes 388
  0.6 36.7 %copy-start = (bf16[8,4,128,128]{3,2,1,0:T(8,128)(2,1)S(1)}, bf16[8,4,128,128]{3,2,1,0:T(8,128)(2,1)}, u32[]{:S(2)}) copy-start(bf16[8,4,128,128]{3,2,1,0:T(8,128)(2,1)} %tiles_ref.1) | copy-start | bytes 3145732
  0.7 36.6 %copy-start.1 = (bf16[512,1024]{1,0:T(8,128)(2,1)S(1)}, bf16[512,1024]{1,0:T(8,128)(2,1)}, u32[]{:S(2)}) copy-start(bf16[512,1024]{1,0:T(8,128)(2,1)} %weight_ref.1) | copy-start | bytes 3145732
  0.7 36.6 %copy-start.6 = (s32[8]{0:T(128)S(1)}, s32[8]{0:T(128)}, u32[]{:S(2)}) copy-start(s32[8]{0:T(128)} %counts_ref.1) | copy-start | bytes 100
  4.7 32.5 %all-to-all-start = ((bf16[8,128,512]{2,1,0:T(8,128)(2,1)}), bf16[8,128,512]{2,1,0:T(8,128)(2,1)S(1)}, u32[]{:S(2)}, u32[]{:S(2)}) async-start(bf16[8,128,512]{2,1,0:T(8,128)(2,1)} %pick.1), calls=%async_computation | async-start | bytes 2097152 | tf_op jit(solution)/shard_map/pick/all_to_all | solution.py:196
  40.2 1.0 copy-start.2
  41.2 0.7 copy-start.4
  41.9 28.7 %copy-start.5 = (bf16[2,128,512]{2,1,0:T(8,128)(2,1)S(1)}, bf16[2,128,512]{2,1,0:T(8,128)(2,1)}, u32[]{:S(2)}) copy-start(bf16[2,128,512]{2,1,0:T(8,128)(2,1)} %copy-done.4) | copy-start | bytes 786436
  41.9 8.4 %collective-permute-start = (bf16[2,128,512]{2,1,0:T(8,128)(2,1)S(1)}, bf16[2,128,512]{2,1,0:T(8,128)(2,1)S(1)}, u32[]{:S(2)}, u32[]{:S(2)}) collective-permute-start(bf16[2,128,512]{2,1,0:T(8,128)(2,1)S(1)} %get-tuple-element.11), channel_id=1, source_target_pairs={{1,2},{3,4},{5,6},{7,0},{2,1},{4,3},{6,5},{0,7},{9,10},{11,12},{13... | collective-permute-start | bytes 786440 | tf_op jit(solution)/shard_map/preact/ppermute | solution.py:21
  43.9 8.4 %collective-permute-start.4 = (bf16[2,128,512]{2,1,0:T(8,128)(2,1)S(1)}, bf16[2,128,512]{2,1,0:T(8,128)(2,1)S(1)}, u32[]{:S(2)}, u32[]{:S(2)}) collective-permute-start(bf16[2,128,512]{2,1,0:T(8,128)(2,1)S(1)} %get-tuple-element.15), channel_id=1, source_target_pairs={{0,1},{2,3},{4,5},{6,7},{1,0},{3,2},{5,4},{7,6},{8,9},{10,11},{12,... | collective-permute-start | bytes 786440 | tf_op jit(solution)/shard_map/preact/ppermute | solution.py:21
  50.4 8.8 %collective-permute-start.1 = (bf16[2,128,512]{2,1,0:T(8,128)(2,1)S(1)}, bf16[2,128,512]{2,1,0:T(8,128)(2,1)S(1)}, u32[]{:S(2)}, u32[]{:S(2)}) collective-permute-start(bf16[2,128,512]{2,1,0:T(8,128)(2,1)S(1)} %add_convert_fusion.3), channel_id=1, source_target_pairs={{0,1},{2,3},{4,5},{6,7},{1,0},{3,2},{5,4},{7,6},{8,9},{10,11},{12,... | collective-permute-start | bytes 786440 | tf_op jit(solution)/shard_map/preact/ppermute | solution.py:21
  52.4 8.7 %collective-permute-start.5 = (bf16[2,128,512]{2,1,0:T(8,128)(2,1)S(1)}, bf16[2,128,512]{2,1,0:T(8,128)(2,1)S(1)}, u32[]{:S(2)}, u32[]{:S(2)}) collective-permute-start(bf16[2,128,512]{2,1,0:T(8,128)(2,1)S(1)} %add_convert_fusion.1), channel_id=1, source_target_pairs={{1,2},{3,4},{5,6},{7,0},{2,1},{4,3},{6,5},{0,7},{9,10},{11,12},{13... | collective-permute-start | bytes 786440 | tf_op jit(solution)/shard_map/preact/ppermute | solution.py:21
  59.2 11.3 %collective-permute-start.2 = (bf16[2,128,512]{2,1,0:T(8,128)(2,1)S(1)}, bf16[2,128,512]{2,1,0:T(8,128)(2,1)S(1)}, u32[]{:S(2)}, u32[]{:S(2)}) collective-permute-start(bf16[2,128,512]{2,1,0:T(8,128)(2,1)S(1)} %add_convert_fusion.2), channel_id=1, source_target_pairs={{1,2},{3,4},{5,6},{7,0},{2,1},{4,3},{6,5},{0,7},{9,10},{11,12},{13... | collective-permute-start | bytes 786440 | tf_op jit(solution)/shard_map/preact/ppermute | solution.py:21
  61.2 18.8 %copy-start.7 = (bf16[128,1024]{1,0:T(8,128)(2,1)S(1)}, bf16[128,1024]{1,0:T(8,128)(2,1)}, u32[]{:S(2)}) copy-start(bf16[128,1024]{1,0:T(8,128)(2,1)} %param.13) | copy-start | bytes 786436
  61.3 11.3 %collective-permute-start.6 = (bf16[2,128,512]{2,1,0:T(8,128)(2,1)S(1)}, bf16[2,128,512]{2,1,0:T(8,128)(2,1)S(1)}, u32[]{:S(2)}, u32[]{:S(2)}) collective-permute-start(bf16[2,128,512]{2,1,0:T(8,128)(2,1)S(1)} %add_convert_fusion), channel_id=1, source_target_pairs={{0,1},{2,3},{4,5},{6,7},{1,0},{3,2},{5,4},{7,6},{8,9},{10,11},{12,... | collective-permute-start | bytes 786440 | tf_op jit(solution)/shard_map/preact/ppermute | solution.py:21
  70.7 6.6 %collective-permute-start.3 = (bf16[128,512]{1,0:T(8,128)(2,1)S(1)}, bf16[128,512]{1,0:T(8,128)(2,1)S(1)}, u32[]{:S(2)}, u32[]{:S(2)}) collective-permute-start(bf16[128,512]{1,0:T(8,128)(2,1)S(1)} %fusion.1), channel_id=1, source_target_pairs={{0,1},{2,3},{4,5},{6,7},{1,0},{3,2},{5,4},{7,6},{8,9},{10,11},{12,... | collective-permute-start | bytes 393224 | tf_op jit(solution)/shard_map/preact/ppermute | solution.py:21
  72.7 6.9 %collective-permute-start.7 = (bf16[128,512]{1,0:T(8,128)(2,1)S(1)}, bf16[128,512]{1,0:T(8,128)(2,1)S(1)}, u32[]{:S(2)}, u32[]{:S(2)}) collective-permute-start(bf16[128,512]{1,0:T(8,128)(2,1)S(1)} %fusion.2), channel_id=1, source_target_pairs={{1,2},{3,4},{5,6},{7,0},{2,1},{4,3},{6,5},{0,7},{9,10},{11,12},{13... | collective-permute-start | bytes 393224 | tf_op jit(solution)/shard_map/preact/ppermute | solution.py:21
  79.7 14.3 %copy-start.3 = (bf16[8,128,512]{2,1,0:T(8,128)(2,1)S(1)}, bf16[8,128,512]{2,1,0:T(8,128)(2,1)}, u32[]{:S(2)}) copy-start(bf16[8,128,512]{2,1,0:T(8,128)(2,1)} %copy-done.2) | copy-start | bytes 3145732
  80.3 24.1 %copy-start.8 = (bf16[128,1024]{1,0:T(8,128)(2,1)}, bf16[128,1024]{1,0:T(8,128)(2,1)S(1)}, u32[]{:S(2)}) copy-start(bf16[128,1024]{1,0:T(8,128)(2,1)S(1)} %get-tuple-element.23) | copy-start | bytes 786436
  80.7 11.3 %collective-permute-start.9 = (bf16[128,512]{1,0:T(8,128)(2,1)S(1)}, bf16[128,512]{1,0:T(8,128)(2,1)S(1)}, u32[]{:S(2)}, u32[]{:S(2)}) collective-permute-start(bf16[128,512]{1,0:T(8,128)(2,1)S(1)} %get-tuple-element.32), channel_id=1, source_target_pairs={{0,8},{8,0},{1,9},{9,1},{2,10},{10,2},{3,11},{11,3},{4,12},{12,4},... | collective-permute-start | bytes 393224 | tf_op jit(solution)/shard_map/swap/ppermute | solution.py:217
  92.0 6.6 %collective-permute-start.10 = (bf16[256,256]{1,0:T(8,128)(2,1)S(1)}, bf16[256,256]{1,0:T(8,128)(2,1)S(1)}, u32[]{:S(2)}, u32[]{:S(2)}) collective-permute-start(bf16[256,256]{1,0:T(8,128)(2,1)S(1)} %get-tuple-element.29), channel_id=1, source_target_pairs={{0,1},{2,3},{4,5},{6,7},{1,0},{3,2},{5,4},{7,6},{8,9},{10,11},{12,... | collective-permute-start | bytes 393224 | tf_op jit(solution)/shard_map/fold/ppermute | solution.py:21
  93.9 29.7 %collective-permute-start.8 = (bf16[8,128,512]{2,1,0:T(8,128)(2,1)S(1)}, bf16[8,128,512]{2,1,0:T(8,128)(2,1)S(1)}, u32[]{:S(2)}, u32[]{:S(2)}) collective-permute-start(bf16[8,128,512]{2,1,0:T(8,128)(2,1)S(1)} %copy-done.3), channel_id=1, source_target_pairs={{0,8},{8,0},{1,9},{9,1},{2,10},{10,2},{3,11},{11,3},{4,12},{12,4},... | collective-permute-start | bytes 3145736 | tf_op jit(solution)/shard_map/aggregate/ppermute | solution.py:199
  96.2 8.1 %collective-permute-start.14 = (bf16[256,256]{1,0:T(8,128)(2,1)S(1)}, bf16[256,256]{1,0:T(8,128)(2,1)S(1)}, u32[]{:S(2)}, u32[]{:S(2)}) collective-permute-start(bf16[256,256]{1,0:T(8,128)(2,1)S(1)} %get-tuple-element.28), channel_id=1, source_target_pairs={{1,2},{3,4},{5,6},{7,0},{2,1},{4,3},{6,5},{0,7},{9,10},{11,12},{13... | collective-permute-start | bytes 393224 | tf_op jit(solution)/shard_map/fold/ppermute | solution.py:21
  98.7 10.4 %collective-permute-start.11 = (bf16[2,256,256]{2,1,0:T(8,128)(2,1)S(1)}, bf16[2,256,256]{2,1,0:T(8,128)(2,1)S(1)}, u32[]{:S(2)}, u32[]{:S(2)}) collective-permute-start(bf16[2,256,256]{2,1,0:T(8,128)(2,1)S(1)} %pad_maximum_fusion.1.refs_0_), channel_id=1, source_target_pairs={{1,2},{3,4},{5,6},{7,0},{2,1},{4,3},{6,5},{0,7},{9,10},{11,12},{13... | collective-permute-start | bytes 786440 | tf_op jit(solution)/shard_map/fold/ppermute | solution.py:21
  104.3 8.4 %collective-permute-start.15 = (bf16[2,256,256]{2,1,0:T(8,128)(2,1)S(1)}, bf16[2,256,256]{2,1,0:T(8,128)(2,1)S(1)}, u32[]{:S(2)}, u32[]{:S(2)}) collective-permute-start(bf16[2,256,256]{2,1,0:T(8,128)(2,1)S(1)} %pad_maximum_fusion.2.refs_4_), channel_id=1, source_target_pairs={{0,1},{2,3},{4,5},{6,7},{1,0},{3,2},{5,4},{7,6},{8,9},{10,11},{12,... | collective-permute-start | bytes 786440 | tf_op jit(solution)/shard_map/fold/ppermute | solution.py:21
  109.1 9.7 %collective-permute-start.12 = (bf16[2,256,256]{2,1,0:T(8,128)(2,1)S(1)}, bf16[2,256,256]{2,1,0:T(8,128)(2,1)S(1)}, u32[]{:S(2)}, u32[]{:S(2)}) collective-permute-start(bf16[2,256,256]{2,1,0:T(8,128)(2,1)S(1)} %collective-permute-done.11.refs_1_), channel_id=1, source_target_pairs={{0,1},{2,3},{4,5},{6,7},{1,0},{3,2},{5,4},{7,6},{8,9},{10,11},{12,... | collective-permute-start | bytes 786440 | tf_op jit(solution)/shard_map/fold/ppermute | solution.py:21
  112.8 8.9 %collective-permute-start.16 = (bf16[2,256,256]{2,1,0:T(8,128)(2,1)S(1)}, bf16[2,256,256]{2,1,0:T(8,128)(2,1)S(1)}, u32[]{:S(2)}, u32[]{:S(2)}) collective-permute-start(bf16[2,256,256]{2,1,0:T(8,128)(2,1)S(1)} %collective-permute-done.15.refs_5_), channel_id=1, source_target_pairs={{1,2},{3,4},{5,6},{7,0},{2,1},{4,3},{6,5},{0,7},{9,10},{11,12},{13... | collective-permute-start | bytes 786440 | tf_op jit(solution)/shard_map/fold/ppermute | solution.py:21
  118.8 9.5 %collective-permute-start.13 = (bf16[2,256,256]{2,1,0:T(8,128)(2,1)S(1)}, bf16[2,256,256]{2,1,0:T(8,128)(2,1)S(1)}, u32[]{:S(2)}, u32[]{:S(2)}) collective-permute-start(bf16[2,256,256]{2,1,0:T(8,128)(2,1)S(1)} %collective-permute-done.12.refs_2_), channel_id=1, source_target_pairs={{1,2},{3,4},{5,6},{7,0},{2,1},{4,3},{6,5},{0,7},{9,10},{11,12},{13... | collective-permute-start | bytes 786440 | tf_op jit(solution)/shard_map/fold/ppermute | solution.py:21
  121.7 7.4 %collective-permute-start.17 = (bf16[2,256,256]{2,1,0:T(8,128)(2,1)S(1)}, bf16[2,256,256]{2,1,0:T(8,128)(2,1)S(1)}, u32[]{:S(2)}, u32[]{:S(2)}) collective-permute-start(bf16[2,256,256]{2,1,0:T(8,128)(2,1)S(1)} %collective-permute-done.16.refs_6_), channel_id=1, source_target_pairs={{0,1},{2,3},{4,5},{6,7},{1,0},{3,2},{5,4},{7,6},{8,9},{10,11},{12,... | collective-permute-start | bytes 786440 | tf_op jit(solution)/shard_map/fold/ppermute | solution.py:21
  189.5 13.2 %collective-permute-start.18 = (bf16[512,512]{1,0:T(8,128)(2,1)S(1)}, bf16[512,512]{1,0:T(8,128)(2,1)S(1)}, u32[]{:S(2)}, u32[]{:S(2)}) collective-permute-start(bf16[512,512]{1,0:T(8,128)(2,1)S(1)} %all_gather.7), channel_id=1, source_target_pairs={{0,8},{8,0},{1,9},{9,1},{2,10},{10,2},{3,11},{11,3},{4,12},{12,4},... | collective-permute-start | bytes 1572872 | tf_op jit(solution)/shard_map/gather_core/ppermute | solution.py:44

commit v7 on v6

--- a/solution.py
+++ b/solution.py
@@ -46,7 +46,7 @@
         return jnp.concatenate([jnp.where(first, part, other), jnp.where(first, other, part)], axis=1).astype(jnp.float32)
 
 
-def pick_kernel(ids_ref, table_ref, out_ref, ids, table, ids_sem, sems):
+def pick_kernel(ids_ref, table_ref, out_ref, ids, table, picked, ids_sem, sems, out_sems):
     slices, _, width = out_ref.shape
     copies = [pltpu.make_async_copy(ids_ref, ids, ids_sem)]
     for j in range(slices):
@@ -57,24 +57,32 @@
     copies[0].wait()
     wanted = lax.broadcasted_iota(jnp.int32, (table.shape[0], ids.shape[1]), 0) == ids[...]
     wanted = wanted.astype(jnp.float32).T.astype(table.dtype)
+    leave = []
     for j in range(slices):
         copies[j + 1].wait()
         rows = jnp.dot(wanted, table[:, j * width:(j + 1) * width], preferred_element_type=jnp.float32)
-        out_ref[j] = rows.astype(out_ref.dtype)
+        picked[j] = rows.astype(picked.dtype)
+        leave.append(pltpu.make_async_copy(picked.at[j], out_ref.at[j], out_sems.at[j]))
+        leave[-1].start()
+    for copy in leave:
+        copy.wait()
 
 
 def pick(table, ids, slices):
     hbm = pl.BlockSpec(memory_space=pltpu.HBM)
     ids = ids.reshape(1, -1)
+    out = jax.ShapeDtypeStruct((slices, ids.shape[1], table.shape[1] // slices), table.dtype)
     return pl.pallas_call(
         pick_kernel,
-        out_shape=jax.ShapeDtypeStruct((slices, ids.shape[1], table.shape[1] // slices), table.dtype),
+        out_shape=out,
         in_specs=[hbm, hbm],
-        out_specs=pl.BlockSpec(memory_space=pltpu.VMEM),
+        out_specs=hbm,
         scratch_shapes=[
             pltpu.VMEM(ids.shape, ids.dtype),
             pltpu.VMEM(table.shape, table.dtype),
+            pltpu.VMEM(out.shape, out.dtype),
             pltpu.SemaphoreType.DMA,
+            pltpu.SemaphoreType.DMA((slices,)),
             pltpu.SemaphoreType.DMA((slices,)),
         ],
         compiler_params=pltpu.CompilerParams(vmem_limit_bytes=60 * 2**20),
@@ -88,7 +96,7 @@
     return lax.rem(2 * lax.rem(pair, FEAT // 2) + member + FEAT - chain, FEAT)
 
 
-def aggregate_kernel(me_ref, ids_ref, counts_ref, slices_ref, tiles_ref, weight_ref, agg_ref, *part_refs):
+def aggregate_kernel(ids_ref, counts_ref, slices_ref, tiles_ref, agg_ref):
     blocks, _, width = slices_ref.shape
     slots = tiles_ref.shape[1]
     ones = jnp.ones((slots * tiles_ref.shape[3], 128), jnp.bfloat16)
@@ -101,6 +109,21 @@
         summed = jnp.dot(lhs, rhs, preferred_element_type=jnp.float32)
         degree = jnp.dot(lhs, ones, preferred_element_type=jnp.float32)
         agg_ref[own] = (summed / jnp.concatenate([degree] * (width // 128), axis=1)).astype(jnp.bfloat16)
+
+
+def mean_of_blocks(ids, counts, slices, tiles):
+    vmem, smem = pl.BlockSpec(memory_space=pltpu.VMEM), pl.BlockSpec(memory_space=pltpu.SMEM)
+    return pl.pallas_call(
+        aggregate_kernel,
+        out_shape=jax.ShapeDtypeStruct(slices.shape, jnp.bfloat16),
+        in_specs=[smem] * 2 + [vmem] * 2,
+        out_specs=vmem,
+        compiler_params=pltpu.CompilerParams(vmem_limit_bytes=16 * 2**20),
+    )(ids, counts, slices, tiles)
+
+
+def project_kernel(me_ref, agg_ref, weight_ref, *part_refs):
+    blocks, rows, _ = agg_ref.shape
     for chain in range(2):
         refs = part_refs[4 * chain:4 * chain + 4]
         cols = refs[0].shape[2]
@@ -108,23 +131,21 @@
         lhs = jnp.concatenate([agg_ref[pair_block(me_ref[0], chain, k, member)] for k, member in order], axis=0)
         parts = jnp.dot(lhs, weight_ref[:, chain * cols:(chain + 1) * cols], preferred_element_type=jnp.float32)
         parts = parts.astype(jnp.bfloat16)
-        rows = parts.shape[0] // blocks
         for i, (k, member) in enumerate(order):
             refs[k][member] = parts[i * rows:(i + 1) * rows]
 
 
-def aggregate_and_project(me, ids, counts, slices, tiles, weight):
-    block_rows = slices.shape[1]
-    vmem, smem = pl.BlockSpec(memory_space=pltpu.VMEM), pl.BlockSpec(memory_space=pltpu.SMEM)
-    pair = jax.ShapeDtypeStruct((2, block_rows, weight.shape[1] // 2), jnp.bfloat16)
-    agg, *parts = pl.pallas_call(
-        aggregate_kernel,
-        out_shape=[jax.ShapeDtypeStruct(slices.shape, jnp.bfloat16)] + [pair] * 8,
-        in_specs=[smem] * 3 + [vmem] * 3,
-        out_specs=[vmem] * 9,
+def project(me, agg, weight):
+    vmem = pl.BlockSpec(memory_space=pltpu.VMEM)
+    pair = jax.ShapeDtypeStruct((2, agg.shape[1], weight.shape[1] // 2), jnp.bfloat16)
+    parts = pl.pallas_call(
+        project_kernel,
+        out_shape=[pair] * 8,
+        in_specs=[pl.BlockSpec(memory_space=pltpu.SMEM), vmem, vmem],
+        out_specs=[vmem] * 8,
         compiler_params=pltpu.CompilerParams(vmem_limit_bytes=16 * 2**20),
-    )(me.reshape(1), ids, counts, slices, tiles, weight)
-    return agg, (parts[:4], parts[4:])
+    )(me.reshape(1), agg, weight)
+    return parts[:4], parts[4:]
 
 
 def add(a, b):
@@ -161,31 +182,30 @@
     return held[0] + held[1]
 
 
-def fold_kernel(me_ref, agg_ref, other_ref, *refs):
-    *grad_refs, out_ref = refs
-    for chain in range(2):
-        cols = grad_refs[0].shape[2]
+def fold_kernel(me_ref, agg_ref, *refs):
+    grad_refs, out_refs = refs[:8], refs[8:]
+    for chain in range(2):
         total = None
         for k in range(4):
-            for member in range(2):
-                block = pair_block(me_ref[0], chain, k, member)
-                rows = jnp.concatenate([agg_ref[block], other_ref[block]], axis=0)
-                term = lax.dot_general(
-                    rows, grad_refs[4 * chain + k][member], (((0,), (0,)), ((), ())), preferred_element_type=jnp.float32
-                )
-                total = term if total is None else total + term
-        out_ref[:, chain * cols:(chain + 1) * cols] = total.astype(out_ref.dtype)
-
-
-def fold(me, agg, other_agg, grads):
+            grads = grad_refs[4 * chain + k][...]
+            rows = jnp.concatenate([agg_ref[pair_block(me_ref[0], chain, k, member)] for member in range(2)], axis=0)
+            term = lax.dot_general(
+                rows, grads.reshape(rows.shape[0], -1), (((0,), (0,)), ((), ())), preferred_element_type=jnp.float32
+            )
+            total = term if total is None else total + term
+        out_refs[chain][...] = total.astype(out_refs[chain].dtype)
+
+
+def fold(me, agg, grads):
     vmem = pl.BlockSpec(memory_space=pltpu.VMEM)
+    out = jax.ShapeDtypeStruct((agg.shape[2], grads[0].shape[2]), jnp.bfloat16)
     return pl.pallas_call(
         fold_kernel,
-        out_shape=jax.ShapeDtypeStruct((agg.shape[2], 2 * grads[0].shape[2]), jnp.bfloat16),
-        in_specs=[pl.BlockSpec(memory_space=pltpu.SMEM)] + [vmem] * (2 + len(grads)),
-        out_specs=vmem,
-        compiler_params=pltpu.CompilerParams(vmem_limit_bytes=12 * 2**20),
-    )(me.reshape(1), agg, other_agg, *grads)
+        out_shape=[out, out],
+        in_specs=[pl.BlockSpec(memory_space=pltpu.SMEM)] + [vmem] * (1 + len(grads)),
+        out_specs=[vmem, vmem],
+        compiler_params=pltpu.CompilerParams(vmem_limit_bytes=16 * 2**20),
+    )(me.reshape(1), agg, *grads)
 
 
 def shards(feature_table, sample_ids, block_ids, block_counts, block_tiles, weight, target):
@@ -195,8 +215,8 @@
     with jax.named_scope("pick"):
         slices = lax.all_to_all(pick(feature_table, sample_ids, block_total), "feat", 0, 0)
     with jax.named_scope("aggregate"):
-        agg, parts = aggregate_and_project(me, block_ids, block_counts, slices, block_tiles, weight)
-        other_agg = lax.ppermute(agg, "core", SWAP)
+        agg = mean_of_blocks(block_ids, block_counts, slices, block_tiles)
+        parts = project(me, agg, weight)
     with jax.named_scope("preact"):
         preact = chain_sum(parts)
     with jax.named_scope("grad"):
@@ -210,14 +230,13 @@
         grad_hidden = scales * cotangent - scales**3 / hidden_width * hidden * projected
         slope = sigmoid_part * (1.0 + preact * (1.0 - sigmoid_part))
         grad_pre = (grad_hidden * slope).astype(jnp.bfloat16)
-    with jax.named_scope("swap"):
+    with jax.named_scope("fold"):
         half = hidden_width // 2
+        left, right = fold(me, agg, chain_gather([grad_pre[:, :half], grad_pre[:, half:]]))
+    with jax.named_scope("sum_core"):
         first = lax.axis_index("core") == 0
-        left, right = grad_pre[:, :half], grad_pre[:, half:]
-        mine, other = jnp.where(first, left, right), lax.ppermute(jnp.where(first, right, left), "core", SWAP)
-        paired = jnp.concatenate([mine, other], axis=0)
-    with jax.named_scope("fold"):
-        folded = fold(me, agg, other_agg, chain_gather([paired[:, :half // 2], paired[:, half // 2:]]))
+        other = lax.ppermute(jnp.where(first, right, left), "core", SWAP)
+        folded = add(jnp.where(first, left, right), other).astype(jnp.bfloat16)
     weight_grad = group_sum(folded)
     return (embedding, weight_grad)
 

time: 205 us -> 208 us (1.015)
  waiting for transfers between devices: 60.1 us -> 67.1 us
  blocking collectives: 58.9 us -> 56.3 us
    ppermute x16, waiting for transfers between devices: 32.8 us -> 39.3 us  [with_neighbour(): return lax.ppermute(block, 'feat', neighbours(chain, odd_step))]
    all_to_all x1, blocking collectives: 24.3 us -> 21.9 us  [exchange_sum(): got = lax.all_to_all(parts, axis, 0, 0)]
    ppermute x2 -> x1, starting transfers between devices: 12.6 us -> 14 us  [shards(): other = lax.ppermute(jnp.where(first, right, left), 'core', SWAP)]
    pallas_call x3 -> x4, Pallas kernels: 8.28 us -> 7.83 us  [the longest x1 3.69 us: pick(): pl.pallas_call(pick_kernel, out_shape=out, in_specs=[hbm, hbm], out_specs...]
  transfers between devices with their start and end apart: 20 -> 19, of which waited for: 15 -> 15; matrix products, arithmetic and copies ran while one was open for 0% -> 0% of each run, Pallas kernels for 0% -> 0%
where the time goes in v7:
time: 208 us; the launch traced here: 207 us
  starting transfers between devices  69.9 us (34%)
  waiting for transfers between devices  67.1 us (32%)
  blocking collectives  56.3 us (27%)
  Pallas kernels  7.83 us (4%)
  other arithmetic  3.67 us (2%)
    ppermute x16, waiting for transfers between devices, with_neighbour(): return lax.ppermute(block, 'feat', neighbours(chain, odd_step))  39.3 us
    ppermute x16, starting transfers between devices, with_neighbour(): return lax.ppermute(block, 'feat', neighbours(chain, odd_step))  38 us
    all_to_all x1, waiting for transfers between devices, shards(): lax.all_to_all(pick(feature_table, sample_ids, block_total), 'feat', 0, 0)  24.8 us
    all_gather x1, blocking collectives, group_sum(): lax.all_gather(part.astype(jnp.bfloat16), ('zo', 'zi'), axis=0, tiled=True)  23.2 us
    all_to_all x1, blocking collectives, exchange_sum(): got = lax.all_to_all(parts, axis, 0, 0)  21.9 us
    ppermute x1, starting transfers between devices, shards(): other = lax.ppermute(jnp.where(first, right, left), 'core', SWAP)  14 us
    all_gather x1, blocking collectives, group_sum(): part = lax.all_gather(part, 'x', axis=0, tiled=True)  11.1 us
    ppermute x1, starting transfers between devices, group_sum(): other = lax.ppermute(part, 'core', SWAP)  10.1 us
  transfers between devices with their start and end apart: 19, of which 15 were waited for; matrix products, arithmetic and copies ran while one was open for 0% of the time, Pallas kernels for 0%

profile of v7, /device:TPU:1, one launch (start us, length us, event | category | flops | bytes accessed | tf_op | source)
XLA Modules:
  0.0 207.2 jit_solution(11757572067495358545)
XLA Ops:
  0.7 3.7 %pick.1 = bf16[8,128,512]{2,1,0:T(8,128)(2,1)} custom-call(s32[1,128]{1,0:T(1,128)} %bitcast.22, bf16[256,4096]{1,0:T(8,128)(2,1)} %table_ref.1), custom_call_target="tpu_custom_call" | custom-call | tf_op jit(solution)/shard_map/pick/pallas_call | solution.py:75
  4.3 7.7 %all-to-all-start = ((bf16[8,128,512]{2,1,0:T(8,128)(2,1)}), bf16[8,128,512]{2,1,0:T(8,128)(2,1)S(1)}, u32[]{:S(2)}, u32[]{:S(2)}) async-start(bf16[8,128,512]{2,1,0:T(8,128)(2,1)} %pick.1), calls=%async_computation | async-start | bytes 2097152 | tf_op jit(solution)/shard_map/pick/all_to_all | solution.py:216
  12.1 24.8 %all-to-all-done.slices_ref = bf16[8,128,512]{2,1,0:T(8,128)(2,1)S(1)} async-done(((bf16[8,128,512]{2,1,0:T(8,128)(2,1)}), bf16[8,128,512]{2,1,0:T(8,128)(2,1)S(1)}, u32[]{:S(2)}, u32[]{:S(2)}) %all-to-all-start) | async-done | bytes 1048608 | tf_op jit(solution)/shard_map/pick/all_to_all | solution.py:216
  41.0 1.9 collective-permute-start
  42.9 1.9 collective-permute-start.4
  44.9 4.5 %collective-permute-done = bf16[2,128,512]{2,1,0:T(8,128)(2,1)S(1)} collective-permute-done((bf16[2,128,512]{2,1,0:T(8,128)(2,1)S(1)}, bf16[2,128,512]{2,1,0:T(8,128)(2,1)S(1)}, u32[]{:S(2)}, u32[]{:S(2)}) %collective-permute-start) | collective-permute-done | bytes 262176 | tf_op jit(solution)/shard_map/preact/ppermute | solution.py:21
  49.4 1.9 collective-permute-start.1
  51.4 3.6 %collective-permute-start.5 = (bf16[2,128,512]{2,1,0:T(8,128)(2,1)S(1)}, bf16[2,128,512]{2,1,0:T(8,128)(2,1)S(1)}, u32[]{:S(2)}, u32[]{:S(2)}) collective-permute-start(bf16[2,128,512]{2,1,0:T(8,128)(2,1)S(1)} %add_convert_fusion.2), channel_id=1, source_target_pairs={{1,2},{3,4},{5,6},{7,0},{2,1},{4,3},{6,5},{0,7},{9,10},{11,12},{13... | collective-permute-start | bytes 786440 | tf_op jit(solution)/shard_map/preact/ppermute | solution.py:21
  55.0 3.2 %collective-permute-done.1 = bf16[2,128,512]{2,1,0:T(8,128)(2,1)S(1)} collective-permute-done((bf16[2,128,512]{2,1,0:T(8,128)(2,1)S(1)}, bf16[2,128,512]{2,1,0:T(8,128)(2,1)S(1)}, u32[]{:S(2)}, u32[]{:S(2)}) %collective-permute-start.1) | collective-permute-done | bytes 262176 | tf_op jit(solution)/shard_map/preact/ppermute | solution.py:21
  58.2 1.9 collective-permute-start.2
  60.3 2.2 %collective-permute-start.6 = (bf16[2,128,512]{2,1,0:T(8,128)(2,1)S(1)}, bf16[2,128,512]{2,1,0:T(8,128)(2,1)S(1)}, u32[]{:S(2)}, u32[]{:S(2)}) collective-permute-start(bf16[2,128,512]{2,1,0:T(8,128)(2,1)S(1)} %add_convert_fusion.1), channel_id=1, source_target_pairs={{0,1},{2,3},{4,5},{6,7},{1,0},{3,2},{5,4},{7,6},{8,9},{10,11},{12,... | collective-permute-start | bytes 786440 | tf_op jit(solution)/shard_map/preact/ppermute | solution.py:21
  62.5 7.1 %collective-permute-done.2 = bf16[2,128,512]{2,1,0:T(8,128)(2,1)S(1)} collective-permute-done((bf16[2,128,512]{2,1,0:T(8,128)(2,1)S(1)}, bf16[2,128,512]{2,1,0:T(8,128)(2,1)S(1)}, u32[]{:S(2)}, u32[]{:S(2)}) %collective-permute-start.2) | collective-permute-done | bytes 262176 | tf_op jit(solution)/shard_map/preact/ppermute | solution.py:21
  69.7 1.9 collective-permute-start.3
  71.7 1.9 collective-permute-start.7
  73.6 2.6 %collective-permute-done.3 = bf16[128,512]{1,0:T(8,128)(2,1)S(1)} collective-permute-done((bf16[128,512]{1,0:T(8,128)(2,1)S(1)}, bf16[128,512]{1,0:T(8,128)(2,1)S(1)}, u32[]{:S(2)}, u32[]{:S(2)}) %collective-permute-start.3) | collective-permute-done | bytes 131104 | tf_op jit(solution)/shard_map/preact/ppermute | solution.py:21
  76.3 2.3 %collective-permute-done.7 = bf16[128,512]{1,0:T(8,128)(2,1)S(1)} collective-permute-done((bf16[128,512]{1,0:T(8,128)(2,1)S(1)}, bf16[128,512]{1,0:T(8,128)(2,1)S(1)}, u32[]{:S(2)}, u32[]{:S(2)}) %collective-permute-start.7) | collective-permute-done | bytes 131104 | tf_op jit(solution)/shard_map/preact/ppermute | solution.py:21
  79.7 1.9 collective-permute-start.12
  81.6 2.4 %collective-permute-start.8 = (bf16[128,512]{1,0:T(8,128)(2,1)S(1)}, bf16[128,512]{1,0:T(8,128)(2,1)S(1)}, u32[]{:S(2)}, u32[]{:S(2)}) collective-permute-start(bf16[128,512]{1,0:T(8,128)(2,1)S(1)} %get-tuple-element.35), channel_id=1, source_target_pairs={{0,1},{2,3},{4,5},{6,7},{1,0},{3,2},{5,4},{7,6},{8,9},{10,11},{12,... | collective-permute-start | bytes 393224 | tf_op jit(solution)/shard_map/fold/ppermute | solution.py:21
  84.1 3.7 %collective-permute-done.12 = bf16[128,512]{1,0:T(8,128)(2,1)S(1)} collective-permute-done((bf16[128,512]{1,0:T(8,128)(2,1)S(1)}, bf16[128,512]{1,0:T(8,128)(2,1)S(1)}, u32[]{:S(2)}, u32[]{:S(2)}) %collective-permute-start.12) | collective-permute-done | bytes 131104 | tf_op jit(solution)/shard_map/fold/ppermute | solution.py:21
  87.8 4.1 %collective-permute-start.9 = (bf16[2,128,512]{2,1,0:T(8,128)(2,1)S(1)}, bf16[2,128,512]{2,1,0:T(8,128)(2,1)S(1)}, u32[]{:S(2)}, u32[]{:S(2)}) collective-permute-start(bf16[2,128,512]{2,1,0:T(8,128)(2,1)S(1)} %pad_maximum_fusion.1.refs_0_), channel_id=1, source_target_pairs={{1,2},{3,4},{5,6},{7,0},{2,1},{4,3},{6,5},{0,7},{9,10},{11,12},{13... | collective-permute-start | bytes 786440 | tf_op jit(solution)/shard_map/fold/ppermute | solution.py:21
  92.0 1.9 collective-permute-start.13
  93.9 3.4 %collective-permute-done.9.refs_1_ = bf16[2,128,512]{2,1,0:T(8,128)(2,1)S(1)} collective-permute-done((bf16[2,128,512]{2,1,0:T(8,128)(2,1)S(1)}, bf16[2,128,512]{2,1,0:T(8,128)(2,1)S(1)}, u32[]{:S(2)}, u32[]{:S(2)}) %collective-permute-start.9) | collective-permute-done | bytes 262176 | tf_op jit(solution)/shard_map/fold/ppermute | solution.py:21
  97.4 1.9 collective-permute-start.10
  100.1 2.9 %collective-permute-start.14 = (bf16[2,128,512]{2,1,0:T(8,128)(2,1)S(1)}, bf16[2,128,512]{2,1,0:T(8,128)(2,1)S(1)}, u32[]{:S(2)}, u32[]{:S(2)}) collective-permute-start(bf16[2,128,512]{2,1,0:T(8,128)(2,1)S(1)} %collective-permute-done.13.refs_5_), channel_id=1, source_target_pairs={{1,2},{3,4},{5,6},{7,0},{2,1},{4,3},{6,5},{0,7},{9,10},{11,12},{13... | collective-permute-start | bytes 786440 | tf_op jit(solution)/shard_map/fold/ppermute | solution.py:21
  104.5 3.7 %collective-permute-start.11 = (bf16[2,128,512]{2,1,0:T(8,128)(2,1)S(1)}, bf16[2,128,512]{2,1,0:T(8,128)(2,1)S(1)}, u32[]{:S(2)}, u32[]{:S(2)}) collective-permute-start(bf16[2,128,512]{2,1,0:T(8,128)(2,1)S(1)} %collective-permute-done.10.refs_2_), channel_id=1, source_target_pairs={{1,2},{3,4},{5,6},{7,0},{2,1},{4,3},{6,5},{0,7},{9,10},{11,12},{13... | collective-permute-start | bytes 786440 | tf_op jit(solution)/shard_map/fold/ppermute | solution.py:21
  108.2 2.6 %collective-permute-done.14.refs_6_ = bf16[2,128,512]{2,1,0:T(8,128)(2,1)S(1)} collective-permute-done((bf16[2,128,512]{2,1,0:T(8,128)(2,1)S(1)}, bf16[2,128,512]{2,1,0:T(8,128)(2,1)S(1)}, u32[]{:S(2)}, u32[]{:S(2)}) %collective-permute-start.14) | collective-permute-done | bytes 262176 | tf_op jit(solution)/shard_map/fold/ppermute | solution.py:21
  113.6 6.7 %collective-permute-done.15.refs_7_ = bf16[2,128,512]{2,1,0:T(8,128)(2,1)S(1)} collective-permute-done((bf16[2,128,512]{2,1,0:T(8,128)(2,1)S(1)}, bf16[2,128,512]{2,1,0:T(8,128)(2,1)S(1)}, u32[]{:S(2)}, u32[]{:S(2)}) %collective-permute-start.15) | collective-permute-done | bytes 262176 | tf_op jit(solution)/shard_map/fold/ppermute | solution.py:21
  121.7 14.0 %collective-permute-start.16 = (bf16[512,512]{1,0:T(8,128)(2,1)S(1)}, bf16[512,512]{1,0:T(8,128)(2,1)S(1)}, u32[]{:S(2)}, u32[]{:S(2)}) collective-permute-start(bf16[512,512]{1,0:T(8,128)(2,1)S(1)} %broadcast_select_fusion.2), channel_id=1, source_target_pairs={{0,8},{8,0},{1,9},{9,1},{2,10},{10,2},{3,11},{11,3},{4,12},{12,4},... | collective-permute-start | bytes 1572872 | tf_op jit(solution)/shard_map/sum_core/ppermute | solution.py:238
  137.4 21.9 %all_to_all.10 = bf16[16,32,512]{2,1,0:T(8,128)(2,1)S(1)} all-to-all(bf16[16,32,512]{2,1,0:T(8,128)(2,1)S(1)} %bitcast.20), channel_id=1, replica_groups=mesh['x'=4,'zo'=3,'zi'=4,'core'=2,'feat'=8] {'x','zi'}, dimensions={0} | all-to-all | bytes 1048576 | tf_op jit(solution)/shard_map/sum_x_zi/all_to_all | solution.py:29
  159.5 23.2 %all_gather.6 = bf16[384,512]{1,0:T(8,128)(2,1)S(1)} all-gather(bf16[32,512]{1,0:T(8,128)(2,1)S(1)} %reduce_sum.44), channel_id=1, replica_groups=mesh['x'=4,'zo'=3,'zi'=4,'core'=2,'feat'=8] {'zo','zi'}, dimensions={0}, use_global_device_ids=true | all-gather | bytes 425984 | tf_op jit(solution)/shard_map/sum_z/all_gather | solution.py:38
  182.7 11.1 %all_gather.7 = bf16[512,512]{1,0:T(8,128)(2,1)S(1)} all-gather(bf16[128,512]{1,0:T(8,128)(2,1)S(1)} %reduce_sum.45), channel_id=1, replica_groups=mesh['x'=4,'zo'=3,'zi'=4,'core'=2,'feat'=8] {'x'}, dimensions={0}, use_global_device_ids=true | all-gather | bytes 655360 | tf_op jit(solution)/shard_map/gather_x/all_gather | solution.py:42
  193.9 10.1 %collective-permute-start.17 = (bf16[512,512]{1,0:T(8,128)(2,1)S(1)}, bf16[512,512]{1,0:T(8,128)(2,1)S(1)}, u32[]{:S(2)}, u32[]{:S(2)}) collective-permute-start(bf16[512,512]{1,0:T(8,128)(2,1)S(1)} %all_gather.7), channel_id=1, source_target_pairs={{0,8},{8,0},{1,9},{9,1},{2,10},{10,2},{3,11},{11,3},{4,12},{12,4},... | collective-permute-start | bytes 1572872 | tf_op jit(solution)/shard_map/gather_core/ppermute | solution.py:44
  (49 shorter events, 17.3 us)
Async XLA Ops:
  0.6 11.4 %copy-start.5 = (s32[8,4]{0,1:T(4,128)S(1)}, s32[8,4]{0,1:T(4,128)}, u32[]{:S(2)}) copy-start(s32[8,4]{0,1:T(4,128)} %param.9) | copy-start | bytes 388
  0.6 36.3 %copy-start.2 = (s32[8]{0:T(128)S(1)}, s32[8]{0:T(128)}, u32[]{:S(2)}) copy-start(s32[8]{0:T(128)} %counts_ref.1) | copy-start | bytes 100
  4.3 32.6 %all-to-all-start = ((bf16[8,128,512]{2,1,0:T(8,128)(2,1)}), bf16[8,128,512]{2,1,0:T(8,128)(2,1)S(1)}, u32[]{:S(2)}, u32[]{:S(2)}) async-start(bf16[8,128,512]{2,1,0:T(8,128)(2,1)} %pick.1), calls=%async_computation | async-start | bytes 2097152 | tf_op jit(solution)/shard_map/pick/all_to_all | solution.py:216
  12.0 27.7 %copy-start = (bf16[512,1024]{1,0:T(8,128)(2,1)S(1)}, bf16[512,1024]{1,0:T(8,128)(2,1)}, u32[]{:S(2)}) copy-start(bf16[512,1024]{1,0:T(8,128)(2,1)} %weight_ref.1) | copy-start | bytes 3145732
  36.9 1.2 copy-start.1
  41.0 8.3 %collective-permute-start = (bf16[2,128,512]{2,1,0:T(8,128)(2,1)S(1)}, bf16[2,128,512]{2,1,0:T(8,128)(2,1)S(1)}, u32[]{:S(2)}, u32[]{:S(2)}) collective-permute-start(bf16[2,128,512]{2,1,0:T(8,128)(2,1)S(1)} %get-tuple-element.12), channel_id=1, source_target_pairs={{1,2},{3,4},{5,6},{7,0},{2,1},{4,3},{6,5},{0,7},{9,10},{11,12},{13... | collective-permute-start | bytes 786440 | tf_op jit(solution)/shard_map/preact/ppermute | solution.py:21
  42.9 8.4 %collective-permute-start.4 = (bf16[2,128,512]{2,1,0:T(8,128)(2,1)S(1)}, bf16[2,128,512]{2,1,0:T(8,128)(2,1)S(1)}, u32[]{:S(2)}, u32[]{:S(2)}) collective-permute-start(bf16[2,128,512]{2,1,0:T(8,128)(2,1)S(1)} %get-tuple-element.16), channel_id=1, source_target_pairs={{0,1},{2,3},{4,5},{6,7},{1,0},{3,2},{5,4},{7,6},{8,9},{10,11},{12,... | collective-permute-start | bytes 786440 | tf_op jit(solution)/shard_map/preact/ppermute | solution.py:21
  49.4 8.8 %collective-permute-start.1 = (bf16[2,128,512]{2,1,0:T(8,128)(2,1)S(1)}, bf16[2,128,512]{2,1,0:T(8,128)(2,1)S(1)}, u32[]{:S(2)}, u32[]{:S(2)}) collective-permute-start(bf16[2,128,512]{2,1,0:T(8,128)(2,1)S(1)} %add_convert_fusion.4), channel_id=1, source_target_pairs={{0,1},{2,3},{4,5},{6,7},{1,0},{3,2},{5,4},{7,6},{8,9},{10,11},{12,... | collective-permute-start | bytes 786440 | tf_op jit(solution)/shard_map/preact/ppermute | solution.py:21
  51.4 8.8 %collective-permute-start.5 = (bf16[2,128,512]{2,1,0:T(8,128)(2,1)S(1)}, bf16[2,128,512]{2,1,0:T(8,128)(2,1)S(1)}, u32[]{:S(2)}, u32[]{:S(2)}) collective-permute-start(bf16[2,128,512]{2,1,0:T(8,128)(2,1)S(1)} %add_convert_fusion.2), channel_id=1, source_target_pairs={{1,2},{3,4},{5,6},{7,0},{2,1},{4,3},{6,5},{0,7},{9,10},{11,12},{13... | collective-permute-start | bytes 786440 | tf_op jit(solution)/shard_map/preact/ppermute | solution.py:21
  58.2 11.4 %collective-permute-start.2 = (bf16[2,128,512]{2,1,0:T(8,128)(2,1)S(1)}, bf16[2,128,512]{2,1,0:T(8,128)(2,1)S(1)}, u32[]{:S(2)}, u32[]{:S(2)}) collective-permute-start(bf16[2,128,512]{2,1,0:T(8,128)(2,1)S(1)} %add_convert_fusion.3), channel_id=1, source_target_pairs={{1,2},{3,4},{5,6},{7,0},{2,1},{4,3},{6,5},{0,7},{9,10},{11,12},{13... | collective-permute-start | bytes 786440 | tf_op jit(solution)/shard_map/preact/ppermute | solution.py:21
  60.2 18.8 %copy-start.3 = (bf16[128,1024]{1,0:T(8,128)(2,1)S(1)}, bf16[128,1024]{1,0:T(8,128)(2,1)}, u32[]{:S(2)}) copy-start(bf16[128,1024]{1,0:T(8,128)(2,1)} %param.13) | copy-start | bytes 786436
  60.3 11.3 %collective-permute-start.6 = (bf16[2,128,512]{2,1,0:T(8,128)(2,1)S(1)}, bf16[2,128,512]{2,1,0:T(8,128)(2,1)S(1)}, u32[]{:S(2)}, u32[]{:S(2)}) collective-permute-start(bf16[2,128,512]{2,1,0:T(8,128)(2,1)S(1)} %add_convert_fusion.1), channel_id=1, source_target_pairs={{0,1},{2,3},{4,5},{6,7},{1,0},{3,2},{5,4},{7,6},{8,9},{10,11},{12,... | collective-permute-start | bytes 786440 | tf_op jit(solution)/shard_map/preact/ppermute | solution.py:21
  69.7 6.6 %collective-permute-start.3 = (bf16[128,512]{1,0:T(8,128)(2,1)S(1)}, bf16[128,512]{1,0:T(8,128)(2,1)S(1)}, u32[]{:S(2)}, u32[]{:S(2)}) collective-permute-start(bf16[128,512]{1,0:T(8,128)(2,1)S(1)} %fusion.1), channel_id=1, source_target_pairs={{0,1},{2,3},{4,5},{6,7},{1,0},{3,2},{5,4},{7,6},{8,9},{10,11},{12,... | collective-permute-start | bytes 393224 | tf_op jit(solution)/shard_map/preact/ppermute | solution.py:21
  71.7 6.9 %collective-permute-start.7 = (bf16[128,512]{1,0:T(8,128)(2,1)S(1)}, bf16[128,512]{1,0:T(8,128)(2,1)S(1)}, u32[]{:S(2)}, u32[]{:S(2)}) collective-permute-start(bf16[128,512]{1,0:T(8,128)(2,1)S(1)} %fusion.2), channel_id=1, source_target_pairs={{1,2},{3,4},{5,6},{7,0},{2,1},{4,3},{6,5},{0,7},{9,10},{11,12},{13... | collective-permute-start | bytes 393224 | tf_op jit(solution)/shard_map/preact/ppermute | solution.py:21
  79.3 42.3 %copy-start.4 = (bf16[128,1024]{1,0:T(8,128)(2,1)}, bf16[128,1024]{1,0:T(8,128)(2,1)S(1)}, u32[]{:S(2)}) copy-start(bf16[128,1024]{1,0:T(8,128)(2,1)S(1)} %get-tuple-element.25) | copy-start | bytes 786436
  79.7 8.1 %collective-permute-start.12 = (bf16[128,512]{1,0:T(8,128)(2,1)S(1)}, bf16[128,512]{1,0:T(8,128)(2,1)S(1)}, u32[]{:S(2)}, u32[]{:S(2)}) collective-permute-start(bf16[128,512]{1,0:T(8,128)(2,1)S(1)} %get-tuple-element.34), channel_id=1, source_target_pairs={{1,2},{3,4},{5,6},{7,0},{2,1},{4,3},{6,5},{0,7},{9,10},{11,12},{13... | collective-permute-start | bytes 393224 | tf_op jit(solution)/shard_map/fold/ppermute | solution.py:21
  81.6 6.2 %collective-permute-start.8 = (bf16[128,512]{1,0:T(8,128)(2,1)S(1)}, bf16[128,512]{1,0:T(8,128)(2,1)S(1)}, u32[]{:S(2)}, u32[]{:S(2)}) collective-permute-start(bf16[128,512]{1,0:T(8,128)(2,1)S(1)} %get-tuple-element.35), channel_id=1, source_target_pairs={{0,1},{2,3},{4,5},{6,7},{1,0},{3,2},{5,4},{7,6},{8,9},{10,11},{12,... | collective-permute-start | bytes 393224 | tf_op jit(solution)/shard_map/fold/ppermute | solution.py:21
  87.8 9.5 %collective-permute-start.9 = (bf16[2,128,512]{2,1,0:T(8,128)(2,1)S(1)}, bf16[2,128,512]{2,1,0:T(8,128)(2,1)S(1)}, u32[]{:S(2)}, u32[]{:S(2)}) collective-permute-start(bf16[2,128,512]{2,1,0:T(8,128)(2,1)S(1)} %pad_maximum_fusion.1.refs_0_), channel_id=1, source_target_pairs={{1,2},{3,4},{5,6},{7,0},{2,1},{4,3},{6,5},{0,7},{9,10},{11,12},{13... | collective-permute-start | bytes 786440 | tf_op jit(solution)/shard_map/fold/ppermute | solution.py:21
  92.0 8.1 %collective-permute-start.13 = (bf16[2,128,512]{2,1,0:T(8,128)(2,1)S(1)}, bf16[2,128,512]{2,1,0:T(8,128)(2,1)S(1)}, u32[]{:S(2)}, u32[]{:S(2)}) collective-permute-start(bf16[2,128,512]{2,1,0:T(8,128)(2,1)S(1)} %pad_maximum_fusion.2.refs_4_), channel_id=1, source_target_pairs={{0,1},{2,3},{4,5},{6,7},{1,0},{3,2},{5,4},{7,6},{8,9},{10,11},{12,... | collective-permute-start | bytes 786440 | tf_op jit(solution)/shard_map/fold/ppermute | solution.py:21
  97.4 7.1 %collective-permute-start.10 = (bf16[2,128,512]{2,1,0:T(8,128)(2,1)S(1)}, bf16[2,128,512]{2,1,0:T(8,128)(2,1)S(1)}, u32[]{:S(2)}, u32[]{:S(2)}) collective-permute-start(bf16[2,128,512]{2,1,0:T(8,128)(2,1)S(1)} %collective-permute-done.9.refs_1_), channel_id=1, source_target_pairs={{0,1},{2,3},{4,5},{6,7},{1,0},{3,2},{5,4},{7,6},{8,9},{10,11},{12,... | collective-permute-start | bytes 786440 | tf_op jit(solution)/shard_map/fold/ppermute | solution.py:21
  100.1 10.6 %collective-permute-start.14 = (bf16[2,128,512]{2,1,0:T(8,128)(2,1)S(1)}, bf16[2,128,512]{2,1,0:T(8,128)(2,1)S(1)}, u32[]{:S(2)}, u32[]{:S(2)}) collective-permute-start(bf16[2,128,512]{2,1,0:T(8,128)(2,1)S(1)} %collective-permute-done.13.refs_5_), channel_id=1, source_target_pairs={{1,2},{3,4},{5,6},{7,0},{2,1},{4,3},{6,5},{0,7},{9,10},{11,12},{13... | collective-permute-start | bytes 786440 | tf_op jit(solution)/shard_map/fold/ppermute | solution.py:21
  104.5 9.1 %collective-permute-start.11 = (bf16[2,128,512]{2,1,0:T(8,128)(2,1)S(1)}, bf16[2,128,512]{2,1,0:T(8,128)(2,1)S(1)}, u32[]{:S(2)}, u32[]{:S(2)}) collective-permute-start(bf16[2,128,512]{2,1,0:T(8,128)(2,1)S(1)} %collective-permute-done.10.refs_2_), channel_id=1, source_target_pairs={{1,2},{3,4},{5,6},{7,0},{2,1},{4,3},{6,5},{0,7},{9,10},{11,12},{13... | collective-permute-start | bytes 786440 | tf_op jit(solution)/shard_map/fold/ppermute | solution.py:21
  110.8 9.5 %collective-permute-start.15 = (bf16[2,128,512]{2,1,0:T(8,128)(2,1)S(1)}, bf16[2,128,512]{2,1,0:T(8,128)(2,1)S(1)}, u32[]{:S(2)}, u32[]{:S(2)}) collective-permute-start(bf16[2,128,512]{2,1,0:T(8,128)(2,1)S(1)} %collective-permute-done.14.refs_6_), channel_id=1, source_target_pairs={{0,1},{2,3},{4,5},{6,7},{1,0},{3,2},{5,4},{7,6},{8,9},{10,11},{12,... | collective-permute-start | bytes 786440 | tf_op jit(solution)/shard_map/fold/ppermute | solution.py:21
  121.7 15.6 %collective-permute-start.16 = (bf16[512,512]{1,0:T(8,128)(2,1)S(1)}, bf16[512,512]{1,0:T(8,128)(2,1)S(1)}, u32[]{:S(2)}, u32[]{:S(2)}) collective-permute-start(bf16[512,512]{1,0:T(8,128)(2,1)S(1)} %broadcast_select_fusion.2), channel_id=1, source_target_pairs={{0,8},{8,0},{1,9},{9,1},{2,10},{10,2},{3,11},{11,3},{4,12},{12,4},... | collective-permute-start | bytes 1572872 | tf_op jit(solution)/shard_map/sum_core/ppermute | solution.py:238
  193.9 11.6 %collective-permute-start.17 = (bf16[512,512]{1,0:T(8,128)(2,1)S(1)}, bf16[512,512]{1,0:T(8,128)(2,1)S(1)}, u32[]{:S(2)}, u32[]{:S(2)}) collective-permute-start(bf16[512,512]{1,0:T(8,128)(2,1)S(1)} %all_gather.7), channel_id=1, source_target_pairs={{0,8},{8,0},{1,9},{9,1},{2,10},{10,2},{3,11},{11,3},{4,12},{12,4},... | collective-permute-start | bytes 1572872 | tf_op jit(solution)/shard_map/gather_core/ppermute | solution.py:44

commit v8 on v5

--- a/solution.py
+++ b/solution.py
@@ -1,3 +1,5 @@
+import functools
+
 import jax
 import jax.numpy as jnp
 from jax import lax
@@ -62,7 +64,7 @@
         out_shape=jax.ShapeDtypeStruct((slices, ids.shape[0], table.shape[1] // slices), table.dtype),
         in_specs=[vmem, vmem],
         out_specs=vmem,
-        compiler_params=pltpu.CompilerParams(vmem_limit_bytes=32 * 2**20),
+        compiler_params=pltpu.CompilerParams(vmem_limit_bytes=16 * 2**20),
     )(ids.reshape(1, -1), table)
 
 
@@ -86,30 +88,47 @@
         summed = jnp.dot(lhs, rhs, preferred_element_type=jnp.float32)
         degree = jnp.dot(lhs, ones, preferred_element_type=jnp.float32)
         agg_ref[own] = (summed / jnp.concatenate([degree] * (width // 128), axis=1)).astype(jnp.bfloat16)
-    for chain in range(2):
-        refs = part_refs[4 * chain:4 * chain + 4]
+    project_kernel((3,), me_ref, agg_ref, weight_ref, *part_refs)
+
+
+def aggregate(me, ids, counts, slices, tiles, weight):
+    vmem, smem = pl.BlockSpec(memory_space=pltpu.VMEM), pl.BlockSpec(memory_space=pltpu.SMEM)
+    pair = jax.ShapeDtypeStruct((2, slices.shape[1], weight.shape[1] // 2), jnp.bfloat16)
+    return pl.pallas_call(
+        aggregate_kernel,
+        out_shape=[jax.ShapeDtypeStruct(slices.shape, jnp.bfloat16), pair, pair],
+        in_specs=[smem] * 3 + [vmem] * 3,
+        out_specs=[vmem] * 3,
+        compiler_params=pltpu.CompilerParams(vmem_limit_bytes=16 * 2**20),
+    )(me.reshape(1), ids, counts, slices, tiles, weight)
+
+
+def project_kernel(wanted, me_ref, agg_ref, weight_ref, *part_refs):
+    rows = agg_ref.shape[1]
+    count = len(wanted)
+    for chain in range(2):
+        refs = part_refs[count * chain:count * (chain + 1)]
         cols = refs[0].shape[2]
-        order = [(k, member) for k in (3, 2, 1, 0) for member in range(2)]
-        lhs = jnp.concatenate([agg_ref[pair_block(me_ref[0], chain, k, member)] for k, member in order], axis=0)
+        blocks = [pair_block(me_ref[0], chain, k, member) for k in wanted for member in range(2)]
+        lhs = jnp.concatenate([agg_ref[block] for block in blocks], axis=0)
         parts = jnp.dot(lhs, weight_ref[:, chain * cols:(chain + 1) * cols], preferred_element_type=jnp.float32)
         parts = parts.astype(jnp.bfloat16)
-        rows = parts.shape[0] // blocks
-        for i, (k, member) in enumerate(order):
-            refs[k][member] = parts[i * rows:(i + 1) * rows]
-
-
-def aggregate_and_project(me, ids, counts, slices, tiles, weight):
-    block_rows = slices.shape[1]
-    vmem, smem = pl.BlockSpec(memory_space=pltpu.VMEM), pl.BlockSpec(memory_space=pltpu.SMEM)
-    pair = jax.ShapeDtypeStruct((2, block_rows, weight.shape[1] // 2), jnp.bfloat16)
-    agg, *parts = pl.pallas_call(
-        aggregate_kernel,
-        out_shape=[jax.ShapeDtypeStruct(slices.shape, jnp.bfloat16)] + [pair] * 8,
-        in_specs=[smem] * 3 + [vmem] * 3,
-        out_specs=[vmem] * 9,
-        compiler_params=pltpu.CompilerParams(vmem_limit_bytes=32 * 2**20),
-    )(me.reshape(1), ids, counts, slices, tiles, weight)
-    return agg, (parts[:4], parts[4:])
+        for i in range(2 * count):
+            refs[i // 2][i % 2] = parts[i * rows:(i + 1) * rows]
+
+
+def project(wanted, me, agg, weight):
+    vmem = pl.BlockSpec(memory_space=pltpu.VMEM)
+    pair = jax.ShapeDtypeStruct((2, agg.shape[1], weight.shape[1] // 2), jnp.bfloat16)
+    count = len(wanted)
+    parts = pl.pallas_call(
+        functools.partial(project_kernel, wanted),
+        out_shape=[pair] * (2 * count),
+        in_specs=[pl.BlockSpec(memory_space=pltpu.SMEM), vmem, vmem],
+        out_specs=[vmem] * (2 * count),
+        compiler_params=pltpu.CompilerParams(vmem_limit_bytes=16 * 2**20),
+    )(me.reshape(1), agg, weight)
+    return parts[:count], parts[count:]
 
 
 def add(a, b):
@@ -123,12 +142,13 @@
         held = [add(got[chain], pairs[chain][k]).astype(jnp.bfloat16) for chain in range(2)]
     sums = []
     got = [with_neighbour(held[chain], chain, 1) for chain in range(2)]
-    both = [add(got[chain], pairs[chain][0]) for chain in range(2)]
     for chain in range(2):
         second = is_second(chain)
-        give = jnp.where(second, both[chain][0], both[chain][1]).astype(jnp.bfloat16)
-        keep = jnp.where(second, both[chain][1], both[chain][0])
-        sums.append(keep + with_neighbour(give, chain, 0).astype(jnp.float32))
+        give, keep = (
+            add(jnp.where(second, x[0], x[1]), jnp.where(second, y[0], y[1]))
+            for x, y in ((got[chain], pairs[chain][0]), (got[chain][::-1], pairs[chain][0][::-1]))
+        )
+        sums.append(keep + with_neighbour(give.astype(jnp.bfloat16), chain, 0).astype(jnp.float32))
     return jnp.concatenate(sums, axis=1)
 
 
@@ -142,33 +162,37 @@
     for k in range(1, 4):
         for chain in range(2):
             held[chain].append(with_neighbour(held[chain][-1], chain, k % 2))
-    return held[0] + held[1]
-
-
-def fold_kernel(me_ref, rows_ref, *refs):
-    *grad_refs, out_ref = refs
+    return held
+
+
+def fold_kernel(wanted, started, me_ref, agg_ref, other_ref, *refs):
+    count = len(wanted)
+    grad_refs, out_ref = refs[started:started + 2 * count], refs[-1]
     for chain in range(2):
         cols = grad_refs[0].shape[2]
-        total = None
-        for k in range(4):
+        place = (slice(None), slice(chain * cols, (chain + 1) * cols))
+        total = refs[0][place] if started else None
+        for i, k in enumerate(wanted):
             for member in range(2):
-                rows = rows_ref[pair_block(me_ref[0], chain, k, member)]
+                block = pair_block(me_ref[0], chain, k, member)
+                rows = jnp.concatenate([agg_ref[block], other_ref[block]], axis=0)
                 term = lax.dot_general(
-                    rows, grad_refs[4 * chain + k][member], (((0,), (0,)), ((), ())), preferred_element_type=jnp.float32
+                    rows, grad_refs[count * chain + i][member], (((0,), (0,)), ((), ())), preferred_element_type=jnp.float32
                 )
                 total = term if total is None else total + term
-        out_ref[:, chain * cols:(chain + 1) * cols] = total.astype(out_ref.dtype)
-
-
-def fold(me, rows, grads):
+        out_ref[place] = total.astype(out_ref.dtype)
+
+
+def fold(wanted, me, agg, other_agg, grads, start, kind):
     vmem = pl.BlockSpec(memory_space=pltpu.VMEM)
+    grads = [*start, *(chain[k] for chain in grads for k in wanted)]
     return pl.pallas_call(
-        fold_kernel,
-        out_shape=jax.ShapeDtypeStruct((rows.shape[2], 2 * grads[0].shape[2]), jnp.bfloat16),
-        in_specs=[pl.BlockSpec(memory_space=pltpu.SMEM), vmem] + [vmem] * len(grads),
+        functools.partial(fold_kernel, wanted, len(start)),
+        out_shape=jax.ShapeDtypeStruct((agg.shape[2], 2 * grads[-1].shape[2]), kind),
+        in_specs=[pl.BlockSpec(memory_space=pltpu.SMEM)] + [vmem] * (2 + len(grads)),
         out_specs=vmem,
-        compiler_params=pltpu.CompilerParams(vmem_limit_bytes=32 * 2**20),
-    )(me.reshape(1), rows, *grads)
+        compiler_params=pltpu.CompilerParams(vmem_limit_bytes=16 * 2**20),
+    )(me.reshape(1), agg, other_agg, *grads)
 
 
 def shards(feature_table, sample_ids, block_ids, block_counts, block_tiles, weight, target):
@@ -178,10 +202,12 @@
     with jax.named_scope("pick"):
         slices = lax.all_to_all(pick(feature_table, sample_ids, block_total), "feat", 0, 0)
     with jax.named_scope("aggregate"):
-        agg, parts = aggregate_and_project(me, block_ids, block_counts, slices, block_tiles, weight)
+        agg, *far = aggregate(me, block_ids, block_counts, slices, block_tiles, weight)
         other_agg = lax.ppermute(agg, "core", SWAP)
+        near = project((0, 1, 2), me, agg, weight)
+        parts = [[*near[chain], far[chain]] for chain in range(2)]
     with jax.named_scope("preact"):
-        preact = chain_sum(parts)
+        preact, other_agg = lax.optimization_barrier((chain_sum(parts), other_agg))
     with jax.named_scope("grad"):
         sigmoid_part = jax.nn.sigmoid(preact)
         hidden = preact * sigmoid_part
@@ -195,12 +221,14 @@
         grad_pre = (grad_hidden * slope).astype(jnp.bfloat16)
     with jax.named_scope("swap"):
         half = hidden_width // 2
-        paired = lax.all_to_all(grad_pre.reshape(block_rows, 2, half).swapaxes(0, 1), "core", 0, 0)
+        first = lax.axis_index("core") == 0
+        left, right = grad_pre[:, :half], grad_pre[:, half:]
+        mine, other = jnp.where(first, left, right), lax.ppermute(jnp.where(first, right, left), "core", SWAP)
+        paired = jnp.concatenate([mine, other], axis=0)
     with jax.named_scope("fold"):
-        first = lax.axis_index("core") == 0
-        rows = jnp.concatenate([jnp.where(first, agg, other_agg), jnp.where(first, other_agg, agg)], axis=1)
-        paired = paired.reshape(2 * block_rows, half)
-        folded = fold(me, rows, chain_gather([paired[:, :half // 2], paired[:, half // 2:]]))
+        grads = chain_gather([paired[:, :half // 2], paired[:, half // 2:]])
+        folded = fold((0, 1, 2), me, agg, other_agg, grads, [], jnp.float32)
+        folded = fold((3,), me, agg, other_agg, grads, [folded], jnp.bfloat16)
     weight_grad = group_sum(folded)
     return (embedding, weight_grad)
 

time: 204 us -> 200 us (0.980)
  blocking collectives: 67 us -> 55.3 us
  starting transfers between devices: 63.1 us -> 73.6 us
  other arithmetic: 5.84 us -> 3.49 us
    all_to_all x1 -> x0, blocking collectives: 12.9 us -> none  [shards(): lax.all_to_all(grad_pre.reshape(block_rows, 2, half).swapaxes(0, 1), 'cor...]
    ppermute x1, starting transfers between devices: 2.55 us -> 11.5 us  [shards(): other_agg = lax.ppermute(agg, 'core', SWAP)]
    ppermute x0 -> x1, starting transfers between devices: none -> 3.26 us  [shards(): lax.ppermute(jnp.where(first, right, left), 'core', SWAP)]
    pallas_call x2 -> x4, Pallas kernels: 4.14 us -> 4.57 us  [the longest x1 2.04 us: aggregate(): pl.pallas_call(aggregate_kernel, out_shape=[jax.ShapeDtypeStruct(slices.s...]
  transfers between devices with their start and end apart: 19 -> 20, of which waited for: 14 -> 14; matrix products, arithmetic and copies ran while one was open for 2% -> 0% of each run, Pallas kernels for 0% -> 1%
where the time goes in v8:
time: 200 us; the launch traced here: 199 us
  starting transfers between devices  73.6 us (37%)
  waiting for transfers between devices  56.4 us (28%)
  blocking collectives  55.3 us (28%)
  Pallas kernels  6.03 us (3%)
  local copies, waits for them, and re-layouts  3.57 us (2%)
  other arithmetic  3.49 us (2%)
    ppermute x16, starting transfers between devices, with_neighbour(): return lax.ppermute(block, 'feat', neighbours(chain, odd_step))  36.6 us
    ppermute x16, waiting for transfers between devices, with_neighbour(): return lax.ppermute(block, 'feat', neighbours(chain, odd_step))  29.1 us
    all_to_all x1, waiting for transfers between devices, shards(): lax.all_to_all(pick(feature_table, sample_ids, block_total), 'feat', 0, 0)  24.8 us
    all_gather x1, blocking collectives, group_sum(): lax.all_gather(part.astype(jnp.bfloat16), ('zo', 'zi'), axis=0, tiled=True)  24.6 us
    all_to_all x1, blocking collectives, exchange_sum(): got = lax.all_to_all(parts, axis, 0, 0)  20.9 us
    ppermute x1, starting transfers between devices, group_sum(): other = lax.ppermute(part, 'core', SWAP)  14.7 us
    ppermute x1, starting transfers between devices, shards(): other_agg = lax.ppermute(agg, 'core', SWAP)  11.5 us
    all_gather x1, blocking collectives, group_sum(): part = lax.all_gather(part, 'x', axis=0, tiled=True)  9.9 us
  transfers between devices with their start and end apart: 20, of which 14 were waited for; matrix products, arithmetic and copies ran while one was open for 0% of the time, Pallas kernels for 1%

profile of v8, /device:TPU:1, one launch (start us, length us, event | category | flops | bytes accessed | tf_op | source)
XLA Modules:
  0.0 199.5 jit_solution(16065957271650929186)
XLA Ops:
  4.3 7.7 %all-to-all-start = ((bf16[8,128,512]{2,1,0:T(8,128)(2,1)}), bf16[8,128,512]{2,1,0:T(8,128)(2,1)S(1)}, u32[]{:S(2)}, u32[]{:S(2)}) async-start(bf16[8,128,512]{2,1,0:T(8,128)(2,1)} %pick.1), calls=%async_computation | async-start | bytes 2097152 | tf_op jit(solution)/shard_map/pick/all_to_all | solution.py:203
  12.1 24.8 %all-to-all-done.slices_ref = bf16[8,128,512]{2,1,0:T(8,128)(2,1)S(1)} async-done(((bf16[8,128,512]{2,1,0:T(8,128)(2,1)}), bf16[8,128,512]{2,1,0:T(8,128)(2,1)S(1)}, u32[]{:S(2)}, u32[]{:S(2)}) %all-to-all-start) | async-done | bytes 1048608 | tf_op jit(solution)/shard_map/pick/all_to_all | solution.py:203
  38.1 2.0 %aggregate.2 = (bf16[8,128,512]{2,1,0:T(8,128)(2,1)S(1)}, bf16[2,128,512]{2,1,0:T(8,128)(2,1)S(1)}, bf16[2,128,512]{2,1,0:T(8,128)(2,1)S(1)}) custom-call(s32[1]{0:T(128)} %bitcast.me_ref, s32[8,4]{1,0:T(8,128)S(1)} %copy.10.ids_ref, s32[8]{0:T(128)S(1)} %copy-done.3, bf16[8,128,512]{2,1,0:T(8,128)(2,1)S(1)} %all-to-all-done.slices_ref, ...), custom_call_target="tpu_custom_call" | custom-call | tf_op jit(solution)/shard_map/aggregate/pallas_call | solution.py:97
  40.2 1.9 collective-permute-start
  42.1 1.9 collective-permute-start.4
  45.0 3.5 %collective-permute-done = bf16[2,128,512]{2,1,0:T(8,128)(2,1)S(1)} collective-permute-done((bf16[2,128,512]{2,1,0:T(8,128)(2,1)S(1)}, bf16[2,128,512]{2,1,0:T(8,128)(2,1)S(1)}, u32[]{:S(2)}, u32[]{:S(2)}) %collective-permute-start) | collective-permute-done | bytes 262176 | tf_op jit(solution)/shard_map/preact/ppermute | solution.py:23
  48.6 1.9 collective-permute-start.1
  50.6 3.6 %collective-permute-start.5 = (bf16[2,128,512]{2,1,0:T(8,128)(2,1)S(1)}, bf16[2,128,512]{2,1,0:T(8,128)(2,1)S(1)}, u32[]{:S(2)}, u32[]{:S(2)}) collective-permute-start(bf16[2,128,512]{2,1,0:T(8,128)(2,1)S(1)} %add_convert_fusion.1), channel_id=1, source_target_pairs={{1,2},{3,4},{5,6},{7,0},{2,1},{4,3},{6,5},{0,7},{9,10},{11,12},{13... | collective-permute-start | bytes 786440 | tf_op jit(solution)/shard_map/preact/ppermute | solution.py:23
  54.2 3.2 %collective-permute-done.1 = bf16[2,128,512]{2,1,0:T(8,128)(2,1)S(1)} collective-permute-done((bf16[2,128,512]{2,1,0:T(8,128)(2,1)S(1)}, bf16[2,128,512]{2,1,0:T(8,128)(2,1)S(1)}, u32[]{:S(2)}, u32[]{:S(2)}) %collective-permute-start.1) | collective-permute-done | bytes 262176 | tf_op jit(solution)/shard_map/preact/ppermute | solution.py:23
  57.4 1.9 collective-permute-start.2
  59.4 2.2 %collective-permute-start.6 = (bf16[2,128,512]{2,1,0:T(8,128)(2,1)S(1)}, bf16[2,128,512]{2,1,0:T(8,128)(2,1)S(1)}, u32[]{:S(2)}, u32[]{:S(2)}) collective-permute-start(bf16[2,128,512]{2,1,0:T(8,128)(2,1)S(1)} %add_convert_fusion), channel_id=1, source_target_pairs={{0,1},{2,3},{4,5},{6,7},{1,0},{3,2},{5,4},{7,6},{8,9},{10,11},{12,... | collective-permute-start | bytes 786440 | tf_op jit(solution)/shard_map/preact/ppermute | solution.py:23
  61.6 11.5 %collective-permute-start.8 = (bf16[8,128,512]{2,1,0:T(8,128)(2,1)S(1)}, bf16[8,128,512]{2,1,0:T(8,128)(2,1)S(1)}, u32[]{:S(2)}, u32[]{:S(2)}) collective-permute-start(bf16[8,128,512]{2,1,0:T(8,128)(2,1)S(1)} %get-tuple-element.14.agg_ref), channel_id=1, source_target_pairs={{0,8},{8,0},{1,9},{9,1},{2,10},{10,2},{3,11},{11,3},{4,12},{12,4},... | collective-permute-start | bytes 3145736 | tf_op jit(solution)/shard_map/aggregate/ppermute | solution.py:206
  73.2 3.8 %collective-permute-start.3 = (bf16[128,512]{1,0:T(8,128)(2,1)S(1)}, bf16[128,512]{1,0:T(8,128)(2,1)S(1)}, u32[]{:S(2)}, u32[]{:S(2)}) collective-permute-start(bf16[128,512]{1,0:T(8,128)(2,1)S(1)} %fusion.1), channel_id=1, source_target_pairs={{0,1},{2,3},{4,5},{6,7},{1,0},{3,2},{5,4},{7,6},{8,9},{10,11},{12,... | collective-permute-start | bytes 393224 | tf_op jit(solution)/shard_map/preact/ppermute | solution.py:23
  77.1 2.0 collective-permute-start.7
  80.9 3.8 %collective-permute-done.7 = bf16[128,512]{1,0:T(8,128)(2,1)S(1)} collective-permute-done((bf16[128,512]{1,0:T(8,128)(2,1)S(1)}, bf16[128,512]{1,0:T(8,128)(2,1)S(1)}, u32[]{:S(2)}, u32[]{:S(2)}) %collective-permute-start.7) | collective-permute-done | bytes 131104 | tf_op jit(solution)/shard_map/preact/ppermute | solution.py:23
  85.9 3.3 %collective-permute-start.9 = (bf16[128,512]{1,0:T(8,128)(2,1)S(1)}, bf16[128,512]{1,0:T(8,128)(2,1)S(1)}, u32[]{:S(2)}, u32[]{:S(2)}) collective-permute-start(bf16[128,512]{1,0:T(8,128)(2,1)S(1)} %get-tuple-element.36), channel_id=1, source_target_pairs={{0,8},{8,0},{1,9},{9,1},{2,10},{10,2},{3,11},{11,3},{4,12},{12,4},... | collective-permute-start | bytes 393224 | tf_op jit(solution)/shard_map/swap/ppermute | solution.py:226
  90.1 2.0 collective-permute-start.13
  92.1 1.9 collective-permute-start.10
  94.0 3.9 %collective-permute-done.13 = bf16[256,256]{1,0:T(8,128)(2,1)S(1)} collective-permute-done((bf16[256,256]{1,0:T(8,128)(2,1)S(1)}, bf16[256,256]{1,0:T(8,128)(2,1)S(1)}, u32[]{:S(2)}, u32[]{:S(2)}) %collective-permute-start.13) | collective-permute-done | bytes 131104 | tf_op jit(solution)/shard_map/fold/ppermute | solution.py:23
  98.0 1.9 collective-permute-start.14
  100.0 3.0 %collective-permute-start.11 = (bf16[2,256,256]{2,1,0:T(8,128)(2,1)S(1)}, bf16[2,256,256]{2,1,0:T(8,128)(2,1)S(1)}, u32[]{:S(2)}, u32[]{:S(2)}) collective-permute-start(bf16[2,256,256]{2,1,0:T(8,128)(2,1)S(1)} %pad_maximum_fusion.1.refs_0_), channel_id=1, source_target_pairs={{1,2},{3,4},{5,6},{7,0},{2,1},{4,3},{6,5},{0,7},{9,10},{11,12},{13... | collective-permute-start | bytes 786440 | tf_op jit(solution)/shard_map/fold/ppermute | solution.py:23
  103.0 3.5 %collective-permute-done.14.refs_4_ = bf16[2,256,256]{2,1,0:T(8,128)(2,1)S(1)} collective-permute-done((bf16[2,256,256]{2,1,0:T(8,128)(2,1)S(1)}, bf16[2,256,256]{2,1,0:T(8,128)(2,1)S(1)}, u32[]{:S(2)}, u32[]{:S(2)}) %collective-permute-start.14) | collective-permute-done | bytes 262176 | tf_op jit(solution)/shard_map/fold/ppermute | solution.py:23
  106.5 2.0 collective-permute-start.15
  109.7 1.9 collective-permute-start.12
  111.7 3.6 %collective-permute-done.15.refs_5_ = bf16[2,256,256]{2,1,0:T(8,128)(2,1)S(1)} collective-permute-done((bf16[2,256,256]{2,1,0:T(8,128)(2,1)S(1)}, bf16[2,256,256]{2,1,0:T(8,128)(2,1)S(1)}, u32[]{:S(2)}, u32[]{:S(2)}) %collective-permute-start.15) | collective-permute-done | bytes 262176 | tf_op jit(solution)/shard_map/fold/ppermute | solution.py:23
  115.3 1.9 collective-permute-start.17
  117.3 2.8 %collective-permute-start.16 = (bf16[2,256,256]{2,1,0:T(8,128)(2,1)S(1)}, bf16[2,256,256]{2,1,0:T(8,128)(2,1)S(1)}, u32[]{:S(2)}, u32[]{:S(2)}) collective-permute-start(bf16[2,256,256]{2,1,0:T(8,128)(2,1)S(1)} %collective-permute-done.12.refs_2_), channel_id=1, source_target_pairs={{1,2},{3,4},{5,6},{7,0},{2,1},{4,3},{6,5},{0,7},{9,10},{11,12},{13... | collective-permute-start | bytes 786440 | tf_op jit(solution)/shard_map/fold/ppermute | solution.py:23
  122.5 3.2 %collective-permute-done.16.refs_1_ = bf16[2,256,256]{2,1,0:T(8,128)(2,1)S(1)} collective-permute-done((bf16[2,256,256]{2,1,0:T(8,128)(2,1)S(1)}, bf16[2,256,256]{2,1,0:T(8,128)(2,1)S(1)}, u32[]{:S(2)}, u32[]{:S(2)}) %collective-permute-start.16) | collective-permute-done | bytes 262176 | tf_op jit(solution)/shard_map/fold/ppermute | solution.py:23
  126.1 20.9 %all_to_all.10 = bf16[16,32,512]{2,1,0:T(8,128)(2,1)S(1)} all-to-all(bf16[16,32,512]{2,1,0:T(8,128)(2,1)S(1)} %bitcast.20), channel_id=1, replica_groups=mesh['x'=4,'zo'=3,'zi'=4,'core'=2,'feat'=8] {'x','zi'}, dimensions={0} | all-to-all | bytes 1048576 | tf_op jit(solution)/shard_map/sum_x_zi/all_to_all | solution.py:31
  147.1 24.6 %all_gather.6 = bf16[384,512]{1,0:T(8,128)(2,1)S(1)} all-gather(bf16[32,512]{1,0:T(8,128)(2,1)S(1)} %reduce_sum.44), channel_id=1, replica_groups=mesh['x'=4,'zo'=3,'zi'=4,'core'=2,'feat'=8] {'zo','zi'}, dimensions={0}, use_global_device_ids=true | all-gather | bytes 425984 | tf_op jit(solution)/shard_map/sum_z/all_gather | solution.py:40
  171.7 9.9 %all_gather.7 = bf16[512,512]{1,0:T(8,128)(2,1)S(1)} all-gather(bf16[128,512]{1,0:T(8,128)(2,1)S(1)} %reduce_sum.45), channel_id=1, replica_groups=mesh['x'=4,'zo'=3,'zi'=4,'core'=2,'feat'=8] {'x'}, dimensions={0}, use_global_device_ids=true | all-gather | bytes 655360 | tf_op jit(solution)/shard_map/gather_x/all_gather | solution.py:44
  181.6 14.7 %collective-permute-start.18 = (bf16[512,512]{1,0:T(8,128)(2,1)S(1)}, bf16[512,512]{1,0:T(8,128)(2,1)S(1)}, u32[]{:S(2)}, u32[]{:S(2)}) collective-permute-start(bf16[512,512]{1,0:T(8,128)(2,1)S(1)} %all_gather.7), channel_id=1, source_target_pairs={{0,8},{8,0},{1,9},{9,1},{2,10},{10,2},{3,11},{11,3},{4,12},{12,4},... | collective-permute-start | bytes 1572872 | tf_op jit(solution)/shard_map/gather_core/ppermute | solution.py:46
  (57 shorter events, 17.9 us)
Async XLA Ops:
  0.6 1.6 copy-start.1
  2.2 0.7 copy-start.4
  2.9 9.1 %copy-start.7 = (s32[8,4]{0,1:T(4,128)S(1)}, s32[8,4]{0,1:T(4,128)}, u32[]{:S(2)}) copy-start(s32[8,4]{0,1:T(4,128)} %param.9) | copy-start | bytes 388
  2.9 34.0 %copy-start = (bf16[512,1024]{1,0:T(8,128)(2,1)S(1)}, bf16[512,1024]{1,0:T(8,128)(2,1)}, u32[]{:S(2)}) copy-start(bf16[512,1024]{1,0:T(8,128)(2,1)} %weight_ref.3) | copy-start | bytes 3145732
  2.9 34.0 %copy-start.3 = (s32[8]{0:T(128)S(1)}, s32[8]{0:T(128)}, u32[]{:S(2)}) copy-start(s32[8]{0:T(128)} %counts_ref.1) | copy-start | bytes 100
  4.3 32.5 %all-to-all-start = ((bf16[8,128,512]{2,1,0:T(8,128)(2,1)}), bf16[8,128,512]{2,1,0:T(8,128)(2,1)S(1)}, u32[]{:S(2)}, u32[]{:S(2)}) async-start(bf16[8,128,512]{2,1,0:T(8,128)(2,1)} %pick.1), calls=%async_computation | async-start | bytes 2097152 | tf_op jit(solution)/shard_map/pick/all_to_all | solution.py:203
  36.9 1.2 copy-start.2
  40.2 8.3 %collective-permute-start = (bf16[2,128,512]{2,1,0:T(8,128)(2,1)S(1)}, bf16[2,128,512]{2,1,0:T(8,128)(2,1)S(1)}, u32[]{:S(2)}, u32[]{:S(2)}) collective-permute-start(bf16[2,128,512]{2,1,0:T(8,128)(2,1)S(1)} %get-tuple-element.13), channel_id=1, source_target_pairs={{1,2},{3,4},{5,6},{7,0},{2,1},{4,3},{6,5},{0,7},{9,10},{11,12},{13... | collective-permute-start | bytes 786440 | tf_op jit(solution)/shard_map/preact/ppermute | solution.py:23
  42.1 8.4 %collective-permute-start.4 = (bf16[2,128,512]{2,1,0:T(8,128)(2,1)S(1)}, bf16[2,128,512]{2,1,0:T(8,128)(2,1)S(1)}, u32[]{:S(2)}, u32[]{:S(2)}) collective-permute-start(bf16[2,128,512]{2,1,0:T(8,128)(2,1)S(1)} %get-tuple-element.18), channel_id=1, source_target_pairs={{0,1},{2,3},{4,5},{6,7},{1,0},{3,2},{5,4},{7,6},{8,9},{10,11},{12,... | collective-permute-start | bytes 786440 | tf_op jit(solution)/shard_map/preact/ppermute | solution.py:23
  48.6 8.8 %collective-permute-start.1 = (bf16[2,128,512]{2,1,0:T(8,128)(2,1)S(1)}, bf16[2,128,512]{2,1,0:T(8,128)(2,1)S(1)}, u32[]{:S(2)}, u32[]{:S(2)}) collective-permute-start(bf16[2,128,512]{2,1,0:T(8,128)(2,1)S(1)} %add_convert_fusion.3), channel_id=1, source_target_pairs={{0,1},{2,3},{4,5},{6,7},{1,0},{3,2},{5,4},{7,6},{8,9},{10,11},{12,... | collective-permute-start | bytes 786440 | tf_op jit(solution)/shard_map/preact/ppermute | solution.py:23
  50.6 8.8 %collective-permute-start.5 = (bf16[2,128,512]{2,1,0:T(8,128)(2,1)S(1)}, bf16[2,128,512]{2,1,0:T(8,128)(2,1)S(1)}, u32[]{:S(2)}, u32[]{:S(2)}) collective-permute-start(bf16[2,128,512]{2,1,0:T(8,128)(2,1)S(1)} %add_convert_fusion.1), channel_id=1, source_target_pairs={{1,2},{3,4},{5,6},{7,0},{2,1},{4,3},{6,5},{0,7},{9,10},{11,12},{13... | collective-permute-start | bytes 786440 | tf_op jit(solution)/shard_map/preact/ppermute | solution.py:23
  57.4 15.7 %collective-permute-start.2 = (bf16[2,128,512]{2,1,0:T(8,128)(2,1)S(1)}, bf16[2,128,512]{2,1,0:T(8,128)(2,1)S(1)}, u32[]{:S(2)}, u32[]{:S(2)}) collective-permute-start(bf16[2,128,512]{2,1,0:T(8,128)(2,1)S(1)} %add_convert_fusion.2), channel_id=1, source_target_pairs={{1,2},{3,4},{5,6},{7,0},{2,1},{4,3},{6,5},{0,7},{9,10},{11,12},{13... | collective-permute-start | bytes 786440 | tf_op jit(solution)/shard_map/preact/ppermute | solution.py:23
  59.4 17.6 %collective-permute-start.6 = (bf16[2,128,512]{2,1,0:T(8,128)(2,1)S(1)}, bf16[2,128,512]{2,1,0:T(8,128)(2,1)S(1)}, u32[]{:S(2)}, u32[]{:S(2)}) collective-permute-start(bf16[2,128,512]{2,1,0:T(8,128)(2,1)S(1)} %add_convert_fusion), channel_id=1, source_target_pairs={{0,1},{2,3},{4,5},{6,7},{1,0},{3,2},{5,4},{7,6},{8,9},{10,11},{12,... | collective-permute-start | bytes 786440 | tf_op jit(solution)/shard_map/preact/ppermute | solution.py:23
  61.6 23.3 %collective-permute-start.8 = (bf16[8,128,512]{2,1,0:T(8,128)(2,1)S(1)}, bf16[8,128,512]{2,1,0:T(8,128)(2,1)S(1)}, u32[]{:S(2)}, u32[]{:S(2)}) collective-permute-start(bf16[8,128,512]{2,1,0:T(8,128)(2,1)S(1)} %get-tuple-element.14.agg_ref), channel_id=1, source_target_pairs={{0,8},{8,0},{1,9},{9,1},{2,10},{10,2},{3,11},{11,3},{4,12},{12,4},... | collective-permute-start | bytes 3145736 | tf_op jit(solution)/shard_map/aggregate/ppermute | solution.py:206
  73.2 11.9 %copy-start.5 = (bf16[128,1024]{1,0:T(8,128)(2,1)S(1)}, bf16[128,1024]{1,0:T(8,128)(2,1)}, u32[]{:S(2)}) copy-start(bf16[128,1024]{1,0:T(8,128)(2,1)} %param.13) | copy-start | bytes 786436
  73.2 7.6 %collective-permute-start.3 = (bf16[128,512]{1,0:T(8,128)(2,1)S(1)}, bf16[128,512]{1,0:T(8,128)(2,1)S(1)}, u32[]{:S(2)}, u32[]{:S(2)}) collective-permute-start(bf16[128,512]{1,0:T(8,128)(2,1)S(1)} %fusion.1), channel_id=1, source_target_pairs={{0,1},{2,3},{4,5},{6,7},{1,0},{3,2},{5,4},{7,6},{8,9},{10,11},{12,... | collective-permute-start | bytes 393224 | tf_op jit(solution)/shard_map/preact/ppermute | solution.py:23
  77.1 7.7 %collective-permute-start.7 = (bf16[128,512]{1,0:T(8,128)(2,1)S(1)}, bf16[128,512]{1,0:T(8,128)(2,1)S(1)}, u32[]{:S(2)}, u32[]{:S(2)}) collective-permute-start(bf16[128,512]{1,0:T(8,128)(2,1)S(1)} %fusion.2), channel_id=1, source_target_pairs={{1,2},{3,4},{5,6},{7,0},{2,1},{4,3},{6,5},{0,7},{9,10},{11,12},{13... | collective-permute-start | bytes 393224 | tf_op jit(solution)/shard_map/preact/ppermute | solution.py:23
  85.5 14.5 %copy-start.6 = (bf16[128,1024]{1,0:T(8,128)(2,1)}, bf16[128,1024]{1,0:T(8,128)(2,1)S(1)}, u32[]{:S(2)}) copy-start(bf16[128,1024]{1,0:T(8,128)(2,1)S(1)} %get-tuple-element.27) | copy-start | bytes 786436
  85.9 4.2 %collective-permute-start.9 = (bf16[128,512]{1,0:T(8,128)(2,1)S(1)}, bf16[128,512]{1,0:T(8,128)(2,1)S(1)}, u32[]{:S(2)}, u32[]{:S(2)}) collective-permute-start(bf16[128,512]{1,0:T(8,128)(2,1)S(1)} %get-tuple-element.36), channel_id=1, source_target_pairs={{0,8},{8,0},{1,9},{9,1},{2,10},{10,2},{3,11},{11,3},{4,12},{12,4},... | collective-permute-start | bytes 393224 | tf_op jit(solution)/shard_map/swap/ppermute | solution.py:226
  90.1 7.8 %collective-permute-start.13 = (bf16[256,256]{1,0:T(8,128)(2,1)S(1)}, bf16[256,256]{1,0:T(8,128)(2,1)S(1)}, u32[]{:S(2)}, u32[]{:S(2)}) collective-permute-start(bf16[256,256]{1,0:T(8,128)(2,1)S(1)} %get-tuple-element.32), channel_id=1, source_target_pairs={{1,2},{3,4},{5,6},{7,0},{2,1},{4,3},{6,5},{0,7},{9,10},{11,12},{13... | collective-permute-start | bytes 393224 | tf_op jit(solution)/shard_map/fold/ppermute | solution.py:23
  92.1 7.8 %collective-permute-start.10 = (bf16[256,256]{1,0:T(8,128)(2,1)S(1)}, bf16[256,256]{1,0:T(8,128)(2,1)S(1)}, u32[]{:S(2)}, u32[]{:S(2)}) collective-permute-start(bf16[256,256]{1,0:T(8,128)(2,1)S(1)} %get-tuple-element.33), channel_id=1, source_target_pairs={{0,1},{2,3},{4,5},{6,7},{1,0},{3,2},{5,4},{7,6},{8,9},{10,11},{12,... | collective-permute-start | bytes 393224 | tf_op jit(solution)/shard_map/fold/ppermute | solution.py:23
  98.0 8.5 %collective-permute-start.14 = (bf16[2,256,256]{2,1,0:T(8,128)(2,1)S(1)}, bf16[2,256,256]{2,1,0:T(8,128)(2,1)S(1)}, u32[]{:S(2)}, u32[]{:S(2)}) collective-permute-start(bf16[2,256,256]{2,1,0:T(8,128)(2,1)S(1)} %pad_maximum_fusion.2.refs_3_), channel_id=1, source_target_pairs={{0,1},{2,3},{4,5},{6,7},{1,0},{3,2},{5,4},{7,6},{8,9},{10,11},{12,... | collective-permute-start | bytes 786440 | tf_op jit(solution)/shard_map/fold/ppermute | solution.py:23
  100.0 9.7 %collective-permute-start.11 = (bf16[2,256,256]{2,1,0:T(8,128)(2,1)S(1)}, bf16[2,256,256]{2,1,0:T(8,128)(2,1)S(1)}, u32[]{:S(2)}, u32[]{:S(2)}) collective-permute-start(bf16[2,256,256]{2,1,0:T(8,128)(2,1)S(1)} %pad_maximum_fusion.1.refs_0_), channel_id=1, source_target_pairs={{1,2},{3,4},{5,6},{7,0},{2,1},{4,3},{6,5},{0,7},{9,10},{11,12},{13... | collective-permute-start | bytes 786440 | tf_op jit(solution)/shard_map/fold/ppermute | solution.py:23
  106.5 8.8 %collective-permute-start.15 = (bf16[2,256,256]{2,1,0:T(8,128)(2,1)S(1)}, bf16[2,256,256]{2,1,0:T(8,128)(2,1)S(1)}, u32[]{:S(2)}, u32[]{:S(2)}) collective-permute-start(bf16[2,256,256]{2,1,0:T(8,128)(2,1)S(1)} %collective-permute-done.14.refs_4_), channel_id=1, source_target_pairs={{1,2},{3,4},{5,6},{7,0},{2,1},{4,3},{6,5},{0,7},{9,10},{11,12},{13... | collective-permute-start | bytes 786440 | tf_op jit(solution)/shard_map/fold/ppermute | solution.py:23
  109.7 7.6 %collective-permute-start.12 = (bf16[2,256,256]{2,1,0:T(8,128)(2,1)S(1)}, bf16[2,256,256]{2,1,0:T(8,128)(2,1)S(1)}, u32[]{:S(2)}, u32[]{:S(2)}) collective-permute-start(bf16[2,256,256]{2,1,0:T(8,128)(2,1)S(1)} %collective-permute-done.11.refs_1_), channel_id=1, source_target_pairs={{0,1},{2,3},{4,5},{6,7},{1,0},{3,2},{5,4},{7,6},{8,9},{10,11},{12,... | collective-permute-start | bytes 786440 | tf_op jit(solution)/shard_map/fold/ppermute | solution.py:23
  115.3 7.2 %collective-permute-start.17 = (bf16[2,256,256]{2,1,0:T(8,128)(2,1)S(1)}, bf16[2,256,256]{2,1,0:T(8,128)(2,1)S(1)}, u32[]{:S(2)}, u32[]{:S(2)}) collective-permute-start(bf16[2,256,256]{2,1,0:T(8,128)(2,1)S(1)} %collective-permute-done.15.refs_5_), channel_id=1, source_target_pairs={{0,1},{2,3},{4,5},{6,7},{1,0},{3,2},{5,4},{7,6},{8,9},{10,11},{12,... | collective-permute-start | bytes 786440 | tf_op jit(solution)/shard_map/fold/ppermute | solution.py:23
  117.3 8.3 %collective-permute-start.16 = (bf16[2,256,256]{2,1,0:T(8,128)(2,1)S(1)}, bf16[2,256,256]{2,1,0:T(8,128)(2,1)S(1)}, u32[]{:S(2)}, u32[]{:S(2)}) collective-permute-start(bf16[2,256,256]{2,1,0:T(8,128)(2,1)S(1)} %collective-permute-done.12.refs_2_), channel_id=1, source_target_pairs={{1,2},{3,4},{5,6},{7,0},{2,1},{4,3},{6,5},{0,7},{9,10},{11,12},{13... | collective-permute-start | bytes 786440 | tf_op jit(solution)/shard_map/fold/ppermute | solution.py:23
  181.6 16.2 %collective-permute-start.18 = (bf16[512,512]{1,0:T(8,128)(2,1)S(1)}, bf16[512,512]{1,0:T(8,128)(2,1)S(1)}, u32[]{:S(2)}, u32[]{:S(2)}) collective-permute-start(bf16[512,512]{1,0:T(8,128)(2,1)S(1)} %all_gather.7), channel_id=1, source_target_pairs={{0,8},{8,0},{1,9},{9,1},{2,10},{10,2},{3,11},{11,3},{4,12},{12,4},... | collective-permute-start | bytes 1572872 | tf_op jit(solution)/shard_map/gather_core/ppermute | solution.py:46

commit v9 on v8

--- a/solution.py
+++ b/solution.py
@@ -48,10 +48,9 @@
         return jnp.concatenate([jnp.where(first, part, other), jnp.where(first, other, part)], axis=1).astype(jnp.float32)
 
 
-def pick_kernel(ids_ref, table_ref, out_ref):
+def pick_kernel(wanted_ref, table_ref, out_ref):
     slices, _, width = out_ref.shape
-    wanted = lax.broadcasted_iota(jnp.int32, (table_ref.shape[0], ids_ref.shape[1]), 0) == ids_ref[...]
-    wanted = wanted.astype(jnp.float32).T.astype(table_ref.dtype)
+    wanted = wanted_ref[...].T.astype(table_ref.dtype)
     for j in range(slices):
         rows = jnp.dot(wanted, table_ref[:, j * width:(j + 1) * width], preferred_element_type=jnp.float32)
         out_ref[j] = rows.astype(out_ref.dtype)
@@ -59,13 +58,15 @@
 
 def pick(table, ids, slices):
     vmem = pl.BlockSpec(memory_space=pltpu.VMEM)
+    shape = (table.shape[0], ids.shape[0])
+    wanted = (lax.broadcasted_iota(jnp.int32, shape, 0) == ids[None, :]).astype(jnp.float32)
     return pl.pallas_call(
         pick_kernel,
         out_shape=jax.ShapeDtypeStruct((slices, ids.shape[0], table.shape[1] // slices), table.dtype),
         in_specs=[vmem, vmem],
         out_specs=vmem,
         compiler_params=pltpu.CompilerParams(vmem_limit_bytes=16 * 2**20),
-    )(ids.reshape(1, -1), table)
+    )(wanted, table)
 
 
 def pair_block(me, chain, k, member):
@@ -166,21 +167,16 @@
 
 
 def fold_kernel(wanted, started, me_ref, agg_ref, other_ref, *refs):
-    count = len(wanted)
-    grad_refs, out_ref = refs[started:started + 2 * count], refs[-1]
-    for chain in range(2):
-        cols = grad_refs[0].shape[2]
-        place = (slice(None), slice(chain * cols, (chain + 1) * cols))
-        total = refs[0][place] if started else None
+    grad_refs, out_ref = refs[started:-1], refs[-1]
+    total = refs[0][...] if started else None
+    for chain, rows_ref in enumerate((agg_ref, other_ref)):
         for i, k in enumerate(wanted):
-            for member in range(2):
-                block = pair_block(me_ref[0], chain, k, member)
-                rows = jnp.concatenate([agg_ref[block], other_ref[block]], axis=0)
-                term = lax.dot_general(
-                    rows, grad_refs[count * chain + i][member], (((0,), (0,)), ((), ())), preferred_element_type=jnp.float32
-                )
-                total = term if total is None else total + term
-        out_ref[place] = total.astype(out_ref.dtype)
+            grads = grad_refs[len(wanted) * chain + i][...]
+            rows = jnp.concatenate([rows_ref[pair_block(me_ref[0], chain, k, member)] for member in range(2)], axis=0)
+            grads = grads.reshape(rows.shape[0], -1)
+            term = lax.dot_general(rows, grads, (((0,), (0,)), ((), ())), preferred_element_type=jnp.float32)
+            total = term if total is None else total + term
+    out_ref[...] = total.astype(out_ref.dtype)
 
 
 def fold(wanted, me, agg, other_agg, grads, start, kind):
@@ -188,7 +184,7 @@
     grads = [*start, *(chain[k] for chain in grads for k in wanted)]
     return pl.pallas_call(
         functools.partial(fold_kernel, wanted, len(start)),
-        out_shape=jax.ShapeDtypeStruct((agg.shape[2], 2 * grads[-1].shape[2]), kind),
+        out_shape=jax.ShapeDtypeStruct((agg.shape[2], grads[-1].shape[2]), kind),
         in_specs=[pl.BlockSpec(memory_space=pltpu.SMEM)] + [vmem] * (2 + len(grads)),
         out_specs=vmem,
         compiler_params=pltpu.CompilerParams(vmem_limit_bytes=16 * 2**20),
@@ -224,9 +220,8 @@
         first = lax.axis_index("core") == 0
         left, right = grad_pre[:, :half], grad_pre[:, half:]
         mine, other = jnp.where(first, left, right), lax.ppermute(jnp.where(first, right, left), "core", SWAP)
-        paired = jnp.concatenate([mine, other], axis=0)
     with jax.named_scope("fold"):
-        grads = chain_gather([paired[:, :half // 2], paired[:, half // 2:]])
+        grads = chain_gather([mine, other])
         folded = fold((0, 1, 2), me, agg, other_agg, grads, [], jnp.float32)
         folded = fold((3,), me, agg, other_agg, grads, [folded], jnp.bfloat16)
     weight_grad = group_sum(folded)

time: 200 us -> 199 us (level)
  starting transfers between devices: 73.6 us -> 70 us
  blocking collectives: 55.3 us -> 58.3 us
    ppermute x1, starting transfers between devices: 14.7 us -> 11.6 us  [group_sum(): other = lax.ppermute(part, 'core', SWAP)]
    all_to_all x1, blocking collectives: 20.9 us -> 23.6 us  [exchange_sum(): got = lax.all_to_all(parts, axis, 0, 0)]
  transfers between devices with their start and end apart: 20 -> 20, of which waited for: 14 -> 13; matrix products, arithmetic and copies ran while one was open for 0% -> 0% of each run, Pallas kernels for 1% -> 1%
where the time goes in v9:
time: 199 us
  starting transfers between devices  70 us (35%)
  blocking collectives  58.3 us (29%)
  waiting for transfers between devices  56.2 us (28%)
  Pallas kernels  5.99 us (3%)
  other arithmetic  4.14 us (2%)
  local copies, waits for them, and re-layouts  2.91 us (1%)
    ppermute x16, starting transfers between devices, with_neighbour(): return lax.ppermute(block, 'feat', neighbours(chain, odd_step))  36 us
    ppermute x16, waiting for transfers between devices, with_neighbour(): return lax.ppermute(block, 'feat', neighbours(chain, odd_step))  29.9 us
    all_to_all x1, waiting for transfers between devices, shards(): lax.all_to_all(pick(feature_table, sample_ids, block_total), 'feat', 0, 0)  24.8 us
    all_gather x1, blocking collectives, group_sum(): lax.all_gather(part.astype(jnp.bfloat16), ('zo', 'zi'), axis=0, tiled=True)  24.2 us
    all_to_all x1, blocking collectives, exchange_sum(): got = lax.all_to_all(parts, axis, 0, 0)  23.6 us
    ppermute x1, starting transfers between devices, group_sum(): other = lax.ppermute(part, 'core', SWAP)  11.6 us
    ppermute x1, starting transfers between devices, shards(): other_agg = lax.ppermute(agg, 'core', SWAP)  11.5 us
    all_gather x1, blocking collectives, group_sum(): part = lax.all_gather(part, 'x', axis=0, tiled=True)  10.5 us
  transfers between devices with their start and end apart: 20, of which 13 were waited for; matrix products, arithmetic and copies ran while one was open for 0% of the time, Pallas kernels for 1%

profile of v9, /device:TPU:1, one launch (start us, length us, event | category | flops | bytes accessed | tf_op | source)
XLA Modules:
  0.0 198.6 jit_solution(2072006159108479687)
XLA Ops:
  4.4 7.7 %all-to-all-start = ((bf16[8,128,512]{2,1,0:T(8,128)(2,1)}), bf16[8,128,512]{2,1,0:T(8,128)(2,1)S(1)}, u32[]{:S(2)}, u32[]{:S(2)}) async-start(bf16[8,128,512]{2,1,0:T(8,128)(2,1)} %pick.1), calls=%async_computation | async-start | bytes 2097152 | tf_op jit(solution)/shard_map/pick/all_to_all | solution.py:199
  12.1 24.8 %all-to-all-done.slices_ref = bf16[8,128,512]{2,1,0:T(8,128)(2,1)S(1)} async-done(((bf16[8,128,512]{2,1,0:T(8,128)(2,1)}), bf16[8,128,512]{2,1,0:T(8,128)(2,1)S(1)}, u32[]{:S(2)}, u32[]{:S(2)}) %all-to-all-start) | async-done | bytes 1048608 | tf_op jit(solution)/shard_map/pick/all_to_all | solution.py:199
  38.1 2.0 %aggregate.2 = (bf16[8,128,512]{2,1,0:T(8,128)(2,1)S(1)}, bf16[2,128,512]{2,1,0:T(8,128)(2,1)S(1)}, bf16[2,128,512]{2,1,0:T(8,128)(2,1)S(1)}) custom-call(s32[1]{0:T(128)} %bitcast.me_ref, s32[8,4]{1,0:T(8,128)S(1)} %copy.10.ids_ref, s32[8]{0:T(128)S(1)} %copy-done.3, bf16[8,128,512]{2,1,0:T(8,128)(2,1)S(1)} %all-to-all-done.slices_ref, ...), custom_call_target="tpu_custom_call" | custom-call | tf_op jit(solution)/shard_map/aggregate/pallas_call | solution.py:98
  40.2 1.9 collective-permute-start
  42.1 1.9 collective-permute-start.4
  45.0 3.5 %collective-permute-done = bf16[2,128,512]{2,1,0:T(8,128)(2,1)S(1)} collective-permute-done((bf16[2,128,512]{2,1,0:T(8,128)(2,1)S(1)}, bf16[2,128,512]{2,1,0:T(8,128)(2,1)S(1)}, u32[]{:S(2)}, u32[]{:S(2)}) %collective-permute-start) | collective-permute-done | bytes 262176 | tf_op jit(solution)/shard_map/preact/ppermute | solution.py:23
  48.6 1.9 collective-permute-start.1
  50.6 3.6 %collective-permute-start.5 = (bf16[2,128,512]{2,1,0:T(8,128)(2,1)S(1)}, bf16[2,128,512]{2,1,0:T(8,128)(2,1)S(1)}, u32[]{:S(2)}, u32[]{:S(2)}) collective-permute-start(bf16[2,128,512]{2,1,0:T(8,128)(2,1)S(1)} %add_convert_fusion.1), channel_id=1, source_target_pairs={{1,2},{3,4},{5,6},{7,0},{2,1},{4,3},{6,5},{0,7},{9,10},{11,12},{13... | collective-permute-start | bytes 786440 | tf_op jit(solution)/shard_map/preact/ppermute | solution.py:23
  54.2 3.2 %collective-permute-done.1 = bf16[2,128,512]{2,1,0:T(8,128)(2,1)S(1)} collective-permute-done((bf16[2,128,512]{2,1,0:T(8,128)(2,1)S(1)}, bf16[2,128,512]{2,1,0:T(8,128)(2,1)S(1)}, u32[]{:S(2)}, u32[]{:S(2)}) %collective-permute-start.1) | collective-permute-done | bytes 262176 | tf_op jit(solution)/shard_map/preact/ppermute | solution.py:23
  57.4 1.9 collective-permute-start.2
  59.4 2.2 %collective-permute-start.6 = (bf16[2,128,512]{2,1,0:T(8,128)(2,1)S(1)}, bf16[2,128,512]{2,1,0:T(8,128)(2,1)S(1)}, u32[]{:S(2)}, u32[]{:S(2)}) collective-permute-start(bf16[2,128,512]{2,1,0:T(8,128)(2,1)S(1)} %add_convert_fusion), channel_id=1, source_target_pairs={{0,1},{2,3},{4,5},{6,7},{1,0},{3,2},{5,4},{7,6},{8,9},{10,11},{12,... | collective-permute-start | bytes 786440 | tf_op jit(solution)/shard_map/preact/ppermute | solution.py:23
  61.6 11.5 %collective-permute-start.8 = (bf16[8,128,512]{2,1,0:T(8,128)(2,1)S(1)}, bf16[8,128,512]{2,1,0:T(8,128)(2,1)S(1)}, u32[]{:S(2)}, u32[]{:S(2)}) collective-permute-start(bf16[8,128,512]{2,1,0:T(8,128)(2,1)S(1)} %get-tuple-element.14.agg_ref), channel_id=1, source_target_pairs={{0,8},{8,0},{1,9},{9,1},{2,10},{10,2},{3,11},{11,3},{4,12},{12,4},... | collective-permute-start | bytes 3145736 | tf_op jit(solution)/shard_map/aggregate/ppermute | solution.py:202
  73.2 3.8 %collective-permute-start.3 = (bf16[128,512]{1,0:T(8,128)(2,1)S(1)}, bf16[128,512]{1,0:T(8,128)(2,1)S(1)}, u32[]{:S(2)}, u32[]{:S(2)}) collective-permute-start(bf16[128,512]{1,0:T(8,128)(2,1)S(1)} %fusion.1), channel_id=1, source_target_pairs={{0,1},{2,3},{4,5},{6,7},{1,0},{3,2},{5,4},{7,6},{8,9},{10,11},{12,... | collective-permute-start | bytes 393224 | tf_op jit(solution)/shard_map/preact/ppermute | solution.py:23
  77.1 2.0 collective-permute-start.7
  80.9 3.8 %collective-permute-done.7 = bf16[128,512]{1,0:T(8,128)(2,1)S(1)} collective-permute-done((bf16[128,512]{1,0:T(8,128)(2,1)S(1)}, bf16[128,512]{1,0:T(8,128)(2,1)S(1)}, u32[]{:S(2)}, u32[]{:S(2)}) %collective-permute-start.7) | collective-permute-done | bytes 131104 | tf_op jit(solution)/shard_map/preact/ppermute | solution.py:23
  85.9 3.3 %collective-permute-start.12 = (bf16[128,512]{1,0:T(8,128)(2,1)S(1)}, bf16[128,512]{1,0:T(8,128)(2,1)S(1)}, u32[]{:S(2)}, u32[]{:S(2)}) collective-permute-start(bf16[128,512]{1,0:T(8,128)(2,1)S(1)} %get-tuple-element.32), channel_id=1, source_target_pairs={{0,8},{8,0},{1,9},{9,1},{2,10},{10,2},{3,11},{11,3},{4,12},{12,4},... | collective-permute-start | bytes 393224 | tf_op jit(solution)/shard_map/swap/ppermute | solution.py:222
  89.2 1.9 collective-permute-start.9
  91.1 2.0 collective-permute-start.13
  93.1 3.1 %collective-permute-done.9 = bf16[128,512]{1,0:T(8,128)(2,1)S(1)} collective-permute-done((bf16[128,512]{1,0:T(8,128)(2,1)S(1)}, bf16[128,512]{1,0:T(8,128)(2,1)S(1)}, u32[]{:S(2)}, u32[]{:S(2)}) %collective-permute-start.9) | collective-permute-done | bytes 131104 | tf_op jit(solution)/shard_map/fold/ppermute | solution.py:23
  96.2 2.0 collective-permute-start.10
  99.4 1.9 collective-permute-start.14
  101.3 5.1 %collective-permute-done.10.refs_1_ = bf16[2,128,512]{2,1,0:T(8,128)(2,1)S(1)} collective-permute-done((bf16[2,128,512]{2,1,0:T(8,128)(2,1)S(1)}, bf16[2,128,512]{2,1,0:T(8,128)(2,1)S(1)}, u32[]{:S(2)}, u32[]{:S(2)}) %collective-permute-start.10) | collective-permute-done | bytes 262176 | tf_op jit(solution)/shard_map/fold/ppermute | solution.py:23
  106.4 1.9 collective-permute-start.11
  108.3 3.1 %collective-permute-start.15 = (bf16[2,128,512]{2,1,0:T(8,128)(2,1)S(1)}, bf16[2,128,512]{2,1,0:T(8,128)(2,1)S(1)}, u32[]{:S(2)}, u32[]{:S(2)}) collective-permute-start(bf16[2,128,512]{2,1,0:T(8,128)(2,1)S(1)} %collective-permute-done.14.refs_4_), channel_id=1, source_target_pairs={{1,2},{3,4},{5,6},{7,0},{2,1},{4,3},{6,5},{0,7},{9,10},{11,12},{13... | collective-permute-start | bytes 786440 | tf_op jit(solution)/shard_map/fold/ppermute | solution.py:23
  111.4 2.9 %collective-permute-done.11.refs_2_ = bf16[2,128,512]{2,1,0:T(8,128)(2,1)S(1)} collective-permute-done((bf16[2,128,512]{2,1,0:T(8,128)(2,1)S(1)}, bf16[2,128,512]{2,1,0:T(8,128)(2,1)S(1)}, u32[]{:S(2)}, u32[]{:S(2)}) %collective-permute-start.11) | collective-permute-done | bytes 262176 | tf_op jit(solution)/shard_map/fold/ppermute | solution.py:23
  114.4 2.1 %collective-permute-start.16 = (bf16[2,128,512]{2,1,0:T(8,128)(2,1)S(1)}, bf16[2,128,512]{2,1,0:T(8,128)(2,1)S(1)}, u32[]{:S(2)}, u32[]{:S(2)}) collective-permute-start(bf16[2,128,512]{2,1,0:T(8,128)(2,1)S(1)} %collective-permute-done.11.refs_2_), channel_id=1, source_target_pairs={{1,2},{3,4},{5,6},{7,0},{2,1},{4,3},{6,5},{0,7},{9,10},{11,12},{13... | collective-permute-start | bytes 786440 | tf_op jit(solution)/shard_map/fold/ppermute | solution.py:23
  120.5 2.2 %collective-permute-done.16.refs_1_ = bf16[2,128,512]{2,1,0:T(8,128)(2,1)S(1)} collective-permute-done((bf16[2,128,512]{2,1,0:T(8,128)(2,1)S(1)}, bf16[2,128,512]{2,1,0:T(8,128)(2,1)S(1)}, u32[]{:S(2)}, u32[]{:S(2)}) %collective-permute-start.16) | collective-permute-done | bytes 262176 | tf_op jit(solution)/shard_map/fold/ppermute | solution.py:23
  122.7 2.2 %collective-permute-done.17.refs_2_ = bf16[2,128,512]{2,1,0:T(8,128)(2,1)S(1)} collective-permute-done((bf16[2,128,512]{2,1,0:T(8,128)(2,1)S(1)}, bf16[2,128,512]{2,1,0:T(8,128)(2,1)S(1)}, u32[]{:S(2)}, u32[]{:S(2)}) %collective-permute-start.17) | collective-permute-done | bytes 262176 | tf_op jit(solution)/shard_map/fold/ppermute | solution.py:23
  125.4 23.6 %all_to_all.10 = bf16[16,32,512]{2,1,0:T(8,128)(2,1)S(1)} all-to-all(bf16[16,32,512]{2,1,0:T(8,128)(2,1)S(1)} %bitcast.19), channel_id=1, replica_groups=mesh['x'=4,'zo'=3,'zi'=4,'core'=2,'feat'=8] {'x','zi'}, dimensions={0} | all-to-all | bytes 1048576 | tf_op jit(solution)/shard_map/sum_x_zi/all_to_all | solution.py:31
  149.0 24.2 %all_gather.6 = bf16[384,512]{1,0:T(8,128)(2,1)S(1)} all-gather(bf16[32,512]{1,0:T(8,128)(2,1)S(1)} %reduce_sum.44), channel_id=1, replica_groups=mesh['x'=4,'zo'=3,'zi'=4,'core'=2,'feat'=8] {'zo','zi'}, dimensions={0}, use_global_device_ids=true | all-gather | bytes 425984 | tf_op jit(solution)/shard_map/sum_z/all_gather | solution.py:40
  173.3 10.5 %all_gather.7 = bf16[512,512]{1,0:T(8,128)(2,1)S(1)} all-gather(bf16[128,512]{1,0:T(8,128)(2,1)S(1)} %reduce_sum.45), channel_id=1, replica_groups=mesh['x'=4,'zo'=3,'zi'=4,'core'=2,'feat'=8] {'x'}, dimensions={0}, use_global_device_ids=true | all-gather | bytes 655360 | tf_op jit(solution)/shard_map/gather_x/all_gather | solution.py:44
  183.9 11.6 %collective-permute-start.18 = (bf16[512,512]{1,0:T(8,128)(2,1)S(1)}, bf16[512,512]{1,0:T(8,128)(2,1)S(1)}, u32[]{:S(2)}, u32[]{:S(2)}) collective-permute-start(bf16[512,512]{1,0:T(8,128)(2,1)S(1)} %all_gather.7), channel_id=1, source_target_pairs={{0,8},{8,0},{1,9},{9,1},{2,10},{10,2},{3,11},{11,3},{4,12},{12,4},... | collective-permute-start | bytes 1572872 | tf_op jit(solution)/shard_map/gather_core/ppermute | solution.py:46
  (55 shorter events, 18.3 us)
Async XLA Ops:
  1.3 1.6 copy-start.1
  2.9 9.1 %copy-start.6 = (s32[8,4]{0,1:T(4,128)S(1)}, s32[8,4]{0,1:T(4,128)}, u32[]{:S(2)}) copy-start(s32[8,4]{0,1:T(4,128)} %param.9) | copy-start | bytes 388
  2.9 34.0 %copy-start = (bf16[512,1024]{1,0:T(8,128)(2,1)S(1)}, bf16[512,1024]{1,0:T(8,128)(2,1)}, u32[]{:S(2)}) copy-start(bf16[512,1024]{1,0:T(8,128)(2,1)} %weight_ref.3) | copy-start | bytes 3145732
  2.9 34.0 %copy-start.3 = (s32[8]{0:T(128)S(1)}, s32[8]{0:T(128)}, u32[]{:S(2)}) copy-start(s32[8]{0:T(128)} %counts_ref.1) | copy-start | bytes 100
  4.4 32.5 %all-to-all-start = ((bf16[8,128,512]{2,1,0:T(8,128)(2,1)}), bf16[8,128,512]{2,1,0:T(8,128)(2,1)S(1)}, u32[]{:S(2)}, u32[]{:S(2)}) async-start(bf16[8,128,512]{2,1,0:T(8,128)(2,1)} %pick.1), calls=%async_computation | async-start | bytes 2097152 | tf_op jit(solution)/shard_map/pick/all_to_all | solution.py:199
  36.9 1.2 copy-start.2
  40.2 8.3 %collective-permute-start = (bf16[2,128,512]{2,1,0:T(8,128)(2,1)S(1)}, bf16[2,128,512]{2,1,0:T(8,128)(2,1)S(1)}, u32[]{:S(2)}, u32[]{:S(2)}) collective-permute-start(bf16[2,128,512]{2,1,0:T(8,128)(2,1)S(1)} %get-tuple-element.13), channel_id=1, source_target_pairs={{1,2},{3,4},{5,6},{7,0},{2,1},{4,3},{6,5},{0,7},{9,10},{11,12},{13... | collective-permute-start | bytes 786440 | tf_op jit(solution)/shard_map/preact/ppermute | solution.py:23
  42.1 8.4 %collective-permute-start.4 = (bf16[2,128,512]{2,1,0:T(8,128)(2,1)S(1)}, bf16[2,128,512]{2,1,0:T(8,128)(2,1)S(1)}, u32[]{:S(2)}, u32[]{:S(2)}) collective-permute-start(bf16[2,128,512]{2,1,0:T(8,128)(2,1)S(1)} %get-tuple-element.18), channel_id=1, source_target_pairs={{0,1},{2,3},{4,5},{6,7},{1,0},{3,2},{5,4},{7,6},{8,9},{10,11},{12,... | collective-permute-start | bytes 786440 | tf_op jit(solution)/shard_map/preact/ppermute | solution.py:23
  48.6 8.8 %collective-permute-start.1 = (bf16[2,128,512]{2,1,0:T(8,128)(2,1)S(1)}, bf16[2,128,512]{2,1,0:T(8,128)(2,1)S(1)}, u32[]{:S(2)}, u32[]{:S(2)}) collective-permute-start(bf16[2,128,512]{2,1,0:T(8,128)(2,1)S(1)} %add_convert_fusion.3), channel_id=1, source_target_pairs={{0,1},{2,3},{4,5},{6,7},{1,0},{3,2},{5,4},{7,6},{8,9},{10,11},{12,... | collective-permute-start | bytes 786440 | tf_op jit(solution)/shard_map/preact/ppermute | solution.py:23
  50.6 8.8 %collective-permute-start.5 = (bf16[2,128,512]{2,1,0:T(8,128)(2,1)S(1)}, bf16[2,128,512]{2,1,0:T(8,128)(2,1)S(1)}, u32[]{:S(2)}, u32[]{:S(2)}) collective-permute-start(bf16[2,128,512]{2,1,0:T(8,128)(2,1)S(1)} %add_convert_fusion.1), channel_id=1, source_target_pairs={{1,2},{3,4},{5,6},{7,0},{2,1},{4,3},{6,5},{0,7},{9,10},{11,12},{13... | collective-permute-start | bytes 786440 | tf_op jit(solution)/shard_map/preact/ppermute | solution.py:23
  57.4 15.7 %collective-permute-start.2 = (bf16[2,128,512]{2,1,0:T(8,128)(2,1)S(1)}, bf16[2,128,512]{2,1,0:T(8,128)(2,1)S(1)}, u32[]{:S(2)}, u32[]{:S(2)}) collective-permute-start(bf16[2,128,512]{2,1,0:T(8,128)(2,1)S(1)} %add_convert_fusion.2), channel_id=1, source_target_pairs={{1,2},{3,4},{5,6},{7,0},{2,1},{4,3},{6,5},{0,7},{9,10},{11,12},{13... | collective-permute-start | bytes 786440 | tf_op jit(solution)/shard_map/preact/ppermute | solution.py:23
  59.4 17.6 %collective-permute-start.6 = (bf16[2,128,512]{2,1,0:T(8,128)(2,1)S(1)}, bf16[2,128,512]{2,1,0:T(8,128)(2,1)S(1)}, u32[]{:S(2)}, u32[]{:S(2)}) collective-permute-start(bf16[2,128,512]{2,1,0:T(8,128)(2,1)S(1)} %add_convert_fusion), channel_id=1, source_target_pairs={{0,1},{2,3},{4,5},{6,7},{1,0},{3,2},{5,4},{7,6},{8,9},{10,11},{12,... | collective-permute-start | bytes 786440 | tf_op jit(solution)/shard_map/preact/ppermute | solution.py:23
  61.6 23.3 %collective-permute-start.8 = (bf16[8,128,512]{2,1,0:T(8,128)(2,1)S(1)}, bf16[8,128,512]{2,1,0:T(8,128)(2,1)S(1)}, u32[]{:S(2)}, u32[]{:S(2)}) collective-permute-start(bf16[8,128,512]{2,1,0:T(8,128)(2,1)S(1)} %get-tuple-element.14.agg_ref), channel_id=1, source_target_pairs={{0,8},{8,0},{1,9},{9,1},{2,10},{10,2},{3,11},{11,3},{4,12},{12,4},... | collective-permute-start | bytes 3145736 | tf_op jit(solution)/shard_map/aggregate/ppermute | solution.py:202
  73.2 11.9 %copy-start.4 = (bf16[128,1024]{1,0:T(8,128)(2,1)S(1)}, bf16[128,1024]{1,0:T(8,128)(2,1)}, u32[]{:S(2)}) copy-start(bf16[128,1024]{1,0:T(8,128)(2,1)} %param.13) | copy-start | bytes 786436
  73.2 7.6 %collective-permute-start.3 = (bf16[128,512]{1,0:T(8,128)(2,1)S(1)}, bf16[128,512]{1,0:T(8,128)(2,1)S(1)}, u32[]{:S(2)}, u32[]{:S(2)}) collective-permute-start(bf16[128,512]{1,0:T(8,128)(2,1)S(1)} %fusion.1), channel_id=1, source_target_pairs={{0,1},{2,3},{4,5},{6,7},{1,0},{3,2},{5,4},{7,6},{8,9},{10,11},{12,... | collective-permute-start | bytes 393224 | tf_op jit(solution)/shard_map/preact/ppermute | solution.py:23
  77.1 7.7 %collective-permute-start.7 = (bf16[128,512]{1,0:T(8,128)(2,1)S(1)}, bf16[128,512]{1,0:T(8,128)(2,1)S(1)}, u32[]{:S(2)}, u32[]{:S(2)}) collective-permute-start(bf16[128,512]{1,0:T(8,128)(2,1)S(1)} %fusion.2), channel_id=1, source_target_pairs={{1,2},{3,4},{5,6},{7,0},{2,1},{4,3},{6,5},{0,7},{9,10},{11,12},{13... | collective-permute-start | bytes 393224 | tf_op jit(solution)/shard_map/preact/ppermute | solution.py:23
  85.5 35.0 %copy-start.5 = (bf16[128,1024]{1,0:T(8,128)(2,1)}, bf16[128,1024]{1,0:T(8,128)(2,1)S(1)}, u32[]{:S(2)}) copy-start(bf16[128,1024]{1,0:T(8,128)(2,1)S(1)} %get-tuple-element.27) | copy-start | bytes 786436
  85.9 5.2 %collective-permute-start.12 = (bf16[128,512]{1,0:T(8,128)(2,1)S(1)}, bf16[128,512]{1,0:T(8,128)(2,1)S(1)}, u32[]{:S(2)}, u32[]{:S(2)}) collective-permute-start(bf16[128,512]{1,0:T(8,128)(2,1)S(1)} %get-tuple-element.32), channel_id=1, source_target_pairs={{0,8},{8,0},{1,9},{9,1},{2,10},{10,2},{3,11},{11,3},{4,12},{12,4},... | collective-permute-start | bytes 393224 | tf_op jit(solution)/shard_map/swap/ppermute | solution.py:222
  89.2 7.0 %collective-permute-start.9 = (bf16[128,512]{1,0:T(8,128)(2,1)S(1)}, bf16[128,512]{1,0:T(8,128)(2,1)S(1)}, u32[]{:S(2)}, u32[]{:S(2)}) collective-permute-start(bf16[128,512]{1,0:T(8,128)(2,1)S(1)} %get-tuple-element.33), channel_id=1, source_target_pairs={{0,1},{2,3},{4,5},{6,7},{1,0},{3,2},{5,4},{7,6},{8,9},{10,11},{12,... | collective-permute-start | bytes 393224 | tf_op jit(solution)/shard_map/fold/ppermute | solution.py:23
  91.1 8.2 %collective-permute-start.13 = (bf16[128,512]{1,0:T(8,128)(2,1)S(1)}, bf16[128,512]{1,0:T(8,128)(2,1)S(1)}, u32[]{:S(2)}, u32[]{:S(2)}) collective-permute-start(bf16[128,512]{1,0:T(8,128)(2,1)S(1)} %collective-permute-done.12), channel_id=1, source_target_pairs={{1,2},{3,4},{5,6},{7,0},{2,1},{4,3},{6,5},{0,7},{9,10},{11,12},{13... | collective-permute-start | bytes 393224 | tf_op jit(solution)/shard_map/fold/ppermute | solution.py:23
  96.2 10.1 %collective-permute-start.10 = (bf16[2,128,512]{2,1,0:T(8,128)(2,1)S(1)}, bf16[2,128,512]{2,1,0:T(8,128)(2,1)S(1)}, u32[]{:S(2)}, u32[]{:S(2)}) collective-permute-start(bf16[2,128,512]{2,1,0:T(8,128)(2,1)S(1)} %pad_maximum_fusion.1.refs_0_), channel_id=1, source_target_pairs={{1,2},{3,4},{5,6},{7,0},{2,1},{4,3},{6,5},{0,7},{9,10},{11,12},{13... | collective-permute-start | bytes 786440 | tf_op jit(solution)/shard_map/fold/ppermute | solution.py:23
  99.4 8.9 %collective-permute-start.14 = (bf16[2,128,512]{2,1,0:T(8,128)(2,1)S(1)}, bf16[2,128,512]{2,1,0:T(8,128)(2,1)S(1)}, u32[]{:S(2)}, u32[]{:S(2)}) collective-permute-start(bf16[2,128,512]{2,1,0:T(8,128)(2,1)S(1)} %pad_maximum_fusion.2.refs_3_), channel_id=1, source_target_pairs={{0,1},{2,3},{4,5},{6,7},{1,0},{3,2},{5,4},{7,6},{8,9},{10,11},{12,... | collective-permute-start | bytes 786440 | tf_op jit(solution)/shard_map/fold/ppermute | solution.py:23
  106.4 8.0 %collective-permute-start.11 = (bf16[2,128,512]{2,1,0:T(8,128)(2,1)S(1)}, bf16[2,128,512]{2,1,0:T(8,128)(2,1)S(1)}, u32[]{:S(2)}, u32[]{:S(2)}) collective-permute-start(bf16[2,128,512]{2,1,0:T(8,128)(2,1)S(1)} %collective-permute-done.10.refs_1_), channel_id=1, source_target_pairs={{0,1},{2,3},{4,5},{6,7},{1,0},{3,2},{5,4},{7,6},{8,9},{10,11},{12,... | collective-permute-start | bytes 786440 | tf_op jit(solution)/shard_map/fold/ppermute | solution.py:23
  108.3 9.2 %collective-permute-start.15 = (bf16[2,128,512]{2,1,0:T(8,128)(2,1)S(1)}, bf16[2,128,512]{2,1,0:T(8,128)(2,1)S(1)}, u32[]{:S(2)}, u32[]{:S(2)}) collective-permute-start(bf16[2,128,512]{2,1,0:T(8,128)(2,1)S(1)} %collective-permute-done.14.refs_4_), channel_id=1, source_target_pairs={{1,2},{3,4},{5,6},{7,0},{2,1},{4,3},{6,5},{0,7},{9,10},{11,12},{13... | collective-permute-start | bytes 786440 | tf_op jit(solution)/shard_map/fold/ppermute | solution.py:23
  114.4 8.3 %collective-permute-start.16 = (bf16[2,128,512]{2,1,0:T(8,128)(2,1)S(1)}, bf16[2,128,512]{2,1,0:T(8,128)(2,1)S(1)}, u32[]{:S(2)}, u32[]{:S(2)}) collective-permute-start(bf16[2,128,512]{2,1,0:T(8,128)(2,1)S(1)} %collective-permute-done.11.refs_2_), channel_id=1, source_target_pairs={{1,2},{3,4},{5,6},{7,0},{2,1},{4,3},{6,5},{0,7},{9,10},{11,12},{13... | collective-permute-start | bytes 786440 | tf_op jit(solution)/shard_map/fold/ppermute | solution.py:23
  117.5 7.4 %collective-permute-start.17 = (bf16[2,128,512]{2,1,0:T(8,128)(2,1)S(1)}, bf16[2,128,512]{2,1,0:T(8,128)(2,1)S(1)}, u32[]{:S(2)}, u32[]{:S(2)}) collective-permute-start(bf16[2,128,512]{2,1,0:T(8,128)(2,1)S(1)} %collective-permute-done.15.refs_5_), channel_id=1, source_target_pairs={{0,1},{2,3},{4,5},{6,7},{1,0},{3,2},{5,4},{7,6},{8,9},{10,11},{12,... | collective-permute-start | bytes 786440 | tf_op jit(solution)/shard_map/fold/ppermute | solution.py:23
  183.9 13.1 %collective-permute-start.18 = (bf16[512,512]{1,0:T(8,128)(2,1)S(1)}, bf16[512,512]{1,0:T(8,128)(2,1)S(1)}, u32[]{:S(2)}, u32[]{:S(2)}) collective-permute-start(bf16[512,512]{1,0:T(8,128)(2,1)S(1)} %all_gather.7), channel_id=1, source_target_pairs={{0,8},{8,0},{1,9},{9,1},{2,10},{10,2},{3,11},{11,3},{4,12},{12,4},... | collective-permute-start | bytes 1572872 | tf_op jit(solution)/shard_map/gather_core/ppermute | solution.py:46

commit v10 on v9

--- a/solution.py
+++ b/solution.py
@@ -76,32 +76,48 @@
     return lax.rem(2 * lax.rem(pair, FEAT // 2) + member + FEAT - chain, FEAT)
 
 
-def aggregate_kernel(me_ref, ids_ref, counts_ref, slices_ref, tiles_ref, weight_ref, agg_ref, *part_refs):
-    blocks, _, width = slices_ref.shape
-    slots = tiles_ref.shape[1]
-    ones = jnp.ones((slots * tiles_ref.shape[3], 128), jnp.bfloat16)
-    for own in range(blocks):
-        lhs = [
-            jnp.where(s < counts_ref[own], tiles_ref[own, s], jnp.zeros((), jnp.bfloat16)) for s in range(slots)
-        ]
-        rhs = [slices_ref[ids_ref[own, s]] for s in range(slots)]
-        lhs, rhs = jnp.concatenate(lhs, axis=1), jnp.concatenate(rhs, axis=0)
-        summed = jnp.dot(lhs, rhs, preferred_element_type=jnp.float32)
-        degree = jnp.dot(lhs, ones, preferred_element_type=jnp.float32)
-        agg_ref[own] = (summed / jnp.concatenate([degree] * (width // 128), axis=1)).astype(jnp.bfloat16)
-    project_kernel((3,), me_ref, agg_ref, weight_ref, *part_refs)
+def mean_block(own, ids_ref, counts_ref, slices_ref, tiles_ref):
+    width, slots = slices_ref.shape[2], tiles_ref.shape[1]
+    lhs = [jnp.where(s < counts_ref[own], tiles_ref[own, s], jnp.zeros((), jnp.bfloat16)) for s in range(slots)]
+    rhs = [slices_ref[ids_ref[own, s]] for s in range(slots)]
+    lhs, rhs = jnp.concatenate(lhs, axis=1), jnp.concatenate(rhs, axis=0)
+    summed = jnp.dot(lhs, rhs, preferred_element_type=jnp.float32)
+    degree = jnp.dot(lhs, jnp.ones((lhs.shape[1], 128), jnp.bfloat16), preferred_element_type=jnp.float32)
+    return (summed / jnp.concatenate([degree] * (width // 128), axis=1)).astype(jnp.bfloat16)
+
+
+def far_kernel(me_ref, ids_ref, counts_ref, slices_ref, tiles_ref, weight_ref, *part_refs):
+    for chain, part_ref in enumerate(part_refs):
+        _, rows, cols = part_ref.shape
+        blocks = [pair_block(me_ref[0], chain, 3, member) for member in range(2)]
+        lhs = jnp.concatenate([mean_block(own, ids_ref, counts_ref, slices_ref, tiles_ref) for own in blocks], axis=0)
+        parts = jnp.dot(lhs, weight_ref[:, chain * cols:(chain + 1) * cols], preferred_element_type=jnp.float32)
+        part_ref[...] = parts.astype(jnp.bfloat16).reshape(2, rows, cols)
+
+
+def near_kernel(me_ref, ids_ref, counts_ref, slices_ref, tiles_ref, weight_ref, agg_ref, *part_refs):
+    for own in range(slices_ref.shape[0]):
+        agg_ref[own] = mean_block(own, ids_ref, counts_ref, slices_ref, tiles_ref)
+    project_kernel((0, 1, 2), me_ref, agg_ref, weight_ref, *part_refs)
 
 
 def aggregate(me, ids, counts, slices, tiles, weight):
     vmem, smem = pl.BlockSpec(memory_space=pltpu.VMEM), pl.BlockSpec(memory_space=pltpu.SMEM)
     pair = jax.ShapeDtypeStruct((2, slices.shape[1], weight.shape[1] // 2), jnp.bfloat16)
-    return pl.pallas_call(
-        aggregate_kernel,
-        out_shape=[jax.ShapeDtypeStruct(slices.shape, jnp.bfloat16), pair, pair],
-        in_specs=[smem] * 3 + [vmem] * 3,
-        out_specs=[vmem] * 3,
-        compiler_params=pltpu.CompilerParams(vmem_limit_bytes=16 * 2**20),
-    )(me.reshape(1), ids, counts, slices, tiles, weight)
+    whole = jax.ShapeDtypeStruct(slices.shape, jnp.bfloat16)
+
+    def call(kernel, out):
+        return pl.pallas_call(
+            kernel,
+            out_shape=out,
+            in_specs=[smem] * 3 + [vmem] * 3,
+            out_specs=[vmem] * len(out),
+            compiler_params=pltpu.CompilerParams(vmem_limit_bytes=16 * 2**20),
+        )(me.reshape(1), ids, counts, slices, tiles, weight)
+
+    far = call(far_kernel, [pair] * 2)
+    agg, *near = call(near_kernel, [whole] + [pair] * 6)
+    return agg, [[*near[3 * chain:3 * chain + 3], far[chain]] for chain in range(2)]
 
 
 def project_kernel(wanted, me_ref, agg_ref, weight_ref, *part_refs):
@@ -116,20 +132,6 @@
         parts = parts.astype(jnp.bfloat16)
         for i in range(2 * count):
             refs[i // 2][i % 2] = parts[i * rows:(i + 1) * rows]
-
-
-def project(wanted, me, agg, weight):
-    vmem = pl.BlockSpec(memory_space=pltpu.VMEM)
-    pair = jax.ShapeDtypeStruct((2, agg.shape[1], weight.shape[1] // 2), jnp.bfloat16)
-    count = len(wanted)
-    parts = pl.pallas_call(
-        functools.partial(project_kernel, wanted),
-        out_shape=[pair] * (2 * count),
-        in_specs=[pl.BlockSpec(memory_space=pltpu.SMEM), vmem, vmem],
-        out_specs=[vmem] * (2 * count),
-        compiler_params=pltpu.CompilerParams(vmem_limit_bytes=16 * 2**20),
-    )(me.reshape(1), agg, weight)
-    return parts[:count], parts[count:]
 
 
 def add(a, b):
@@ -198,10 +200,8 @@
     with jax.named_scope("pick"):
         slices = lax.all_to_all(pick(feature_table, sample_ids, block_total), "feat", 0, 0)
     with jax.named_scope("aggregate"):
-        agg, *far = aggregate(me, block_ids, block_counts, slices, block_tiles, weight)
+        agg, parts = aggregate(me, block_ids, block_counts, slices, block_tiles, weight)
         other_agg = lax.ppermute(agg, "core", SWAP)
-        near = project((0, 1, 2), me, agg, weight)
-        parts = [[*near[chain], far[chain]] for chain in range(2)]
     with jax.named_scope("preact"):
         preact, other_agg = lax.optimization_barrier((chain_sum(parts), other_agg))
     with jax.named_scope("grad"):

time: 199 us -> 198 us (level)
  waiting for transfers between devices: 56.2 us -> 41.9 us
  starting transfers between devices: 70 us -> 82.9 us
    ppermute x16, starting transfers between devices: 36 us -> 51.2 us  [with_neighbour(): return lax.ppermute(block, 'feat', neighbours(chain, odd_step))]
    ppermute x16, waiting for transfers between devices: 29.9 us -> 15.6 us  [with_neighbour(): return lax.ppermute(block, 'feat', neighbours(chain, odd_step))]
    ppermute x1, starting transfers between devices: 11.5 us -> 9.14 us  [shards(): other_agg = lax.ppermute(agg, 'core', SWAP)]
    unnamed x15 -> x25, local copies, waits for them, and re-layouts: 2.91 us -> 4.33 us
  transfers between devices with their start and end apart: 20 -> 20, of which waited for: 13 -> 11; matrix products, arithmetic and copies ran while one was open for 0% -> 0% of each run, Pallas kernels for 1% -> 2%
where the time goes in v10:
time: 198 us; the launch traced here: 197 us
  starting transfers between devices  82.9 us (42%)
  blocking collectives  56.9 us (29%)
  waiting for transfers between devices  41.9 us (21%)
  Pallas kernels  6.16 us (3%)
  local copies, waits for them, and re-layouts  4.33 us (2%)
  other arithmetic  4.17 us (2%)
    ppermute x16, starting transfers between devices, with_neighbour(): return lax.ppermute(block, 'feat', neighbours(chain, odd_step))  51.2 us
    all_to_all x1, waiting for transfers between devices, shards(): lax.all_to_all(pick(feature_table, sample_ids, block_total), 'feat', 0, 0)  24.8 us
    all_gather x1, blocking collectives, group_sum(): lax.all_gather(part.astype(jnp.bfloat16), ('zo', 'zi'), axis=0, tiled=True)  24.2 us
    all_to_all x1, blocking collectives, exchange_sum(): got = lax.all_to_all(parts, axis, 0, 0)  22.1 us
    ppermute x16, waiting for transfers between devices, with_neighbour(): return lax.ppermute(block, 'feat', neighbours(chain, odd_step))  15.6 us
    ppermute x1, starting transfers between devices, group_sum(): other = lax.ppermute(part, 'core', SWAP)  11.6 us
    all_gather x1, blocking collectives, group_sum(): part = lax.all_gather(part, 'x', axis=0, tiled=True)  10.5 us
    ppermute x1, starting transfers between devices, shards(): other_agg = lax.ppermute(agg, 'core', SWAP)  9.14 us
  transfers between devices with their start and end apart: 20, of which 11 were waited for; matrix products, arithmetic and copies ran while one was open for 0% of the time, Pallas kernels for 2%

profile of v10, /device:TPU:1, one launch (start us, length us, event | category | flops | bytes accessed | tf_op | source)
XLA Modules:
  0.0 197.4 jit_solution(11775782700758409402)
XLA Ops:
  4.4 7.7 %all-to-all-start = ((bf16[8,128,512]{2,1,0:T(8,128)(2,1)}), bf16[8,128,512]{2,1,0:T(8,128)(2,1)S(1)}, u32[]{:S(2)}, u32[]{:S(2)}) async-start(bf16[8,128,512]{2,1,0:T(8,128)(2,1)} %copy-done.4), calls=%async_computation | async-start | bytes 2097152 | tf_op jit(solution)/shard_map/pick/all_to_all | solution.py:201
  12.1 24.8 %all-to-all-done.slices_ref = bf16[8,128,512]{2,1,0:T(8,128)(2,1)S(1)} async-done(((bf16[8,128,512]{2,1,0:T(8,128)(2,1)}), bf16[8,128,512]{2,1,0:T(8,128)(2,1)S(1)}, u32[]{:S(2)}, u32[]{:S(2)}) %all-to-all-start) | async-done | bytes 1048608 | tf_op jit(solution)/shard_map/pick/all_to_all | solution.py:201
  36.9 1.6 aggregate.2
  38.5 1.9 collective-permute-start
  40.5 1.9 collective-permute-start.4
  42.4 2.5 %aggregate.3 = (bf16[8,128,512]{2,1,0:T(8,128)(2,1)S(1)}, bf16[2,128,512]{2,1,0:T(8,128)(2,1)S(1)}, bf16[2,128,512]{2,1,0:T(8,128)(2,1)S(1)}, bf16[2,128,512]{2,...) custom-call(s32[1]{0:T(128)} %bitcast.me_ref, ...), custom_call_target="tpu_custom_call" | custom-call | tf_op jit(solution)/shard_map/aggregate/pallas_call | solution.py:110
  47.0 3.3 %collective-permute-start.1 = (bf16[2,128,512]{2,1,0:T(8,128)(2,1)S(1)}, bf16[2,128,512]{2,1,0:T(8,128)(2,1)S(1)}, u32[]{:S(2)}, u32[]{:S(2)}) collective-permute-start(bf16[2,128,512]{2,1,0:T(8,128)(2,1)S(1)} %add_convert_fusion.3), channel_id=1, source_target_pairs={{0,1},{2,3},{4,5},{6,7},{1,0},{3,2},{5,4},{7,6},{8,9},{10,11},{12,... | collective-permute-start | bytes 786440 | tf_op jit(solution)/shard_map/preact/ppermute | solution.py:23
  50.3 4.6 %collective-permute-start.5 = (bf16[2,128,512]{2,1,0:T(8,128)(2,1)S(1)}, bf16[2,128,512]{2,1,0:T(8,128)(2,1)S(1)}, u32[]{:S(2)}, u32[]{:S(2)}) collective-permute-start(bf16[2,128,512]{2,1,0:T(8,128)(2,1)S(1)} %add_convert_fusion.1), channel_id=1, source_target_pairs={{1,2},{3,4},{5,6},{7,0},{2,1},{4,3},{6,5},{0,7},{9,10},{11,12},{13... | collective-permute-start | bytes 786440 | tf_op jit(solution)/shard_map/preact/ppermute | solution.py:23
  55.8 4.9 %collective-permute-start.2 = (bf16[2,128,512]{2,1,0:T(8,128)(2,1)S(1)}, bf16[2,128,512]{2,1,0:T(8,128)(2,1)S(1)}, u32[]{:S(2)}, u32[]{:S(2)}) collective-permute-start(bf16[2,128,512]{2,1,0:T(8,128)(2,1)S(1)} %add_convert_fusion.2), channel_id=1, source_target_pairs={{1,2},{3,4},{5,6},{7,0},{2,1},{4,3},{6,5},{0,7},{9,10},{11,12},{13... | collective-permute-start | bytes 786440 | tf_op jit(solution)/shard_map/preact/ppermute | solution.py:23
  60.7 1.9 collective-permute-start.6
  62.7 9.1 %collective-permute-start.8 = (bf16[8,128,512]{2,1,0:T(8,128)(2,1)S(1)}, bf16[8,128,512]{2,1,0:T(8,128)(2,1)S(1)}, u32[]{:S(2)}, u32[]{:S(2)}) collective-permute-start(bf16[8,128,512]{2,1,0:T(8,128)(2,1)S(1)} %copy-done.3), channel_id=1, source_target_pairs={{0,8},{8,0},{1,9},{9,1},{2,10},{10,2},{3,11},{11,3},{4,12},{12,4},... | collective-permute-start | bytes 3145736 | tf_op jit(solution)/shard_map/aggregate/ppermute | solution.py:204
  71.9 3.8 %collective-permute-start.3 = (bf16[128,512]{1,0:T(8,128)(2,1)S(1)}, bf16[128,512]{1,0:T(8,128)(2,1)S(1)}, u32[]{:S(2)}, u32[]{:S(2)}) collective-permute-start(bf16[128,512]{1,0:T(8,128)(2,1)S(1)} %fusion.1), channel_id=1, source_target_pairs={{0,1},{2,3},{4,5},{6,7},{1,0},{3,2},{5,4},{7,6},{8,9},{10,11},{12,... | collective-permute-start | bytes 393224 | tf_op jit(solution)/shard_map/preact/ppermute | solution.py:23
  75.8 4.6 %collective-permute-start.7 = (bf16[128,512]{1,0:T(8,128)(2,1)S(1)}, bf16[128,512]{1,0:T(8,128)(2,1)S(1)}, u32[]{:S(2)}, u32[]{:S(2)}) collective-permute-start(bf16[128,512]{1,0:T(8,128)(2,1)S(1)} %fusion.2), channel_id=1, source_target_pairs={{1,2},{3,4},{5,6},{7,0},{2,1},{4,3},{6,5},{0,7},{9,10},{11,12},{13... | collective-permute-start | bytes 393224 | tf_op jit(solution)/shard_map/preact/ppermute | solution.py:23
  80.5 3.0 %collective-permute-done.7 = bf16[128,512]{1,0:T(8,128)(2,1)S(1)} collective-permute-done((bf16[128,512]{1,0:T(8,128)(2,1)S(1)}, bf16[128,512]{1,0:T(8,128)(2,1)S(1)}, u32[]{:S(2)}, u32[]{:S(2)}) %collective-permute-start.7) | collective-permute-done | bytes 131104 | tf_op jit(solution)/shard_map/preact/ppermute | solution.py:23
  84.6 3.2 %collective-permute-start.12 = (bf16[128,512]{1,0:T(8,128)(2,1)S(1)}, bf16[128,512]{1,0:T(8,128)(2,1)S(1)}, u32[]{:S(2)}, u32[]{:S(2)}) collective-permute-start(bf16[128,512]{1,0:T(8,128)(2,1)S(1)} %get-tuple-element.32), channel_id=1, source_target_pairs={{0,8},{8,0},{1,9},{9,1},{2,10},{10,2},{3,11},{11,3},{4,12},{12,4},... | collective-permute-start | bytes 393224 | tf_op jit(solution)/shard_map/swap/ppermute | solution.py:222
  87.9 1.9 collective-permute-start.9
  89.8 4.6 %collective-permute-start.13 = (bf16[128,512]{1,0:T(8,128)(2,1)S(1)}, bf16[128,512]{1,0:T(8,128)(2,1)S(1)}, u32[]{:S(2)}, u32[]{:S(2)}) collective-permute-start(bf16[128,512]{1,0:T(8,128)(2,1)S(1)} %collective-permute-done.12), channel_id=1, source_target_pairs={{1,2},{3,4},{5,6},{7,0},{2,1},{4,3},{6,5},{0,7},{9,10},{11,12},{13... | collective-permute-start | bytes 393224 | tf_op jit(solution)/shard_map/fold/ppermute | solution.py:23
  95.0 4.6 %collective-permute-start.10 = (bf16[2,128,512]{2,1,0:T(8,128)(2,1)S(1)}, bf16[2,128,512]{2,1,0:T(8,128)(2,1)S(1)}, u32[]{:S(2)}, u32[]{:S(2)}) collective-permute-start(bf16[2,128,512]{2,1,0:T(8,128)(2,1)S(1)} %pad_maximum_fusion.1.refs_0_), channel_id=1, source_target_pairs={{1,2},{3,4},{5,6},{7,0},{2,1},{4,3},{6,5},{0,7},{9,10},{11,12},{13... | collective-permute-start | bytes 786440 | tf_op jit(solution)/shard_map/fold/ppermute | solution.py:23
  99.6 1.9 collective-permute-start.14
  101.5 3.6 %collective-permute-done.10.refs_1_ = bf16[2,128,512]{2,1,0:T(8,128)(2,1)S(1)} collective-permute-done((bf16[2,128,512]{2,1,0:T(8,128)(2,1)S(1)}, bf16[2,128,512]{2,1,0:T(8,128)(2,1)S(1)}, u32[]{:S(2)}, u32[]{:S(2)}) %collective-permute-start.10) | collective-permute-done | bytes 262176 | tf_op jit(solution)/shard_map/fold/ppermute | solution.py:23
  105.1 1.9 collective-permute-start.11
  108.2 3.4 %collective-permute-start.15 = (bf16[2,128,512]{2,1,0:T(8,128)(2,1)S(1)}, bf16[2,128,512]{2,1,0:T(8,128)(2,1)S(1)}, u32[]{:S(2)}, u32[]{:S(2)}) collective-permute-start(bf16[2,128,512]{2,1,0:T(8,128)(2,1)S(1)} %collective-permute-done.14.refs_4_), channel_id=1, source_target_pairs={{1,2},{3,4},{5,6},{7,0},{2,1},{4,3},{6,5},{0,7},{9,10},{11,12},{13... | collective-permute-start | bytes 786440 | tf_op jit(solution)/shard_map/fold/ppermute | solution.py:23
  111.6 1.8 collective-permute-done.11.refs_2_
  113.4 4.3 %collective-permute-start.16 = (bf16[2,128,512]{2,1,0:T(8,128)(2,1)S(1)}, bf16[2,128,512]{2,1,0:T(8,128)(2,1)S(1)}, u32[]{:S(2)}, u32[]{:S(2)}) collective-permute-start(bf16[2,128,512]{2,1,0:T(8,128)(2,1)S(1)} %collective-permute-done.11.refs_2_), channel_id=1, source_target_pairs={{1,2},{3,4},{5,6},{7,0},{2,1},{4,3},{6,5},{0,7},{9,10},{11,12},{13... | collective-permute-start | bytes 786440 | tf_op jit(solution)/shard_map/fold/ppermute | solution.py:23
  117.7 1.9 collective-permute-start.17
  120.6 2.1 %collective-permute-done.16.refs_1_ = bf16[2,128,512]{2,1,0:T(8,128)(2,1)S(1)} collective-permute-done((bf16[2,128,512]{2,1,0:T(8,128)(2,1)S(1)}, bf16[2,128,512]{2,1,0:T(8,128)(2,1)S(1)}, u32[]{:S(2)}, u32[]{:S(2)}) %collective-permute-start.16) | collective-permute-done | bytes 262176 | tf_op jit(solution)/shard_map/fold/ppermute | solution.py:23
  122.7 2.3 %collective-permute-done.17.refs_2_ = bf16[2,128,512]{2,1,0:T(8,128)(2,1)S(1)} collective-permute-done((bf16[2,128,512]{2,1,0:T(8,128)(2,1)S(1)}, bf16[2,128,512]{2,1,0:T(8,128)(2,1)S(1)}, u32[]{:S(2)}, u32[]{:S(2)}) %collective-permute-start.17) | collective-permute-done | bytes 262176 | tf_op jit(solution)/shard_map/fold/ppermute | solution.py:23
  125.6 22.1 %all_to_all.10 = bf16[16,32,512]{2,1,0:T(8,128)(2,1)S(1)} all-to-all(bf16[16,32,512]{2,1,0:T(8,128)(2,1)S(1)} %bitcast.19), channel_id=1, replica_groups=mesh['x'=4,'zo'=3,'zi'=4,'core'=2,'feat'=8] {'x','zi'}, dimensions={0} | all-to-all | bytes 1048576 | tf_op jit(solution)/shard_map/sum_x_zi/all_to_all | solution.py:31
  147.8 24.2 %all_gather.6 = bf16[384,512]{1,0:T(8,128)(2,1)S(1)} all-gather(bf16[32,512]{1,0:T(8,128)(2,1)S(1)} %reduce_sum.44), channel_id=1, replica_groups=mesh['x'=4,'zo'=3,'zi'=4,'core'=2,'feat'=8] {'zo','zi'}, dimensions={0}, use_global_device_ids=true | all-gather | bytes 425984 | tf_op jit(solution)/shard_map/sum_z/all_gather | solution.py:40
  172.0 10.5 %all_gather.7 = bf16[512,512]{1,0:T(8,128)(2,1)S(1)} all-gather(bf16[128,512]{1,0:T(8,128)(2,1)S(1)} %reduce_sum.45), channel_id=1, replica_groups=mesh['x'=4,'zo'=3,'zi'=4,'core'=2,'feat'=8] {'x'}, dimensions={0}, use_global_device_ids=true | all-gather | bytes 655360 | tf_op jit(solution)/shard_map/gather_x/all_gather | solution.py:44
  182.6 11.6 %collective-permute-start.18 = (bf16[512,512]{1,0:T(8,128)(2,1)S(1)}, bf16[512,512]{1,0:T(8,128)(2,1)S(1)}, u32[]{:S(2)}, u32[]{:S(2)}) collective-permute-start(bf16[512,512]{1,0:T(8,128)(2,1)S(1)} %all_gather.7), channel_id=1, source_target_pairs={{0,8},{8,0},{1,9},{9,1},{2,10},{10,2},{3,11},{11,3},{4,12},{12,4},... | collective-permute-start | bytes 1572872 | tf_op jit(solution)/shard_map/gather_core/ppermute | solution.py:46
  195.8 1.6 maximum_convert_fusion
  (65 shorter events, 13.2 us)
Async XLA Ops:
  1.3 1.6 copy-start.5
  2.9 9.1 %copy-start.11 = (s32[8,4]{0,1:T(4,128)S(1)}, s32[8,4]{0,1:T(4,128)}, u32[]{:S(2)}) copy-start(s32[8,4]{0,1:T(4,128)} %param.9) | copy-start | bytes 388
  2.9 34.0 %copy-start = (bf16[8,4,128,128]{3,2,1,0:T(8,128)(2,1)S(1)}, bf16[8,4,128,128]{3,2,1,0:T(8,128)(2,1)}, u32[]{:S(2)}) copy-start(bf16[8,4,128,128]{3,2,1,0:T(8,128)(2,1)} %tiles_ref.3) | copy-start | bytes 3145732
  2.9 34.0 %copy-start.1 = (bf16[512,1024]{1,0:T(8,128)(2,1)S(1)}, bf16[512,1024]{1,0:T(8,128)(2,1)}, u32[]{:S(2)}) copy-start(bf16[512,1024]{1,0:T(8,128)(2,1)} %weight_ref.3) | copy-start | bytes 3145732
  2.9 34.0 %copy-start.8 = (s32[8]{0:T(128)S(1)}, s32[8]{0:T(128)}, u32[]{:S(2)}) copy-start(s32[8]{0:T(128)} %counts_ref.3) | copy-start | bytes 100
  3.4 1.0 copy-start.4
  4.4 32.5 %all-to-all-start = ((bf16[8,128,512]{2,1,0:T(8,128)(2,1)}), bf16[8,128,512]{2,1,0:T(8,128)(2,1)S(1)}, u32[]{:S(2)}, u32[]{:S(2)}) async-start(bf16[8,128,512]{2,1,0:T(8,128)(2,1)} %copy-done.4), calls=%async_computation | async-start | bytes 2097152 | tf_op jit(solution)/shard_map/pick/all_to_all | solution.py:201
  38.5 8.3 %collective-permute-start = (bf16[2,128,512]{2,1,0:T(8,128)(2,1)S(1)}, bf16[2,128,512]{2,1,0:T(8,128)(2,1)S(1)}, u32[]{:S(2)}, u32[]{:S(2)}) collective-permute-start(bf16[2,128,512]{2,1,0:T(8,128)(2,1)S(1)} %get-tuple-element.13), channel_id=1, source_target_pairs={{1,2},{3,4},{5,6},{7,0},{2,1},{4,3},{6,5},{0,7},{9,10},{11,12},{13... | collective-permute-start | bytes 786440 | tf_op jit(solution)/shard_map/preact/ppermute | solution.py:23
  40.5 9.7 %collective-permute-start.4 = (bf16[2,128,512]{2,1,0:T(8,128)(2,1)S(1)}, bf16[2,128,512]{2,1,0:T(8,128)(2,1)S(1)}, u32[]{:S(2)}, u32[]{:S(2)}) collective-permute-start(bf16[2,128,512]{2,1,0:T(8,128)(2,1)S(1)} %get-tuple-element.17), channel_id=1, source_target_pairs={{0,1},{2,3},{4,5},{6,7},{1,0},{3,2},{5,4},{7,6},{8,9},{10,11},{12,... | collective-permute-start | bytes 786440 | tf_op jit(solution)/shard_map/preact/ppermute | solution.py:23
  45.0 1.0 copy-start.2
  45.9 0.7 copy-start.6
  46.9 15.8 %copy-start.3 = (bf16[8,128,512]{2,1,0:T(8,128)(2,1)S(1)}, bf16[8,128,512]{2,1,0:T(8,128)(2,1)}, u32[]{:S(2)}) copy-start(bf16[8,128,512]{2,1,0:T(8,128)(2,1)} %copy-done.2) | copy-start | bytes 3145732
  46.9 25.0 %copy-start.7 = (bf16[2,128,512]{2,1,0:T(8,128)(2,1)S(1)}, bf16[2,128,512]{2,1,0:T(8,128)(2,1)}, u32[]{:S(2)}) copy-start(bf16[2,128,512]{2,1,0:T(8,128)(2,1)} %copy-done.6) | copy-start | bytes 786436
  47.0 8.8 %collective-permute-start.1 = (bf16[2,128,512]{2,1,0:T(8,128)(2,1)S(1)}, bf16[2,128,512]{2,1,0:T(8,128)(2,1)S(1)}, u32[]{:S(2)}, u32[]{:S(2)}) collective-permute-start(bf16[2,128,512]{2,1,0:T(8,128)(2,1)S(1)} %add_convert_fusion.3), channel_id=1, source_target_pairs={{0,1},{2,3},{4,5},{6,7},{1,0},{3,2},{5,4},{7,6},{8,9},{10,11},{12,... | collective-permute-start | bytes 786440 | tf_op jit(solution)/shard_map/preact/ppermute | solution.py:23
  50.3 10.3 %collective-permute-start.5 = (bf16[2,128,512]{2,1,0:T(8,128)(2,1)S(1)}, bf16[2,128,512]{2,1,0:T(8,128)(2,1)S(1)}, u32[]{:S(2)}, u32[]{:S(2)}) collective-permute-start(bf16[2,128,512]{2,1,0:T(8,128)(2,1)S(1)} %add_convert_fusion.1), channel_id=1, source_target_pairs={{1,2},{3,4},{5,6},{7,0},{2,1},{4,3},{6,5},{0,7},{9,10},{11,12},{13... | collective-permute-start | bytes 786440 | tf_op jit(solution)/shard_map/preact/ppermute | solution.py:23
  55.8 16.1 %collective-permute-start.2 = (bf16[2,128,512]{2,1,0:T(8,128)(2,1)S(1)}, bf16[2,128,512]{2,1,0:T(8,128)(2,1)S(1)}, u32[]{:S(2)}, u32[]{:S(2)}) collective-permute-start(bf16[2,128,512]{2,1,0:T(8,128)(2,1)S(1)} %add_convert_fusion.2), channel_id=1, source_target_pairs={{1,2},{3,4},{5,6},{7,0},{2,1},{4,3},{6,5},{0,7},{9,10},{11,12},{13... | collective-permute-start | bytes 786440 | tf_op jit(solution)/shard_map/preact/ppermute | solution.py:23
  60.7 15.0 %collective-permute-start.6 = (bf16[2,128,512]{2,1,0:T(8,128)(2,1)S(1)}, bf16[2,128,512]{2,1,0:T(8,128)(2,1)S(1)}, u32[]{:S(2)}, u32[]{:S(2)}) collective-permute-start(bf16[2,128,512]{2,1,0:T(8,128)(2,1)S(1)} %add_convert_fusion), channel_id=1, source_target_pairs={{0,1},{2,3},{4,5},{6,7},{1,0},{3,2},{5,4},{7,6},{8,9},{10,11},{12,... | collective-permute-start | bytes 786440 | tf_op jit(solution)/shard_map/preact/ppermute | solution.py:23
  62.7 20.9 %collective-permute-start.8 = (bf16[8,128,512]{2,1,0:T(8,128)(2,1)S(1)}, bf16[8,128,512]{2,1,0:T(8,128)(2,1)S(1)}, u32[]{:S(2)}, u32[]{:S(2)}) collective-permute-start(bf16[8,128,512]{2,1,0:T(8,128)(2,1)S(1)} %copy-done.3), channel_id=1, source_target_pairs={{0,8},{8,0},{1,9},{9,1},{2,10},{10,2},{3,11},{11,3},{4,12},{12,4},... | collective-permute-start | bytes 3145736 | tf_op jit(solution)/shard_map/aggregate/ppermute | solution.py:204
  71.9 12.0 %copy-start.9 = (bf16[128,1024]{1,0:T(8,128)(2,1)S(1)}, bf16[128,1024]{1,0:T(8,128)(2,1)}, u32[]{:S(2)}) copy-start(bf16[128,1024]{1,0:T(8,128)(2,1)} %param.13) | copy-start | bytes 786436
  71.9 8.5 %collective-permute-start.3 = (bf16[128,512]{1,0:T(8,128)(2,1)S(1)}, bf16[128,512]{1,0:T(8,128)(2,1)S(1)}, u32[]{:S(2)}, u32[]{:S(2)}) collective-permute-start(bf16[128,512]{1,0:T(8,128)(2,1)S(1)} %fusion.1), channel_id=1, source_target_pairs={{0,1},{2,3},{4,5},{6,7},{1,0},{3,2},{5,4},{7,6},{8,9},{10,11},{12,... | collective-permute-start | bytes 393224 | tf_op jit(solution)/shard_map/preact/ppermute | solution.py:23
  75.8 7.7 %collective-permute-start.7 = (bf16[128,512]{1,0:T(8,128)(2,1)S(1)}, bf16[128,512]{1,0:T(8,128)(2,1)S(1)}, u32[]{:S(2)}, u32[]{:S(2)}) collective-permute-start(bf16[128,512]{1,0:T(8,128)(2,1)S(1)} %fusion.2), channel_id=1, source_target_pairs={{1,2},{3,4},{5,6},{7,0},{2,1},{4,3},{6,5},{0,7},{9,10},{11,12},{13... | collective-permute-start | bytes 393224 | tf_op jit(solution)/shard_map/preact/ppermute | solution.py:23
  84.2 36.4 %copy-start.10 = (bf16[128,1024]{1,0:T(8,128)(2,1)}, bf16[128,1024]{1,0:T(8,128)(2,1)S(1)}, u32[]{:S(2)}) copy-start(bf16[128,1024]{1,0:T(8,128)(2,1)S(1)} %get-tuple-element.27) | copy-start | bytes 786436
  84.6 5.2 %collective-permute-start.12 = (bf16[128,512]{1,0:T(8,128)(2,1)S(1)}, bf16[128,512]{1,0:T(8,128)(2,1)S(1)}, u32[]{:S(2)}, u32[]{:S(2)}) collective-permute-start(bf16[128,512]{1,0:T(8,128)(2,1)S(1)} %get-tuple-element.32), channel_id=1, source_target_pairs={{0,8},{8,0},{1,9},{9,1},{2,10},{10,2},{3,11},{11,3},{4,12},{12,4},... | collective-permute-start | bytes 393224 | tf_op jit(solution)/shard_map/swap/ppermute | solution.py:222
  87.9 7.0 %collective-permute-start.9 = (bf16[128,512]{1,0:T(8,128)(2,1)S(1)}, bf16[128,512]{1,0:T(8,128)(2,1)S(1)}, u32[]{:S(2)}, u32[]{:S(2)}) collective-permute-start(bf16[128,512]{1,0:T(8,128)(2,1)S(1)} %get-tuple-element.33), channel_id=1, source_target_pairs={{0,1},{2,3},{4,5},{6,7},{1,0},{3,2},{5,4},{7,6},{8,9},{10,11},{12,... | collective-permute-start | bytes 393224 | tf_op jit(solution)/shard_map/fold/ppermute | solution.py:23
  89.8 9.7 %collective-permute-start.13 = (bf16[128,512]{1,0:T(8,128)(2,1)S(1)}, bf16[128,512]{1,0:T(8,128)(2,1)S(1)}, u32[]{:S(2)}, u32[]{:S(2)}) collective-permute-start(bf16[128,512]{1,0:T(8,128)(2,1)S(1)} %collective-permute-done.12), channel_id=1, source_target_pairs={{1,2},{3,4},{5,6},{7,0},{2,1},{4,3},{6,5},{0,7},{9,10},{11,12},{13... | collective-permute-start | bytes 393224 | tf_op jit(solution)/shard_map/fold/ppermute | solution.py:23
  95.0 10.1 %collective-permute-start.10 = (bf16[2,128,512]{2,1,0:T(8,128)(2,1)S(1)}, bf16[2,128,512]{2,1,0:T(8,128)(2,1)S(1)}, u32[]{:S(2)}, u32[]{:S(2)}) collective-permute-start(bf16[2,128,512]{2,1,0:T(8,128)(2,1)S(1)} %pad_maximum_fusion.1.refs_0_), channel_id=1, source_target_pairs={{1,2},{3,4},{5,6},{7,0},{2,1},{4,3},{6,5},{0,7},{9,10},{11,12},{13... | collective-permute-start | bytes 786440 | tf_op jit(solution)/shard_map/fold/ppermute | solution.py:23
  99.6 8.6 %collective-permute-start.14 = (bf16[2,128,512]{2,1,0:T(8,128)(2,1)S(1)}, bf16[2,128,512]{2,1,0:T(8,128)(2,1)S(1)}, u32[]{:S(2)}, u32[]{:S(2)}) collective-permute-start(bf16[2,128,512]{2,1,0:T(8,128)(2,1)S(1)} %pad_maximum_fusion.2.refs_3_), channel_id=1, source_target_pairs={{0,1},{2,3},{4,5},{6,7},{1,0},{3,2},{5,4},{7,6},{8,9},{10,11},{12,... | collective-permute-start | bytes 786440 | tf_op jit(solution)/shard_map/fold/ppermute | solution.py:23
  105.1 8.3 %collective-permute-start.11 = (bf16[2,128,512]{2,1,0:T(8,128)(2,1)S(1)}, bf16[2,128,512]{2,1,0:T(8,128)(2,1)S(1)}, u32[]{:S(2)}, u32[]{:S(2)}) collective-permute-start(bf16[2,128,512]{2,1,0:T(8,128)(2,1)S(1)} %collective-permute-done.10.refs_1_), channel_id=1, source_target_pairs={{0,1},{2,3},{4,5},{6,7},{1,0},{3,2},{5,4},{7,6},{8,9},{10,11},{12,... | collective-permute-start | bytes 786440 | tf_op jit(solution)/shard_map/fold/ppermute | solution.py:23
  108.2 9.4 %collective-permute-start.15 = (bf16[2,128,512]{2,1,0:T(8,128)(2,1)S(1)}, bf16[2,128,512]{2,1,0:T(8,128)(2,1)S(1)}, u32[]{:S(2)}, u32[]{:S(2)}) collective-permute-start(bf16[2,128,512]{2,1,0:T(8,128)(2,1)S(1)} %collective-permute-done.14.refs_4_), channel_id=1, source_target_pairs={{1,2},{3,4},{5,6},{7,0},{2,1},{4,3},{6,5},{0,7},{9,10},{11,12},{13... | collective-permute-start | bytes 786440 | tf_op jit(solution)/shard_map/fold/ppermute | solution.py:23
  113.4 9.4 %collective-permute-start.16 = (bf16[2,128,512]{2,1,0:T(8,128)(2,1)S(1)}, bf16[2,128,512]{2,1,0:T(8,128)(2,1)S(1)}, u32[]{:S(2)}, u32[]{:S(2)}) collective-permute-start(bf16[2,128,512]{2,1,0:T(8,128)(2,1)S(1)} %collective-permute-done.11.refs_2_), channel_id=1, source_target_pairs={{1,2},{3,4},{5,6},{7,0},{2,1},{4,3},{6,5},{0,7},{9,10},{11,12},{13... | collective-permute-start | bytes 786440 | tf_op jit(solution)/shard_map/fold/ppermute | solution.py:23
  117.7 7.4 %collective-permute-start.17 = (bf16[2,128,512]{2,1,0:T(8,128)(2,1)S(1)}, bf16[2,128,512]{2,1,0:T(8,128)(2,1)S(1)}, u32[]{:S(2)}, u32[]{:S(2)}) collective-permute-start(bf16[2,128,512]{2,1,0:T(8,128)(2,1)S(1)} %collective-permute-done.15.refs_5_), channel_id=1, source_target_pairs={{0,1},{2,3},{4,5},{6,7},{1,0},{3,2},{5,4},{7,6},{8,9},{10,11},{12,... | collective-permute-start | bytes 786440 | tf_op jit(solution)/shard_map/fold/ppermute | solution.py:23
  182.6 13.1 %collective-permute-start.18 = (bf16[512,512]{1,0:T(8,128)(2,1)S(1)}, bf16[512,512]{1,0:T(8,128)(2,1)S(1)}, u32[]{:S(2)}, u32[]{:S(2)}) collective-permute-start(bf16[512,512]{1,0:T(8,128)(2,1)S(1)} %all_gather.7), channel_id=1, source_target_pairs={{0,8},{8,0},{1,9},{9,1},{2,10},{10,2},{3,11},{11,3},{4,12},{12,4},... | collective-permute-start | bytes 1572872 | tf_op jit(solution)/shard_map/gather_core/ppermute | solution.py:46

commit v11 on v10

--- a/solution.py
+++ b/solution.py
@@ -65,7 +65,7 @@
         out_shape=jax.ShapeDtypeStruct((slices, ids.shape[0], table.shape[1] // slices), table.dtype),
         in_specs=[vmem, vmem],
         out_specs=vmem,
-        compiler_params=pltpu.CompilerParams(vmem_limit_bytes=16 * 2**20),
+        compiler_params=pltpu.CompilerParams(vmem_limit_bytes=60 * 2**20),
     )(wanted, table)
 
 

time: 198 us -> 199 us (level)
  Pallas kernels: 6.16 us -> 9.03 us
  local copies, waits for them, and re-layouts: 4.33 us -> 1.78 us
    pallas_call x1, Pallas kernels: 0.49 us -> 3.26 us  [pick(): pl.pallas_call(pick_kernel, out_shape=jax.ShapeDtypeStruct((slices, ids.s...]
    unnamed x25 -> x21, local copies, waits for them, and re-layouts: 4.33 us -> 1.78 us
where the time goes in v11:
time: 199 us; the launch traced here: 198 us
  starting transfers between devices  82.9 us (42%)
  blocking collectives  57 us (29%)
  waiting for transfers between devices  41.7 us (21%)
  Pallas kernels  9.03 us (5%)
  other arithmetic  4.8 us (2%)
    ppermute x16, starting transfers between devices, with_neighbour(): return lax.ppermute(block, 'feat', neighbours(chain, odd_step))  51.3 us
    all_to_all x1, waiting for transfers between devices, shards(): lax.all_to_all(pick(feature_table, sample_ids, block_total), 'feat', 0, 0)  24.8 us
    all_gather x1, blocking collectives, group_sum(): lax.all_gather(part.astype(jnp.bfloat16), ('zo', 'zi'), axis=0, tiled=True)  24.2 us
    all_to_all x1, blocking collectives, exchange_sum(): got = lax.all_to_all(parts, axis, 0, 0)  22.2 us
    ppermute x16, waiting for transfers between devices, with_neighbour(): return lax.ppermute(block, 'feat', neighbours(chain, odd_step))  15.4 us
    ppermute x1, starting transfers between devices, group_sum(): other = lax.ppermute(part, 'core', SWAP)  11.6 us
    all_gather x1, blocking collectives, group_sum(): part = lax.all_gather(part, 'x', axis=0, tiled=True)  10.5 us
    ppermute x1, starting transfers between devices, shards(): other_agg = lax.ppermute(agg, 'core', SWAP)  9.14 us
  transfers between devices with their start and end apart: 20, of which 11 were waited for; matrix products, arithmetic and copies ran while one was open for 0% of the time, Pallas kernels for 2%

profile of v11, /device:TPU:1, one launch (start us, length us, event | category | flops | bytes accessed | tf_op | source)
XLA Modules:
  0.0 198.3 jit_solution(11717980008527317667)
XLA Ops:
  2.0 3.3 %pick.1 = bf16[8,128,512]{2,1,0:T(8,128)(2,1)} custom-call(f32[256,128]{1,0:T(8,128)} %fusion.3.wanted_ref, bf16[256,4096]{1,0:T(8,128)(2,1)} %table_ref.1), custom_call_target="tpu_custom_call" | custom-call | tf_op jit(solution)/shard_map/pick/pallas_call | solution.py:63
  5.2 7.7 %all-to-all-start = ((bf16[8,128,512]{2,1,0:T(8,128)(2,1)}), bf16[8,128,512]{2,1,0:T(8,128)(2,1)S(1)}, u32[]{:S(2)}, u32[]{:S(2)}) async-start(bf16[8,128,512]{2,1,0:T(8,128)(2,1)} %pick.1), calls=%async_computation | async-start | bytes 2097152 | tf_op jit(solution)/shard_map/pick/all_to_all | solution.py:201
  13.0 24.8 %all-to-all-done.slices_ref = bf16[8,128,512]{2,1,0:T(8,128)(2,1)S(1)} async-done(((bf16[8,128,512]{2,1,0:T(8,128)(2,1)}), bf16[8,128,512]{2,1,0:T(8,128)(2,1)S(1)}, u32[]{:S(2)}, u32[]{:S(2)}) %all-to-all-start) | async-done | bytes 1048608 | tf_op jit(solution)/shard_map/pick/all_to_all | solution.py:201
  37.8 1.6 aggregate.2
  39.4 1.9 collective-permute-start
  41.4 1.9 collective-permute-start.4
  43.3 2.6 %aggregate.3 = (bf16[8,128,512]{2,1,0:T(8,128)(2,1)S(1)}, bf16[2,128,512]{2,1,0:T(8,128)(2,1)S(1)}, bf16[2,128,512]{2,1,0:T(8,128)(2,1)S(1)}, bf16[2,128,512]{2,...) custom-call(s32[1]{0:T(128)} %bitcast.me_ref, ...), custom_call_target="tpu_custom_call" | custom-call | tf_op jit(solution)/shard_map/aggregate/pallas_call | solution.py:110
  47.8 3.3 %collective-permute-start.1 = (bf16[2,128,512]{2,1,0:T(8,128)(2,1)S(1)}, bf16[2,128,512]{2,1,0:T(8,128)(2,1)S(1)}, u32[]{:S(2)}, u32[]{:S(2)}) collective-permute-start(bf16[2,128,512]{2,1,0:T(8,128)(2,1)S(1)} %add_convert_fusion.3), channel_id=1, source_target_pairs={{0,1},{2,3},{4,5},{6,7},{1,0},{3,2},{5,4},{7,6},{8,9},{10,11},{12,... | collective-permute-start | bytes 786440 | tf_op jit(solution)/shard_map/preact/ppermute | solution.py:23
  51.2 4.6 %collective-permute-start.5 = (bf16[2,128,512]{2,1,0:T(8,128)(2,1)S(1)}, bf16[2,128,512]{2,1,0:T(8,128)(2,1)S(1)}, u32[]{:S(2)}, u32[]{:S(2)}) collective-permute-start(bf16[2,128,512]{2,1,0:T(8,128)(2,1)S(1)} %add_convert_fusion.1), channel_id=1, source_target_pairs={{1,2},{3,4},{5,6},{7,0},{2,1},{4,3},{6,5},{0,7},{9,10},{11,12},{13... | collective-permute-start | bytes 786440 | tf_op jit(solution)/shard_map/preact/ppermute | solution.py:23
  56.6 4.9 %collective-permute-start.2 = (bf16[2,128,512]{2,1,0:T(8,128)(2,1)S(1)}, bf16[2,128,512]{2,1,0:T(8,128)(2,1)S(1)}, u32[]{:S(2)}, u32[]{:S(2)}) collective-permute-start(bf16[2,128,512]{2,1,0:T(8,128)(2,1)S(1)} %add_convert_fusion.2), channel_id=1, source_target_pairs={{1,2},{3,4},{5,6},{7,0},{2,1},{4,3},{6,5},{0,7},{9,10},{11,12},{13... | collective-permute-start | bytes 786440 | tf_op jit(solution)/shard_map/preact/ppermute | solution.py:23
  61.6 1.9 collective-permute-start.6
  63.6 9.1 %collective-permute-start.8 = (bf16[8,128,512]{2,1,0:T(8,128)(2,1)S(1)}, bf16[8,128,512]{2,1,0:T(8,128)(2,1)S(1)}, u32[]{:S(2)}, u32[]{:S(2)}) collective-permute-start(bf16[8,128,512]{2,1,0:T(8,128)(2,1)S(1)} %copy-done.3), channel_id=1, source_target_pairs={{0,8},{8,0},{1,9},{9,1},{2,10},{10,2},{3,11},{11,3},{4,12},{12,4},... | collective-permute-start | bytes 3145736 | tf_op jit(solution)/shard_map/aggregate/ppermute | solution.py:204
  72.8 3.8 %collective-permute-start.3 = (bf16[128,512]{1,0:T(8,128)(2,1)S(1)}, bf16[128,512]{1,0:T(8,128)(2,1)S(1)}, u32[]{:S(2)}, u32[]{:S(2)}) collective-permute-start(bf16[128,512]{1,0:T(8,128)(2,1)S(1)} %fusion.1), channel_id=1, source_target_pairs={{0,1},{2,3},{4,5},{6,7},{1,0},{3,2},{5,4},{7,6},{8,9},{10,11},{12,... | collective-permute-start | bytes 393224 | tf_op jit(solution)/shard_map/preact/ppermute | solution.py:23
  76.7 4.6 %collective-permute-start.7 = (bf16[128,512]{1,0:T(8,128)(2,1)S(1)}, bf16[128,512]{1,0:T(8,128)(2,1)S(1)}, u32[]{:S(2)}, u32[]{:S(2)}) collective-permute-start(bf16[128,512]{1,0:T(8,128)(2,1)S(1)} %fusion.2), channel_id=1, source_target_pairs={{1,2},{3,4},{5,6},{7,0},{2,1},{4,3},{6,5},{0,7},{9,10},{11,12},{13... | collective-permute-start | bytes 393224 | tf_op jit(solution)/shard_map/preact/ppermute | solution.py:23
  81.4 3.0 %collective-permute-done.7 = bf16[128,512]{1,0:T(8,128)(2,1)S(1)} collective-permute-done((bf16[128,512]{1,0:T(8,128)(2,1)S(1)}, bf16[128,512]{1,0:T(8,128)(2,1)S(1)}, u32[]{:S(2)}, u32[]{:S(2)}) %collective-permute-start.7) | collective-permute-done | bytes 131104 | tf_op jit(solution)/shard_map/preact/ppermute | solution.py:23
  85.5 3.2 %collective-permute-start.12 = (bf16[128,512]{1,0:T(8,128)(2,1)S(1)}, bf16[128,512]{1,0:T(8,128)(2,1)S(1)}, u32[]{:S(2)}, u32[]{:S(2)}) collective-permute-start(bf16[128,512]{1,0:T(8,128)(2,1)S(1)} %get-tuple-element.32), channel_id=1, source_target_pairs={{0,8},{8,0},{1,9},{9,1},{2,10},{10,2},{3,11},{11,3},{4,12},{12,4},... | collective-permute-start | bytes 393224 | tf_op jit(solution)/shard_map/swap/ppermute | solution.py:222
  88.7 1.9 collective-permute-start.9
  90.7 4.6 %collective-permute-start.13 = (bf16[128,512]{1,0:T(8,128)(2,1)S(1)}, bf16[128,512]{1,0:T(8,128)(2,1)S(1)}, u32[]{:S(2)}, u32[]{:S(2)}) collective-permute-start(bf16[128,512]{1,0:T(8,128)(2,1)S(1)} %collective-permute-done.12), channel_id=1, source_target_pairs={{1,2},{3,4},{5,6},{7,0},{2,1},{4,3},{6,5},{0,7},{9,10},{11,12},{13... | collective-permute-start | bytes 393224 | tf_op jit(solution)/shard_map/fold/ppermute | solution.py:23
  95.8 4.6 %collective-permute-start.10 = (bf16[2,128,512]{2,1,0:T(8,128)(2,1)S(1)}, bf16[2,128,512]{2,1,0:T(8,128)(2,1)S(1)}, u32[]{:S(2)}, u32[]{:S(2)}) collective-permute-start(bf16[2,128,512]{2,1,0:T(8,128)(2,1)S(1)} %pad_maximum_fusion.1.refs_0_), channel_id=1, source_target_pairs={{1,2},{3,4},{5,6},{7,0},{2,1},{4,3},{6,5},{0,7},{9,10},{11,12},{13... | collective-permute-start | bytes 786440 | tf_op jit(solution)/shard_map/fold/ppermute | solution.py:23
  100.5 1.9 collective-permute-start.14
  102.4 3.6 %collective-permute-done.10.refs_1_ = bf16[2,128,512]{2,1,0:T(8,128)(2,1)S(1)} collective-permute-done((bf16[2,128,512]{2,1,0:T(8,128)(2,1)S(1)}, bf16[2,128,512]{2,1,0:T(8,128)(2,1)S(1)}, u32[]{:S(2)}, u32[]{:S(2)}) %collective-permute-start.10) | collective-permute-done | bytes 262176 | tf_op jit(solution)/shard_map/fold/ppermute | solution.py:23
  106.0 1.9 collective-permute-start.11
  109.1 3.4 %collective-permute-start.15 = (bf16[2,128,512]{2,1,0:T(8,128)(2,1)S(1)}, bf16[2,128,512]{2,1,0:T(8,128)(2,1)S(1)}, u32[]{:S(2)}, u32[]{:S(2)}) collective-permute-start(bf16[2,128,512]{2,1,0:T(8,128)(2,1)S(1)} %collective-permute-done.14.refs_4_), channel_id=1, source_target_pairs={{1,2},{3,4},{5,6},{7,0},{2,1},{4,3},{6,5},{0,7},{9,10},{11,12},{13... | collective-permute-start | bytes 786440 | tf_op jit(solution)/shard_map/fold/ppermute | solution.py:23
  112.5 1.8 collective-permute-done.11.refs_2_
  114.2 4.3 %collective-permute-start.16 = (bf16[2,128,512]{2,1,0:T(8,128)(2,1)S(1)}, bf16[2,128,512]{2,1,0:T(8,128)(2,1)S(1)}, u32[]{:S(2)}, u32[]{:S(2)}) collective-permute-start(bf16[2,128,512]{2,1,0:T(8,128)(2,1)S(1)} %collective-permute-done.11.refs_2_), channel_id=1, source_target_pairs={{1,2},{3,4},{5,6},{7,0},{2,1},{4,3},{6,5},{0,7},{9,10},{11,12},{13... | collective-permute-start | bytes 786440 | tf_op jit(solution)/shard_map/fold/ppermute | solution.py:23
  118.5 1.9 collective-permute-start.17
  121.5 2.1 %collective-permute-done.16.refs_1_ = bf16[2,128,512]{2,1,0:T(8,128)(2,1)S(1)} collective-permute-done((bf16[2,128,512]{2,1,0:T(8,128)(2,1)S(1)}, bf16[2,128,512]{2,1,0:T(8,128)(2,1)S(1)}, u32[]{:S(2)}, u32[]{:S(2)}) %collective-permute-start.16) | collective-permute-done | bytes 262176 | tf_op jit(solution)/shard_map/fold/ppermute | solution.py:23
  123.6 2.3 %collective-permute-done.17.refs_2_ = bf16[2,128,512]{2,1,0:T(8,128)(2,1)S(1)} collective-permute-done((bf16[2,128,512]{2,1,0:T(8,128)(2,1)S(1)}, bf16[2,128,512]{2,1,0:T(8,128)(2,1)S(1)}, u32[]{:S(2)}, u32[]{:S(2)}) %collective-permute-start.17) | collective-permute-done | bytes 262176 | tf_op jit(solution)/shard_map/fold/ppermute | solution.py:23
  126.4 22.2 %all_to_all.10 = bf16[16,32,512]{2,1,0:T(8,128)(2,1)S(1)} all-to-all(bf16[16,32,512]{2,1,0:T(8,128)(2,1)S(1)} %bitcast.19), channel_id=1, replica_groups=mesh['x'=4,'zo'=3,'zi'=4,'core'=2,'feat'=8] {'x','zi'}, dimensions={0} | all-to-all | bytes 1048576 | tf_op jit(solution)/shard_map/sum_x_zi/all_to_all | solution.py:31
  148.7 24.2 %all_gather.6 = bf16[384,512]{1,0:T(8,128)(2,1)S(1)} all-gather(bf16[32,512]{1,0:T(8,128)(2,1)S(1)} %reduce_sum.44), channel_id=1, replica_groups=mesh['x'=4,'zo'=3,'zi'=4,'core'=2,'feat'=8] {'zo','zi'}, dimensions={0}, use_global_device_ids=true | all-gather | bytes 425984 | tf_op jit(solution)/shard_map/sum_z/all_gather | solution.py:40
  173.0 10.5 %all_gather.7 = bf16[512,512]{1,0:T(8,128)(2,1)S(1)} all-gather(bf16[128,512]{1,0:T(8,128)(2,1)S(1)} %reduce_sum.45), channel_id=1, replica_groups=mesh['x'=4,'zo'=3,'zi'=4,'core'=2,'feat'=8] {'x'}, dimensions={0}, use_global_device_ids=true | all-gather | bytes 655360 | tf_op jit(solution)/shard_map/gather_x/all_gather | solution.py:44
  183.5 11.6 %collective-permute-start.18 = (bf16[512,512]{1,0:T(8,128)(2,1)S(1)}, bf16[512,512]{1,0:T(8,128)(2,1)S(1)}, u32[]{:S(2)}, u32[]{:S(2)}) collective-permute-start(bf16[512,512]{1,0:T(8,128)(2,1)S(1)} %all_gather.7), channel_id=1, source_target_pairs={{0,8},{8,0},{1,9},{9,1},{2,10},{10,2},{3,11},{11,3},{4,12},{12,4},... | collective-permute-start | bytes 1572872 | tf_op jit(solution)/shard_map/gather_core/ppermute | solution.py:46
  (61 shorter events, 12.2 us)
Async XLA Ops:
  2.0 10.9 %copy-start.9 = (s32[8,4]{0,1:T(4,128)S(1)}, s32[8,4]{0,1:T(4,128)}, u32[]{:S(2)}) copy-start(s32[8,4]{0,1:T(4,128)} %param.9) | copy-start | bytes 388
  2.0 35.8 %copy-start = (bf16[8,4,128,128]{3,2,1,0:T(8,128)(2,1)S(1)}, bf16[8,4,128,128]{3,2,1,0:T(8,128)(2,1)}, u32[]{:S(2)}) copy-start(bf16[8,4,128,128]{3,2,1,0:T(8,128)(2,1)} %tiles_ref.3) | copy-start | bytes 3145732
  2.0 35.8 %copy-start.1 = (bf16[512,1024]{1,0:T(8,128)(2,1)S(1)}, bf16[512,1024]{1,0:T(8,128)(2,1)}, u32[]{:S(2)}) copy-start(bf16[512,1024]{1,0:T(8,128)(2,1)} %weight_ref.3) | copy-start | bytes 3145732
  2.0 35.8 %copy-start.6 = (s32[8]{0:T(128)S(1)}, s32[8]{0:T(128)}, u32[]{:S(2)}) copy-start(s32[8]{0:T(128)} %counts_ref.3) | copy-start | bytes 100
  5.2 32.5 %all-to-all-start = ((bf16[8,128,512]{2,1,0:T(8,128)(2,1)}), bf16[8,128,512]{2,1,0:T(8,128)(2,1)S(1)}, u32[]{:S(2)}, u32[]{:S(2)}) async-start(bf16[8,128,512]{2,1,0:T(8,128)(2,1)} %pick.1), calls=%async_computation | async-start | bytes 2097152 | tf_op jit(solution)/shard_map/pick/all_to_all | solution.py:201
  39.4 8.3 %collective-permute-start = (bf16[2,128,512]{2,1,0:T(8,128)(2,1)S(1)}, bf16[2,128,512]{2,1,0:T(8,128)(2,1)S(1)}, u32[]{:S(2)}, u32[]{:S(2)}) collective-permute-start(bf16[2,128,512]{2,1,0:T(8,128)(2,1)S(1)} %get-tuple-element.13), channel_id=1, source_target_pairs={{1,2},{3,4},{5,6},{7,0},{2,1},{4,3},{6,5},{0,7},{9,10},{11,12},{13... | collective-permute-start | bytes 786440 | tf_op jit(solution)/shard_map/preact/ppermute | solution.py:23
  41.4 9.8 %collective-permute-start.4 = (bf16[2,128,512]{2,1,0:T(8,128)(2,1)S(1)}, bf16[2,128,512]{2,1,0:T(8,128)(2,1)S(1)}, u32[]{:S(2)}, u32[]{:S(2)}) collective-permute-start(bf16[2,128,512]{2,1,0:T(8,128)(2,1)S(1)} %get-tuple-element.17), channel_id=1, source_target_pairs={{0,1},{2,3},{4,5},{6,7},{1,0},{3,2},{5,4},{7,6},{8,9},{10,11},{12,... | collective-permute-start | bytes 786440 | tf_op jit(solution)/shard_map/preact/ppermute | solution.py:23
  45.9 1.0 copy-start.2
  46.9 0.7 copy-start.4
  47.7 15.8 %copy-start.3 = (bf16[8,128,512]{2,1,0:T(8,128)(2,1)S(1)}, bf16[8,128,512]{2,1,0:T(8,128)(2,1)}, u32[]{:S(2)}) copy-start(bf16[8,128,512]{2,1,0:T(8,128)(2,1)} %copy-done.2) | copy-start | bytes 3145732
  47.8 25.0 %copy-start.5 = (bf16[2,128,512]{2,1,0:T(8,128)(2,1)S(1)}, bf16[2,128,512]{2,1,0:T(8,128)(2,1)}, u32[]{:S(2)}) copy-start(bf16[2,128,512]{2,1,0:T(8,128)(2,1)} %copy-done.4) | copy-start | bytes 786436
  47.8 8.8 %collective-permute-start.1 = (bf16[2,128,512]{2,1,0:T(8,128)(2,1)S(1)}, bf16[2,128,512]{2,1,0:T(8,128)(2,1)S(1)}, u32[]{:S(2)}, u32[]{:S(2)}) collective-permute-start(bf16[2,128,512]{2,1,0:T(8,128)(2,1)S(1)} %add_convert_fusion.3), channel_id=1, source_target_pairs={{0,1},{2,3},{4,5},{6,7},{1,0},{3,2},{5,4},{7,6},{8,9},{10,11},{12,... | collective-permute-start | bytes 786440 | tf_op jit(solution)/shard_map/preact/ppermute | solution.py:23
  51.2 10.3 %collective-permute-start.5 = (bf16[2,128,512]{2,1,0:T(8,128)(2,1)S(1)}, bf16[2,128,512]{2,1,0:T(8,128)(2,1)S(1)}, u32[]{:S(2)}, u32[]{:S(2)}) collective-permute-start(bf16[2,128,512]{2,1,0:T(8,128)(2,1)S(1)} %add_convert_fusion.1), channel_id=1, source_target_pairs={{1,2},{3,4},{5,6},{7,0},{2,1},{4,3},{6,5},{0,7},{9,10},{11,12},{13... | collective-permute-start | bytes 786440 | tf_op jit(solution)/shard_map/preact/ppermute | solution.py:23
  56.6 16.1 %collective-permute-start.2 = (bf16[2,128,512]{2,1,0:T(8,128)(2,1)S(1)}, bf16[2,128,512]{2,1,0:T(8,128)(2,1)S(1)}, u32[]{:S(2)}, u32[]{:S(2)}) collective-permute-start(bf16[2,128,512]{2,1,0:T(8,128)(2,1)S(1)} %add_convert_fusion.2), channel_id=1, source_target_pairs={{1,2},{3,4},{5,6},{7,0},{2,1},{4,3},{6,5},{0,7},{9,10},{11,12},{13... | collective-permute-start | bytes 786440 | tf_op jit(solution)/shard_map/preact/ppermute | solution.py:23
  61.6 15.0 %collective-permute-start.6 = (bf16[2,128,512]{2,1,0:T(8,128)(2,1)S(1)}, bf16[2,128,512]{2,1,0:T(8,128)(2,1)S(1)}, u32[]{:S(2)}, u32[]{:S(2)}) collective-permute-start(bf16[2,128,512]{2,1,0:T(8,128)(2,1)S(1)} %add_convert_fusion), channel_id=1, source_target_pairs={{0,1},{2,3},{4,5},{6,7},{1,0},{3,2},{5,4},{7,6},{8,9},{10,11},{12,... | collective-permute-start | bytes 786440 | tf_op jit(solution)/shard_map/preact/ppermute | solution.py:23
  63.6 20.9 %collective-permute-start.8 = (bf16[8,128,512]{2,1,0:T(8,128)(2,1)S(1)}, bf16[8,128,512]{2,1,0:T(8,128)(2,1)S(1)}, u32[]{:S(2)}, u32[]{:S(2)}) collective-permute-start(bf16[8,128,512]{2,1,0:T(8,128)(2,1)S(1)} %copy-done.3), channel_id=1, source_target_pairs={{0,8},{8,0},{1,9},{9,1},{2,10},{10,2},{3,11},{11,3},{4,12},{12,4},... | collective-permute-start | bytes 3145736 | tf_op jit(solution)/shard_map/aggregate/ppermute | solution.py:204
  72.8 12.0 %copy-start.7 = (bf16[128,1024]{1,0:T(8,128)(2,1)S(1)}, bf16[128,1024]{1,0:T(8,128)(2,1)}, u32[]{:S(2)}) copy-start(bf16[128,1024]{1,0:T(8,128)(2,1)} %param.13) | copy-start | bytes 786436
  72.8 8.5 %collective-permute-start.3 = (bf16[128,512]{1,0:T(8,128)(2,1)S(1)}, bf16[128,512]{1,0:T(8,128)(2,1)S(1)}, u32[]{:S(2)}, u32[]{:S(2)}) collective-permute-start(bf16[128,512]{1,0:T(8,128)(2,1)S(1)} %fusion.1), channel_id=1, source_target_pairs={{0,1},{2,3},{4,5},{6,7},{1,0},{3,2},{5,4},{7,6},{8,9},{10,11},{12,... | collective-permute-start | bytes 393224 | tf_op jit(solution)/shard_map/preact/ppermute | solution.py:23
  76.7 7.7 %collective-permute-start.7 = (bf16[128,512]{1,0:T(8,128)(2,1)S(1)}, bf16[128,512]{1,0:T(8,128)(2,1)S(1)}, u32[]{:S(2)}, u32[]{:S(2)}) collective-permute-start(bf16[128,512]{1,0:T(8,128)(2,1)S(1)} %fusion.2), channel_id=1, source_target_pairs={{1,2},{3,4},{5,6},{7,0},{2,1},{4,3},{6,5},{0,7},{9,10},{11,12},{13... | collective-permute-start | bytes 393224 | tf_op jit(solution)/shard_map/preact/ppermute | solution.py:23
  85.1 36.4 %copy-start.8 = (bf16[128,1024]{1,0:T(8,128)(2,1)}, bf16[128,1024]{1,0:T(8,128)(2,1)S(1)}, u32[]{:S(2)}) copy-start(bf16[128,1024]{1,0:T(8,128)(2,1)S(1)} %get-tuple-element.27) | copy-start | bytes 786436
  85.5 5.2 %collective-permute-start.12 = (bf16[128,512]{1,0:T(8,128)(2,1)S(1)}, bf16[128,512]{1,0:T(8,128)(2,1)S(1)}, u32[]{:S(2)}, u32[]{:S(2)}) collective-permute-start(bf16[128,512]{1,0:T(8,128)(2,1)S(1)} %get-tuple-element.32), channel_id=1, source_target_pairs={{0,8},{8,0},{1,9},{9,1},{2,10},{10,2},{3,11},{11,3},{4,12},{12,4},... | collective-permute-start | bytes 393224 | tf_op jit(solution)/shard_map/swap/ppermute | solution.py:222
  88.7 7.0 %collective-permute-start.9 = (bf16[128,512]{1,0:T(8,128)(2,1)S(1)}, bf16[128,512]{1,0:T(8,128)(2,1)S(1)}, u32[]{:S(2)}, u32[]{:S(2)}) collective-permute-start(bf16[128,512]{1,0:T(8,128)(2,1)S(1)} %get-tuple-element.33), channel_id=1, source_target_pairs={{0,1},{2,3},{4,5},{6,7},{1,0},{3,2},{5,4},{7,6},{8,9},{10,11},{12,... | collective-permute-start | bytes 393224 | tf_op jit(solution)/shard_map/fold/ppermute | solution.py:23
  90.7 9.7 %collective-permute-start.13 = (bf16[128,512]{1,0:T(8,128)(2,1)S(1)}, bf16[128,512]{1,0:T(8,128)(2,1)S(1)}, u32[]{:S(2)}, u32[]{:S(2)}) collective-permute-start(bf16[128,512]{1,0:T(8,128)(2,1)S(1)} %collective-permute-done.12), channel_id=1, source_target_pairs={{1,2},{3,4},{5,6},{7,0},{2,1},{4,3},{6,5},{0,7},{9,10},{11,12},{13... | collective-permute-start | bytes 393224 | tf_op jit(solution)/shard_map/fold/ppermute | solution.py:23
  95.8 10.1 %collective-permute-start.10 = (bf16[2,128,512]{2,1,0:T(8,128)(2,1)S(1)}, bf16[2,128,512]{2,1,0:T(8,128)(2,1)S(1)}, u32[]{:S(2)}, u32[]{:S(2)}) collective-permute-start(bf16[2,128,512]{2,1,0:T(8,128)(2,1)S(1)} %pad_maximum_fusion.1.refs_0_), channel_id=1, source_target_pairs={{1,2},{3,4},{5,6},{7,0},{2,1},{4,3},{6,5},{0,7},{9,10},{11,12},{13... | collective-permute-start | bytes 786440 | tf_op jit(solution)/shard_map/fold/ppermute | solution.py:23
  100.5 8.6 %collective-permute-start.14 = (bf16[2,128,512]{2,1,0:T(8,128)(2,1)S(1)}, bf16[2,128,512]{2,1,0:T(8,128)(2,1)S(1)}, u32[]{:S(2)}, u32[]{:S(2)}) collective-permute-start(bf16[2,128,512]{2,1,0:T(8,128)(2,1)S(1)} %pad_maximum_fusion.2.refs_3_), channel_id=1, source_target_pairs={{0,1},{2,3},{4,5},{6,7},{1,0},{3,2},{5,4},{7,6},{8,9},{10,11},{12,... | collective-permute-start | bytes 786440 | tf_op jit(solution)/shard_map/fold/ppermute | solution.py:23
  106.0 8.3 %collective-permute-start.11 = (bf16[2,128,512]{2,1,0:T(8,128)(2,1)S(1)}, bf16[2,128,512]{2,1,0:T(8,128)(2,1)S(1)}, u32[]{:S(2)}, u32[]{:S(2)}) collective-permute-start(bf16[2,128,512]{2,1,0:T(8,128)(2,1)S(1)} %collective-permute-done.10.refs_1_), channel_id=1, source_target_pairs={{0,1},{2,3},{4,5},{6,7},{1,0},{3,2},{5,4},{7,6},{8,9},{10,11},{12,... | collective-permute-start | bytes 786440 | tf_op jit(solution)/shard_map/fold/ppermute | solution.py:23
  109.1 9.4 %collective-permute-start.15 = (bf16[2,128,512]{2,1,0:T(8,128)(2,1)S(1)}, bf16[2,128,512]{2,1,0:T(8,128)(2,1)S(1)}, u32[]{:S(2)}, u32[]{:S(2)}) collective-permute-start(bf16[2,128,512]{2,1,0:T(8,128)(2,1)S(1)} %collective-permute-done.14.refs_4_), channel_id=1, source_target_pairs={{1,2},{3,4},{5,6},{7,0},{2,1},{4,3},{6,5},{0,7},{9,10},{11,12},{13... | collective-permute-start | bytes 786440 | tf_op jit(solution)/shard_map/fold/ppermute | solution.py:23
  114.2 9.4 %collective-permute-start.16 = (bf16[2,128,512]{2,1,0:T(8,128)(2,1)S(1)}, bf16[2,128,512]{2,1,0:T(8,128)(2,1)S(1)}, u32[]{:S(2)}, u32[]{:S(2)}) collective-permute-start(bf16[2,128,512]{2,1,0:T(8,128)(2,1)S(1)} %collective-permute-done.11.refs_2_), channel_id=1, source_target_pairs={{1,2},{3,4},{5,6},{7,0},{2,1},{4,3},{6,5},{0,7},{9,10},{11,12},{13... | collective-permute-start | bytes 786440 | tf_op jit(solution)/shard_map/fold/ppermute | solution.py:23
  118.5 7.4 %collective-permute-start.17 = (bf16[2,128,512]{2,1,0:T(8,128)(2,1)S(1)}, bf16[2,128,512]{2,1,0:T(8,128)(2,1)S(1)}, u32[]{:S(2)}, u32[]{:S(2)}) collective-permute-start(bf16[2,128,512]{2,1,0:T(8,128)(2,1)S(1)} %collective-permute-done.15.refs_5_), channel_id=1, source_target_pairs={{0,1},{2,3},{4,5},{6,7},{1,0},{3,2},{5,4},{7,6},{8,9},{10,11},{12,... | collective-permute-start | bytes 786440 | tf_op jit(solution)/shard_map/fold/ppermute | solution.py:23
  183.5 13.1 %collective-permute-start.18 = (bf16[512,512]{1,0:T(8,128)(2,1)S(1)}, bf16[512,512]{1,0:T(8,128)(2,1)S(1)}, u32[]{:S(2)}, u32[]{:S(2)}) collective-permute-start(bf16[512,512]{1,0:T(8,128)(2,1)S(1)} %all_gather.7), channel_id=1, source_target_pairs={{0,8},{8,0},{1,9},{9,1},{2,10},{10,2},{3,11},{11,3},{4,12},{12,4},... | collective-permute-start | bytes 1572872 | tf_op jit(solution)/shard_map/gather_core/ppermute | solution.py:46
